TPU v7x, 32 devices: a whole 2x2x4 slice. The times are simulated.
32 devices in a mesh: tm: 8 (over y, x, core), gz: 4 (over z).
Axes of the slice: x: 2, y: 2, z: 4, core: 2. Of those that a mesh axis runs over, the one named last changes fastest.
Arguments:
- state_rhs: float32 [32, 128, 2048], P('tm', 'gz'), may hold values from -6 to 6
- adjoint_rhs: float32 [32, 128, 2048], P('tm', 'gz'), may hold values from -6 to 6
- diffusivity: float32 [128, 2048], P('gz'), may hold values from 0.02 to 2
- velocity: float32 [3, 128, 2048], P(None, 'gz'), may hold values from -4 to 4
Outputs:
- state_out: float32 [32, 128, 2048], P('tm', 'gz')
- adjoint_out: float32 [32, 128, 2048], P('tm', 'gz')
All inputs are finite; a program needn't handle non-finite values.
Results may differ from a plain program's by a relative error of at most 0.0003.
Values sent between devices are 32-bit elements; how exact they have to be, the bound alone decides.
No kernel may reach another device: no remote copies, remote signals or barrier semaphores. Data moves between devices by JAX's collectives and lax.ppermute only.
A program may use at most 128 MiB of HBM per device.

v0:
```python
import math

import jax
import jax.numpy as jnp
from jax import lax
from jax.sharding import PartitionSpec as P

NY = 64


alpha_wrap = 0.1
beta_couple = 0.5
gamma_couple = 0.5


def padded(cells, sides, width):
    for axis, dim in sides:
        count = lax.axis_size(axis)
        ends = count - 1
        head = lax.slice_in_dim(cells, 0, width, axis=dim)
        tail = lax.slice_in_dim(cells, cells.shape[dim] - width, cells.shape[dim], axis=dim)
        cells = jnp.concatenate(
            [
                lax.ppermute(tail, axis, [(i, (i + 1) % count) for i in range(ends)]),
                cells,
                lax.ppermute(head, axis, [((i + 1) % count, i) for i in range(ends)]),
            ],
            axis=dim,
        )
    return cells


def swapped(value, axis, bit):
    mask = 2**bit
    pairs = [(source, source ^ mask) for source in range(lax.axis_size(axis))]
    return lax.ppermute(value, axis, pairs)


def ahead_flat(field, stride):
    pad_shape = field.shape[:-1] + (stride,)
    return jnp.concatenate([field[..., stride:], jnp.zeros(pad_shape, field.dtype)], axis=-1)


def behind_flat(field, stride):
    pad_shape = field.shape[:-1] + (stride,)
    return jnp.concatenate([jnp.zeros(pad_shape, field.dtype), field[..., :-stride]], axis=-1)


def neighbour_pairs(field, field_pad, width_y):
    column = jnp.arange(field.shape[-1], dtype=jnp.int32) % width_y
    nothing = jnp.zeros((), field.dtype)
    y_ahead = jnp.where(column == width_y - 1, nothing, ahead_flat(field, 1))
    y_behind = jnp.where(column == 0, nothing, behind_flat(field, 1))
    return [
        (field_pad[..., 2:, :], field_pad[..., :-2, :]),
        (ahead_flat(field, width_y), behind_flat(field, width_y)),
        (y_ahead, y_behind),
    ]


def face_weights(kappa, kappa_pad, width_y):
    pairs = neighbour_pairs(kappa, kappa_pad, width_y)
    weights = []
    diagonal = jnp.zeros_like(kappa)
    for ahead, behind in pairs:
        face_ahead = jnp.where(ahead > 0.0, 0.5 * (kappa + ahead), kappa)
        face_behind = jnp.where(behind > 0.0, 0.5 * (kappa + behind), kappa)
        weights.append((face_ahead, face_behind))
        diagonal = diagonal + face_ahead + face_behind
    return (weights, diagonal)


def coupling(field, field_pad, weights, velocity, width_y):
    sign = jnp.array([1.0, -1.0, 1.0, -1.0], field.dtype).reshape((4,) + (1,) * (field.ndim - 1))
    pairs = neighbour_pairs(field, field_pad, width_y)
    speeds = [velocity[2], velocity[0], velocity[1]]
    total = jnp.zeros_like(field)
    for index in range(3):
        ahead, behind = pairs[index]
        face_ahead, face_behind = weights[index]
        total = (
            total
            + face_ahead * ahead
            + face_behind * behind
            - sign * (0.5 * speeds[index]) * (ahead - behind)
        )
    return total


def apply_split(stacked, lam_real, lam_real_other, lam_imag, diagonal):
    shifted = lam_real + diagonal
    shifted_other = lam_real_other + diagonal
    determinant = shifted * shifted + lam_imag * lam_imag + beta_couple * gamma_couple
    determinant_other = (
        shifted_other * shifted_other + lam_imag * lam_imag + beta_couple * gamma_couple
    )
    state_real, adjoint_real, state_imag, adjoint_imag = (
        stacked[0],
        stacked[1],
        stacked[2],
        stacked[3],
    )
    out_state_real = (
        shifted * state_real + lam_imag * state_imag + beta_couple * adjoint_real
    ) / determinant
    out_state_imag = (
        shifted_other * state_imag - lam_imag * state_real + beta_couple * adjoint_imag
    ) / determinant_other
    out_adjoint_real = (
        shifted * adjoint_real - lam_imag * adjoint_imag - gamma_couple * state_real
    ) / determinant
    out_adjoint_imag = (
        shifted_other * adjoint_imag + lam_imag * adjoint_real - gamma_couple * state_imag
    ) / determinant_other
    return jnp.stack([out_state_real, out_adjoint_real, out_state_imag, out_adjoint_imag])


def mix_rows(matrix, data):
    return jnp.einsum("ab,sbm->sam", matrix, data, precision=lax.Precision.HIGHEST)


def body(state_rhs, adjoint_rhs, diffusivity, velocity):
    steps_local, depth, cells = state_rhs.shape
    ranks = lax.axis_size("tm")
    rank = lax.axis_index("tm")
    total = steps_local * ranks
    two_pi = 2.0 * math.pi
    ratio = alpha_wrap ** (1.0 / total)
    kappa_pad = padded(diffusivity, (("gz", 0),), 1)
    weights, diagonal = face_weights(diffusivity, kappa_pad, NY)
    fields = jnp.stack([state_rhs, adjoint_rhs])
    local_steps = jnp.arange(steps_local, dtype=jnp.int32)
    bits = ranks.bit_length() - 1
    times_here = rank * steps_local + local_steps
    damping = jnp.power(jnp.float32(alpha_wrap), times_here.astype(jnp.float32) / total)
    scaled = fields * damping[None, :, None, None]
    top = bits - 1
    partner = swapped(scaled, "tm", top)
    high = rank >> top & 1 == 1
    position = (rank & (1 << top) - 1).astype(jnp.float32)
    cosine = jnp.cos(math.pi * position / (1 << top))
    sine = jnp.sin(math.pi * position / (1 << top))
    spread = partner - scaled
    real_part = jnp.where(high, spread * cosine, scaled + partner)
    imag_part = jnp.where(high, -spread * sine, jnp.zeros_like(spread))
    data = jnp.concatenate([real_part, imag_part])
    for level in range(1, bits):
        bit = bits - 1 - level
        half = 1 << bit
        partner = swapped(data, "tm", bit)
        high = rank >> bit & 1 == 1
        position = (rank & half - 1).astype(jnp.float32)
        cosine = jnp.cos(math.pi * position / half)
        sine = jnp.sin(math.pi * position / half)
        spread = partner - data
        turned = jnp.concatenate(
            [spread[:2] * cosine + spread[2:] * sine, spread[2:] * cosine - spread[:2] * sine]
        )
        data = jnp.where(high, turned, data + partner)
    reversed_rank = jnp.zeros((), jnp.int32)
    for bit in range(bits):
        reversed_rank = reversed_rank + ((rank >> bit & 1) << bits - 1 - bit)
    frequency = reversed_rank + ranks * local_steps
    phase = (frequency[:, None] * local_steps[None, :] % total).astype(jnp.float32) * (
        two_pi / total
    )
    grid_real = jnp.cos(phase)
    grid_imag = -jnp.sin(phase)
    flat = data.reshape(4, steps_local, depth * cells)
    out_real = mix_rows(grid_real, flat[:2]) - mix_rows(grid_imag, flat[2:])
    out_imag = mix_rows(grid_real, flat[2:]) + mix_rows(grid_imag, flat[:2])
    blocks = jnp.concatenate([out_real, out_imag]).reshape(4, steps_local, depth, cells)
    angle = (frequency % total).astype(jnp.float32) * (two_pi / total)
    lam_real = (1.0 - ratio * jnp.cos(angle)).reshape(steps_local, 1, 1)
    lam_imag = (ratio * jnp.sin(angle)).reshape(steps_local, 1, 1)
    first = apply_split(blocks, lam_real, lam_real, lam_imag, diagonal)
    first_pad = padded(first, (("gz", 2),), 1)
    solved = apply_split(
        blocks + coupling(first, first_pad, weights, velocity, NY),
        lam_real,
        lam_real,
        lam_imag,
        diagonal,
    )
    phase = (local_steps[:, None] * frequency[None, :] % total).astype(jnp.float32) * (
        two_pi / total
    )
    grid_real = jnp.cos(phase)
    grid_imag = jnp.sin(phase)
    flat = solved.reshape(4, steps_local, depth * cells)
    back_real = mix_rows(grid_real, flat[:2]) - mix_rows(grid_imag, flat[2:])
    back_imag = mix_rows(grid_real, flat[2:]) + mix_rows(grid_imag, flat[:2])
    data = jnp.concatenate([back_real, back_imag]).reshape(4, steps_local, depth, cells)
    for bit in range(bits):
        half = 1 << bit
        partner = swapped(data, "tm", bit)
        high = rank >> bit & 1 == 1
        position = (rank & half - 1).astype(jnp.float32)
        cosine = jnp.cos(math.pi * position / half)
        sine = jnp.sin(math.pi * position / half)
        other = jnp.where(high, data, partner)
        base = jnp.where(high, partner, data)
        turned = jnp.concatenate(
            [other[:2] * cosine - other[2:] * sine, other[:2] * sine + other[2:] * cosine]
        )
        data = jnp.where(high, base - turned, base + turned)
    undo = jnp.power(jnp.float32(alpha_wrap), -times_here.astype(jnp.float32) / total) / total
    result = data[:2] * undo[None, :, None, None]
    return (result[0], result[1])


def solution(mesh):
    placed = (P("tm", "gz", None), P("tm", "gz", None), P("gz", None), P(None, "gz", None))
    return jax.shard_map(
        body,
        mesh=mesh,
        in_specs=placed,
        out_specs=(P("tm", "gz", None), P("tm", "gz", None)),
        check_vma=False,
    )
```

profile of v0, /device:TPU:0, one launch (start us, length us, event | category | flops | bytes accessed | tf_op | source)
XLA Modules:
  0.0 490.5 jit_solution(17700927046102706822)
XLA Ops:
  2.6 3.0 collective-permute-start.2
  5.8 45.6 %collective-permute-done.2 = f32[2,4,32,2048]{3,2,1,0:T(8,128)} collective-permute-done((f32[2,4,32,2048]{3,2,1,0:T(8,128)S(1)}, f32[2,4,32,2048]{3,2,1,0:T(8,128)}, u32[]{:S(2)}, u32[]{:S(2)}) %collective-permute-start.2) | collective-permute-done | bytes 2097184 | tf_op jit(solution)/shard_map/ppermute | solution.py:36
  58.4 90.2 %collective-permute-done.3 = f32[4,4,32,2048]{3,2,1,0:T(8,128)} collective-permute-done((f32[4,4,32,2048]{3,2,1,0:T(8,128)}, f32[4,4,32,2048]{3,2,1,0:T(8,128)}, u32[]{:S(2)}, u32[]{:S(2)}) %collective-permute-start.3) | collective-permute-done | bytes 4194336 | tf_op jit(solution)/shard_map/ppermute | solution.py:36
  148.6 3.6 fusion.108
  153.8 5.5 %maximum_select_fusion = f32[4,4,32,2048]{3,2,1,0:T(8,128)} fusion(f32[2,4,32,2048]{3,2,1,0:T(8,128)S(1)} %get-tuple-element.30, f32[2,4,32,2048]{3,2,1,0:T(8,128)S(1)} %get-tuple-element.29, f32[4,4,32,2048]{3,2,1,0:T(8,128)} %collective-permute-done.3, pred[]{:T(512)S(6)} %eq.33, f32[2,4,32,2048]{3,2,1,0:T(8,128)S(1)} %copy-done.2, ...), kind=kLoop, calls=%fused_computation.26 | loop fusion | flops 4194304 | bytes 16777216 | tf_op jit(solution)/shard_map/jit(_where)/select_n | solution.py:159
  159.3 3.5 collective-permute-start.1
  169.9 4.2 sub.130
  174.6 4.8 maximum_select_fusion.1
  181.6 3.0 slice.181
  184.6 3.7 slice.183
  188.3 4.0 fusion.55
  192.3 4.0 fusion.57
  196.3 4.2 fusion.2
  200.5 4.7 fusion.3
  205.3 3.0 pad_maximum_fusion.9
  208.5 2.8 fusion.6
  213.3 4.9 fusion.112
  218.1 3.5 collective-permute-start.6
  222.9 4.8 fusion.111
  227.7 6.2 %reshape.290 = f32[4,4,32,2048]{3,2,1,0:T(8,128)} reshape(f32[4,4,65536]{2,1,0:T(4,128)} %pad_maximum_fusion.9) | data formatting | bytes 8388608 | tf_op jit(solution)/shard_map/reshape | solution.py:172
  233.9 12.3 %subtract_add_fusion = f32[4,4,32,2048]{3,2,1,0:T(8,128)S(1)} fusion(f32[4,4,32,2048]{3,2,1,0:T(8,128)} %reshape.290, f32[4,4,32,2047]{3,2,1,0:T(8,128)} %get-tuple-element.24, f32[4,4,32,2047]{3,2,1,0:T(8,128)} %get-tuple-element.23, f32[4,4,32,1984]{3,2,1,0:T(8,128)} %get-tuple-element.22, f32[4,4,32,1984]{3,2,1,0:T(8,128)} %get-tuple-element.21, ...), kind=kLoop, calls=%fused_computation.35 | loop fusion | flops 32505856 | bytes 34078720 | tf_op jit(solution)/shard_map/add | solution.py:179
  249.9 2.7 slice.204
  252.6 4.9 fusion.51
  259.0 3.6 slice.203
  262.6 5.5 %fusion.53 = f32[2,65536,4]{1,2,0:T(4,128)S(1)} fusion(f32[2,4,65536]{2,1,0:T(4,128)} %slice.203, s32[4]{0:T(128)S(1)} %multiply_add_fusion.5), kind=kOutput, calls=%fused_computation.143 | convolution fusion | flops 25166048 | bytes 4194320 | tf_op jit(solution)/shard_map/ab,sbm->sam/dot_general | solution.py:119
  268.1 4.3 fusion
  272.4 4.1 fusion.1
  276.5 2.9 pad_maximum_fusion.11
  279.4 6.3 %reshape.291 = f32[4,4,32,2048]{3,2,1,0:T(8,128)} reshape(f32[4,4,65536]{2,1,0:T(4,128)} %pad_maximum_fusion.11) | data formatting | bytes 8388608 | tf_op jit(solution)/shard_map/reshape | solution.py:193
  285.8 7.4 %collective-permute-done.7 = f32[4,4,32,2048]{3,2,1,0:T(8,128)S(1)} collective-permute-done((f32[4,4,32,2048]{3,2,1,0:T(8,128)}, f32[4,4,32,2048]{3,2,1,0:T(8,128)S(1)}, u32[]{:S(2)}, u32[]{:S(2)}) %collective-permute-start.7) | collective-permute-done | bytes 4194336 | tf_op jit(solution)/shard_map/ppermute | solution.py:36
  299.6 90.6 %collective-permute-done.8 = f32[4,4,32,2048]{3,2,1,0:T(8,128)S(1)} collective-permute-done((f32[4,4,32,2048]{3,2,1,0:T(8,128)S(1)}, f32[4,4,32,2048]{3,2,1,0:T(8,128)S(1)}, u32[]{:S(2)}, u32[]{:S(2)}) %collective-permute-start.8) | collective-permute-done | bytes 4194336 | tf_op jit(solution)/shard_map/ppermute | solution.py:36
  394.9 91.7 %collective-permute-done.9 = f32[4,4,32,2048]{3,2,1,0:T(8,128)S(1)} collective-permute-done((f32[4,4,32,2048]{3,2,1,0:T(8,128)S(1)}, f32[4,4,32,2048]{3,2,1,0:T(8,128)S(1)}, u32[]{:S(2)}, u32[]{:S(2)}) %collective-permute-start.9) | collective-permute-done | bytes 4194336 | tf_op jit(solution)/shard_map/ppermute | solution.py:36
  (79 shorter events, 43.4 us)
Async XLA Ops:
  0.6 50.7 %copy-start.8 = (f32[4,32,2048]{2,1,0:T(8,128)S(1)}, f32[4,32,2048]{2,1,0:T(8,128)}, u32[]{:S(2)}) copy-start(f32[4,32,2048]{2,1,0:T(8,128)} %param.6) | copy-start | bytes 3145732
  2.6 48.8 %collective-permute-start.2 = (f32[2,4,32,2048]{3,2,1,0:T(8,128)S(1)}, f32[2,4,32,2048]{3,2,1,0:T(8,128)}, u32[]{:S(2)}, u32[]{:S(2)}) collective-permute-start(f32[2,4,32,2048]{3,2,1,0:T(8,128)S(1)} %maximum_multiply_fusion), channel_id=1, source_target_pairs={{0,16},{4,20},{8,24},{12,28},{16,0},{20,4},{24,8},{28,12},{1,17},{... | collective-permute-start | bytes 6291464 | tf_op jit(solution)/shard_map/ppermute | solution.py:36
  53.8 2.6 copy-start.1
  56.5 92.1 %collective-permute-start.3 = (f32[4,4,32,2048]{3,2,1,0:T(8,128)}, f32[4,4,32,2048]{3,2,1,0:T(8,128)}, u32[]{:S(2)}, u32[]{:S(2)}) collective-permute-start(f32[4,4,32,2048]{3,2,1,0:T(8,128)} %pad_maximum_fusion.8), channel_id=1, source_target_pairs={{0,8},{4,12},{8,0},{12,4},{16,24},{20,28},{24,16},{28,20},{1,9},{5... | collective-permute-start | bytes 12582920 | tf_op jit(solution)/shard_map/ppermute | solution.py:36
  152.2 1.6 copy-start.2
  153.8 5.5 %copy-start.7 = (f32[32,2048]{1,0:T(8,128)S(1)}, f32[32,2048]{1,0:T(8,128)}, u32[]{:S(2)}) copy-start(f32[32,2048]{1,0:T(8,128)} %param.7) | copy-start | bytes 786436
  159.3 5.3 %copy-start.10 = (f32[3,32,2048]{2,1,0:T(8,128)S(1)}, f32[3,32,2048]{2,1,0:T(8,128)}, u32[]{:S(2)}) copy-start(f32[3,32,2048]{2,1,0:T(8,128)} %param.8) | copy-start | bytes 2359300
  159.3 5.3 %copy-start.15 = (f32[4]{0:T(128)S(1)}, f32[4]{0:T(128)}, u32[]{:S(2)}) copy-start(f32[4]{0:T(128)} %constant.103.clone) | copy-start | bytes 52
  159.3 10.6 %collective-permute-start.4 = (f32[4,4,32,2048]{3,2,1,0:T(8,128)}, f32[4,4,32,2048]{3,2,1,0:T(8,128)}, u32[]{:S(2)}, u32[]{:S(2)}) collective-permute-start(f32[4,4,32,2048]{3,2,1,0:T(8,128)} %maximum_select_fusion), channel_id=1, source_target_pairs={{0,4},{4,0},{8,12},{12,8},{16,20},{20,16},{24,28},{28,24},{1,5},{5... | collective-permute-start | bytes 12582920 | tf_op jit(solution)/shard_map/ppermute | solution.py:36
  159.3 7.2 %collective-permute-start.1 = (f32[1,2048]{1,0:T(1,128)S(1)}, f32[1,2048]{1,0:T(1,128)S(1)}, u32[]{:S(2)}, u32[]{:S(2)}) collective-permute-start(f32[1,2048]{1,0:T(1,128)S(1)} %get-tuple-element.51), channel_id=1, source_target_pairs={{0,1},{1,2},{2,3},{4,5},{5,6},{6,7},{8,9},{9,10},{10,11},{12,13},{... | collective-permute-start | bytes 24584 | tf_op jit(solution)/shard_map/ppermute | solution.py:24
  162.9 5.5 %collective-permute-start = (f32[1,2048]{1,0:T(1,128)S(1)}, f32[1,2048]{1,0:T(1,128)S(1)}, u32[]{:S(2)}, u32[]{:S(2)}) collective-permute-start(f32[1,2048]{1,0:T(1,128)S(1)} %get-tuple-element.50), channel_id=1, source_target_pairs={{1,0},{2,1},{3,2},{5,4},{6,5},{7,6},{9,8},{10,9},{11,10},{13,12},{... | collective-permute-start | bytes 24584 | tf_op jit(solution)/shard_map/ppermute | solution.py:26
  164.3 44.2 %copy-start.11 = (f32[4]{0:T(128)}, f32[4]{0:T(128)S(1)}, u32[]{:S(2)}) copy-start(f32[4]{0:T(128)S(1)} %get-tuple-element.56) | copy-start | bytes 52
  166.5 41.9 %copy-start.13 = (f32[4]{0:T(128)}, f32[4]{0:T(128)S(1)}, u32[]{:S(2)}) copy-start(f32[4]{0:T(128)S(1)} %fusion.107) | copy-start | bytes 52
  188.3 4.0 copy-start.3
  211.3 1.0 copy-start.5
  218.1 15.8 %collective-permute-start.6 = (f32[4,4,1,2048]{3,2,1,0:T(1,128)}, f32[4,4,1,2048]{3,2,1,0:T(1,128)S(1)}, u32[]{:S(2)}, u32[]{:S(2)}) collective-permute-start(f32[4,4,1,2048]{3,2,1,0:T(1,128)} %get-tuple-element.20), channel_id=1, source_target_pairs={{0,1},{1,2},{2,3},{4,5},{5,6},{6,7},{8,9},{9,10},{10,11},{12,13},{... | collective-permute-start | bytes 393224 | tf_op jit(solution)/shard_map/ppermute | solution.py:24
  221.6 12.3 %collective-permute-start.5 = (f32[4,4,1,2048]{3,2,1,0:T(1,128)}, f32[4,4,1,2048]{3,2,1,0:T(1,128)}, u32[]{:S(2)}, u32[]{:S(2)}) collective-permute-start(f32[4,4,1,2048]{3,2,1,0:T(1,128)} %get-tuple-element.19), channel_id=1, source_target_pairs={{1,0},{2,1},{3,2},{5,4},{6,5},{7,6},{9,8},{10,9},{11,10},{13,12},{... | collective-permute-start | bytes 393224 | tf_op jit(solution)/shard_map/ppermute | solution.py:26
  233.9 12.3 %copy-start.12 = (f32[4]{0:T(128)S(1)}, f32[4]{0:T(128)}, u32[]{:S(2)}) copy-start(f32[4]{0:T(128)} %copy-done.11) | copy-start | bytes 52
  233.9 12.3 %copy-start.14 = (f32[4]{0:T(128)S(1)}, f32[4]{0:T(128)}, u32[]{:S(2)}) copy-start(f32[4]{0:T(128)} %copy-done.13) | copy-start | bytes 52
  252.6 4.9 %copy-start.9 = (f32[1,4,32,2048]{3,2,1,0:T(8,128)S(1)}, f32[1,4,32,2048]{3,2,1,0:T(8,128)}, u32[]{:S(2)}) copy-start(f32[1,4,32,2048]{3,2,1,0:T(8,128)} %get-tuple-element.10) | copy-start | bytes 3145732
  262.6 5.5 %copy-start.4 = (f32[2,4,65536]{2,1,0:T(4,128)S(1)}, f32[2,4,65536]{2,1,0:T(4,128)}, u32[]{:S(2)}) copy-start(f32[2,4,65536]{2,1,0:T(4,128)} %slice.203) | copy-start | bytes 6291460
  262.6 5.5 %copy-start.6 = (f32[2,65536,4]{1,2,0:T(4,128)S(1)}, f32[2,65536,4]{1,2,0:T(4,128)}, u32[]{:S(2)}) copy-start(f32[2,65536,4]{1,2,0:T(4,128)} %fusion.51) | copy-start | bytes 6291460
  285.8 7.4 %collective-permute-start.7 = (f32[4,4,32,2048]{3,2,1,0:T(8,128)}, f32[4,4,32,2048]{3,2,1,0:T(8,128)S(1)}, u32[]{:S(2)}, u32[]{:S(2)}) collective-permute-start(f32[4,4,32,2048]{3,2,1,0:T(8,128)} %reshape.291), channel_id=1, source_target_pairs={{0,4},{4,0},{8,12},{12,8},{16,20},{20,16},{24,28},{28,24},{1,5},{5... | collective-permute-start | bytes 12582920 | tf_op jit(solution)/shard_map/ppermute | solution.py:36
  294.0 2.2 copy-start
  298.0 92.1 %collective-permute-start.8 = (f32[4,4,32,2048]{3,2,1,0:T(8,128)S(1)}, f32[4,4,32,2048]{3,2,1,0:T(8,128)S(1)}, u32[]{:S(2)}, u32[]{:S(2)}) collective-permute-start(f32[4,4,32,2048]{3,2,1,0:T(8,128)S(1)} %add_select_fusion.1), channel_id=1, source_target_pairs={{0,8},{4,12},{8,0},{12,4},{16,24},{20,28},{24,16},{28,20},{1,9},{5... | collective-permute-start | bytes 12582920 | tf_op jit(solution)/shard_map/ppermute | solution.py:36
  393.3 93.3 %collective-permute-start.9 = (f32[4,4,32,2048]{3,2,1,0:T(8,128)S(1)}, f32[4,4,32,2048]{3,2,1,0:T(8,128)S(1)}, u32[]{:S(2)}, u32[]{:S(2)}) collective-permute-start(f32[4,4,32,2048]{3,2,1,0:T(8,128)S(1)} %add_select_fusion), channel_id=1, source_target_pairs={{0,16},{4,20},{8,24},{12,28},{16,0},{20,4},{24,8},{28,12},{1,17},{... | collective-permute-start | bytes 12582920 | tf_op jit(solution)/shard_map/ppermute | solution.py:36
where the time goes:
time: 497 us; the launch traced here: 490 us
  waiting for transfers between devices  327 us (66%)
  other arithmetic  66.2 us (13%)
  local copies, waits for them, and re-layouts  42.1 us (8%)
  matrix products  35.6 us (7%)
  starting transfers between devices  17.5 us (4%)
    ppermute x6, waiting for transfers between devices, swapped(): return lax.ppermute(value, axis, pairs)  325 us
    dot_general x8, matrix products, mix_rows(): jnp.einsum('ab,sbm->sam', matrix, data, precision=lax.Precision.HIGHEST)  35.6 us
    add x1, other arithmetic, body(): blocks + coupling(first, first_pad, weights, velocity, NY)  12.3 us
    select_n x2, other arithmetic, body(): data = jnp.where(high, turned, data + partner)  10.3 us
  transfers between devices with their start and end apart: 10, of which 6 were waited for; matrix products, arithmetic and copies ran while one was open for 3% of the time, Pallas kernels for 0%

commit v1 on v0

v1 whole, which is shorter than its diff:
```python
import functools
import math

import jax
import jax.numpy as jnp
from jax import lax
from jax.experimental import pallas as pl
from jax.experimental.pallas import tpu as pltpu
from jax.sharding import PartitionSpec as P

NY = 64
LANES = 128

alpha_wrap = 0.1
beta_couple = 0.5
gamma_couple = 0.5


def this_core():
    return lax.rem(lax.axis_index("tm"), 2)


def this_chip():
    return lax.div(lax.axis_index("tm"), 2)


def lane_block(start):
    return pl.ds(pl.multiple_of(start, LANES), LANES)


def power(value, count):
    result = None
    while count:
        if count & 1:
            result = value if result is None else result * value
        count >>= 1
        if count:
            value = value * value
    return result


def step_scale(ratio, steps, chips, sign):
    chip = this_chip()
    base = jnp.float32(1.0)
    bit = 0
    while 1 << bit < chips:
        factor = ratio ** (sign * steps * (1 << bit))
        base = base * jnp.where(lax.rem(lax.div(chip, 1 << bit), 2) == 1, factor, 1.0)
        bit += 1
    return [base * (ratio ** (sign * step)) for step in range(steps)]


def side_values(field, left, right, before, after):
    rows = field.shape[0]
    lane = lax.broadcasted_iota(jnp.int32, field.shape, 1)
    row = lax.broadcasted_iota(jnp.int32, field.shape, 0)
    z_ahead = jnp.where(row == rows - 1, after, pltpu.roll(field, rows - 1, 0))
    z_behind = jnp.where(row == 0, before, pltpu.roll(field, 1, 0))
    turned = pltpu.roll(field, NY, 1)
    x_ahead = jnp.where(lane < NY, turned, pltpu.roll(right, NY, 1))
    x_behind = jnp.where(lane < NY, pltpu.roll(left, NY, 1), turned)
    y_ahead = pltpu.roll(field, LANES - 1, 1)
    y_behind = pltpu.roll(field, 1, 1)
    return ((z_ahead, z_behind), (x_ahead, x_behind), (y_ahead, y_behind))


def faces(kappa_ref, outer_ref, group, half):
    core = this_core()
    groups = kappa_ref.shape[1] // LANES
    own = pl.ds(pl.multiple_of(core * half, 8), half)
    here = lane_block(group * LANES)
    kappa = kappa_ref[own, here]
    left = kappa_ref[own, lane_block(jnp.maximum(group - 1, 0) * LANES)]
    right = kappa_ref[own, lane_block(jnp.minimum(group + 1, groups - 1) * LANES)]
    outer = outer_ref[0:1, here]
    before = jnp.where(core == 0, outer, kappa_ref[half - 1 : half, here])
    after = jnp.where(core == 0, kappa_ref[half : half + 1, here], outer)
    pairs = side_values(kappa, left, right, before, after)
    lane = lax.broadcasted_iota(jnp.int32, kappa.shape, 1)
    column = lax.rem(lane, NY)
    inside = (
        (pairs[0][0] > 0.0, pairs[0][1] > 0.0),
        (
            jnp.logical_or(lane < NY, group < groups - 1),
            jnp.logical_or(lane >= NY, group > 0),
        ),
        (column < NY - 1, column > 0),
    )
    weights = [
        [jnp.where(ok, 0.5 * (kappa + value), kappa) for ok, value in zip(oks, values)]
        for oks, values in zip(inside, pairs)
    ]
    return weights, inside


def cell_factors(diagonal, ratio):
    shifted = 1.0 + diagonal
    lifted = shifted * shifted - (ratio * ratio + beta_couple * gamma_couple)
    mix = shifted / (lifted + jnp.sqrt(lifted * lifted + shifted * shifted))
    inverse = 1.0 / (shifted + 0.5 * mix)
    return ratio * inverse, inverse, mix * inverse, 1.0 / shifted


def ordered(own, other, step, steps_local):
    mine = this_core() == step // steps_local
    index = step % steps_local
    return jnp.where(mine, own(index), other(index))


def local_ends(values, decay, inverse, mixed, upright, steps):
    back = None
    last = None
    weight = None
    for step in reversed(range(steps)):
        state, adjoint = values(step)
        drive = inverse * adjoint - mixed * state
        back = drive if back is None else decay * back + drive
        term = state + 0.5 * back
        last = term if last is None else last + weight * term
        weight = decay if weight is None else weight * decay
    return back, last * upright


def solve_steps(values, decay, inverse, mixed, upright, ratio, back_in, state_in, steps, put):
    backs = [None] * steps
    back = back_in
    for step in reversed(range(steps)):
        state, adjoint = values(step)
        back = decay * back + (inverse * adjoint - mixed * state)
        backs[step] = back
    gain = ratio * mixed
    half_up = 0.5 * upright
    previous = state_in
    for step in range(steps):
        state, _ = values(step)
        current = decay * previous + (upright * state + half_up * backs[step])
        put(step, current, backs[step] - gain * previous)
        previous = current


def first_kernel(ratio, steps_local, chips, own_s, own_a, other_s, other_a, kappa_ref, outer_ref, factor_ref, near_ref, far_ref):
    steps = 2 * steps_local
    half = own_s.shape[1]
    tile = half // 2
    groups = own_s.shape[2] // LANES
    scales = step_scale(ratio, steps, chips, 1)

    def one(index, carry):
        here = lane_block(index * LANES)
        weights, _ = faces(kappa_ref, outer_ref, pl.program_id(0) * groups + index, half)
        diagonal = weights[0][0] + weights[0][1]
        diagonal = diagonal + weights[1][0] + weights[1][1]
        diagonal = diagonal + weights[2][0] + weights[2][1]
        decay, inverse, mixed, upright = cell_factors(diagonal, ratio)
        for slot, value in enumerate((decay, inverse, mixed, upright)):
            factor_ref[slot, :, here] = value

        def values(step):
            return (
                ordered(lambda i: own_s[i, :, here], lambda i: other_s[i, :, here], step, steps_local) * scales[step],
                ordered(lambda i: own_a[i, :, here], lambda i: other_a[i, :, here], step, steps_local) * scales[step],
            )

        back, last = local_ends(values, decay, inverse, mixed, upright, steps)
        near_ref[0, :, here] = back[:tile]
        near_ref[1, :, here] = last[:tile]
        far_ref[0, :, here] = back[tile:]
        far_ref[1, :, here] = last[tile:]
        return carry

    lax.fori_loop(0, groups, one, 0)


def ring_factors(factors, steps, chips):
    decay, _, _, upright = factors
    block = power(decay, steps)
    square = decay * decay
    response = (0.5 * upright) * decay * (1.0 - block * block) / (1.0 - square)
    closing = 1.0 / (1.0 - power(block, chips))
    return block, response, closing


def contribution(ends, offset, block, response, closing):
    back, last = ends
    square = block * block
    if offset == 0:
        up, down, cross = square * block, square * block, 1.0 + square + square * square * (1.0 + square)
    elif offset == 1:
        up, down, cross = None, square, block * (1.0 + square) * (1.0 + square)
    elif offset == 2:
        up, down, cross = block, block, 2.0 * square * (1.0 + square)
    else:
        up, down, cross = square, None, block * (1.0 + square) * (1.0 + square)
    entering_back = back if up is None else up * back
    entering_state = last if down is None else down * last
    entering_state = entering_state + (cross * response * closing) * back
    return closing * entering_back, closing * entering_state


def either(flag, one, other):
    return tuple(jnp.where(flag, a, b) for a, b in zip(one, other))


def relay_kernel(steps, factor_ref, near_ref, near_in, far_ref, far_in, near_out, far_out):
    tile, cells = near_ref.shape[1:]
    odd = lax.rem(this_chip(), 2) == 1

    def one(index, carry):
        here = lane_block(index * LANES)
        for rows, mine, theirs, out, first in (
            (slice(0, tile), near_ref, near_in, near_out, True),
            (slice(tile, 2 * tile), far_ref, far_in, far_out, False),
        ):
            factors = [factor_ref[slot, rows, here] for slot in range(4)]
            ring = ring_factors(factors, steps, 4)
            a = (mine[0, :, here], mine[1, :, here])
            b = (theirs[0, :, here], theirs[1, :, here])
            if first:
                one_part = contribution(a, 2, *ring)
                other_part = either(odd, contribution(b, 1, *ring), contribution(b, 3, *ring))
            else:
                one_part = either(odd, contribution(a, 1, *ring), contribution(a, 3, *ring))
                other_part = either(odd, contribution(b, 3, *ring), contribution(b, 1, *ring))
            out[0, :, here] = one_part[0] + other_part[0]
            out[1, :, here] = one_part[1] + other_part[1]
        return carry

    lax.fori_loop(0, cells // LANES, one, 0)


def entering(factors, near, near_in, near_tail, far, far_in, far_tail, here, tile, steps):
    odd = lax.rem(this_chip(), 2) == 1
    backs, states = [], []
    for rows, mine, theirs, tail, first in (
        (slice(0, tile), near, near_in, near_tail, True),
        (slice(tile, 2 * tile), far, far_in, far_tail, False),
    ):
        ring = ring_factors([f[rows] for f in factors], steps, 4)
        a = (mine[0, :, here], mine[1, :, here])
        b = (theirs[0, :, here], theirs[1, :, here])
        own = contribution(a, 0, *ring)
        if first:
            near_by = either(odd, contribution(b, 3, *ring), contribution(b, 1, *ring))
        else:
            near_by = contribution(b, 2, *ring)
        backs.append(own[0] + near_by[0] + tail[0, :, here])
        states.append(own[1] + near_by[1] + tail[1, :, here])
    return jnp.concatenate(backs, axis=0), jnp.concatenate(states, axis=0)


def sweep_kernel(ratio, steps_local, chips, own_s, own_a, other_s, other_a, factor_ref, *rest):
    *ends, first_ref, edge_ref, inner_ref = rest
    steps = 2 * steps_local
    half = own_s.shape[1]
    groups = own_s.shape[2] // LANES
    scales = step_scale(ratio, steps, chips, 1)
    core = this_core()

    def one(index, carry):
        here = lane_block(index * LANES)
        factors = [factor_ref[slot, :, here] for slot in range(4)]

        def values(step):
            return (
                ordered(lambda i: own_s[i, :, here], lambda i: other_s[i, :, here], step, steps_local) * scales[step],
                ordered(lambda i: own_a[i, :, here], lambda i: other_a[i, :, here], step, steps_local) * scales[step],
            )

        back_in, state_in = enter_values(ends, factors, here, half, steps)

        def put(step, state, adjoint):
            for field, value in enumerate((state, adjoint)):
                slot = 2 * step + field
                first_ref[slot, :, here] = value
                head, tail = value[0:1], value[half - 1 : half]
                edge_ref[slot : slot + 1, here] = jnp.where(core == 0, head, tail)
                inner_ref[slot : slot + 1, here] = jnp.where(core == 0, tail, head)

        solve_steps(values, *factors, ratio, back_in, state_in, steps, put)
        return carry

    lax.fori_loop(0, groups, one, 0)


def enter_values(ends, factors, here, half, steps):
    if len(ends) == 1:
        return ends[0][0, :, here], ends[0][1, :, here]
    return entering(factors, *ends, here, half // 2, steps)


def coupling_kernel(ratio, steps, first_ref, outer_ref, inner_ref, kappa_ref, outer_kappa, velocity_ref, factor_ref, coupled_ref, near_ref, far_ref):
    half = first_ref.shape[1]
    tile = half // 2
    groups = coupled_ref.shape[2] // LANES
    total = first_ref.shape[2] // LANES
    core = this_core()

    def one(index, carry):
        here = lane_block(index * LANES)
        group = pl.program_id(0) * groups + index
        there = lane_block(group * LANES)
        left = lane_block(jnp.maximum(group - 1, 0) * LANES)
        right = lane_block(jnp.minimum(group + 1, total - 1) * LANES)
        weights, inside = faces(kappa_ref, outer_kappa, group, half)
        own = pl.ds(pl.multiple_of(core * half, 8), half)
        tables = ([], [])
        for direction, component in enumerate((2, 0, 1)):
            drift = 0.5 * velocity_ref[component, :, here]
            ahead, behind = weights[direction]
            ok_ahead, ok_behind = inside[direction]
            for field, sign in enumerate((1.0, -1.0)):
                tables[field].append(
                    (
                        jnp.where(ok_ahead, ahead - sign * drift, 0.0),
                        jnp.where(ok_behind, behind + sign * drift, 0.0),
                    )
                )
        decay, inverse, mixed, upright = [factor_ref[slot, :, here] for slot in range(4)]

        def values(step):
            results = []
            for field in range(2):
                slot = 2 * step + field
                outer = outer_ref[slot : slot + 1, there]
                inner = inner_ref[slot : slot + 1, there]
                before = jnp.where(core == 0, outer, inner)
                after = jnp.where(core == 0, inner, outer)
                pairs = side_values(first_ref[slot, :, there], first_ref[slot, :, left], first_ref[slot, :, right], before, after)
                result = None
                for (ahead, behind), (c_ahead, c_behind) in zip(pairs, tables[field]):
                    term = c_ahead * ahead + c_behind * behind
                    result = term if result is None else result + term
                coupled_ref[slot, :, here] = result
                results.append(result)
            return results

        back, last = local_ends(values, decay, inverse, mixed, upright, steps)
        near_ref[0, :, here] = back[:tile]
        near_ref[1, :, here] = last[:tile]
        far_ref[0, :, here] = back[tile:]
        far_ref[1, :, here] = last[tile:]
        return carry

    lax.fori_loop(0, groups, one, 0)


def last_kernel(ratio, steps_local, chips, coupled_ref, first_ref, factor_ref, *rest):
    *ends, keep_ref, send_ref = rest
    steps = 2 * steps_local
    half = first_ref.shape[1]
    groups = first_ref.shape[2] // LANES
    scales = step_scale(ratio, steps, chips, -1)
    core = this_core()

    def one(index, carry):
        here = lane_block(index * LANES)
        factors = [factor_ref[slot, :, here] for slot in range(4)]

        def values(step):
            return coupled_ref[2 * step, :, here], coupled_ref[2 * step + 1, :, here]

        back_in, state_in = enter_values(ends, factors, here, half, steps)
        pending = {}

        def put(step, state, adjoint):
            for field, value in enumerate((state, adjoint)):
                done = (first_ref[2 * step + field, :, here] + value) * scales[step]
                if step < steps_local:
                    pending[step, field] = done
                else:
                    early = pending[step - steps_local, field]
                    slot = step - steps_local
                    keep_ref[field, slot, :, here] = jnp.where(core == 0, early, done)
                    send_ref[field, slot, :, here] = jnp.where(core == 0, done, early)

        solve_steps(values, *factors, ratio, back_in, state_in, steps, put)
        return carry

    lax.fori_loop(0, groups, one, 0)


def body(state_rhs, adjoint_rhs, diffusivity, velocity):
    steps_local, depth, cells = state_rhs.shape
    ranks = lax.axis_size("tm")
    slabs = lax.axis_size("gz")
    chips = ranks // 2
    total = steps_local * ranks
    steps = 2 * steps_local
    half = depth // 2
    tile = half // 2
    ratio = alpha_wrap ** (1.0 / total)
    core = this_core()
    f32 = jnp.float32

    def partner(value, mask):
        return lax.ppermute(value, "tm", [(i, i ^ mask) for i in range(ranks)])

    outward = []
    for t in range(ranks):
        for g in range(slabs):
            to = g - 1 if t % 2 == 0 else g + 1
            if 0 <= to < slabs:
                outward.append((t * slabs + g, (t ^ 1) * slabs + to))

    def across(value):
        return lax.ppermute(value, ("tm", "gz"), outward)

    other_s = partner(state_rhs, 1)
    other_a = partner(adjoint_rhs, 1)
    outer_kappa = across(jnp.where(core == 0, diffusivity[:1], diffusivity[depth - 1 :]))

    width = 512
    blocks = cells // width
    raw = pl.BlockSpec((steps_local, half, width), lambda i: (0, this_core(), i))
    whole = lambda *shape: pl.BlockSpec(shape, lambda i: (0,) * len(shape))
    strip = lambda *shape: pl.BlockSpec(shape + (width,), lambda i: (0,) * len(shape) + (i,))
    params = pltpu.CompilerParams(vmem_limit_bytes=48 * 1024 * 1024)
    shape = lambda *s: jax.ShapeDtypeStruct(s, f32)
    ends_shape = [shape(2, tile, cells)] * 2
    ends_spec = [strip(2, tile)] * 2

    factors, near, far = pl.pallas_call(
        functools.partial(first_kernel, ratio, steps_local, chips),
        grid=(blocks,),
        in_specs=[raw] * 4 + [whole(depth, cells), whole(1, cells)],
        out_specs=[strip(4, half)] + ends_spec,
        out_shape=[shape(4, half, cells)] + ends_shape,
        compiler_params=params,
        name="ends_of_first",
    )(state_rhs, adjoint_rhs, other_s, other_a, diffusivity, outer_kappa)

    def exchange(near, far):
        if chips != 4:
            gathered = lax.all_gather(jnp.concatenate([near, far], axis=1), "tm")
            gathered = lax.dynamic_index_in_dim(
                gathered.reshape((chips, 2) + gathered.shape[1:]), core, 1, keepdims=False
            )
            block, response, closing = ring_factors([factors[i] for i in range(4)], steps, chips)
            at = lambda array, index: lax.dynamic_index_in_dim(array, lax.rem(index + 2 * chips, chips), 0, keepdims=False)
            chip = this_chip()

            def entering_back(where):
                value = jnp.zeros((half, cells), f32)
                for offset in reversed(range(chips)):
                    value = block * value + at(gathered[:, 0], where + 1 + offset)
                return value * closing

            value = jnp.zeros((half, cells), f32)
            for offset in reversed(range(chips)):
                source = chip - 1 - offset
                value = block * value + at(gathered[:, 1], source) + response * entering_back(source)
            return [jnp.stack([entering_back(chip), value * closing])]
        near_in, far_in = partner(near, 2), partner(far, 4)
        near_out, far_out = pl.pallas_call(
            functools.partial(relay_kernel, steps),
            out_shape=ends_shape,
            compiler_params=params,
            name="relay",
        )(factors, near, near_in, far, far_in)
        return [near, near_in, partner(near_out, 4), far, far_in, partner(far_out, 2)]

    def end_specs(ends):
        return [strip(*end.shape[:-1]) for end in ends]

    ends = exchange(near, far)
    first, edge, inner_edge = pl.pallas_call(
        functools.partial(sweep_kernel, ratio, steps_local, chips),
        grid=(blocks,),
        in_specs=[raw] * 4 + [strip(4, half)] + end_specs(ends),
        out_specs=[strip(2 * steps, half), strip(2 * steps), strip(2 * steps)],
        out_shape=[shape(2 * steps, half, cells), shape(2 * steps, cells), shape(2 * steps, cells)],
        compiler_params=params,
        name="first_sweep",
    )(state_rhs, adjoint_rhs, other_s, other_a, factors, *ends)

    outer = across(edge)
    inner = partner(inner_edge, 1)
    coupled, near, far = pl.pallas_call(
        functools.partial(coupling_kernel, ratio, steps),
        grid=(blocks,),
        in_specs=[
            whole(2 * steps, half, cells),
            whole(2 * steps, cells),
            whole(2 * steps, cells),
            whole(depth, cells),
            whole(1, cells),
            pl.BlockSpec((3, half, width), lambda i: (0, this_core(), i)),
            strip(4, half),
        ],
        out_specs=[strip(2 * steps, half)] + ends_spec,
        out_shape=[shape(2 * steps, half, cells)] + ends_shape,
        compiler_params=params,
        name="couplings",
    )(first, outer, inner, diffusivity, outer_kappa, velocity, factors)

    ends = exchange(near, far)
    keep, send = pl.pallas_call(
        functools.partial(last_kernel, ratio, steps_local, chips),
        grid=(blocks,),
        in_specs=[strip(2 * steps, half)] * 2 + [strip(4, half)] + end_specs(ends),
        out_specs=[strip(2, steps_local, half)] * 2,
        out_shape=[shape(2, steps_local, half, cells)] * 2,
        compiler_params=params,
        name="second_sweep",
    )(coupled, first, factors, *ends)

    received = partner(send, 1)
    upper = jnp.where(core == 0, keep, received)
    lower = jnp.where(core == 0, received, keep)
    result = jnp.concatenate([upper, lower], axis=2)
    return result[0], result[1]


def solution(mesh):
    placed = (P("tm", "gz", None), P("tm", "gz", None), P("gz", None), P(None, "gz", None))
    return jax.shard_map(
        body,
        mesh=mesh,
        in_specs=placed,
        out_specs=(P("tm", "gz", None), P("tm", "gz", None)),
        check_vma=False,
    )
```

time: 497 us -> 63.8 us (0.13); the launches traced: 490 us -> 63 us
  waiting for transfers between devices: 327 us -> 24.6 us
  other arithmetic: 66.2 us -> 2.51 us
  local copies, waits for them, and re-layouts: 42.1 us -> 3.41 us
  matrix products: 35.6 us -> 0 us
  Pallas kernels: 0 us -> 16.2 us
    ppermute x10 -> x14, waiting for transfers between devices: 327 us -> 24.6 us  [the longest x12 24.6 us: partner(): return lax.ppermute(value, 'tm', [(i, i ^ mask) for i in range(ranks)])]
    dot_general x8 -> x0, matrix products: 35.6 us -> none  [mix_rows(): jnp.einsum('ab,sbm->sam', matrix, data, precision=lax.Precision.HIGHEST)]
    slice x12 -> x0, local copies, waits for them, and re-layouts: 25.4 us -> none  [the longest x2 9.65 us: ahead_flat(): field[..., stride:]]
    select_n x8 -> x2, other arithmetic: 18.8 us -> 1.04 us  [the longest x1 0.88 us: body(): jnp.where(core == 0, diffusivity[:1], diffusivity[depth - 1:])]
    pallas_call x0 -> x6, Pallas kernels: none -> 16.2 us  [the longest x1 6.23 us: body(): pl.pallas_call(functools.partial(coupling_kernel, ratio, steps), grid=(bl...]
    add x5 -> x0, other arithmetic: 15.1 us -> none  [the longest x1 12.3 us: body(): blocks + coupling(first, first_pad, weights, velocity, NY)]
    reshape x2 -> x0, local copies, waits for them, and re-layouts: 12.5 us -> none  [the longest x1 6.34 us: body(): jnp.concatenate([back_real, back_imag])]
    sub x5 -> x0, other arithmetic: 9.81 us -> none  [the longest x2 7.85 us: body(): spread = partner - data]
  transfers between devices with their start and end apart: 10 -> 14, of which waited for: 6 -> 12; matrix products, arithmetic and copies ran while one was open for 3% -> 1% of each run, Pallas kernels for 0% -> 0%
where the time goes in v1:
time: 63.8 us; the launch traced here: 63 us
  waiting for transfers between devices  24.6 us (39%)
  Pallas kernels  16.2 us (25%)
  starting transfers between devices  15.6 us (24%)
  local copies, waits for them, and re-layouts  3.41 us (5%)
  other arithmetic  2.51 us (4%)
  between operations  0.73 us (1%)
    ppermute x12, waiting for transfers between devices, partner(): return lax.ppermute(value, 'tm', [(i, i ^ mask) for i in range(ranks)])  24.6 us
    ppermute x12, starting transfers between devices, partner(): return lax.ppermute(value, 'tm', [(i, i ^ mask) for i in range(ranks)])  14.3 us
    pallas_call x1, Pallas kernels, body(): pl.pallas_call(functools.partial(coupling_kernel, ratio, steps), grid=(bl...  6.23 us
    unnamed x14, local copies, waits for them, and re-layouts  3.41 us
    pallas_call x1, Pallas kernels, body(): pl.pallas_call(functools.partial(last_kernel, ratio, steps_local, chips),...  3.32 us
    pallas_call x1, Pallas kernels, body(): pl.pallas_call(functools.partial(sweep_kernel, ratio, steps_local, chips)...  3.05 us
    pallas_call x1, Pallas kernels, body(): pl.pallas_call(functools.partial(first_kernel, ratio, steps_local, chips)...  2.94 us
    squeeze x1, other arithmetic, body(): return (result[0], result[1])  1.46 us
  transfers between devices with their start and end apart: 14, of which 12 were waited for; matrix products, arithmetic and copies ran while one was open for 1% of the time, Pallas kernels for 0%

profile of v1, /device:TPU:0, one launch (start us, length us, event | category | flops | bytes accessed | tf_op | source)
XLA Modules:
  0.0 63.0 jit_solution(4967963764211971641)
XLA Ops:
  0.6 0.5 collective-permute-start
  1.2 0.9 %broadcast_select_fusion.2 = f32[1,2048]{1,0:T(1,128)S(1)} fusion(pred[]{:T(512)S(6)} %eq.2, f32[32,2048]{1,0:T(8,128)} %kappa_ref.3), kind=kLoop, calls=%fused_computation.8 | loop fusion | flops 2048 | bytes 24577 | tf_op jit(solution)/shard_map/jit(_where)/select_n | solution.py:410
  2.1 0.7 %collective-permute-start.2 = (f32[1,2048]{1,0:T(1,128)S(1)}, f32[1,2048]{1,0:T(1,128)S(1)}, u32[]{:S(2)}, u32[]{:S(2)}) collective-permute-start(f32[1,2048]{1,0:T(1,128)S(1)} %broadcast_select_fusion.2), channel_id=1, source_target_pairs={{1,4},{2,5},{3,6},{4,1},{5,2},{6,3},{9,12},{10,13},{11,14},{12,9},... | collective-permute-start | bytes 24584 | tf_op jit(solution)/shard_map/ppermute | solution.py:406
  2.8 0.9 %collective-permute-done.other_s = f32[4,32,2048]{2,1,0:T(8,128)S(1)} collective-permute-done((f32[4,32,2048]{2,1,0:T(8,128)}, f32[4,32,2048]{2,1,0:T(8,128)S(1)}, u32[]{:S(2)}, u32[]{:S(2)}) %collective-permute-start) | collective-permute-done | bytes 1048608 | tf_op jit(solution)/shard_map/ppermute | solution.py:396
  3.6 1.5 %collective-permute-done.1.other_a = f32[4,32,2048]{2,1,0:T(8,128)S(1)} collective-permute-done((f32[4,32,2048]{2,1,0:T(8,128)}, f32[4,32,2048]{2,1,0:T(8,128)S(1)}, u32[]{:S(2)}, u32[]{:S(2)}) %collective-permute-start.1) | collective-permute-done | bytes 1048608 | tf_op jit(solution)/shard_map/ppermute | solution.py:396
  5.1 1.2 %copy-done = f32[4,32,2048]{2,1,0:T(8,128)S(1)} copy-done((f32[4,32,2048]{2,1,0:T(8,128)S(1)}, f32[4,32,2048]{2,1,0:T(8,128)}, u32[]{:S(2)}) %copy-start) | copy-done | bytes 1048600
  6.4 1.2 %copy-done.2 = f32[4,32,2048]{2,1,0:T(8,128)S(1)} copy-done((f32[4,32,2048]{2,1,0:T(8,128)S(1)}, f32[4,32,2048]{2,1,0:T(8,128)}, u32[]{:S(2)}) %copy-start.2) | copy-done | bytes 1048600
  7.6 0.9 %copy-done.4 = f32[32,2048]{1,0:T(8,128)S(1)} copy-done((f32[32,2048]{1,0:T(8,128)S(1)}, f32[32,2048]{1,0:T(8,128)}, u32[]{:S(2)}) %copy-start.4) | copy-done | bytes 262168
  8.5 2.9 %ends_of_first.1 = (f32[4,16,2048]{2,1,0:T(8,128)S(1)}, f32[2,8,2048]{2,1,0:T(8,128)S(1)}, f32[2,8,2048]{2,1,0:T(8,128)S(1)}) custom-call(f32[4,32,2048]{2,1,0:T(8,128)S(1)} %copy-done, f32[4,32,2048]{2,1,0:T(8,128)S(1)} %copy-done.2, f32[4,32,2048]{2,1,0:T(8,128)S(1)} %collective-permute-done.other_s, f32[4,32,2048]{2,1,0:T(8,128)S(1)} %collective-permute-done.1.other_a, ...), custom_call_target="tpu_custom_call" | custom-call | tf_op jit(solution)/shard_map/ends_of_first/pallas_call | solution.py:422
  11.5 2.9 %collective-permute-start.3 = (f32[2,8,2048]{2,1,0:T(8,128)S(1)}, f32[2,8,2048]{2,1,0:T(8,128)S(1)}, u32[]{:S(2)}, u32[]{:S(2)}) collective-permute-start(f32[2,8,2048]{2,1,0:T(8,128)S(1)} %get-tuple-element.18.near_ref.rest_0_), channel_id=1, source_target_pairs={{0,8},{4,12},{8,0},{12,4},{16,24},{20,28},{24,16},{28,20},{1,9},{5... | collective-permute-start | bytes 393224 | tf_op jit(solution)/shard_map/ppermute | solution.py:396
  14.4 1.5 %collective-permute-start.4 = (f32[2,8,2048]{2,1,0:T(8,128)S(1)}, f32[2,8,2048]{2,1,0:T(8,128)S(1)}, u32[]{:S(2)}, u32[]{:S(2)}) collective-permute-start(f32[2,8,2048]{2,1,0:T(8,128)S(1)} %get-tuple-element.19.far_ref.rest_3_), channel_id=1, source_target_pairs={{0,16},{4,20},{8,24},{12,28},{16,0},{20,4},{24,8},{28,12},{1,17},{... | collective-permute-start | bytes 393224 | tf_op jit(solution)/shard_map/ppermute | solution.py:396
  15.9 1.4 %collective-permute-done.3.near_in.rest_1_ = f32[2,8,2048]{2,1,0:T(8,128)S(1)} collective-permute-done((f32[2,8,2048]{2,1,0:T(8,128)S(1)}, f32[2,8,2048]{2,1,0:T(8,128)S(1)}, u32[]{:S(2)}, u32[]{:S(2)}) %collective-permute-start.3) | collective-permute-done | bytes 131104 | tf_op jit(solution)/shard_map/ppermute | solution.py:396
  17.4 2.6 %collective-permute-done.4.far_in.rest_4_ = f32[2,8,2048]{2,1,0:T(8,128)S(1)} collective-permute-done((f32[2,8,2048]{2,1,0:T(8,128)S(1)}, f32[2,8,2048]{2,1,0:T(8,128)S(1)}, u32[]{:S(2)}, u32[]{:S(2)}) %collective-permute-start.4) | collective-permute-done | bytes 131104 | tf_op jit(solution)/shard_map/ppermute | solution.py:396
  20.3 1.6 %collective-permute-start.5 = (f32[2,8,2048]{2,1,0:T(8,128)S(1)}, f32[2,8,2048]{2,1,0:T(8,128)S(1)}, u32[]{:S(2)}, u32[]{:S(2)}) collective-permute-start(f32[2,8,2048]{2,1,0:T(8,128)S(1)} %get-tuple-element.20), channel_id=1, source_target_pairs={{0,16},{4,20},{8,24},{12,28},{16,0},{20,4},{24,8},{28,12},{1,17},{... | collective-permute-start | bytes 393224 | tf_op jit(solution)/shard_map/ppermute | solution.py:396
  21.9 0.5 collective-permute-start.6
  22.4 4.0 %collective-permute-done.5.rest_2_ = f32[2,8,2048]{2,1,0:T(8,128)S(1)} collective-permute-done((f32[2,8,2048]{2,1,0:T(8,128)S(1)}, f32[2,8,2048]{2,1,0:T(8,128)S(1)}, u32[]{:S(2)}, u32[]{:S(2)}) %collective-permute-start.5) | collective-permute-done | bytes 131104 | tf_op jit(solution)/shard_map/ppermute | solution.py:396
  26.4 1.2 %collective-permute-done.6.rest_5_ = f32[2,8,2048]{2,1,0:T(8,128)S(1)} collective-permute-done((f32[2,8,2048]{2,1,0:T(8,128)S(1)}, f32[2,8,2048]{2,1,0:T(8,128)S(1)}, u32[]{:S(2)}, u32[]{:S(2)}) %collective-permute-start.6) | collective-permute-done | bytes 131104 | tf_op jit(solution)/shard_map/ppermute | solution.py:396
  27.7 3.1 %first_sweep.1 = (f32[16,16,2048]{2,1,0:T(8,128)}, f32[16,2048]{1,0:T(8,128)S(1)}, f32[16,2048]{1,0:T(8,128)S(1)}) custom-call(f32[4,32,2048]{2,1,0:T(8,128)S(1)} %copy-done.1, f32[4,32,2048]{2,1,0:T(8,128)S(1)} %copy-done.3, f32[4,32,2048]{2,1,0:T(8,128)S(1)} %collective-permute-done.other_s, f32[4,32,2048]{2,1,0:T(8,128)S(1)} %collective-permute-done.1.other_a, ...), custom_call_target="tpu_custom_call" | custom-call | tf_op jit(solution)/shard_map/first_sweep/pallas_call | solution.py:466
  30.7 0.7 %collective-permute-start.7 = (f32[16,2048]{1,0:T(8,128)S(1)}, f32[16,2048]{1,0:T(8,128)S(1)}, u32[]{:S(2)}, u32[]{:S(2)}) collective-permute-start(f32[16,2048]{1,0:T(8,128)S(1)} %get-tuple-element.23), channel_id=1, source_target_pairs={{1,4},{2,5},{3,6},{4,1},{5,2},{6,3},{9,12},{10,13},{11,14},{12,9},... | collective-permute-start | bytes 393224 | tf_op jit(solution)/shard_map/ppermute | solution.py:406
  31.4 3.9 %collective-permute-start.8 = (f32[16,2048]{1,0:T(8,128)S(1)}, f32[16,2048]{1,0:T(8,128)S(1)}, u32[]{:S(2)}, u32[]{:S(2)}) collective-permute-start(f32[16,2048]{1,0:T(8,128)S(1)} %get-tuple-element.24), channel_id=1, source_target_pairs={{0,4},{4,0},{8,12},{12,8},{16,20},{20,16},{24,28},{28,24},{1,5},{5... | collective-permute-start | bytes 393224 | tf_op jit(solution)/shard_map/ppermute | solution.py:396
  35.3 1.0 %collective-permute-done.8.inner_ref = f32[16,2048]{1,0:T(8,128)S(1)} collective-permute-done((f32[16,2048]{1,0:T(8,128)S(1)}, f32[16,2048]{1,0:T(8,128)S(1)}, u32[]{:S(2)}, u32[]{:S(2)}) %collective-permute-start.8) | collective-permute-done | bytes 131104 | tf_op jit(solution)/shard_map/ppermute | solution.py:396
  36.3 6.2 %couplings.1 = (f32[16,16,2048]{2,1,0:T(8,128)S(1)}, f32[2,8,2048]{2,1,0:T(8,128)S(1)}, f32[2,8,2048]{2,1,0:T(8,128)S(1)}) custom-call(f32[16,16,2048]{2,1,0:T(8,128)} %get-tuple-element.22.first_ref, f32[16,2048]{1,0:T(8,128)S(1)} %collective-permute-done.7.outer_ref, f32[16,2048]{1,0:T(8,128)S(1)} %collective-permute-done.8.inner_ref, ...), custom_call_target="tpu_custom_call" | custom-call | tf_op jit(solution)/shard_map/couplings/pallas_call | solution.py:478
  42.5 0.6 collective-permute-start.9
  43.1 0.5 collective-permute-start.10
  43.6 4.7 %collective-permute-done.9.near_in.rest_1_ = f32[2,8,2048]{2,1,0:T(8,128)S(1)} collective-permute-done((f32[2,8,2048]{2,1,0:T(8,128)S(1)}, f32[2,8,2048]{2,1,0:T(8,128)S(1)}, u32[]{:S(2)}, u32[]{:S(2)}) %collective-permute-start.9) | collective-permute-done | bytes 131104 | tf_op jit(solution)/shard_map/ppermute | solution.py:396
  48.3 0.9 %collective-permute-done.10.far_in.rest_4_ = f32[2,8,2048]{2,1,0:T(8,128)S(1)} collective-permute-done((f32[2,8,2048]{2,1,0:T(8,128)S(1)}, f32[2,8,2048]{2,1,0:T(8,128)S(1)}, u32[]{:S(2)}, u32[]{:S(2)}) %collective-permute-start.10) | collective-permute-done | bytes 131104 | tf_op jit(solution)/shard_map/ppermute | solution.py:396
  49.5 0.6 collective-permute-start.11
  50.1 1.5 %collective-permute-start.12 = (f32[2,8,2048]{2,1,0:T(8,128)S(1)}, f32[2,8,2048]{2,1,0:T(8,128)S(1)}, u32[]{:S(2)}, u32[]{:S(2)}) collective-permute-start(f32[2,8,2048]{2,1,0:T(8,128)S(1)} %get-tuple-element.29), channel_id=1, source_target_pairs={{0,8},{4,12},{8,0},{12,4},{16,24},{20,28},{24,16},{28,20},{1,9},{5... | collective-permute-start | bytes 393224 | tf_op jit(solution)/shard_map/ppermute | solution.py:396
  51.6 3.5 %collective-permute-done.11.rest_2_ = f32[2,8,2048]{2,1,0:T(8,128)S(1)} collective-permute-done((f32[2,8,2048]{2,1,0:T(8,128)S(1)}, f32[2,8,2048]{2,1,0:T(8,128)S(1)}, u32[]{:S(2)}, u32[]{:S(2)}) %collective-permute-start.11) | collective-permute-done | bytes 131104 | tf_op jit(solution)/shard_map/ppermute | solution.py:396
  55.3 3.3 %second_sweep.1 = (f32[2,4,16,2048]{3,2,1,0:T(8,128)S(1)}, f32[2,4,16,2048]{3,2,1,0:T(8,128)S(1)}) custom-call(f32[16,16,2048]{2,1,0:T(8,128)S(1)} %get-tuple-element.25.coupled_ref, f32[16,16,2048]{2,1,0:T(8,128)} %get-tuple-element.22.first_ref, f32[4,16,2048]{2,1,0:T(8,128)S(1)} %get-tuple-element.17.factor_ref, ...), custom_call_target="tpu_custom_call" | custom-call | tf_op jit(solution)/shard_map/second_sweep/pallas_call | solution.py:497
  58.8 2.6 %collective-permute-done.13 = f32[2,4,16,2048]{3,2,1,0:T(8,128)S(1)} collective-permute-done((f32[2,4,16,2048]{3,2,1,0:T(8,128)S(1)}, f32[2,4,16,2048]{3,2,1,0:T(8,128)S(1)}, u32[]{:S(2)}, u32[]{:S(2)}) %collective-permute-start.13) | collective-permute-done | bytes 1048608 | tf_op jit(solution)/shard_map/ppermute | solution.py:396
  61.6 1.5 %fusion.2 = (f32[4,32,2048]{2,1,0:T(8,128)}, f32[4,32,2048]{2,1,0:T(8,128)}) fusion(f32[2,4,16,2048]{3,2,1,0:T(8,128)S(1)} %get-tuple-element.34, f32[2,4,16,2048]{3,2,1,0:T(8,128)S(1)} %get-tuple-element.35), kind=kLoop, calls=%fused_computation.5 | loop fusion | flops 524288 | bytes 4194304 | tf_op jit(solution)/shard_map/squeeze | solution.py:511
  (19 shorter events, 1.2 us)
Async XLA Ops:
  0.6 3.0 %collective-permute-start = (f32[4,32,2048]{2,1,0:T(8,128)}, f32[4,32,2048]{2,1,0:T(8,128)S(1)}, u32[]{:S(2)}, u32[]{:S(2)}) collective-permute-start(f32[4,32,2048]{2,1,0:T(8,128)} %own_s.3), channel_id=1, source_target_pairs={{0,4},{4,0},{8,12},{12,8},{16,20},{20,16},{24,28},{28,24},{1,5},{5... | collective-permute-start | bytes 3145736 | tf_op jit(solution)/shard_map/ppermute | solution.py:396
  1.1 4.0 %collective-permute-start.1 = (f32[4,32,2048]{2,1,0:T(8,128)}, f32[4,32,2048]{2,1,0:T(8,128)S(1)}, u32[]{:S(2)}, u32[]{:S(2)}) collective-permute-start(f32[4,32,2048]{2,1,0:T(8,128)} %own_a.3), channel_id=1, source_target_pairs={{0,4},{4,0},{8,12},{12,8},{16,20},{20,16},{24,28},{28,24},{1,5},{5... | collective-permute-start | bytes 3145736 | tf_op jit(solution)/shard_map/ppermute | solution.py:396
  2.1 0.7 %collective-permute-start.2 = (f32[1,2048]{1,0:T(1,128)S(1)}, f32[1,2048]{1,0:T(1,128)S(1)}, u32[]{:S(2)}, u32[]{:S(2)}) collective-permute-start(f32[1,2048]{1,0:T(1,128)S(1)} %broadcast_select_fusion.2), channel_id=1, source_target_pairs={{1,4},{2,5},{3,6},{4,1},{5,2},{6,3},{9,12},{10,13},{11,14},{12,9},... | collective-permute-start | bytes 24584 | tf_op jit(solution)/shard_map/ppermute | solution.py:406
  5.1 1.2 %copy-start = (f32[4,32,2048]{2,1,0:T(8,128)S(1)}, f32[4,32,2048]{2,1,0:T(8,128)}, u32[]{:S(2)}) copy-start(f32[4,32,2048]{2,1,0:T(8,128)} %own_s.3) | copy-start | bytes 3145732
  6.4 1.2 %copy-start.2 = (f32[4,32,2048]{2,1,0:T(8,128)S(1)}, f32[4,32,2048]{2,1,0:T(8,128)}, u32[]{:S(2)}) copy-start(f32[4,32,2048]{2,1,0:T(8,128)} %own_a.3) | copy-start | bytes 3145732
  7.6 0.9 %copy-start.4 = (f32[32,2048]{1,0:T(8,128)S(1)}, f32[32,2048]{1,0:T(8,128)}, u32[]{:S(2)}) copy-start(f32[32,2048]{1,0:T(8,128)} %kappa_ref.3) | copy-start | bytes 786436
  8.5 19.1 %copy-start.1 = (f32[4,32,2048]{2,1,0:T(8,128)S(1)}, f32[4,32,2048]{2,1,0:T(8,128)}, u32[]{:S(2)}) copy-start(f32[4,32,2048]{2,1,0:T(8,128)} %own_s.3) | copy-start | bytes 3145732
  8.5 19.1 %copy-start.3 = (f32[4,32,2048]{2,1,0:T(8,128)S(1)}, f32[4,32,2048]{2,1,0:T(8,128)}, u32[]{:S(2)}) copy-start(f32[4,32,2048]{2,1,0:T(8,128)} %own_a.3) | copy-start | bytes 3145732
  11.5 5.9 %collective-permute-start.3 = (f32[2,8,2048]{2,1,0:T(8,128)S(1)}, f32[2,8,2048]{2,1,0:T(8,128)S(1)}, u32[]{:S(2)}, u32[]{:S(2)}) collective-permute-start(f32[2,8,2048]{2,1,0:T(8,128)S(1)} %get-tuple-element.18.near_ref.rest_0_), channel_id=1, source_target_pairs={{0,8},{4,12},{8,0},{12,4},{16,24},{20,28},{24,16},{28,20},{1,9},{5... | collective-permute-start | bytes 393224 | tf_op jit(solution)/shard_map/ppermute | solution.py:396
  14.4 5.6 %collective-permute-start.4 = (f32[2,8,2048]{2,1,0:T(8,128)S(1)}, f32[2,8,2048]{2,1,0:T(8,128)S(1)}, u32[]{:S(2)}, u32[]{:S(2)}) collective-permute-start(f32[2,8,2048]{2,1,0:T(8,128)S(1)} %get-tuple-element.19.far_ref.rest_3_), channel_id=1, source_target_pairs={{0,16},{4,20},{8,24},{12,28},{16,0},{20,4},{24,8},{28,12},{1,17},{... | collective-permute-start | bytes 393224 | tf_op jit(solution)/shard_map/ppermute | solution.py:396
  20.3 6.1 %collective-permute-start.5 = (f32[2,8,2048]{2,1,0:T(8,128)S(1)}, f32[2,8,2048]{2,1,0:T(8,128)S(1)}, u32[]{:S(2)}, u32[]{:S(2)}) collective-permute-start(f32[2,8,2048]{2,1,0:T(8,128)S(1)} %get-tuple-element.20), channel_id=1, source_target_pairs={{0,16},{4,20},{8,24},{12,28},{16,0},{20,4},{24,8},{28,12},{1,17},{... | collective-permute-start | bytes 393224 | tf_op jit(solution)/shard_map/ppermute | solution.py:396
  21.9 14.4 %copy-start.5 = (f32[32,2048]{1,0:T(8,128)S(1)}, f32[32,2048]{1,0:T(8,128)}, u32[]{:S(2)}) copy-start(f32[32,2048]{1,0:T(8,128)} %kappa_ref.3) | copy-start | bytes 786436
  21.9 14.4 %copy-start.6 = (f32[3,32,2048]{2,1,0:T(8,128)S(1)}, f32[3,32,2048]{2,1,0:T(8,128)}, u32[]{:S(2)}) copy-start(f32[3,32,2048]{2,1,0:T(8,128)} %velocity_ref.1) | copy-start | bytes 2359300
  21.9 5.8 %collective-permute-start.6 = (f32[2,8,2048]{2,1,0:T(8,128)S(1)}, f32[2,8,2048]{2,1,0:T(8,128)S(1)}, u32[]{:S(2)}, u32[]{:S(2)}) collective-permute-start(f32[2,8,2048]{2,1,0:T(8,128)S(1)} %get-tuple-element.21), channel_id=1, source_target_pairs={{0,8},{4,12},{8,0},{12,4},{16,24},{20,28},{24,16},{28,20},{1,9},{5... | collective-permute-start | bytes 393224 | tf_op jit(solution)/shard_map/ppermute | solution.py:396
  30.7 4.6 %collective-permute-start.7 = (f32[16,2048]{1,0:T(8,128)S(1)}, f32[16,2048]{1,0:T(8,128)S(1)}, u32[]{:S(2)}, u32[]{:S(2)}) collective-permute-start(f32[16,2048]{1,0:T(8,128)S(1)} %get-tuple-element.23), channel_id=1, source_target_pairs={{1,4},{2,5},{3,6},{4,1},{5,2},{6,3},{9,12},{10,13},{11,14},{12,9},... | collective-permute-start | bytes 393224 | tf_op jit(solution)/shard_map/ppermute | solution.py:406
  31.4 4.9 %collective-permute-start.8 = (f32[16,2048]{1,0:T(8,128)S(1)}, f32[16,2048]{1,0:T(8,128)S(1)}, u32[]{:S(2)}, u32[]{:S(2)}) collective-permute-start(f32[16,2048]{1,0:T(8,128)S(1)} %get-tuple-element.24), channel_id=1, source_target_pairs={{0,4},{4,0},{8,12},{12,8},{16,20},{20,16},{24,28},{28,24},{1,5},{5... | collective-permute-start | bytes 393224 | tf_op jit(solution)/shard_map/ppermute | solution.py:396
  42.5 5.8 %collective-permute-start.9 = (f32[2,8,2048]{2,1,0:T(8,128)S(1)}, f32[2,8,2048]{2,1,0:T(8,128)S(1)}, u32[]{:S(2)}, u32[]{:S(2)}) collective-permute-start(f32[2,8,2048]{2,1,0:T(8,128)S(1)} %get-tuple-element.26.near_ref.rest_0_), channel_id=1, source_target_pairs={{0,8},{4,12},{8,0},{12,4},{16,24},{20,28},{24,16},{28,20},{1,9},{5... | collective-permute-start | bytes 393224 | tf_op jit(solution)/shard_map/ppermute | solution.py:396
  43.1 6.1 %collective-permute-start.10 = (f32[2,8,2048]{2,1,0:T(8,128)S(1)}, f32[2,8,2048]{2,1,0:T(8,128)S(1)}, u32[]{:S(2)}, u32[]{:S(2)}) collective-permute-start(f32[2,8,2048]{2,1,0:T(8,128)S(1)} %get-tuple-element.27.far_ref.rest_3_), channel_id=1, source_target_pairs={{0,16},{4,20},{8,24},{12,28},{16,0},{20,4},{24,8},{28,12},{1,17},{... | collective-permute-start | bytes 393224 | tf_op jit(solution)/shard_map/ppermute | solution.py:396
  49.5 5.6 %collective-permute-start.11 = (f32[2,8,2048]{2,1,0:T(8,128)S(1)}, f32[2,8,2048]{2,1,0:T(8,128)S(1)}, u32[]{:S(2)}, u32[]{:S(2)}) collective-permute-start(f32[2,8,2048]{2,1,0:T(8,128)S(1)} %get-tuple-element.28), channel_id=1, source_target_pairs={{0,16},{4,20},{8,24},{12,28},{16,0},{20,4},{24,8},{28,12},{1,17},{... | collective-permute-start | bytes 393224 | tf_op jit(solution)/shard_map/ppermute | solution.py:396
  50.1 5.2 %collective-permute-start.12 = (f32[2,8,2048]{2,1,0:T(8,128)S(1)}, f32[2,8,2048]{2,1,0:T(8,128)S(1)}, u32[]{:S(2)}, u32[]{:S(2)}) collective-permute-start(f32[2,8,2048]{2,1,0:T(8,128)S(1)} %get-tuple-element.29), channel_id=1, source_target_pairs={{0,8},{4,12},{8,0},{12,4},{16,24},{20,28},{24,16},{28,20},{1,9},{5... | collective-permute-start | bytes 393224 | tf_op jit(solution)/shard_map/ppermute | solution.py:396
  58.7 2.7 %collective-permute-start.13 = (f32[2,4,16,2048]{3,2,1,0:T(8,128)S(1)}, f32[2,4,16,2048]{3,2,1,0:T(8,128)S(1)}, u32[]{:S(2)}, u32[]{:S(2)}) collective-permute-start(f32[2,4,16,2048]{3,2,1,0:T(8,128)S(1)} %get-tuple-element.31), channel_id=1, source_target_pairs={{0,4},{4,0},{8,12},{12,8},{16,20},{20,16},{24,28},{28,24},{1,5},{5... | collective-permute-start | bytes 3145736 | tf_op jit(solution)/shard_map/ppermute | solution.py:396

commit v2 on v1

v2 whole, which is shorter than its diff:
```python
import functools
import math

import jax
import jax.numpy as jnp
from jax import lax
from jax.experimental import pallas as pl
from jax.experimental.pallas import tpu as pltpu
from jax.sharding import PartitionSpec as P

NY = 64
LANES = 128

alpha_wrap = 0.1
beta_couple = 0.5
gamma_couple = 0.5


def this_core():
    return lax.rem(lax.axis_index("tm"), 2)


def this_chip():
    return lax.div(lax.axis_index("tm"), 2)


def lane_block(start):
    return pl.ds(pl.multiple_of(start, LANES), LANES)


def power(value, count):
    result = None
    while count:
        if count & 1:
            result = value if result is None else result * value
        count >>= 1
        if count:
            value = value * value
    return result


def step_scale(ratio, steps, chips, sign):
    chip = this_chip()
    base = jnp.float32(1.0)
    bit = 0
    while 1 << bit < chips:
        factor = ratio ** (sign * steps * (1 << bit))
        base = base * jnp.where(lax.rem(lax.div(chip, 1 << bit), 2) == 1, factor, 1.0)
        bit += 1
    return [base * (ratio ** (sign * step)) for step in range(steps)]


def side_values(field, left, right, before, after):
    rows = field.shape[0]
    lane = lax.broadcasted_iota(jnp.int32, field.shape, 1)
    row = lax.broadcasted_iota(jnp.int32, field.shape, 0)
    z_ahead = jnp.where(row == rows - 1, after, pltpu.roll(field, rows - 1, 0))
    z_behind = jnp.where(row == 0, before, pltpu.roll(field, 1, 0))
    turned = pltpu.roll(field, NY, 1)
    x_ahead = jnp.where(lane < NY, turned, pltpu.roll(right, NY, 1))
    x_behind = jnp.where(lane < NY, pltpu.roll(left, NY, 1), turned)
    y_ahead = pltpu.roll(field, LANES - 1, 1)
    y_behind = pltpu.roll(field, 1, 1)
    return ((z_ahead, z_behind), (x_ahead, x_behind), (y_ahead, y_behind))


def faces(kappa_ref, outer, group, half):
    core = this_core()
    groups = kappa_ref.shape[1] // LANES
    own = pl.ds(pl.multiple_of(core * half, 8), half)
    here = lane_block(group * LANES)
    kappa = kappa_ref[own, here]
    left = kappa_ref[own, lane_block(jnp.maximum(group - 1, 0) * LANES)]
    right = kappa_ref[own, lane_block(jnp.minimum(group + 1, groups - 1) * LANES)]
    before = jnp.where(core == 0, outer, kappa_ref[half - 1 : half, here])
    after = jnp.where(core == 0, kappa_ref[half : half + 1, here], outer)
    pairs = side_values(kappa, left, right, before, after)
    lane = lax.broadcasted_iota(jnp.int32, kappa.shape, 1)
    column = lax.rem(lane, NY)
    inside = (
        (pairs[0][0] > 0.0, pairs[0][1] > 0.0),
        (
            jnp.logical_or(lane < NY, group < groups - 1),
            jnp.logical_or(lane >= NY, group > 0),
        ),
        (column < NY - 1, column > 0),
    )
    weights = [
        [jnp.where(ok, 0.5 * (kappa + value), kappa) for ok, value in zip(oks, values)]
        for oks, values in zip(inside, pairs)
    ]
    return weights, inside


def total_weight(weights):
    diagonal = weights[0][0] + weights[0][1]
    diagonal = diagonal + weights[1][0] + weights[1][1]
    return diagonal + weights[2][0] + weights[2][1]


def layer_diagonal(kappa, ahead, behind):
    rows = kappa.shape[0]
    lane = lax.broadcasted_iota(jnp.int32, kappa.shape, 1)
    row = lax.broadcasted_iota(jnp.int32, kappa.shape, 0)
    column = lax.rem(lane, NY)
    turned = pltpu.roll(kappa, NY, 1)
    x_ahead = jnp.where(lane < NY, turned, pltpu.roll(turned, rows - 1, 0))
    x_behind = jnp.where(lane < NY, pltpu.roll(turned, 1, 0), turned)
    pairs = (
        (ahead, ahead > 0.0),
        (behind, behind > 0.0),
        (x_ahead, jnp.logical_or(lane < NY, row < rows - 1)),
        (x_behind, jnp.logical_or(lane >= NY, row > 0)),
        (pltpu.roll(kappa, LANES - 1, 1), column < NY - 1),
        (pltpu.roll(kappa, 1, 1), column > 0),
    )
    total = None
    for value, ok in pairs:
        weight = jnp.where(ok, 0.5 * (kappa + value), kappa)
        total = weight if total is None else total + weight
    return total


def cell_factors(diagonal, ratio):
    shifted = 1.0 + diagonal
    lifted = shifted * shifted - (ratio * ratio + beta_couple * gamma_couple)
    mix = shifted / (lifted + jnp.sqrt(lifted * lifted + shifted * shifted))
    inverse = 1.0 / (shifted + 0.5 * mix)
    return ratio * inverse, inverse, mix * inverse, 1.0 / shifted


def local_ends(values, decay, inverse, mixed, upright, steps):
    back = None
    last = None
    weight = None
    for step in reversed(range(steps)):
        state, adjoint = values(step)
        drive = inverse * adjoint - mixed * state
        back = drive if back is None else decay * back + drive
        term = state + 0.5 * back
        last = term if last is None else last + weight * term
        weight = decay if weight is None else weight * decay
    return back, last * upright


def solve_steps(values, decay, inverse, mixed, upright, ratio, back_in, state_in, steps, put):
    backs = [None] * steps
    back = back_in
    for step in reversed(range(steps)):
        state, adjoint = values(step)
        drive = inverse * adjoint - mixed * state
        back = drive if back is None else decay * back + drive
        backs[step] = back
    gain = ratio * mixed
    half_up = 0.5 * upright
    previous = state_in
    for step in range(steps):
        state, _ = values(step)
        current = upright * state + half_up * backs[step]
        adjoint = backs[step]
        if previous is not None:
            current = current + decay * previous
            adjoint = adjoint - gain * previous
        put(step, current, adjoint)
        previous = current
    return backs[0], previous


def pack_kernel(state, adjoint, kappa, keep, send, slab, outer_cross, outer_straight, inner_keep, inner_send, layers, sems):
    steps_local = state.shape[0]
    half = keep.shape[2]
    core = this_core()
    mine = pl.ds(pl.multiple_of(core * half, 8), half)
    others = pl.ds(pl.multiple_of((1 - core) * half, 8), half)
    copies = [pltpu.make_async_copy(kappa, slab, sems.at[4])]
    for field, source in enumerate((state, adjoint)):
        copies.append(pltpu.make_async_copy(source.at[:, mine, :], keep.at[field], sems.at[2 * field]))
        copies.append(pltpu.make_async_copy(source.at[:, others, :], send.at[field], sems.at[2 * field + 1]))
    for copy in copies:
        copy.start()

    def lay(source, rows, target):
        for group in range(target.shape[0]):
            lanes = slice(group * LANES, (group + 1) * LANES)
            one, other = [source[row : row + 1, lanes] for row in rows]
            target[group : group + 1, :] = jnp.where(core == 0, one, other)

    copies[0].wait()
    last = 2 * half - 1
    lay(slab, (0, last), outer_cross.at[2 * steps_local])
    lay(slab, (1, last - 1), outer_cross.at[2 * steps_local + 1])
    for slot, row in enumerate((0, half - 1, half, half + 1)):
        lay(slab, (row, last - row), layers.at[slot])
    for copy in copies[1:]:
        copy.wait()
    near, far = (0, half - 1), (half - 1, 0)
    for index in range(steps_local):
        for field in range(2):
            slot = 2 * index + field
            lay(keep.at[field, index], near, outer_cross.at[slot])
            lay(send.at[field, index], far, outer_straight.at[slot])
            lay(send.at[field, index], near, inner_keep.at[slot])
            lay(keep.at[field, index], far, inner_send.at[slot])


def ends_kernel(ratio, chips, keep, other, slab, cross, straight, inner_keep, inner_other, layers, raw_ref, factor_ref, near_ref, far_ref):
    steps_local, half, cells = keep.shape[1:]
    steps = 2 * steps_local
    tile = half // 2
    groups = cells // LANES
    core = this_core()
    scales = step_scale(ratio, steps, chips, 1)

    def order(position, index):
        sub = core if position == 0 else 1 - core
        return sub * steps + 2 * index, jnp.where(sub == 0, scales[index], scales[steps_local + index])

    def set_factors(diagonal, here):
        for slot, value in enumerate(cell_factors(diagonal, ratio)):
            factor_ref[slot, :, here] = value

    def prepare(group, carry):
        here = lane_block(group * LANES)
        weights, _ = faces(slab, cross[steps, pl.ds(group, 1), :], group, half)
        set_factors(total_weight(weights), here)
        for position, source in enumerate((keep, other)):
            for index in range(steps_local):
                slot, scale = order(position, index)
                for field in range(2):
                    raw_ref[slot + field, :, here] = source[field, index, :, here] * scale
        return carry

    lax.fori_loop(0, groups, prepare, 0)
    outer, inner = slice(cells, cells + LANES), slice(cells + LANES, cells + 2 * LANES)
    set_factors(layer_diagonal(cross[steps], layers[0], cross[steps + 1]), outer)
    set_factors(layer_diagonal(layers[2], layers[1], layers[3]), inner)
    for sources, here in (((straight, cross), outer), ((inner_keep, inner_other), inner)):
        for position, source in enumerate(sources):
            for index in range(steps_local):
                slot, scale = order(position, index)
                for field in range(2):
                    raw_ref[slot + field, :, here] = source[2 * index + field] * scale

    def one(group, carry):
        here = lane_block(group * LANES)
        factors = [factor_ref[slot, :, here] for slot in range(4)]
        values = lambda step: (raw_ref[2 * step, :, here], raw_ref[2 * step + 1, :, here])
        put_ends(local_ends(values, *factors, steps), near_ref, far_ref, here, tile)
        return carry

    lax.fori_loop(0, groups + 2, one, 0)


def put_ends(ends, near_ref, far_ref, here, tile):
    for slot, value in enumerate(ends):
        near_ref[slot, :, here] = value[:tile]
        far_ref[slot, :, here] = value[tile:]


def power_sum(value, count):
    total = None
    for _ in range(count):
        total = 1.0 if total is None else 1.0 + value * total
    return total


def response_of(decay, upright, steps):
    return (0.5 * upright) * decay * power_sum(decay * decay, steps)


def ring_factors(factors, steps, chips):
    decay, _, _, upright = factors
    block = power(decay, steps)
    return block, response_of(decay, upright, steps), 1.0 / (1.0 - power(block, chips))


def contribution(ends, offset, block, response, closing):
    back, last = ends
    square = block * block
    if offset == 0:
        up, down, cross = square * block, square * block, 1.0 + square + square * square * (1.0 + square)
    elif offset == 1:
        up, down, cross = None, square, block * (1.0 + square) * (1.0 + square)
    elif offset == 2:
        up, down, cross = block, block, 2.0 * square * (1.0 + square)
    else:
        up, down, cross = square, None, block * (1.0 + square) * (1.0 + square)
    entering_back = back if up is None else up * back
    entering_state = last if down is None else down * last
    entering_state = entering_state + (cross * response * closing) * back
    return closing * entering_back, closing * entering_state


def either(flag, one, other):
    return tuple(jnp.where(flag, a, b) for a, b in zip(one, other))


def relay_kernel(steps, factor_ref, near_ref, near_in, far_ref, far_in, near_out, far_out):
    tile, cells = near_ref.shape[1:]
    odd = lax.rem(this_chip(), 2) == 1

    def one(index, carry):
        here = lane_block(index * LANES)
        for rows, mine, theirs, out, first in (
            (slice(0, tile), near_ref, near_in, near_out, True),
            (slice(tile, 2 * tile), far_ref, far_in, far_out, False),
        ):
            factors = [factor_ref[slot, rows, here] for slot in range(4)]
            ring = ring_factors(factors, steps, 4)
            a = (mine[0, :, here], mine[1, :, here])
            b = (theirs[0, :, here], theirs[1, :, here])
            if first:
                one_part = contribution(a, 2, *ring)
                other_part = either(odd, contribution(b, 1, *ring), contribution(b, 3, *ring))
            else:
                one_part = either(odd, contribution(a, 1, *ring), contribution(a, 3, *ring))
                other_part = either(odd, contribution(b, 3, *ring), contribution(b, 1, *ring))
            out[0, :, here] = one_part[0] + other_part[0]
            out[1, :, here] = one_part[1] + other_part[1]
        return carry

    lax.fori_loop(0, cells // LANES, one, 0)


def entering(factors, near, near_in, near_tail, far, far_in, far_tail, here, tile, steps):
    odd = lax.rem(this_chip(), 2) == 1
    backs, states = [], []
    for rows, mine, theirs, tail, first in (
        (slice(0, tile), near, near_in, near_tail, True),
        (slice(tile, 2 * tile), far, far_in, far_tail, False),
    ):
        ring = ring_factors([f[rows] for f in factors], steps, 4)
        a = (mine[0, :, here], mine[1, :, here])
        b = (theirs[0, :, here], theirs[1, :, here])
        own = contribution(a, 0, *ring)
        if first:
            near_by = either(odd, contribution(b, 3, *ring), contribution(b, 1, *ring))
        else:
            near_by = contribution(b, 2, *ring)
        backs.append(own[0] + near_by[0] + tail[0, :, here])
        states.append(own[1] + near_by[1] + tail[1, :, here])
    return jnp.concatenate(backs, axis=0), jnp.concatenate(states, axis=0)


def enter_values(ends, factors, here, half, steps):
    if len(ends) == 1:
        return ends[0][0, :, here], ends[0][1, :, here]
    return entering(factors, *ends, here, half // 2, steps)


def couplings_kernel(ratio, steps, raw_ref, factor_ref, slab, cross, velocity_ref, *rest):
    *ends, first_ref, coupled_ref, near_ref, far_ref, layers = rest
    half = raw_ref.shape[1]
    tile = half // 2
    cells = slab.shape[1]
    groups = cells // LANES
    core = this_core()

    def sweep(side, group, carry):
        here = lane_block(group * LANES)
        factors = [factor_ref[slot, :, here] for slot in range(4)]
        values = lambda step: (raw_ref[2 * step, :, here], raw_ref[2 * step + 1, :, here])

        def put(step, state, adjoint):
            if side is None:
                first_ref[2 * step, :, here] = state
                first_ref[2 * step + 1, :, here] = adjoint
            else:
                layers[side, 2 * step] = state
                layers[side, 2 * step + 1] = adjoint

        solve_steps(values, *factors, ratio, *enter_values(ends, factors, here, half, steps), steps, put)
        return carry

    lax.fori_loop(0, groups, functools.partial(sweep, None), 0)
    for side in range(2):
        sweep(side, groups + side, 0)

    def one(group, carry):
        here = lane_block(group * LANES)
        left = lane_block(jnp.maximum(group - 1, 0) * LANES)
        right = lane_block(jnp.minimum(group + 1, groups - 1) * LANES)
        row = pl.ds(group, 1)
        own = pl.ds(pl.multiple_of(core * half, 8), half)
        weights, inside = faces(slab, cross[steps, row, :], group, half)
        tables = ([], [])
        for direction, component in enumerate((2, 0, 1)):
            drift = 0.5 * velocity_ref[component, own, here]
            ahead, behind = weights[direction]
            ok_ahead, ok_behind = inside[direction]
            for field, sign in enumerate((1.0, -1.0)):
                tables[field].append(
                    (
                        jnp.where(ok_ahead, ahead - sign * drift, 0.0),
                        jnp.where(ok_behind, behind + sign * drift, 0.0),
                    )
                )
        factors = [factor_ref[slot, :, here] for slot in range(4)]

        def values(step):
            results = []
            for field in range(2):
                slot = 2 * step + field
                outer = layers[0, slot, row, :]
                inner = layers[1, slot, row, :]
                before = jnp.where(core == 0, outer, inner)
                after = jnp.where(core == 0, inner, outer)
                pairs = side_values(first_ref[slot, :, here], first_ref[slot, :, left], first_ref[slot, :, right], before, after)
                result = None
                for (ahead, behind), (c_ahead, c_behind) in zip(pairs, tables[field]):
                    term = c_ahead * ahead + c_behind * behind
                    result = term if result is None else result + term
                coupled_ref[slot, :, here] = result
                results.append(result)
            return results

        put_ends(local_ends(values, *factors, steps), near_ref, far_ref, here, tile)
        return carry

    lax.fori_loop(0, groups, one, 0)


def parts_kernel(ratio, steps_local, coupled_ref, first_ref, factor_ref, keep, send, middle_ref):
    groups = coupled_ref.shape[2] // LANES
    core = this_core()

    def one(group, carry):
        here = lane_block(group * LANES)
        factors = [factor_ref[slot, :, here] for slot in range(4)]
        results = {}
        for sub in range(2):
            offset = 2 * steps_local * sub

            def values(step):
                return coupled_ref[offset + 2 * step, :, here], coupled_ref[offset + 2 * step + 1, :, here]

            def put(step, state, adjoint):
                results[sub, step] = (state, adjoint)

            back, last = solve_steps(values, *factors, ratio, None, None, steps_local, put)
            if sub == 1:
                middle_ref[0, :, here] = back
            else:
                middle_ref[1, :, here] = last
        for step in range(steps_local):
            for field in range(2):
                early, late = [
                    first_ref[2 * steps_local * sub + 2 * step + field, :, here] + results[sub, step][field]
                    for sub in range(2)
                ]
                keep[field, step, :, here] = jnp.where(core == 0, early, late)
                send[field, step, :, here] = jnp.where(core == 0, late, early)
        return carry

    lax.fori_loop(0, groups, one, 0)


def carry_kernel(steps_local, factor_ref, middle_ref, *rest):
    *ends, keep, send = rest
    half, cells = middle_ref.shape[1:]
    core = this_core()

    def one(group, carry):
        here = lane_block(group * LANES)
        factors = [factor_ref[slot, :, here] for slot in range(4)]
        decay, _, _, upright = factors
        back, state = enter_values(ends, factors, here, half, 2 * steps_local)
        block = power(decay, steps_local)
        early_back = middle_ref[0, :, here] + block * back
        late_state = middle_ref[1, :, here] + block * state + response_of(decay, upright, steps_local) * early_back
        for slot, (early, late) in enumerate(((early_back, back), (state, late_state))):
            keep[slot, :, here] = jnp.where(core == 0, early, late)
            send[slot, :, here] = jnp.where(core == 0, late, early)
        return carry

    lax.fori_loop(0, cells // LANES, one, 0)


def finish_kernel(ratio, chips, keep, other, keep_in, other_in, factor_ref, other_factor, state_out, adjoint_out, result, sems):
    steps_local, half, cells = keep.shape[1:]
    core = this_core()
    whole = step_scale(ratio, 2 * steps_local, chips, -1)
    scales = [jnp.where(core == 0, whole[step], whole[steps_local + step]) for step in range(steps_local)]
    copies = []
    for part, (parts, entered, table) in enumerate(((keep, keep_in, factor_ref), (other, other_in, other_factor))):

        def one(group, carry):
            here = lane_block(group * LANES)
            decay, _, mixed, upright = [table[slot, :, here] for slot in range(4)]
            backs = [entered[0, :, here]]
            for _ in range(steps_local):
                backs.append(decay * backs[-1])
            backs = backs[:0:-1]
            gain = ratio * mixed
            half_up = 0.5 * upright
            previous = entered[1, :, here]
            for step in range(steps_local):
                current = decay * previous + half_up * backs[step]
                result[part, 0, step, :, here] = (parts[0, step, :, here] + current) * scales[step]
                result[part, 1, step, :, here] = (parts[1, step, :, here] + (backs[step] - gain * previous)) * scales[step]
                previous = current
            return carry

        lax.fori_loop(0, cells // LANES, one, 0)
        rows = pl.ds(pl.multiple_of((core if part == 0 else 1 - core) * half, 8), half)
        for field, out in enumerate((state_out, adjoint_out)):
            copies.append(pltpu.make_async_copy(result.at[part, field], out.at[:, rows, :], sems.at[part, field]))
            copies[-1].start()
    for copy in copies:
        copy.wait()


def body(state_rhs, adjoint_rhs, diffusivity, velocity):
    steps_local, depth, cells = state_rhs.shape
    ranks = lax.axis_size("tm")
    slabs = lax.axis_size("gz")
    chips = ranks // 2
    total = steps_local * ranks
    steps = 2 * steps_local
    half = depth // 2
    tile = half // 2
    groups = cells // LANES
    wide = cells + 2 * LANES
    ratio = alpha_wrap ** (1.0 / total)
    core = this_core()
    f32 = jnp.float32
    anywhere = pl.BlockSpec(memory_space=pl.ANY)

    def partner(value, mask):
        return lax.ppermute(value, "tm", [(i, i ^ mask) for i in range(ranks)])

    def outward(value, flip):
        pairs = []
        for t in range(ranks):
            for g in range(slabs):
                down = (t + flip) % 2 == 1
                to = g - 1 if down else g + 1
                if 0 <= to < slabs:
                    pairs.append((t * slabs + g, (t ^ flip) * slabs + to))
        return lax.ppermute(value, ("tm", "gz"), pairs)

    def call(kernel, name, out_shape, *args, **kwargs):
        shapes = [jax.ShapeDtypeStruct(s, f32) for s in out_shape]
        return pl.pallas_call(
            kernel,
            out_shape=shapes,
            compiler_params=pltpu.CompilerParams(vmem_limit_bytes=32 * 1024 * 1024),
            name=name,
            **kwargs,
        )(*args)

    layer = (groups, LANES)
    halves = (2, steps_local, half, cells)
    keep, send, slab, cross, straight, inner_keep, inner_send, layers = call(
        pack_kernel,
        "halves_and_layers",
        [halves, halves, (depth, cells), (steps + 2,) + layer, (steps,) + layer, (steps,) + layer, (steps,) + layer, (4,) + layer],
        state_rhs,
        adjoint_rhs,
        diffusivity,
        in_specs=[anywhere] * 3,
        scratch_shapes=[pltpu.SemaphoreType.DMA((5,))],
    )
    other = partner(send, 1)
    inner_other = partner(inner_send, 1)
    cross = outward(cross, 1)
    straight = outward(straight, 0)
    ends_shape = [(2, tile, wide)] * 2
    raw, factors, near, far = call(
        functools.partial(ends_kernel, ratio, chips),
        "ends_of_first",
        [(2 * steps, half, wide), (4, half, wide)] + ends_shape,
        keep,
        other,
        slab,
        cross,
        straight,
        inner_keep,
        inner_other,
        layers,
    )

    def exchange(near, far):
        width = near.shape[2]
        if chips != 4:
            gathered = lax.all_gather(jnp.concatenate([near, far], axis=1), "tm")
            gathered = lax.dynamic_index_in_dim(
                gathered.reshape((chips, 2) + gathered.shape[1:]), core, 1, keepdims=False
            )
            block, response, closing = ring_factors([factors[i, :, :width] for i in range(4)], steps, chips)
            at = lambda array, index: lax.dynamic_index_in_dim(array, lax.rem(index + 2 * chips, chips), 0, keepdims=False)
            chip = this_chip()

            def entering_back(where):
                value = jnp.zeros((half, width), f32)
                for offset in reversed(range(chips)):
                    value = block * value + at(gathered[:, 0], where + 1 + offset)
                return value * closing

            value = jnp.zeros((half, width), f32)
            for offset in reversed(range(chips)):
                source = chip - 1 - offset
                value = block * value + at(gathered[:, 1], source) + response * entering_back(source)
            return [jnp.stack([entering_back(chip), value * closing])]
        near_in, far_in = partner(near, 2), partner(far, 4)
        near_out, far_out = call(
            functools.partial(relay_kernel, steps), "relay", [near.shape] * 2, factors, near, near_in, far, far_in
        )
        return [near, near_in, partner(near_out, 4), far, far_in, partner(far_out, 2)]

    ends = exchange(near, far)
    other_factors = partner(factors, 1)
    first, coupled, near, far = call(
        functools.partial(couplings_kernel, ratio, steps),
        "first_sweep_and_couplings",
        [(2 * steps, half, cells)] * 2 + [(2, tile, cells)] * 2,
        raw,
        factors,
        slab,
        cross,
        velocity,
        *ends,
        scratch_shapes=[pltpu.VMEM((2, 2 * steps) + layer, f32)],
    )
    ends = exchange(near, far)
    keep, send, middle = call(
        functools.partial(parts_kernel, ratio, steps_local),
        "own_steps",
        [halves, halves, (2, half, cells)],
        coupled,
        first,
        factors,
    )
    other = partner(send, 1)
    keep_in, send_in = call(
        functools.partial(carry_kernel, steps_local), "entering", [(2, half, cells)] * 2, factors, middle, *ends
    )
    other_in = partner(send_in, 1)
    return call(
        functools.partial(finish_kernel, ratio, chips),
        "finish",
        [(steps_local, depth, cells)] * 2,
        keep,
        other,
        keep_in,
        other_in,
        factors,
        other_factors,
        out_specs=[anywhere] * 2,
        scratch_shapes=[pltpu.VMEM((2,) + halves, f32), pltpu.SemaphoreType.DMA((2, 2))],
    )


def solution(mesh):
    placed = (P("tm", "gz", None), P("tm", "gz", None), P("gz", None), P(None, "gz", None))
    return jax.shard_map(
        body,
        mesh=mesh,
        in_specs=placed,
        out_specs=(P("tm", "gz", None), P("tm", "gz", None)),
        check_vma=False,
    )
```

time: 63.8 us -> 54.9 us (0.86)
  Pallas kernels: 16.2 us -> 11.9 us
  waiting for transfers between devices: 24.6 us -> 21.8 us
  other arithmetic: 2.51 us -> 0 us
  starting transfers between devices: 15.6 us -> 16.8 us
    ppermute x2, starting transfers between devices: 1.32 us -> 6.54 us  [outward(): return lax.ppermute(value, ('tm', 'gz'), pairs)]
    ppermute x12 -> x13, waiting for transfers between devices: 24.6 us -> 20 us  [partner(): return lax.ppermute(value, 'tm', [(i, i ^ mask) for i in range(ranks)])]
    pallas_call x6 -> x8, Pallas kernels: 16.2 us -> 11.9 us  [call(): pl.pallas_call(kernel, out_shape=shapes, compiler_params=pltpu.CompilerPa...]
    ppermute x12 -> x13, starting transfers between devices: 14.3 us -> 10.2 us  [partner(): return lax.ppermute(value, 'tm', [(i, i ^ mask) for i in range(ranks)])]
    ppermute x2, waiting for transfers between devices: 0.01 us -> 1.81 us  [outward(): return lax.ppermute(value, ('tm', 'gz'), pairs)]
    squeeze x1 -> x0, other arithmetic: 1.46 us -> none  [body(): return (result[0], result[1])]
    select_n x2 -> x0, other arithmetic: 1.04 us -> none  [the longest x1 0.88 us: body(): jnp.where(core == 0, diffusivity[:1], diffusivity[depth - 1:])]
    unnamed x14 -> x8, local copies, waits for them, and re-layouts: 3.41 us -> 3.4 us
  transfers between devices with their start and end apart: 14 -> 15, of which waited for: 12 -> 10; matrix products, arithmetic and copies ran while one was open for 1% -> 0% of each run, Pallas kernels for 0% -> 2%
where the time goes in v2:
time: 54.9 us; the launch traced here: 54.6 us
  waiting for transfers between devices  21.8 us (40%)
  starting transfers between devices  16.8 us (31%)
  Pallas kernels  11.9 us (22%)
  local copies, waits for them, and re-layouts  3.4 us (6%)
  between operations  0.75 us (1%)
    ppermute x13, waiting for transfers between devices, partner(): return lax.ppermute(value, 'tm', [(i, i ^ mask) for i in range(ranks)])  20 us
    pallas_call x8, Pallas kernels, call(): pl.pallas_call(kernel, out_shape=shapes, compiler_params=pltpu.CompilerPa...  11.9 us
    ppermute x13, starting transfers between devices, partner(): return lax.ppermute(value, 'tm', [(i, i ^ mask) for i in range(ranks)])  10.2 us
    ppermute x2, starting transfers between devices, outward(): return lax.ppermute(value, ('tm', 'gz'), pairs)  6.54 us
    unnamed x8, local copies, waits for them, and re-layouts  3.4 us
    ppermute x2, waiting for transfers between devices, outward(): return lax.ppermute(value, ('tm', 'gz'), pairs)  1.81 us
  transfers between devices with their start and end apart: 15, of which 10 were waited for; matrix products, arithmetic and copies ran while one was open for 0% of the time, Pallas kernels for 2%

profile of v2, /device:TPU:0, one launch (start us, length us, event | category | flops | bytes accessed | tf_op | source)
XLA Modules:
  0.0 54.6 jit_solution(4824037206508826509)
XLA Ops:
  0.6 1.2 %copy-done = f32[4,32,2048]{2,1,0:T(8,128)S(1)} copy-done((f32[4,32,2048]{2,1,0:T(8,128)S(1)}, f32[4,32,2048]{2,1,0:T(8,128)}, u32[]{:S(2)}) %copy-start) | copy-done | bytes 1048600
  1.9 1.2 %copy-done.1 = f32[4,32,2048]{2,1,0:T(8,128)S(1)} copy-done((f32[4,32,2048]{2,1,0:T(8,128)S(1)}, f32[4,32,2048]{2,1,0:T(8,128)}, u32[]{:S(2)}) %copy-start.1) | copy-done | bytes 1048600
  3.1 0.9 %copy-done.3 = f32[32,2048]{1,0:T(8,128)S(1)} copy-done((f32[32,2048]{1,0:T(8,128)S(1)}, f32[32,2048]{1,0:T(8,128)}, u32[]{:S(2)}) %copy-start.3) | copy-done | bytes 262168
  4.0 0.4 halves_and_layers.1
  4.5 0.5 collective-permute-start
  5.0 0.7 %collective-permute-start.1 = (f32[10,16,128]{2,1,0:T(8,128)S(1)}, f32[10,16,128]{2,1,0:T(8,128)S(1)}, u32[]{:S(2)}, u32[]{:S(2)}) collective-permute-start(f32[10,16,128]{2,1,0:T(8,128)S(1)} %get-tuple-element.30), channel_id=1, source_target_pairs={{1,4},{2,5},{3,6},{4,1},{5,2},{6,3},{9,12},{10,13},{11,14},{12,9},... | collective-permute-start | bytes 245768 | tf_op jit(solution)/shard_map/ppermute | solution.py:540
  5.7 5.9 %collective-permute-start.2 = (f32[8,16,128]{2,1,0:T(8,128)S(1)}, f32[8,16,128]{2,1,0:T(8,128)S(1)}, u32[]{:S(2)}, u32[]{:S(2)}) collective-permute-start(f32[8,16,128]{2,1,0:T(8,128)S(1)} %get-tuple-element.31), channel_id=1, source_target_pairs={{0,1},{1,2},{2,3},{5,4},{6,5},{7,6},{8,9},{9,10},{10,11},{13,12},{... | collective-permute-start | bytes 196616 | tf_op jit(solution)/shard_map/ppermute | solution.py:540
  11.6 1.8 %collective-permute-done.2.straight = f32[8,16,128]{2,1,0:T(8,128)S(1)} collective-permute-done((f32[8,16,128]{2,1,0:T(8,128)S(1)}, f32[8,16,128]{2,1,0:T(8,128)S(1)}, u32[]{:S(2)}, u32[]{:S(2)}) %collective-permute-start.2) | collective-permute-done | bytes 65568 | tf_op jit(solution)/shard_map/ppermute | solution.py:540
  13.5 2.5 %ends_of_first.1 = (f32[16,16,2304]{2,1,0:T(8,128)S(1)}, f32[4,16,2304]{2,1,0:T(8,128)S(1)}, f32[2,8,2304]{2,1,0:T(8,128)S(1)}, f32[2,8,2304]{2,1,0:T(8,128)S(1)}) custom-call(f32[2,4,16,2048]{3,2,1,0:T(8,128)S(1)} %get-tuple-element.27.keep, f32[2,4,16,2048]{3,2,1,0:T(8,128)S(1)} %collective-permute-done.other, f32[32,2048]{1,0:T(8,128)S(1)} %get-tuple-element.29.slab, ...), custom_call_target="tpu_custom_call" | custom-call | tf_op jit(solution)/shard_map/ends_of_first/pallas_call | solution.py:544
  16.0 2.0 %collective-permute-start.4 = (f32[2,8,2304]{2,1,0:T(8,128)S(1)}, f32[2,8,2304]{2,1,0:T(8,128)S(1)}, u32[]{:S(2)}, u32[]{:S(2)}) collective-permute-start(f32[2,8,2304]{2,1,0:T(8,128)S(1)} %get-tuple-element.37.near_ref.rest_0_), channel_id=1, source_target_pairs={{0,8},{4,12},{8,0},{12,4},{16,24},{20,28},{24,16},{28,20},{1,9},{5... | collective-permute-start | bytes 442376 | tf_op jit(solution)/shard_map/ppermute | solution.py:530
  17.9 1.5 %collective-permute-start.5 = (f32[2,8,2304]{2,1,0:T(8,128)S(1)}, f32[2,8,2304]{2,1,0:T(8,128)S(1)}, u32[]{:S(2)}, u32[]{:S(2)}) collective-permute-start(f32[2,8,2304]{2,1,0:T(8,128)S(1)} %get-tuple-element.38.far_ref.rest_3_), channel_id=1, source_target_pairs={{0,16},{4,20},{8,24},{12,28},{16,0},{20,4},{24,8},{28,12},{1,17},{... | collective-permute-start | bytes 442376 | tf_op jit(solution)/shard_map/ppermute | solution.py:530
  19.4 3.0 %collective-permute-done.4.near_in.rest_1_ = f32[2,8,2304]{2,1,0:T(8,128)S(1)} collective-permute-done((f32[2,8,2304]{2,1,0:T(8,128)S(1)}, f32[2,8,2304]{2,1,0:T(8,128)S(1)}, u32[]{:S(2)}, u32[]{:S(2)}) %collective-permute-start.4) | collective-permute-done | bytes 147488 | tf_op jit(solution)/shard_map/ppermute | solution.py:530
  22.4 1.9 %collective-permute-done.5.far_in.rest_4_ = f32[2,8,2304]{2,1,0:T(8,128)S(1)} collective-permute-done((f32[2,8,2304]{2,1,0:T(8,128)S(1)}, f32[2,8,2304]{2,1,0:T(8,128)S(1)}, u32[]{:S(2)}, u32[]{:S(2)}) %collective-permute-start.5) | collective-permute-done | bytes 147488 | tf_op jit(solution)/shard_map/ppermute | solution.py:530
  24.3 0.4 relay.2
  24.8 1.6 %collective-permute-start.6 = (f32[2,8,2304]{2,1,0:T(8,128)S(1)}, f32[2,8,2304]{2,1,0:T(8,128)S(1)}, u32[]{:S(2)}, u32[]{:S(2)}) collective-permute-start(f32[2,8,2304]{2,1,0:T(8,128)S(1)} %get-tuple-element.39), channel_id=1, source_target_pairs={{0,16},{4,20},{8,24},{12,28},{16,0},{20,4},{24,8},{28,12},{1,17},{... | collective-permute-start | bytes 442376 | tf_op jit(solution)/shard_map/ppermute | solution.py:530
  26.3 0.5 collective-permute-start.7
  26.9 3.5 %collective-permute-done.6.rest_2_ = f32[2,8,2304]{2,1,0:T(8,128)S(1)} collective-permute-done((f32[2,8,2304]{2,1,0:T(8,128)S(1)}, f32[2,8,2304]{2,1,0:T(8,128)S(1)}, u32[]{:S(2)}, u32[]{:S(2)}) %collective-permute-start.6) | collective-permute-done | bytes 147488 | tf_op jit(solution)/shard_map/ppermute | solution.py:530
  30.4 1.2 %collective-permute-done.7.rest_5_ = f32[2,8,2304]{2,1,0:T(8,128)S(1)} collective-permute-done((f32[2,8,2304]{2,1,0:T(8,128)S(1)}, f32[2,8,2304]{2,1,0:T(8,128)S(1)}, u32[]{:S(2)}, u32[]{:S(2)}) %collective-permute-start.7) | collective-permute-done | bytes 147488 | tf_op jit(solution)/shard_map/ppermute | solution.py:530
  31.6 5.3 %first_sweep_and_couplings.1 = (f32[16,16,2048]{2,1,0:T(8,128)S(1)}, f32[16,16,2048]{2,1,0:T(8,128)S(1)}, f32[2,8,2048]{2,1,0:T(8,128)S(1)}, f32[2,8,2048]{2,1,0:T(8,128)S(1)}) custom-call(f32[16,16,2304]{2,1,0:T(8,128)S(1)} %get-tuple-element.35.raw_ref, f32[4,16,2304]{2,1,0:T(8,128)S(1)} %get-tuple-element.36.factor_ref, ...), custom_call_target="tpu_custom_call" | custom-call | tf_op jit(solution)/shard_map/first_sweep_and_couplings/pallas_call | solution.py:544
  36.9 0.8 %own_steps.1 = (f32[2,4,16,2048]{3,2,1,0:T(8,128)S(1)}, f32[2,4,16,2048]{3,2,1,0:T(8,128)S(1)}, f32[2,16,2048]{2,1,0:T(8,128)S(1)}) custom-call(f32[16,16,2048]{2,1,0:T(8,128)S(1)} %get-tuple-element.41.coupled_ref, f32[16,16,2048]{2,1,0:T(8,128)S(1)} %get-tuple-element.42.first_ref, f32[4,16,2304]{2,1,0:T(8,128)S(1)} %get-tuple-element.36.factor_ref), custom_call_target="tpu_custom_call" | custom-call | tf_op jit(solution)/shard_map/own_steps/pallas_call | solution.py:544
  37.7 0.5 collective-permute-start.14
  38.2 0.5 collective-permute-start.10
  38.7 0.7 %collective-permute-start.9 = (f32[2,8,2048]{2,1,0:T(8,128)S(1)}, f32[2,8,2048]{2,1,0:T(8,128)S(1)}, u32[]{:S(2)}, u32[]{:S(2)}) collective-permute-start(f32[2,8,2048]{2,1,0:T(8,128)S(1)} %get-tuple-element.46.near_ref.rest_0_), channel_id=1, source_target_pairs={{0,8},{4,12},{8,0},{12,4},{16,24},{20,28},{24,16},{28,20},{1,9},{5... | collective-permute-start | bytes 393224 | tf_op jit(solution)/shard_map/ppermute | solution.py:530
  39.5 4.2 %collective-permute-done.10.far_in.rest_4_ = f32[2,8,2048]{2,1,0:T(8,128)S(1)} collective-permute-done((f32[2,8,2048]{2,1,0:T(8,128)S(1)}, f32[2,8,2048]{2,1,0:T(8,128)S(1)}, u32[]{:S(2)}, u32[]{:S(2)}) %collective-permute-start.10) | collective-permute-done | bytes 131104 | tf_op jit(solution)/shard_map/ppermute | solution.py:530
  43.9 0.4 relay.3
  44.3 1.6 %collective-permute-start.11 = (f32[2,8,2048]{2,1,0:T(8,128)S(1)}, f32[2,8,2048]{2,1,0:T(8,128)S(1)}, u32[]{:S(2)}, u32[]{:S(2)}) collective-permute-start(f32[2,8,2048]{2,1,0:T(8,128)S(1)} %get-tuple-element.48), channel_id=1, source_target_pairs={{0,16},{4,20},{8,24},{12,28},{16,0},{20,4},{24,8},{28,12},{1,17},{... | collective-permute-start | bytes 393224 | tf_op jit(solution)/shard_map/ppermute | solution.py:530
  45.9 0.6 %collective-permute-start.12 = (f32[2,8,2048]{2,1,0:T(8,128)S(1)}, f32[2,8,2048]{2,1,0:T(8,128)S(1)}, u32[]{:S(2)}, u32[]{:S(2)}) collective-permute-start(f32[2,8,2048]{2,1,0:T(8,128)S(1)} %get-tuple-element.49), channel_id=1, source_target_pairs={{0,8},{4,12},{8,0},{12,4},{16,24},{20,28},{24,16},{28,20},{1,9},{5... | collective-permute-start | bytes 393224 | tf_op jit(solution)/shard_map/ppermute | solution.py:530
  46.5 2.9 %collective-permute-done.11.rest_2_ = f32[2,8,2048]{2,1,0:T(8,128)S(1)} collective-permute-done((f32[2,8,2048]{2,1,0:T(8,128)S(1)}, f32[2,8,2048]{2,1,0:T(8,128)S(1)}, u32[]{:S(2)}, u32[]{:S(2)}) %collective-permute-start.11) | collective-permute-done | bytes 131104 | tf_op jit(solution)/shard_map/ppermute | solution.py:530
  49.4 1.5 %collective-permute-done.12.rest_5_ = f32[2,8,2048]{2,1,0:T(8,128)S(1)} collective-permute-done((f32[2,8,2048]{2,1,0:T(8,128)S(1)}, f32[2,8,2048]{2,1,0:T(8,128)S(1)}, u32[]{:S(2)}, u32[]{:S(2)}) %collective-permute-start.12) | collective-permute-done | bytes 131104 | tf_op jit(solution)/shard_map/ppermute | solution.py:530
  50.9 0.5 entering.1
  51.4 1.5 %collective-permute-done.13.other_in = f32[2,16,2048]{2,1,0:T(8,128)S(1)} collective-permute-done((f32[2,16,2048]{2,1,0:T(8,128)S(1)}, f32[2,16,2048]{2,1,0:T(8,128)S(1)}, u32[]{:S(2)}, u32[]{:S(2)}) %collective-permute-start.13) | collective-permute-done | bytes 262176 | tf_op jit(solution)/shard_map/ppermute | solution.py:530
  53.0 1.7 %finish.1 = (f32[4,32,2048]{2,1,0:T(8,128)}, f32[4,32,2048]{2,1,0:T(8,128)}) custom-call(f32[2,4,16,2048]{3,2,1,0:T(8,128)S(1)} %get-tuple-element.43.keep, f32[2,4,16,2048]{3,2,1,0:T(8,128)S(1)} %collective-permute-done.8.other, f32[2,16,2048]{2,1,0:T(8,128)S(1)} %get-tuple-element.50.keep_in, f32[2,16,2048]{2,1,0:T(8,128)S(1)} %collective-permute-done.13.other_in, ...), custom_call_target="tpu_custom_call" | custom-call | tf_op jit(solution)/shard_map/finish/pallas_call | solution.py:544
  (14 shorter events, 0.5 us)
Async XLA Ops:
  0.6 1.2 %copy-start = (f32[4,32,2048]{2,1,0:T(8,128)S(1)}, f32[4,32,2048]{2,1,0:T(8,128)}, u32[]{:S(2)}) copy-start(f32[4,32,2048]{2,1,0:T(8,128)} %state.1) | copy-start | bytes 3145732
  1.9 1.2 %copy-start.1 = (f32[4,32,2048]{2,1,0:T(8,128)S(1)}, f32[4,32,2048]{2,1,0:T(8,128)}, u32[]{:S(2)}) copy-start(f32[4,32,2048]{2,1,0:T(8,128)} %adjoint.1) | copy-start | bytes 3145732
  3.1 0.9 %copy-start.3 = (f32[32,2048]{1,0:T(8,128)S(1)}, f32[32,2048]{1,0:T(8,128)}, u32[]{:S(2)}) copy-start(f32[32,2048]{1,0:T(8,128)} %kappa.1) | copy-start | bytes 786436
  4.5 27.1 %copy-start.2 = (f32[3,32,2048]{2,1,0:T(8,128)S(1)}, f32[3,32,2048]{2,1,0:T(8,128)}, u32[]{:S(2)}) copy-start(f32[3,32,2048]{2,1,0:T(8,128)} %velocity_ref.1) | copy-start | bytes 2359300
  4.5 9.0 %collective-permute-start = (f32[2,4,16,2048]{3,2,1,0:T(8,128)S(1)}, f32[2,4,16,2048]{3,2,1,0:T(8,128)S(1)}, u32[]{:S(2)}, u32[]{:S(2)}) collective-permute-start(f32[2,4,16,2048]{3,2,1,0:T(8,128)S(1)} %get-tuple-element.28), channel_id=1, source_target_pairs={{0,4},{4,0},{8,12},{12,8},{16,20},{20,16},{24,28},{28,24},{1,5},{5... | collective-permute-start | bytes 3145736 | tf_op jit(solution)/shard_map/ppermute | solution.py:530
  5.0 8.5 %collective-permute-start.1 = (f32[10,16,128]{2,1,0:T(8,128)S(1)}, f32[10,16,128]{2,1,0:T(8,128)S(1)}, u32[]{:S(2)}, u32[]{:S(2)}) collective-permute-start(f32[10,16,128]{2,1,0:T(8,128)S(1)} %get-tuple-element.30), channel_id=1, source_target_pairs={{1,4},{2,5},{3,6},{4,1},{5,2},{6,3},{9,12},{10,13},{11,14},{12,9},... | collective-permute-start | bytes 245768 | tf_op jit(solution)/shard_map/ppermute | solution.py:540
  5.7 7.8 %collective-permute-start.2 = (f32[8,16,128]{2,1,0:T(8,128)S(1)}, f32[8,16,128]{2,1,0:T(8,128)S(1)}, u32[]{:S(2)}, u32[]{:S(2)}) collective-permute-start(f32[8,16,128]{2,1,0:T(8,128)S(1)} %get-tuple-element.31), channel_id=1, source_target_pairs={{0,1},{1,2},{2,3},{5,4},{6,5},{7,6},{8,9},{9,10},{10,11},{13,12},{... | collective-permute-start | bytes 196616 | tf_op jit(solution)/shard_map/ppermute | solution.py:540
  11.6 1.9 %collective-permute-start.3 = (f32[8,16,128]{2,1,0:T(8,128)S(1)}, f32[8,16,128]{2,1,0:T(8,128)S(1)}, u32[]{:S(2)}, u32[]{:S(2)}) collective-permute-start(f32[8,16,128]{2,1,0:T(8,128)S(1)} %get-tuple-element.33), channel_id=1, source_target_pairs={{0,4},{4,0},{8,12},{12,8},{16,20},{20,16},{24,28},{28,24},{1,5},{5... | collective-permute-start | bytes 196616 | tf_op jit(solution)/shard_map/ppermute | solution.py:530
  16.0 6.4 %collective-permute-start.4 = (f32[2,8,2304]{2,1,0:T(8,128)S(1)}, f32[2,8,2304]{2,1,0:T(8,128)S(1)}, u32[]{:S(2)}, u32[]{:S(2)}) collective-permute-start(f32[2,8,2304]{2,1,0:T(8,128)S(1)} %get-tuple-element.37.near_ref.rest_0_), channel_id=1, source_target_pairs={{0,8},{4,12},{8,0},{12,4},{16,24},{20,28},{24,16},{28,20},{1,9},{5... | collective-permute-start | bytes 442376 | tf_op jit(solution)/shard_map/ppermute | solution.py:530
  17.9 6.4 %collective-permute-start.5 = (f32[2,8,2304]{2,1,0:T(8,128)S(1)}, f32[2,8,2304]{2,1,0:T(8,128)S(1)}, u32[]{:S(2)}, u32[]{:S(2)}) collective-permute-start(f32[2,8,2304]{2,1,0:T(8,128)S(1)} %get-tuple-element.38.far_ref.rest_3_), channel_id=1, source_target_pairs={{0,16},{4,20},{8,24},{12,28},{16,0},{20,4},{24,8},{28,12},{1,17},{... | collective-permute-start | bytes 442376 | tf_op jit(solution)/shard_map/ppermute | solution.py:530
  24.8 5.6 %collective-permute-start.6 = (f32[2,8,2304]{2,1,0:T(8,128)S(1)}, f32[2,8,2304]{2,1,0:T(8,128)S(1)}, u32[]{:S(2)}, u32[]{:S(2)}) collective-permute-start(f32[2,8,2304]{2,1,0:T(8,128)S(1)} %get-tuple-element.39), channel_id=1, source_target_pairs={{0,16},{4,20},{8,24},{12,28},{16,0},{20,4},{24,8},{28,12},{1,17},{... | collective-permute-start | bytes 442376 | tf_op jit(solution)/shard_map/ppermute | solution.py:530
  26.3 5.3 %collective-permute-start.7 = (f32[2,8,2304]{2,1,0:T(8,128)S(1)}, f32[2,8,2304]{2,1,0:T(8,128)S(1)}, u32[]{:S(2)}, u32[]{:S(2)}) collective-permute-start(f32[2,8,2304]{2,1,0:T(8,128)S(1)} %get-tuple-element.40), channel_id=1, source_target_pairs={{0,8},{4,12},{8,0},{12,4},{16,24},{20,28},{24,16},{28,20},{1,9},{5... | collective-permute-start | bytes 442376 | tf_op jit(solution)/shard_map/ppermute | solution.py:530
  37.6 15.3 %collective-permute-start.8 = (f32[2,4,16,2048]{3,2,1,0:T(8,128)S(1)}, f32[2,4,16,2048]{3,2,1,0:T(8,128)S(1)}, u32[]{:S(2)}, u32[]{:S(2)}) collective-permute-start(f32[2,4,16,2048]{3,2,1,0:T(8,128)S(1)} %get-tuple-element.44), channel_id=1, source_target_pairs={{0,4},{4,0},{8,12},{12,8},{16,20},{20,16},{24,28},{28,24},{1,5},{5... | collective-permute-start | bytes 3145736 | tf_op jit(solution)/shard_map/ppermute | solution.py:530
  37.7 13.7 %collective-permute-start.14 = (f32[4,16,2304]{2,1,0:T(8,128)S(1)}, f32[4,16,2304]{2,1,0:T(8,128)S(1)}, u32[]{:S(2)}, u32[]{:S(2)}) collective-permute-start(f32[4,16,2304]{2,1,0:T(8,128)S(1)} %get-tuple-element.36.factor_ref), channel_id=1, source_target_pairs={{0,4},{4,0},{8,12},{12,8},{16,20},{20,16},{24,28},{28,24},{1,5},{5... | collective-permute-start | bytes 1769480 | tf_op jit(solution)/shard_map/ppermute | solution.py:530
  38.2 5.5 %collective-permute-start.10 = (f32[2,8,2048]{2,1,0:T(8,128)S(1)}, f32[2,8,2048]{2,1,0:T(8,128)S(1)}, u32[]{:S(2)}, u32[]{:S(2)}) collective-permute-start(f32[2,8,2048]{2,1,0:T(8,128)S(1)} %get-tuple-element.47.far_ref.rest_3_), channel_id=1, source_target_pairs={{0,16},{4,20},{8,24},{12,28},{16,0},{20,4},{24,8},{28,12},{1,17},{... | collective-permute-start | bytes 393224 | tf_op jit(solution)/shard_map/ppermute | solution.py:530
  38.7 5.2 %collective-permute-start.9 = (f32[2,8,2048]{2,1,0:T(8,128)S(1)}, f32[2,8,2048]{2,1,0:T(8,128)S(1)}, u32[]{:S(2)}, u32[]{:S(2)}) collective-permute-start(f32[2,8,2048]{2,1,0:T(8,128)S(1)} %get-tuple-element.46.near_ref.rest_0_), channel_id=1, source_target_pairs={{0,8},{4,12},{8,0},{12,4},{16,24},{20,28},{24,16},{28,20},{1,9},{5... | collective-permute-start | bytes 393224 | tf_op jit(solution)/shard_map/ppermute | solution.py:530
  44.3 5.0 %collective-permute-start.11 = (f32[2,8,2048]{2,1,0:T(8,128)S(1)}, f32[2,8,2048]{2,1,0:T(8,128)S(1)}, u32[]{:S(2)}, u32[]{:S(2)}) collective-permute-start(f32[2,8,2048]{2,1,0:T(8,128)S(1)} %get-tuple-element.48), channel_id=1, source_target_pairs={{0,16},{4,20},{8,24},{12,28},{16,0},{20,4},{24,8},{28,12},{1,17},{... | collective-permute-start | bytes 393224 | tf_op jit(solution)/shard_map/ppermute | solution.py:530
  45.9 5.0 %collective-permute-start.12 = (f32[2,8,2048]{2,1,0:T(8,128)S(1)}, f32[2,8,2048]{2,1,0:T(8,128)S(1)}, u32[]{:S(2)}, u32[]{:S(2)}) collective-permute-start(f32[2,8,2048]{2,1,0:T(8,128)S(1)} %get-tuple-element.49), channel_id=1, source_target_pairs={{0,8},{4,12},{8,0},{12,4},{16,24},{20,28},{24,16},{28,20},{1,9},{5... | collective-permute-start | bytes 393224 | tf_op jit(solution)/shard_map/ppermute | solution.py:530
  51.3 1.6 %collective-permute-start.13 = (f32[2,16,2048]{2,1,0:T(8,128)S(1)}, f32[2,16,2048]{2,1,0:T(8,128)S(1)}, u32[]{:S(2)}, u32[]{:S(2)}) collective-permute-start(f32[2,16,2048]{2,1,0:T(8,128)S(1)} %get-tuple-element.51), channel_id=1, source_target_pairs={{0,4},{4,0},{8,12},{12,8},{16,20},{20,16},{24,28},{28,24},{1,5},{5... | collective-permute-start | bytes 786440 | tf_op jit(solution)/shard_map/ppermute | solution.py:530

commit v3 on v2

v3 whole, which is shorter than its diff:
```python
import functools
import math

import jax
import jax.numpy as jnp
from jax import lax
from jax.experimental import pallas as pl
from jax.experimental.pallas import tpu as pltpu
from jax.sharding import PartitionSpec as P

NY = 64
LANES = 128

alpha_wrap = 0.1
beta_couple = 0.5
gamma_couple = 0.5


def this_core():
    return lax.rem(lax.axis_index("tm"), 2)


def this_chip():
    return lax.div(lax.axis_index("tm"), 2)


def lane_block(start, width=LANES):
    return pl.ds(pl.multiple_of(start, LANES), width)


def each_block(cells, width, work):
    def one(index, carry):
        work(lane_block(index * width, width))
        return carry

    lax.fori_loop(0, cells // width, one, 0)
    if cells % width:
        work(slice(cells - cells % width, cells))


def power(value, count):
    result = None
    while count:
        if count & 1:
            result = value if result is None else result * value
        count >>= 1
        if count:
            value = value * value
    return result


def step_scale(ratio, steps, chips, sign):
    chip = this_chip()
    base = jnp.float32(1.0)
    bit = 0
    while 1 << bit < chips:
        factor = ratio ** (sign * steps * (1 << bit))
        base = base * jnp.where(lax.rem(lax.div(chip, 1 << bit), 2) == 1, factor, 1.0)
        bit += 1
    return [base * (ratio ** (sign * step)) for step in range(steps)]


OUTER, INNER = 0, 1
UNROLL_ENDS = 4
UNROLL_COUPLINGS = 2


def tile_rows(side, half, depth):
    core = this_core()
    tile = half // 2
    return core * (depth - tile) if side == OUTER else tile + core * tile


def faces(side, slab, outer, group, half):
    core = this_core()
    depth, cells = slab.shape
    tile = half // 2
    groups = cells // LANES
    own = pl.ds(pl.multiple_of(tile_rows(side, half, depth), 8), tile)
    here = lane_block(group * LANES)
    kappa = slab[own, here]
    left = slab[own, lane_block(jnp.maximum(group - 1, 0) * LANES)]
    right = slab[own, lane_block(jnp.minimum(group + 1, groups - 1) * LANES)]
    mirrored = lambda row: jnp.where(core == 0, slab[row : row + 1, here], slab[depth - 1 - row : depth - row, here])
    outward = outer if side == OUTER else mirrored(tile - 1)
    inward = mirrored(tile if side == OUTER else half)
    first, last = edge_rows(kappa.shape)
    shift, back = z_shifts(tile)
    lane = lax.broadcasted_iota(jnp.int32, kappa.shape, 1)
    column = lax.rem(lane, NY)
    low = lane < NY
    turned = pltpu.roll(kappa, NY, 1)
    outward = jnp.where(first, outward, pltpu.roll(kappa, shift, 0))
    inward = jnp.where(last, inward, pltpu.roll(kappa, back, 0))
    pairs = (
        ((outward, outward > 0.0), (inward, inward > 0.0)),
        (
            (jnp.where(low, turned, pltpu.roll(right, NY, 1)), jnp.logical_or(low, group < groups - 1)),
            (jnp.where(low, pltpu.roll(left, NY, 1), turned), jnp.logical_or(lane >= NY, group > 0)),
        ),
        ((pltpu.roll(kappa, LANES - 1, 1), column < NY - 1), (pltpu.roll(kappa, 1, 1), column > 0)),
    )
    return [[(jnp.where(ok, 0.5 * (kappa + value), kappa), ok) for value, ok in pair] for pair in pairs]


def edge_rows(shape):
    core = this_core()
    row = lax.broadcasted_iota(jnp.int32, shape, 0)
    last = shape[0] - 1
    return row == core * last, row == (1 - core) * last


def z_shifts(tile):
    core = this_core()
    return 1 + core * (tile - 2), tile - 1 - core * (tile - 2)


def total_weight(weights):
    total = None
    for pair in weights:
        for weight, _ in pair:
            total = weight if total is None else total + weight
    return total


def layer_diagonal(kappa, ahead, behind):
    rows = kappa.shape[0]
    lane = lax.broadcasted_iota(jnp.int32, kappa.shape, 1)
    row = lax.broadcasted_iota(jnp.int32, kappa.shape, 0)
    column = lax.rem(lane, NY)
    turned = pltpu.roll(kappa, NY, 1)
    x_ahead = jnp.where(lane < NY, turned, pltpu.roll(turned, rows - 1, 0))
    x_behind = jnp.where(lane < NY, pltpu.roll(turned, 1, 0), turned)
    pairs = (
        (ahead, ahead > 0.0),
        (behind, behind > 0.0),
        (x_ahead, jnp.logical_or(lane < NY, row < rows - 1)),
        (x_behind, jnp.logical_or(lane >= NY, row > 0)),
        (pltpu.roll(kappa, LANES - 1, 1), column < NY - 1),
        (pltpu.roll(kappa, 1, 1), column > 0),
    )
    total = None
    for value, ok in pairs:
        weight = jnp.where(ok, 0.5 * (kappa + value), kappa)
        total = weight if total is None else total + weight
    return total


def cell_factors(diagonal, ratio):
    shifted = 1.0 + diagonal
    lifted = shifted * shifted - (ratio * ratio + beta_couple * gamma_couple)
    mix = shifted / (lifted + jnp.sqrt(lifted * lifted + shifted * shifted))
    inverse = 1.0 / (shifted + 0.5 * mix)
    return ratio * inverse, inverse, mix * inverse, 1.0 / shifted


def local_ends(values, decay, inverse, mixed, upright, steps):
    back = None
    last = None
    weight = None
    for step in reversed(range(steps)):
        state, adjoint = values(step)
        drive = inverse * adjoint - mixed * state
        back = drive if back is None else decay * back + drive
        term = state + 0.5 * back
        last = term if last is None else last + weight * term
        weight = decay if weight is None else weight * decay
    return back, last * upright


def solve_steps(values, decay, inverse, mixed, upright, ratio, back_in, state_in, steps, put):
    backs = [None] * steps
    back = back_in
    for step in reversed(range(steps)):
        state, adjoint = values(step)
        drive = inverse * adjoint - mixed * state
        back = drive if back is None else decay * back + drive
        backs[step] = back
    gain = ratio * mixed
    half_up = 0.5 * upright
    previous = state_in
    for step in range(steps):
        state, _ = values(step)
        current = upright * state + half_up * backs[step]
        adjoint = backs[step]
        if previous is not None:
            current = current + decay * previous
            adjoint = adjoint - gain * previous
        put(step, current, adjoint)
        previous = current
    return backs[0], previous


def pack_kernel(state, adjoint, kappa, keep, send, slab, outer_cross, outer_straight, inner_keep, inner_send, layers, sems):
    steps_local = state.shape[0]
    half = keep.shape[2]
    core = this_core()
    mine = pl.ds(pl.multiple_of(core * half, 8), half)
    others = pl.ds(pl.multiple_of((1 - core) * half, 8), half)
    copies = [pltpu.make_async_copy(kappa, slab, sems.at[4])]
    for field, source in enumerate((state, adjoint)):
        copies.append(pltpu.make_async_copy(source.at[:, mine, :], keep.at[field], sems.at[2 * field]))
        copies.append(pltpu.make_async_copy(source.at[:, others, :], send.at[field], sems.at[2 * field + 1]))
    for copy in copies:
        copy.start()

    def lay(source, rows, target):
        for group in range(target.shape[0]):
            lanes = slice(group * LANES, (group + 1) * LANES)
            one, other = [source[row : row + 1, lanes] for row in rows]
            target[group : group + 1, :] = jnp.where(core == 0, one, other)

    copies[0].wait()
    last = 2 * half - 1
    lay(slab, (0, last), outer_cross.at[2 * steps_local])
    lay(slab, (1, last - 1), outer_cross.at[2 * steps_local + 1])
    for slot, row in enumerate((0, half - 1, half, half + 1)):
        lay(slab, (row, last - row), layers.at[slot])
    for copy in copies[1:]:
        copy.wait()
    near, far = (0, half - 1), (half - 1, 0)
    for index in range(steps_local):
        for field in range(2):
            slot = 2 * index + field
            lay(keep.at[field, index], near, outer_cross.at[slot])
            lay(send.at[field, index], far, outer_straight.at[slot])
            lay(send.at[field, index], near, inner_keep.at[slot])
            lay(keep.at[field, index], far, inner_send.at[slot])


def ends_kernel(side, ratio, chips, keep, other, slab, near_cut, near_cut_other, layers, *rest):
    kappa_cut = rest[0] if side == OUTER else None
    raw_ref, factor_ref, ends_ref = rest[-3:]
    steps_local, half, cells = keep.shape[1:]
    steps = 2 * steps_local
    tile = half // 2
    groups = cells // LANES
    core = this_core()
    scales = step_scale(ratio, steps, chips, 1)
    own = pl.ds(pl.multiple_of((core if side == OUTER else 1 - core) * tile, 8), tile)
    places = []
    for position in range(2):
        sub = core if position == 0 else 1 - core
        for index in range(steps_local):
            scale = jnp.where(sub == 0, scales[index], scales[steps_local + index])
            places.append((position, index, sub * steps + 2 * index, scale))

    def work(diagonal, loads, stores):
        factors = cell_factors(diagonal, ratio)
        for slot, value in enumerate(factors):
            stores(factor_ref, slot, value)
        for position, index, slot, scale in places:
            for field in range(2):
                stores(raw_ref, slot + field, loads(position, index, field) * scale)

    def put_ends(here):
        factors = [factor_ref[slot, :, here] for slot in range(4)]
        values = lambda step: (raw_ref[2 * step, :, here], raw_ref[2 * step + 1, :, here])
        for slot, value in enumerate(local_ends(values, *factors, steps)):
            ends_ref[slot, :, here] = value

    def one(group, carry):
        here = lane_block(group * LANES)
        beyond = kappa_cut[steps, pl.ds(group, 1), :] if side == OUTER else None
        diagonal = total_weight(faces(side, slab, beyond, group, half))

        def stores(ref, slot, value):
            ref[slot, :, here] = value

        work(diagonal, lambda position, index, field: (keep, other)[position][field, index, own, here], stores)
        put_ends(here)
        return carry

    lax.fori_loop(0, groups, one, 0, unroll=UNROLL_ENDS)

    def stores_cut(ref, slot, value):
        for part in range(2):
            lanes = slice(cells + part * LANES, cells + (part + 1) * LANES)
            ref[slot, :, lanes] = value[part * tile : (part + 1) * tile]

    if side == OUTER:
        diagonal = layer_diagonal(kappa_cut[steps], layers[0], kappa_cut[steps + 1])
    else:
        diagonal = layer_diagonal(layers[2], layers[1], layers[3])
    sources = (near_cut, near_cut_other)
    work(diagonal, lambda position, index, field: sources[position][2 * index + field], stores_cut)
    for part in range(2):
        put_ends(slice(cells + part * LANES, cells + (part + 1) * LANES))


def power_sum(value, count):
    total = None
    for _ in range(count):
        total = 1.0 if total is None else 1.0 + value * total
    return total


def response_of(decay, upright, steps):
    return (0.5 * upright) * decay * power_sum(decay * decay, steps)


def ring_factors(factors, steps, chips):
    decay, _, _, upright = factors
    block = power(decay, steps)
    return block, response_of(decay, upright, steps), 1.0 / (1.0 - power(block, chips))


def contribution(ends, offset, block, response, closing):
    back, last = ends
    square = block * block
    if offset == 0:
        up, down, cross = square * block, square * block, 1.0 + square + square * square * (1.0 + square)
    elif offset == 1:
        up, down, cross = None, square, block * (1.0 + square) * (1.0 + square)
    elif offset == 2:
        up, down, cross = block, block, 2.0 * square * (1.0 + square)
    else:
        up, down, cross = square, None, block * (1.0 + square) * (1.0 + square)
    entering_back = back if up is None else up * back
    entering_state = last if down is None else down * last
    entering_state = entering_state + (cross * response * closing) * back
    return closing * entering_back, closing * entering_state


def either(flag, one, other):
    return tuple(jnp.where(flag, a, b) for a, b in zip(one, other))


def relay_kernel(side, steps, factor_ref, mine, theirs, out):
    odd = lax.rem(this_chip(), 2) == 1

    def one(here):
        ring = ring_factors([factor_ref[slot, :, here] for slot in range(4)], steps, 4)
        a = (mine[0, :, here], mine[1, :, here])
        b = (theirs[0, :, here], theirs[1, :, here])
        if side == OUTER:
            one_part = contribution(a, 2, *ring)
            other_part = either(odd, contribution(b, 1, *ring), contribution(b, 3, *ring))
        else:
            one_part = either(odd, contribution(a, 1, *ring), contribution(a, 3, *ring))
            other_part = either(odd, contribution(b, 3, *ring), contribution(b, 1, *ring))
        out[0, :, here] = one_part[0] + other_part[0]
        out[1, :, here] = one_part[1] + other_part[1]

    each_block(mine.shape[2], 4 * LANES, one)


def entering(side, factors, ends, here, steps):
    if len(ends) == 1:
        return ends[0][0, :, here], ends[0][1, :, here]
    odd = lax.rem(this_chip(), 2) == 1
    mine, theirs, tail = ends
    ring = ring_factors(factors, steps, 4)
    own = contribution((mine[0, :, here], mine[1, :, here]), 0, *ring)
    b = (theirs[0, :, here], theirs[1, :, here])
    if side == OUTER:
        near_by = either(odd, contribution(b, 3, *ring), contribution(b, 1, *ring))
    else:
        near_by = contribution(b, 2, *ring)
    return own[0] + near_by[0] + tail[0, :, here], own[1] + near_by[1] + tail[1, :, here]


def sweep_kernel(side, ratio, raw_ref, factor_ref, *rest):
    *ends, first_ref, turned_ref, layer_ref = rest
    tile = raw_ref.shape[1]
    steps = raw_ref.shape[0] // 2
    cells = first_ref.shape[2]

    def sweep(put, here):
        factors = [factor_ref[slot, :, here] for slot in range(4)]
        values = lambda step: (raw_ref[2 * step, :, here], raw_ref[2 * step + 1, :, here])
        solve_steps(values, *factors, ratio, *entering(side, factors, ends, here, steps), steps, put)

    def own(here):
        def put(step, state, adjoint):
            for field, value in enumerate((state, adjoint)):
                slot = 2 * step + field
                first_ref[slot, :, here] = value
                turned_ref[slot, :, here] = turned(value)

        sweep(put, here)

    each_block(cells, 2 * LANES, own)

    def put_layer(step, state, adjoint):
        for field, value in enumerate((state, adjoint)):
            for part in range(2):
                layer_ref[2 * step + field, part * tile : (part + 1) * tile, :] = value[:, part * LANES : (part + 1) * LANES]

    sweep(put_layer, slice(cells, cells + 2 * LANES))


def turned(value):
    parts = [pltpu.roll(value[:, i : i + LANES], NY, 1) for i in range(0, value.shape[1], LANES)]
    return parts[0] if len(parts) == 1 else jnp.concatenate(parts, axis=1)


def couplings_kernel(side, first_ref, turned_ref, next_ref, layer_ref, slab, velocity_ref, factor_ref, *rest):
    coupled_ref, ends_ref = rest[-2:]
    slots, tile, cells = first_ref.shape
    steps = slots // 2
    depth = slab.shape[0]
    half = 2 * tile
    groups = cells // LANES
    core = this_core()
    own = pl.ds(pl.multiple_of(tile_rows(side, half, depth), 8), tile)
    out_shift, in_shift = z_shifts(tile)

    def one(group, carry):
        here = lane_block(group * LANES)
        left = lane_block(jnp.maximum(group - 1, 0) * LANES)
        right = lane_block(jnp.minimum(group + 1, groups - 1) * LANES)
        row = pl.ds(group, 1)
        beyond = rest[0][steps, row, :] if side == OUTER else None
        weights = faces(side, slab, beyond, group, half)
        lane = lax.broadcasted_iota(jnp.int32, (tile, LANES), 1)
        low = lane < NY
        first, last = edge_rows((tile, LANES))
        drifts = [0.5 * velocity_ref[component, own, here] for component in (2, 0, 1)]
        drifts[0] = jnp.where(core == 0, -drifts[0], drifts[0])
        tables = []
        for sign in (1.0, -1.0):
            one_way, other_way = [], []
            for ((ahead, ok_ahead), (behind, ok_behind)), drift in zip(weights, drifts):
                one_way.append(jnp.where(ok_ahead, ahead - sign * drift, 0.0))
                other_way.append(jnp.where(ok_behind, behind + sign * drift, 0.0))
            x_same = jnp.where(low, one_way[1], other_way[1])
            x_next = jnp.where(low, other_way[1], one_way[1])
            tables.append((one_way[0], other_way[0], x_same, x_next, one_way[2], other_way[2]))
        factors = [factor_ref[slot, :, here] for slot in range(4)]

        def values(step):
            results = []
            for field in range(2):
                slot = 2 * step + field
                c_out, c_in, x_same, x_next, c_ahead, c_behind = tables[field]
                value = first_ref[slot, :, here]
                following = next_ref[slot, :, here]
                cut = layer_ref[slot, row, :]
                if side == OUTER:
                    outward = jnp.where(first, cut, pltpu.roll(value, out_shift, 0))
                    inward = pltpu.roll(jnp.where(first, following, value), in_shift, 0)
                else:
                    outward = pltpu.roll(jnp.where(last, following, value), out_shift, 0)
                    inward = jnp.where(last, cut, pltpu.roll(value, in_shift, 0))
                result = c_out * outward + c_in * inward
                beside = jnp.where(low, turned_ref[slot, :, left], turned_ref[slot, :, right])
                result = result + (x_same * turned_ref[slot, :, here] + x_next * beside)
                result = result + (c_ahead * pltpu.roll(value, LANES - 1, 1) + c_behind * pltpu.roll(value, 1, 1))
                coupled_ref[slot, :, here] = result
                results.append(result)
            return results

        for slot, value in enumerate(local_ends(values, *factors, steps)):
            ends_ref[slot, :, here] = value
        return carry

    lax.fori_loop(0, groups, one, 0, unroll=UNROLL_COUPLINGS)


def parts_kernel(ratio, outer, outer_first, outer_factors, inner, inner_first, inner_factors, keep, send, middle):
    steps_local = keep.shape[1]
    tile, cells = outer.shape[1:]
    core = this_core()
    for side, (coupled_ref, first_ref, factor_ref) in enumerate(
        ((outer, outer_first, outer_factors), (inner, inner_first, inner_factors))
    ):
        rows = slice(side * tile, (side + 1) * tile)

        def one(here):
            factors = [factor_ref[slot, :, here] for slot in range(4)]
            results = {}
            for sub in range(2):
                offset = 2 * steps_local * sub

                def values(step):
                    return coupled_ref[offset + 2 * step, :, here], coupled_ref[offset + 2 * step + 1, :, here]

                def put(step, state, adjoint):
                    results[sub, step] = (state, adjoint)

                back, last = solve_steps(values, *factors, ratio, None, None, steps_local, put)
                middle[1 - sub, rows, here] = last if sub == 0 else back
            for step in range(steps_local):
                for field in range(2):
                    early, late = [
                        first_ref[2 * steps_local * sub + 2 * step + field, :, here] + results[sub, step][field]
                        for sub in range(2)
                    ]
                    keep[field, step, rows, here] = jnp.where(core == 0, early, late)
                    send[field, step, rows, here] = jnp.where(core == 0, late, early)

        each_block(cells, 2 * LANES, one)


def carry_kernel(side, steps_local, factor_ref, middle, *rest):
    *ends, keep, send = rest
    tile, cells = keep.shape[1:]
    rows = slice(side * tile, (side + 1) * tile)
    core = this_core()

    def one(here):
        factors = [factor_ref[slot, :, here] for slot in range(4)]
        decay, _, _, upright = factors
        back, state = entering(side, factors, ends, here, 2 * steps_local)
        block = power(decay, steps_local)
        early_back = middle[0, rows, here] + block * back
        late_state = middle[1, rows, here] + block * state + response_of(decay, upright, steps_local) * early_back
        for slot, (early, late) in enumerate(((early_back, back), (state, late_state))):
            keep[slot, :, here] = jnp.where(core == 0, early, late)
            send[slot, :, here] = jnp.where(core == 0, late, early)

    each_block(cells, 4 * LANES, one)


def finish_kernel(side, ratio, chips, keep, other, keep_in, other_in, factor_ref, other_factor, *rest):
    state_out, adjoint_out, result, sems = rest[-4:]
    steps_local = keep.shape[1]
    tile, cells = keep_in.shape[1:]
    half = 2 * tile
    depth = state_out.shape[1]
    core = this_core()
    whole = step_scale(ratio, 2 * steps_local, chips, -1)
    scales = [jnp.where(core == 0, whole[step], whole[steps_local + step]) for step in range(steps_local)]
    held = slice(side * tile, (side + 1) * tile)
    start = tile_rows(side, half, depth)
    copies = []
    for part, (parts, entered, table) in enumerate(((keep, keep_in, factor_ref), (other, other_in, other_factor))):

        def one(here):
            decay, _, mixed, upright = [table[slot, :, here] for slot in range(4)]
            backs = [entered[0, :, here]]
            for _ in range(steps_local):
                backs.append(decay * backs[-1])
            backs = backs[:0:-1]
            gain = ratio * mixed
            half_up = 0.5 * upright
            previous = entered[1, :, here]
            for step in range(steps_local):
                current = decay * previous + half_up * backs[step]
                adjoint = backs[step] - gain * previous
                result[part, 0, step, :, here] = (parts[0, step, held, here] + current) * scales[step]
                result[part, 1, step, :, here] = (parts[1, step, held, here] + adjoint) * scales[step]
                previous = current

        each_block(cells, 4 * LANES, one)
        rows = pl.ds(pl.multiple_of(start if part == 0 else depth - tile - start, 8), tile)
        for field, out in enumerate((state_out, adjoint_out)):
            copies.append(pltpu.make_async_copy(result.at[part, field], out.at[:, rows, :], sems.at[part, field]))
            copies[-1].start()
    for copy in copies:
        copy.wait()


def either(flag, one, other):
    return tuple(jnp.where(flag, a, b) for a, b in zip(one, other))


def body(state_rhs, adjoint_rhs, diffusivity, velocity):
    steps_local, depth, cells = state_rhs.shape
    ranks = lax.axis_size("tm")
    slabs = lax.axis_size("gz")
    chips = ranks // 2
    total = steps_local * ranks
    steps = 2 * steps_local
    half = depth // 2
    tile = half // 2
    groups = cells // LANES
    wide = cells + 2 * LANES
    ratio = alpha_wrap ** (1.0 / total)
    core = this_core()
    f32 = jnp.float32
    anywhere = pl.BlockSpec(memory_space=pl.ANY)

    def partner(value, mask):
        return lax.ppermute(value, "tm", [(i, i ^ mask) for i in range(ranks)])

    def outward(value, flip):
        pairs = []
        for t in range(ranks):
            for g in range(slabs):
                down = (t + flip) % 2 == 1
                to = g - 1 if down else g + 1
                if 0 <= to < slabs:
                    pairs.append((t * slabs + g, (t ^ flip) * slabs + to))
        return lax.ppermute(value, ("tm", "gz"), pairs)

    def call(kernel, name, out_shape, *args, room=32, **kwargs):
        shapes = [jax.ShapeDtypeStruct(s, f32) for s in out_shape]
        return pl.pallas_call(
            kernel,
            out_shape=shapes,
            compiler_params=pltpu.CompilerParams(vmem_limit_bytes=room * 1024 * 1024),
            name=name,
            **kwargs,
        )(*args)

    layer = (groups, LANES)
    halves = (2, steps_local, half, cells)
    keep, send, slab, cross, straight, inner_keep, inner_send, layers = call(
        pack_kernel,
        "halves_and_layers",
        [halves, halves, (depth, cells), (steps + 2,) + layer, (steps,) + layer, (steps,) + layer, (steps,) + layer, (4,) + layer],
        state_rhs,
        adjoint_rhs,
        diffusivity,
        in_specs=[pl.BlockSpec(memory_space=pltpu.HBM)] * 3,
        scratch_shapes=[pltpu.SemaphoreType.DMA((5,))],
    )
    other = partner(send, 1)
    inner_other = partner(inner_send, 1)
    cross = outward(cross, 1)
    straight = outward(straight, 0)

    def first_ends(side, *args):
        return call(
            functools.partial(ends_kernel, side, ratio, chips),
            ("outer", "inner")[side] + "_ends",
            [(2 * steps, tile, wide), (4, tile, wide), (2, tile, wide)],
            keep,
            other,
            slab,
            *args,
        )

    inner_raw, inner_factors, inner_ends = first_ends(INNER, inner_keep, inner_other, layers)
    outer_raw, outer_factors, outer_ends = first_ends(OUTER, straight, cross, layers, cross)

    def exchange(side, mine, factors):
        width = mine.shape[2]
        if chips != 4:
            gathered = lax.dynamic_index_in_dim(
                lax.all_gather(mine, "tm").reshape((chips, 2) + mine.shape), core, 1, keepdims=False
            )
            block, response, closing = ring_factors([factors[i, :, :width] for i in range(4)], steps, chips)
            at = lambda array, index: lax.dynamic_index_in_dim(array, lax.rem(index + 2 * chips, chips), 0, keepdims=False)
            chip = this_chip()

            def entering_back(where):
                value = jnp.zeros((tile, width), f32)
                for offset in reversed(range(chips)):
                    value = block * value + at(gathered[:, 0], where + 1 + offset)
                return value * closing

            value = jnp.zeros((tile, width), f32)
            for offset in reversed(range(chips)):
                source = chip - 1 - offset
                value = block * value + at(gathered[:, 1], source) + response * entering_back(source)
            return [jnp.stack([entering_back(chip), value * closing])]
        masks = (2, 4) if side == OUTER else (4, 2)
        theirs = partner(mine, masks[0])
        (passed,) = call(
            functools.partial(relay_kernel, side, steps),
            ("outer", "inner")[side] + "_relay",
            [mine.shape],
            factors,
            mine,
            theirs,
        )
        return [mine, theirs, partner(passed, masks[1])]

    def first_sweep(side, raw, factors, ends):
        return call(
            functools.partial(sweep_kernel, side, ratio),
            ("outer", "inner")[side] + "_first_sweep",
            [(2 * steps, tile, cells)] * 2 + [(2 * steps,) + layer],
            raw,
            factors,
            *ends,
        )

    inner_first, inner_turned, inner_layer = first_sweep(
        INNER, inner_raw, inner_factors, exchange(INNER, inner_ends, inner_factors)
    )
    outer_first, outer_turned, outer_layer = first_sweep(
        OUTER, outer_raw, outer_factors, exchange(OUTER, outer_ends, outer_factors)
    )
    inner_factors_other = partner(inner_factors, 1)
    outer_factors_other = partner(outer_factors, 1)

    def couplings(side, *args):
        return call(
            functools.partial(couplings_kernel, side),
            ("outer", "inner")[side] + "_couplings",
            [(2 * steps, tile, cells), (2, tile, cells)],
            *args,
        )

    inner_coupled, inner_ends = couplings(
        INNER, inner_first, inner_turned, outer_first, inner_layer, slab, velocity, inner_factors
    )
    outer_coupled, outer_ends = couplings(
        OUTER, outer_first, outer_turned, inner_first, outer_layer, slab, velocity, outer_factors, cross
    )
    inner_entered = exchange(INNER, inner_ends, inner_factors)
    outer_entered = exchange(OUTER, outer_ends, outer_factors)
    keep, send, middle = call(
        functools.partial(parts_kernel, ratio),
        "own_steps",
        [halves, halves, (2, half, cells)],
        outer_coupled,
        outer_first,
        outer_factors,
        inner_coupled,
        inner_first,
        inner_factors,
    )
    other = partner(send, 1)

    def finish(side, entered, factors, factors_other, results):
        keep_in, send_in = call(
            functools.partial(carry_kernel, side, steps_local),
            ("outer", "inner")[side] + "_entering",
            [(2, tile, cells)] * 2,
            factors,
            middle,
            *entered,
        )
        other_in = partner(send_in, 1)
        vmem = pl.BlockSpec(memory_space=pltpu.VMEM)
        return call(
            functools.partial(finish_kernel, side, ratio, chips),
            ("outer", "inner")[side] + "_finish",
            [(steps_local, depth, cells)] * 2,
            keep,
            other,
            keep_in,
            other_in,
            factors,
            factors_other,
            *results,
            in_specs=[vmem] * 6 + [anywhere] * len(results),
            out_specs=[anywhere] * 2,
            scratch_shapes=[pltpu.VMEM((2, 2, steps_local, tile, cells), f32), pltpu.SemaphoreType.DMA((2, 2))],
            input_output_aliases={6 + i: i for i in range(len(results))},
            room=40,
        )

    results = finish(INNER, inner_entered, inner_factors, inner_factors_other, ())
    return finish(OUTER, outer_entered, outer_factors, outer_factors_other, results)


def solution(mesh):
    placed = (P("tm", "gz", None), P("tm", "gz", None), P("gz", None), P(None, "gz", None))
    return jax.shard_map(
        body,
        mesh=mesh,
        in_specs=placed,
        out_specs=(P("tm", "gz", None), P("tm", "gz", None)),
        check_vma=False,
    )
```

time: 54.9 us -> 49.5 us (0.902)
  waiting for transfers between devices: 21.8 us -> 14.2 us
  starting transfers between devices: 16.8 us -> 19.4 us
    ppermute x13 -> x15, waiting for transfers between devices: 20 us -> 12.4 us  [partner(): return lax.ppermute(value, 'tm', [(i, i ^ mask) for i in range(ranks)])]
    ppermute x13 -> x15, starting transfers between devices: 10.2 us -> 13 us  [partner(): return lax.ppermute(value, 'tm', [(i, i ^ mask) for i in range(ranks)])]
    pallas_call x8 -> x16, Pallas kernels: 11.9 us -> 11.5 us  [call(): pl.pallas_call(kernel, out_shape=shapes, compiler_params=pltpu.CompilerPa...]
  transfers between devices with their start and end apart: 15 -> 17, of which waited for: 10 -> 9; matrix products, arithmetic and copies ran while one was open for 0% -> 0% of each run, Pallas kernels for 2% -> 10%
where the time goes in v3:
time: 49.5 us; the launch traced here: 49.3 us
  starting transfers between devices  19.4 us (39%)
  waiting for transfers between devices  14.2 us (29%)
  Pallas kernels  11.5 us (23%)
  local copies, waits for them, and re-layouts  3.4 us (7%)
  between operations  0.82 us (2%)
    ppermute x15, starting transfers between devices, partner(): return lax.ppermute(value, 'tm', [(i, i ^ mask) for i in range(ranks)])  13 us
    ppermute x15, waiting for transfers between devices, partner(): return lax.ppermute(value, 'tm', [(i, i ^ mask) for i in range(ranks)])  12.4 us
    pallas_call x16, Pallas kernels, call(): pl.pallas_call(kernel, out_shape=shapes, compiler_params=pltpu.CompilerPa...  11.5 us
    ppermute x2, starting transfers between devices, outward(): return lax.ppermute(value, ('tm', 'gz'), pairs)  6.41 us
    unnamed x8, local copies, waits for them, and re-layouts  3.4 us
    ppermute x2, waiting for transfers between devices, outward(): return lax.ppermute(value, ('tm', 'gz'), pairs)  1.81 us
  transfers between devices with their start and end apart: 17, of which 9 were waited for; matrix products, arithmetic and copies ran while one was open for 0% of the time, Pallas kernels for 10%

profile of v3, /device:TPU:0, one launch (start us, length us, event | category | flops | bytes accessed | tf_op | source)
XLA Modules:
  0.0 49.3 jit_solution(13075851857012984295)
XLA Ops:
  0.6 1.2 %copy-done.1 = f32[4,32,2048]{2,1,0:T(8,128)S(1)} copy-done((f32[4,32,2048]{2,1,0:T(8,128)S(1)}, f32[4,32,2048]{2,1,0:T(8,128)}, u32[]{:S(2)}) %copy-start.1) | copy-done | bytes 1048600
  1.9 1.2 %copy-done.2 = f32[4,32,2048]{2,1,0:T(8,128)S(1)} copy-done((f32[4,32,2048]{2,1,0:T(8,128)S(1)}, f32[4,32,2048]{2,1,0:T(8,128)}, u32[]{:S(2)}) %copy-start.2) | copy-done | bytes 1048600
  3.1 0.9 %copy-done.3 = f32[32,2048]{1,0:T(8,128)S(1)} copy-done((f32[32,2048]{1,0:T(8,128)S(1)}, f32[32,2048]{1,0:T(8,128)}, u32[]{:S(2)}) %copy-start.3) | copy-done | bytes 262168
  4.5 0.5 %collective-permute-start = (f32[2,4,16,2048]{3,2,1,0:T(8,128)S(1)}, f32[2,4,16,2048]{3,2,1,0:T(8,128)S(1)}, u32[]{:S(2)}, u32[]{:S(2)}) collective-permute-start(f32[2,4,16,2048]{3,2,1,0:T(8,128)S(1)} %get-tuple-element.36), channel_id=1, source_target_pairs={{0,4},{4,0},{8,12},{12,8},{16,20},{20,16},{24,28},{28,24},{1,5},{5... | collective-permute-start | bytes 3145736 | tf_op jit(solution)/shard_map/ppermute | solution.py:576
  5.0 0.7 %collective-permute-start.2 = (f32[10,16,128]{2,1,0:T(8,128)S(1)}, f32[10,16,128]{2,1,0:T(8,128)S(1)}, u32[]{:S(2)}, u32[]{:S(2)}) collective-permute-start(f32[10,16,128]{2,1,0:T(8,128)S(1)} %get-tuple-element.39), channel_id=1, source_target_pairs={{1,4},{2,5},{3,6},{4,1},{5,2},{6,3},{9,12},{10,13},{11,14},{12,9},... | collective-permute-start | bytes 245768 | tf_op jit(solution)/shard_map/ppermute | solution.py:586
  5.7 5.8 %collective-permute-start.1 = (f32[8,16,128]{2,1,0:T(8,128)S(1)}, f32[8,16,128]{2,1,0:T(8,128)S(1)}, u32[]{:S(2)}, u32[]{:S(2)}) collective-permute-start(f32[8,16,128]{2,1,0:T(8,128)S(1)} %get-tuple-element.38), channel_id=1, source_target_pairs={{0,1},{1,2},{2,3},{5,4},{6,5},{7,6},{8,9},{9,10},{10,11},{13,12},{... | collective-permute-start | bytes 196616 | tf_op jit(solution)/shard_map/ppermute | solution.py:586
  11.5 1.8 %collective-permute-done.1.near_cut = f32[8,16,128]{2,1,0:T(8,128)S(1)} collective-permute-done((f32[8,16,128]{2,1,0:T(8,128)S(1)}, f32[8,16,128]{2,1,0:T(8,128)S(1)}, u32[]{:S(2)}, u32[]{:S(2)}) %collective-permute-start.1) | collective-permute-done | bytes 65568 | tf_op jit(solution)/shard_map/ppermute | solution.py:586
  13.3 0.9 %outer_ends.1 = (f32[16,8,2304]{2,1,0:T(8,128)S(1)}, f32[4,8,2304]{2,1,0:T(8,128)S(1)}, f32[2,8,2304]{2,1,0:T(8,128)S(1)}) custom-call(f32[2,4,16,2048]{3,2,1,0:T(8,128)S(1)} %get-tuple-element.35.keep, f32[2,4,16,2048]{3,2,1,0:T(8,128)S(1)} %collective-permute-done.other, f32[32,2048]{1,0:T(8,128)S(1)} %get-tuple-element.37.slab, ...), custom_call_target="tpu_custom_call" | custom-call | tf_op jit(solution)/shard_map/outer_ends/pallas_call | solution.py:590
  14.2 2.1 %collective-permute-start.3 = (f32[2,8,2304]{2,1,0:T(8,128)S(1)}, f32[2,8,2304]{2,1,0:T(8,128)S(1)}, u32[]{:S(2)}, u32[]{:S(2)}) collective-permute-start(f32[2,8,2304]{2,1,0:T(8,128)S(1)} %get-tuple-element.43.mine.rest_0_), channel_id=1, source_target_pairs={{0,8},{4,12},{8,0},{12,4},{16,24},{20,28},{24,16},{28,20},{1,9},{5... | collective-permute-start | bytes 442376 | tf_op jit(solution)/shard_map/ppermute | solution.py:576
  16.3 0.9 %inner_ends.1 = (f32[16,8,2304]{2,1,0:T(8,128)S(1)}, f32[4,8,2304]{2,1,0:T(8,128)S(1)}, f32[2,8,2304]{2,1,0:T(8,128)S(1)}) custom-call(f32[2,4,16,2048]{3,2,1,0:T(8,128)S(1)} %get-tuple-element.35.keep, f32[2,4,16,2048]{3,2,1,0:T(8,128)S(1)} %collective-permute-done.other, f32[32,2048]{1,0:T(8,128)S(1)} %get-tuple-element.37.slab, ...), custom_call_target="tpu_custom_call" | custom-call | tf_op jit(solution)/shard_map/inner_ends/pallas_call | solution.py:590
  17.2 1.6 %collective-permute-start.6 = (f32[2,8,2304]{2,1,0:T(8,128)S(1)}, f32[2,8,2304]{2,1,0:T(8,128)S(1)}, u32[]{:S(2)}, u32[]{:S(2)}) collective-permute-start(f32[2,8,2304]{2,1,0:T(8,128)S(1)} %get-tuple-element.50.mine.rest_0_), channel_id=1, source_target_pairs={{0,16},{4,20},{8,24},{12,28},{16,0},{20,4},{24,8},{28,12},{1,17},{... | collective-permute-start | bytes 442376 | tf_op jit(solution)/shard_map/ppermute | solution.py:576
  18.8 1.8 %collective-permute-done.3.theirs.rest_1_ = f32[2,8,2304]{2,1,0:T(8,128)S(1)} collective-permute-done((f32[2,8,2304]{2,1,0:T(8,128)S(1)}, f32[2,8,2304]{2,1,0:T(8,128)S(1)}, u32[]{:S(2)}, u32[]{:S(2)}) %collective-permute-start.3) | collective-permute-done | bytes 147488 | tf_op jit(solution)/shard_map/ppermute | solution.py:576
  20.8 2.3 %collective-permute-start.4 = (f32[2,8,2304]{2,1,0:T(8,128)S(1)}, f32[2,8,2304]{2,1,0:T(8,128)S(1)}, u32[]{:S(2)}, u32[]{:S(2)}) collective-permute-start(f32[2,8,2304]{2,1,0:T(8,128)S(1)} %outer_relay.2), channel_id=1, source_target_pairs={{0,16},{4,20},{8,24},{12,28},{16,0},{20,4},{24,8},{28,12},{1,17},{... | collective-permute-start | bytes 442376 | tf_op jit(solution)/shard_map/ppermute | solution.py:576
  23.1 0.4 collective-permute-done.6.theirs.rest_1_
  23.7 1.1 %collective-permute-start.7 = (f32[2,8,2304]{2,1,0:T(8,128)S(1)}, f32[2,8,2304]{2,1,0:T(8,128)S(1)}, u32[]{:S(2)}, u32[]{:S(2)}) collective-permute-start(f32[2,8,2304]{2,1,0:T(8,128)S(1)} %inner_relay.2), channel_id=1, source_target_pairs={{0,8},{4,12},{8,0},{12,4},{16,24},{20,28},{24,16},{28,20},{1,9},{5... | collective-permute-start | bytes 442376 | tf_op jit(solution)/shard_map/ppermute | solution.py:576
  24.8 2.3 %collective-permute-done.4.rest_2_ = f32[2,8,2304]{2,1,0:T(8,128)S(1)} collective-permute-done((f32[2,8,2304]{2,1,0:T(8,128)S(1)}, f32[2,8,2304]{2,1,0:T(8,128)S(1)}, u32[]{:S(2)}, u32[]{:S(2)}) %collective-permute-start.4) | collective-permute-done | bytes 147488 | tf_op jit(solution)/shard_map/ppermute | solution.py:576
  27.1 1.1 %outer_first_sweep.1 = (f32[16,8,2048]{2,1,0:T(8,128)S(1)}, f32[16,8,2048]{2,1,0:T(8,128)S(1)}, f32[16,16,128]{2,1,0:T(8,128)S(1)}) custom-call(f32[16,8,2304]{2,1,0:T(8,128)S(1)} %get-tuple-element.41.raw_ref, f32[4,8,2304]{2,1,0:T(8,128)S(1)} %get-tuple-element.42.factor_ref.outer_factors, f32[2,8,2304]{2,1,0:T(8,128)S(1)} %get-tuple-element.43.mine.rest_0_, ...), custom_call_target="tpu_custom_call" | custom-call | tf_op jit(solution)/shard_map/outer_first_sweep/pallas_call | solution.py:590
  28.3 1.0 %collective-permute-done.7.rest_2_ = f32[2,8,2304]{2,1,0:T(8,128)S(1)} collective-permute-done((f32[2,8,2304]{2,1,0:T(8,128)S(1)}, f32[2,8,2304]{2,1,0:T(8,128)S(1)}, u32[]{:S(2)}, u32[]{:S(2)}) %collective-permute-start.7) | collective-permute-done | bytes 147488 | tf_op jit(solution)/shard_map/ppermute | solution.py:576
  29.3 1.1 %inner_first_sweep.1 = (f32[16,8,2048]{2,1,0:T(8,128)S(1)}, f32[16,8,2048]{2,1,0:T(8,128)S(1)}, f32[16,16,128]{2,1,0:T(8,128)S(1)}) custom-call(f32[16,8,2304]{2,1,0:T(8,128)S(1)} %get-tuple-element.48.raw_ref, f32[4,8,2304]{2,1,0:T(8,128)S(1)} %get-tuple-element.49.factor_ref.inner_factors, f32[2,8,2304]{2,1,0:T(8,128)S(1)} %get-tuple-element.50.mine.rest_0_, ...), custom_call_target="tpu_custom_call" | custom-call | tf_op jit(solution)/shard_map/inner_first_sweep/pallas_call | solution.py:590
  30.4 1.5 %inner_couplings.1 = (f32[16,8,2048]{2,1,0:T(8,128)S(1)}, f32[2,8,2048]{2,1,0:T(8,128)S(1)}) custom-call(f32[16,8,2048]{2,1,0:T(8,128)S(1)} %get-tuple-element.51.next_ref.first_ref.inner_first, f32[16,8,2048]{2,1,0:T(8,128)S(1)} %get-tuple-element.54.turned_ref, f32[16,8,2048]{2,1,0:T(8,128)S(1)} %get-tuple-element.44.first_ref.next_ref.outer_first, ...), custom_call_target="tpu_custom_call" | custom-call | tf_op jit(solution)/shard_map/inner_couplings/pallas_call | solution.py:590
  31.9 1.5 %outer_couplings.1 = (f32[16,8,2048]{2,1,0:T(8,128)S(1)}, f32[2,8,2048]{2,1,0:T(8,128)S(1)}) custom-call(f32[16,8,2048]{2,1,0:T(8,128)S(1)} %get-tuple-element.44.first_ref.next_ref.outer_first, f32[16,8,2048]{2,1,0:T(8,128)S(1)} %get-tuple-element.45.turned_ref, f32[16,8,2048]{2,1,0:T(8,128)S(1)} %get-tuple-element.51.next_ref.first_ref.inner_first, ...), custom_call_target="tpu_custom_call" | custom-call | tf_op jit(solution)/shard_map/outer_couplings/pallas_call | solution.py:590
  33.5 0.6 %own_steps.1 = (f32[2,4,16,2048]{3,2,1,0:T(8,128)S(1)}, f32[2,4,16,2048]{3,2,1,0:T(8,128)S(1)}, f32[2,16,2048]{2,1,0:T(8,128)S(1)}) custom-call(f32[16,8,2048]{2,1,0:T(8,128)S(1)} %get-tuple-element.53.outer, f32[16,8,2048]{2,1,0:T(8,128)S(1)} %get-tuple-element.44.first_ref.next_ref.outer_first, ...), custom_call_target="tpu_custom_call" | custom-call | tf_op jit(solution)/shard_map/own_steps/pallas_call | solution.py:590
  34.2 1.6 %collective-permute-start.13 = (f32[2,8,2048]{2,1,0:T(8,128)S(1)}, f32[2,8,2048]{2,1,0:T(8,128)S(1)}, u32[]{:S(2)}, u32[]{:S(2)}) collective-permute-start(f32[2,8,2048]{2,1,0:T(8,128)S(1)} %get-tuple-element.63.mine.rest_0_), channel_id=1, source_target_pairs={{0,16},{4,20},{8,24},{12,28},{16,0},{20,4},{24,8},{28,12},{1,17},{... | collective-permute-start | bytes 393224 | tf_op jit(solution)/shard_map/ppermute | solution.py:576
  35.8 0.7 %collective-permute-start.9 = (f32[2,8,2048]{2,1,0:T(8,128)S(1)}, f32[2,8,2048]{2,1,0:T(8,128)S(1)}, u32[]{:S(2)}, u32[]{:S(2)}) collective-permute-start(f32[2,8,2048]{2,1,0:T(8,128)S(1)} %get-tuple-element.60.mine.rest_0_), channel_id=1, source_target_pairs={{0,8},{4,12},{8,0},{12,4},{16,24},{20,28},{24,16},{28,20},{1,9},{5... | collective-permute-start | bytes 393224 | tf_op jit(solution)/shard_map/ppermute | solution.py:576
  36.4 0.5 %collective-permute-start.12 = (f32[4,8,2304]{2,1,0:T(8,128)S(1)}, f32[4,8,2304]{2,1,0:T(8,128)S(1)}, u32[]{:S(2)}, u32[]{:S(2)}) collective-permute-start(f32[4,8,2304]{2,1,0:T(8,128)S(1)} %get-tuple-element.42.factor_ref.outer_factors), channel_id=1, source_target_pairs={{0,4},{4,0},{8,12},{12,8},{16,20},{20,16},{24,28},{28,24},{1,5},{5... | collective-permute-start | bytes 884744 | tf_op jit(solution)/shard_map/ppermute | solution.py:576
  37.0 3.1 %collective-permute-done.13.theirs.rest_1_ = f32[2,8,2048]{2,1,0:T(8,128)S(1)} collective-permute-done((f32[2,8,2048]{2,1,0:T(8,128)S(1)}, f32[2,8,2048]{2,1,0:T(8,128)S(1)}, u32[]{:S(2)}, u32[]{:S(2)}) %collective-permute-start.13) | collective-permute-done | bytes 131104 | tf_op jit(solution)/shard_map/ppermute | solution.py:576
  40.2 1.1 %collective-permute-start.14 = (f32[2,8,2048]{2,1,0:T(8,128)S(1)}, f32[2,8,2048]{2,1,0:T(8,128)S(1)}, u32[]{:S(2)}, u32[]{:S(2)}) collective-permute-start(f32[2,8,2048]{2,1,0:T(8,128)S(1)} %inner_relay.3), channel_id=1, source_target_pairs={{0,8},{4,12},{8,0},{12,4},{16,24},{20,28},{24,16},{28,20},{1,9},{5... | collective-permute-start | bytes 393224 | tf_op jit(solution)/shard_map/ppermute | solution.py:576
  41.5 1.3 %collective-permute-start.10 = (f32[2,8,2048]{2,1,0:T(8,128)S(1)}, f32[2,8,2048]{2,1,0:T(8,128)S(1)}, u32[]{:S(2)}, u32[]{:S(2)}) collective-permute-start(f32[2,8,2048]{2,1,0:T(8,128)S(1)} %outer_relay.3), channel_id=1, source_target_pairs={{0,16},{4,20},{8,24},{12,28},{16,0},{20,4},{24,8},{28,12},{1,17},{... | collective-permute-start | bytes 393224 | tf_op jit(solution)/shard_map/ppermute | solution.py:576
  42.7 2.6 %collective-permute-done.14.rest_2_ = f32[2,8,2048]{2,1,0:T(8,128)S(1)} collective-permute-done((f32[2,8,2048]{2,1,0:T(8,128)S(1)}, f32[2,8,2048]{2,1,0:T(8,128)S(1)}, u32[]{:S(2)}, u32[]{:S(2)}) %collective-permute-start.14) | collective-permute-done | bytes 131104 | tf_op jit(solution)/shard_map/ppermute | solution.py:576
  45.6 0.9 %collective-permute-done.10.rest_2_ = f32[2,8,2048]{2,1,0:T(8,128)S(1)} collective-permute-done((f32[2,8,2048]{2,1,0:T(8,128)S(1)}, f32[2,8,2048]{2,1,0:T(8,128)S(1)}, u32[]{:S(2)}, u32[]{:S(2)}) %collective-permute-start.10) | collective-permute-done | bytes 131104 | tf_op jit(solution)/shard_map/ppermute | solution.py:576
  47.0 1.1 %inner_finish.1 = (f32[4,32,2048]{2,1,0:T(8,128)}, f32[4,32,2048]{2,1,0:T(8,128)}) custom-call(f32[2,4,16,2048]{3,2,1,0:T(8,128)S(1)} %get-tuple-element.57.keep, f32[2,4,16,2048]{3,2,1,0:T(8,128)S(1)} %collective-permute-done.8.other, f32[2,8,2048]{2,1,0:T(8,128)S(1)} %get-tuple-element.64.keep_in, f32[2,8,2048]{2,1,0:T(8,128)S(1)} %collective-permute-done.15.other_in, ...), custom_call_target="tpu_custom_call" | custom-call | tf_op jit(solution)/shard_map/inner_finish/pallas_call | solution.py:590
  48.1 1.1 %outer_finish.1 = (f32[4,32,2048]{2,1,0:T(8,128)}, f32[4,32,2048]{2,1,0:T(8,128)}) custom-call(f32[2,4,16,2048]{3,2,1,0:T(8,128)S(1)} %get-tuple-element.57.keep, f32[2,4,16,2048]{3,2,1,0:T(8,128)S(1)} %collective-permute-done.8.other, f32[2,8,2048]{2,1,0:T(8,128)S(1)} %get-tuple-element.61.keep_in, ...), custom_call_target="tpu_custom_call", output_to_operand_aliasing={{0}: (6, {}), {1}: (7, {})} | custom-call | tf_op jit(solution)/shard_map/outer_finish/pallas_call | solution.py:590
  (26 shorter events, 2.0 us)
Async XLA Ops:
  0.6 1.2 %copy-start.1 = (f32[4,32,2048]{2,1,0:T(8,128)S(1)}, f32[4,32,2048]{2,1,0:T(8,128)}, u32[]{:S(2)}) copy-start(f32[4,32,2048]{2,1,0:T(8,128)} %state.1) | copy-start | bytes 3145732
  1.9 1.2 %copy-start.2 = (f32[4,32,2048]{2,1,0:T(8,128)S(1)}, f32[4,32,2048]{2,1,0:T(8,128)}, u32[]{:S(2)}) copy-start(f32[4,32,2048]{2,1,0:T(8,128)} %adjoint.1) | copy-start | bytes 3145732
  3.1 0.9 %copy-start.3 = (f32[32,2048]{1,0:T(8,128)S(1)}, f32[32,2048]{1,0:T(8,128)}, u32[]{:S(2)}) copy-start(f32[32,2048]{1,0:T(8,128)} %kappa.1) | copy-start | bytes 786436
  4.5 8.8 %collective-permute-start = (f32[2,4,16,2048]{3,2,1,0:T(8,128)S(1)}, f32[2,4,16,2048]{3,2,1,0:T(8,128)S(1)}, u32[]{:S(2)}, u32[]{:S(2)}) collective-permute-start(f32[2,4,16,2048]{3,2,1,0:T(8,128)S(1)} %get-tuple-element.36), channel_id=1, source_target_pairs={{0,4},{4,0},{8,12},{12,8},{16,20},{20,16},{24,28},{28,24},{1,5},{5... | collective-permute-start | bytes 3145736 | tf_op jit(solution)/shard_map/ppermute | solution.py:576
  5.0 8.3 %collective-permute-start.2 = (f32[10,16,128]{2,1,0:T(8,128)S(1)}, f32[10,16,128]{2,1,0:T(8,128)S(1)}, u32[]{:S(2)}, u32[]{:S(2)}) collective-permute-start(f32[10,16,128]{2,1,0:T(8,128)S(1)} %get-tuple-element.39), channel_id=1, source_target_pairs={{1,4},{2,5},{3,6},{4,1},{5,2},{6,3},{9,12},{10,13},{11,14},{12,9},... | collective-permute-start | bytes 245768 | tf_op jit(solution)/shard_map/ppermute | solution.py:586
  5.7 7.7 %collective-permute-start.1 = (f32[8,16,128]{2,1,0:T(8,128)S(1)}, f32[8,16,128]{2,1,0:T(8,128)S(1)}, u32[]{:S(2)}, u32[]{:S(2)}) collective-permute-start(f32[8,16,128]{2,1,0:T(8,128)S(1)} %get-tuple-element.38), channel_id=1, source_target_pairs={{0,1},{1,2},{2,3},{5,4},{6,5},{7,6},{8,9},{9,10},{10,11},{13,12},{... | collective-permute-start | bytes 196616 | tf_op jit(solution)/shard_map/ppermute | solution.py:586
  11.4 4.9 %collective-permute-start.5 = (f32[8,16,128]{2,1,0:T(8,128)S(1)}, f32[8,16,128]{2,1,0:T(8,128)S(1)}, u32[]{:S(2)}, u32[]{:S(2)}) collective-permute-start(f32[8,16,128]{2,1,0:T(8,128)S(1)} %get-tuple-element.47), channel_id=1, source_target_pairs={{0,4},{4,0},{8,12},{12,8},{16,20},{20,16},{24,28},{28,24},{1,5},{5... | collective-permute-start | bytes 196616 | tf_op jit(solution)/shard_map/ppermute | solution.py:576
  14.2 6.4 %collective-permute-start.3 = (f32[2,8,2304]{2,1,0:T(8,128)S(1)}, f32[2,8,2304]{2,1,0:T(8,128)S(1)}, u32[]{:S(2)}, u32[]{:S(2)}) collective-permute-start(f32[2,8,2304]{2,1,0:T(8,128)S(1)} %get-tuple-element.43.mine.rest_0_), channel_id=1, source_target_pairs={{0,8},{4,12},{8,0},{12,4},{16,24},{20,28},{24,16},{28,20},{1,9},{5... | collective-permute-start | bytes 442376 | tf_op jit(solution)/shard_map/ppermute | solution.py:576
  17.2 6.3 %collective-permute-start.6 = (f32[2,8,2304]{2,1,0:T(8,128)S(1)}, f32[2,8,2304]{2,1,0:T(8,128)S(1)}, u32[]{:S(2)}, u32[]{:S(2)}) collective-permute-start(f32[2,8,2304]{2,1,0:T(8,128)S(1)} %get-tuple-element.50.mine.rest_0_), channel_id=1, source_target_pairs={{0,16},{4,20},{8,24},{12,28},{16,0},{20,4},{24,8},{28,12},{1,17},{... | collective-permute-start | bytes 442376 | tf_op jit(solution)/shard_map/ppermute | solution.py:576
  20.8 6.3 %collective-permute-start.4 = (f32[2,8,2304]{2,1,0:T(8,128)S(1)}, f32[2,8,2304]{2,1,0:T(8,128)S(1)}, u32[]{:S(2)}, u32[]{:S(2)}) collective-permute-start(f32[2,8,2304]{2,1,0:T(8,128)S(1)} %outer_relay.2), channel_id=1, source_target_pairs={{0,16},{4,20},{8,24},{12,28},{16,0},{20,4},{24,8},{28,12},{1,17},{... | collective-permute-start | bytes 442376 | tf_op jit(solution)/shard_map/ppermute | solution.py:576
  23.7 5.5 %collective-permute-start.7 = (f32[2,8,2304]{2,1,0:T(8,128)S(1)}, f32[2,8,2304]{2,1,0:T(8,128)S(1)}, u32[]{:S(2)}, u32[]{:S(2)}) collective-permute-start(f32[2,8,2304]{2,1,0:T(8,128)S(1)} %inner_relay.2), channel_id=1, source_target_pairs={{0,8},{4,12},{8,0},{12,4},{16,24},{20,28},{24,16},{28,20},{1,9},{5... | collective-permute-start | bytes 442376 | tf_op jit(solution)/shard_map/ppermute | solution.py:576
  28.3 2.1 %copy-start = (f32[3,32,2048]{2,1,0:T(8,128)S(1)}, f32[3,32,2048]{2,1,0:T(8,128)}, u32[]{:S(2)}) copy-start(f32[3,32,2048]{2,1,0:T(8,128)} %velocity_ref.3) | copy-start | bytes 2359300
  34.1 12.9 %collective-permute-start.8 = (f32[2,4,16,2048]{3,2,1,0:T(8,128)S(1)}, f32[2,4,16,2048]{3,2,1,0:T(8,128)S(1)}, u32[]{:S(2)}, u32[]{:S(2)}) collective-permute-start(f32[2,4,16,2048]{3,2,1,0:T(8,128)S(1)} %get-tuple-element.58), channel_id=1, source_target_pairs={{0,4},{4,0},{8,12},{12,8},{16,20},{20,16},{24,28},{28,24},{1,5},{5... | collective-permute-start | bytes 3145736 | tf_op jit(solution)/shard_map/ppermute | solution.py:576
  34.2 5.9 %collective-permute-start.13 = (f32[2,8,2048]{2,1,0:T(8,128)S(1)}, f32[2,8,2048]{2,1,0:T(8,128)S(1)}, u32[]{:S(2)}, u32[]{:S(2)}) collective-permute-start(f32[2,8,2048]{2,1,0:T(8,128)S(1)} %get-tuple-element.63.mine.rest_0_), channel_id=1, source_target_pairs={{0,16},{4,20},{8,24},{12,28},{16,0},{20,4},{24,8},{28,12},{1,17},{... | collective-permute-start | bytes 393224 | tf_op jit(solution)/shard_map/ppermute | solution.py:576
  35.8 5.6 %collective-permute-start.9 = (f32[2,8,2048]{2,1,0:T(8,128)S(1)}, f32[2,8,2048]{2,1,0:T(8,128)S(1)}, u32[]{:S(2)}, u32[]{:S(2)}) collective-permute-start(f32[2,8,2048]{2,1,0:T(8,128)S(1)} %get-tuple-element.60.mine.rest_0_), channel_id=1, source_target_pairs={{0,8},{4,12},{8,0},{12,4},{16,24},{20,28},{24,16},{28,20},{1,9},{5... | collective-permute-start | bytes 393224 | tf_op jit(solution)/shard_map/ppermute | solution.py:576
  36.4 10.4 %collective-permute-start.16 = (f32[4,8,2304]{2,1,0:T(8,128)S(1)}, f32[4,8,2304]{2,1,0:T(8,128)S(1)}, u32[]{:S(2)}, u32[]{:S(2)}) collective-permute-start(f32[4,8,2304]{2,1,0:T(8,128)S(1)} %get-tuple-element.49.factor_ref.inner_factors), channel_id=1, source_target_pairs={{0,4},{4,0},{8,12},{12,8},{16,20},{20,16},{24,28},{28,24},{1,5},{5... | collective-permute-start | bytes 884744 | tf_op jit(solution)/shard_map/ppermute | solution.py:576
  36.4 11.7 %collective-permute-start.12 = (f32[4,8,2304]{2,1,0:T(8,128)S(1)}, f32[4,8,2304]{2,1,0:T(8,128)S(1)}, u32[]{:S(2)}, u32[]{:S(2)}) collective-permute-start(f32[4,8,2304]{2,1,0:T(8,128)S(1)} %get-tuple-element.42.factor_ref.outer_factors), channel_id=1, source_target_pairs={{0,4},{4,0},{8,12},{12,8},{16,20},{20,16},{24,28},{28,24},{1,5},{5... | collective-permute-start | bytes 884744 | tf_op jit(solution)/shard_map/ppermute | solution.py:576
  40.2 5.1 %collective-permute-start.14 = (f32[2,8,2048]{2,1,0:T(8,128)S(1)}, f32[2,8,2048]{2,1,0:T(8,128)S(1)}, u32[]{:S(2)}, u32[]{:S(2)}) collective-permute-start(f32[2,8,2048]{2,1,0:T(8,128)S(1)} %inner_relay.3), channel_id=1, source_target_pairs={{0,8},{4,12},{8,0},{12,4},{16,24},{20,28},{24,16},{28,20},{1,9},{5... | collective-permute-start | bytes 393224 | tf_op jit(solution)/shard_map/ppermute | solution.py:576
  41.5 5.0 %collective-permute-start.10 = (f32[2,8,2048]{2,1,0:T(8,128)S(1)}, f32[2,8,2048]{2,1,0:T(8,128)S(1)}, u32[]{:S(2)}, u32[]{:S(2)}) collective-permute-start(f32[2,8,2048]{2,1,0:T(8,128)S(1)} %outer_relay.3), channel_id=1, source_target_pairs={{0,16},{4,20},{8,24},{12,28},{16,0},{20,4},{24,8},{28,12},{1,17},{... | collective-permute-start | bytes 393224 | tf_op jit(solution)/shard_map/ppermute | solution.py:576
  45.6 1.4 %collective-permute-start.15 = (f32[2,8,2048]{2,1,0:T(8,128)S(1)}, f32[2,8,2048]{2,1,0:T(8,128)S(1)}, u32[]{:S(2)}, u32[]{:S(2)}) collective-permute-start(f32[2,8,2048]{2,1,0:T(8,128)S(1)} %get-tuple-element.65), channel_id=1, source_target_pairs={{0,4},{4,0},{8,12},{12,8},{16,20},{20,16},{24,28},{28,24},{1,5},{5... | collective-permute-start | bytes 393224 | tf_op jit(solution)/shard_map/ppermute | solution.py:576
  46.7 1.4 %collective-permute-start.11 = (f32[2,8,2048]{2,1,0:T(8,128)S(1)}, f32[2,8,2048]{2,1,0:T(8,128)S(1)}, u32[]{:S(2)}, u32[]{:S(2)}) collective-permute-start(f32[2,8,2048]{2,1,0:T(8,128)S(1)} %get-tuple-element.62), channel_id=1, source_target_pairs={{0,4},{4,0},{8,12},{12,8},{16,20},{20,16},{24,28},{28,24},{1,5},{5... | collective-permute-start | bytes 393224 | tf_op jit(solution)/shard_map/ppermute | solution.py:576

commit v4 on v3

--- a/solution.py
+++ b/solution.py
@@ -61,6 +61,18 @@
 
 
 OUTER, INNER = 0, 1
+MICROSECONDS = {
+    'halves': 2,
+    'outermost': 0.3,
+    'ends': 1,
+    'relay': 0.2,
+    'first_sweep': 1.1,
+    'couplings': 1.5,
+    'own_steps': 0.7,
+    'entering': 0.2,
+    'finish_own': 1.2,
+    'finish_other': 1.2,
+}
 UNROLL_ENDS = 4
 UNROLL_COUPLINGS = 2
 
@@ -191,47 +203,56 @@
     return backs[0], previous
 
 
-def pack_kernel(state, adjoint, kappa, keep, send, slab, outer_cross, outer_straight, inner_keep, inner_send, layers, sems):
-    steps_local = state.shape[0]
-    half = keep.shape[2]
+def pack_kernel(state, adjoint, kappa, keep, send, slab, edge, edge_send, layers, sems):
+    steps_local, depth, cells = state.shape
+    half = depth // 2
     core = this_core()
     mine = pl.ds(pl.multiple_of(core * half, 8), half)
     others = pl.ds(pl.multiple_of((1 - core) * half, 8), half)
+    within = pl.ds(0, cells)
     copies = [pltpu.make_async_copy(kappa, slab, sems.at[4])]
     for field, source in enumerate((state, adjoint)):
-        copies.append(pltpu.make_async_copy(source.at[:, mine, :], keep.at[field], sems.at[2 * field]))
-        copies.append(pltpu.make_async_copy(source.at[:, others, :], send.at[field], sems.at[2 * field + 1]))
+        copies.append(pltpu.make_async_copy(source.at[:, mine, :], keep.at[field, :, :, within], sems.at[2 * field]))
+        copies.append(pltpu.make_async_copy(source.at[:, others, :], send.at[field, :, :, within], sems.at[2 * field + 1]))
     for copy in copies:
         copy.start()
 
     def lay(source, rows, target):
-        for group in range(target.shape[0]):
+        for group in range(cells // LANES):
             lanes = slice(group * LANES, (group + 1) * LANES)
             one, other = [source[row : row + 1, lanes] for row in rows]
             target[group : group + 1, :] = jnp.where(core == 0, one, other)
 
     copies[0].wait()
-    last = 2 * half - 1
-    lay(slab, (0, last), outer_cross.at[2 * steps_local])
-    lay(slab, (1, last - 1), outer_cross.at[2 * steps_local + 1])
+    last = depth - 1
+    lay(slab, (0, last), edge.at[2 * steps_local])
+    lay(slab, (1, last - 1), edge.at[2 * steps_local + 1])
     for slot, row in enumerate((0, half - 1, half, half + 1)):
         lay(slab, (row, last - row), layers.at[slot])
     for copy in copies[1:]:
         copy.wait()
     near, far = (0, half - 1), (half - 1, 0)
+    beyond = pl.ds(cells, LANES)
     for index in range(steps_local):
         for field in range(2):
             slot = 2 * index + field
-            lay(keep.at[field, index], near, outer_cross.at[slot])
-            lay(send.at[field, index], far, outer_straight.at[slot])
-            lay(send.at[field, index], near, inner_keep.at[slot])
-            lay(keep.at[field, index], far, inner_send.at[slot])
-
-
-def ends_kernel(side, ratio, chips, keep, other, slab, near_cut, near_cut_other, layers, *rest):
-    kappa_cut = rest[0] if side == OUTER else None
+            lay(keep.at[field, index], near, edge.at[slot])
+            lay(send.at[field, index], far, edge_send.at[slot])
+            lay(send.at[field, index], near, keep.at[field, index, :, beyond])
+            lay(keep.at[field, index], far, send.at[field, index, :, beyond])
+
+
+def join_kernel(edge, edge_other, swap, both, swap_out):
+    count = edge.shape[0]
+    both[:count] = edge[...]
+    both[count:] = edge_other[...]
+
+
+def ends_kernel(side, ratio, chips, keep, other, slab, layers, *rest):
+    cut = rest[0] if side == OUTER else None
     raw_ref, factor_ref, ends_ref = rest[-3:]
     steps_local, half, cells = keep.shape[1:]
+    cells = cells - LANES
     steps = 2 * steps_local
     tile = half // 2
     groups = cells // LANES
@@ -261,7 +282,7 @@
 
     def one(group, carry):
         here = lane_block(group * LANES)
-        beyond = kappa_cut[steps, pl.ds(group, 1), :] if side == OUTER else None
+        beyond = cut[steps, pl.ds(group, 1), :] if side == OUTER else None
         diagonal = total_weight(faces(side, slab, beyond, group, half))
 
         def stores(ref, slot, value):
@@ -279,11 +300,13 @@
             ref[slot, :, lanes] = value[part * tile : (part + 1) * tile]
 
     if side == OUTER:
-        diagonal = layer_diagonal(kappa_cut[steps], layers[0], kappa_cut[steps + 1])
+        diagonal = layer_diagonal(cut[steps], layers[0], cut[steps + 1])
+        starts = (steps + 2, 0)
+        loads = lambda position, index, field: cut[starts[position] + 2 * index + field]
     else:
         diagonal = layer_diagonal(layers[2], layers[1], layers[3])
-    sources = (near_cut, near_cut_other)
-    work(diagonal, lambda position, index, field: sources[position][2 * index + field], stores_cut)
+        loads = lambda position, index, field: (keep, other)[position][field, index, :, cells:]
+    work(diagonal, loads, stores_cut)
     for part in range(2):
         put_ends(slice(cells + part * LANES, cells + (part + 1) * LANES))
 
@@ -458,8 +481,14 @@
     lax.fori_loop(0, groups, one, 0, unroll=UNROLL_COUPLINGS)
 
 
-def parts_kernel(ratio, outer, outer_first, outer_factors, inner, inner_first, inner_factors, keep, send, middle):
-    steps_local = keep.shape[1]
+def finish_factors(ratio, factors):
+    decay, _, mixed, upright = factors
+    return decay, ratio * mixed, 0.5 * upright
+
+
+def parts_kernel(ratio, outer, outer_first, outer_factors, inner, inner_first, inner_factors, *rest):
+    keep, send, middle = rest[-3:]
+    steps_local = keep.shape[0] // 2
     tile, cells = outer.shape[1:]
     core = this_core()
     for side, (coupled_ref, first_ref, factor_ref) in enumerate(
@@ -469,6 +498,8 @@
 
         def one(here):
             factors = [factor_ref[slot, :, here] for slot in range(4)]
+            for slot, value in enumerate(finish_factors(ratio, factors)):
+                send[2 * steps_local + slot, rows, here] = value
             results = {}
             for sub in range(2):
                 offset = 2 * steps_local * sub
@@ -487,8 +518,9 @@
                         first_ref[2 * steps_local * sub + 2 * step + field, :, here] + results[sub, step][field]
                         for sub in range(2)
                     ]
-                    keep[field, step, rows, here] = jnp.where(core == 0, early, late)
-                    send[field, step, rows, here] = jnp.where(core == 0, late, early)
+                    slot = 2 * step + field
+                    keep[slot, rows, here] = jnp.where(core == 0, early, late)
+                    send[slot, rows, here] = jnp.where(core == 0, late, early)
 
         each_block(cells, 2 * LANES, one)
 
@@ -513,47 +545,43 @@
     each_block(cells, 4 * LANES, one)
 
 
-def finish_kernel(side, ratio, chips, keep, other, keep_in, other_in, factor_ref, other_factor, *rest):
+def finish_kernel(theirs, ratio, chips, parts, *rest):
     state_out, adjoint_out, result, sems = rest[-4:]
-    steps_local = keep.shape[1]
-    tile, cells = keep_in.shape[1:]
-    half = 2 * tile
-    depth = state_out.shape[1]
+    tile, cells = rest[0].shape[1:]
+    steps_local, depth = state_out.shape[:2]
     core = this_core()
     whole = step_scale(ratio, 2 * steps_local, chips, -1)
     scales = [jnp.where(core == 0, whole[step], whole[steps_local + step]) for step in range(steps_local)]
-    held = slice(side * tile, (side + 1) * tile)
-    start = tile_rows(side, half, depth)
     copies = []
-    for part, (parts, entered, table) in enumerate(((keep, keep_in, factor_ref), (other, other_in, other_factor))):
+    for side in (OUTER, INNER):
+        entered = rest[side]
+        held = slice(side * tile, (side + 1) * tile)
+        start = tile_rows(side, 2 * tile, depth)
+        rows = pl.ds(pl.multiple_of(depth - tile - start if theirs else start, 8), tile)
 
         def one(here):
-            decay, _, mixed, upright = [table[slot, :, here] for slot in range(4)]
+            if theirs:
+                decay, gain, half_up = [parts[2 * steps_local + slot, held, here] for slot in range(3)]
+            else:
+                decay, gain, half_up = finish_factors(ratio, [rest[2 + side][slot, :, here] for slot in range(4)])
             backs = [entered[0, :, here]]
             for _ in range(steps_local):
                 backs.append(decay * backs[-1])
             backs = backs[:0:-1]
-            gain = ratio * mixed
-            half_up = 0.5 * upright
             previous = entered[1, :, here]
             for step in range(steps_local):
                 current = decay * previous + half_up * backs[step]
                 adjoint = backs[step] - gain * previous
-                result[part, 0, step, :, here] = (parts[0, step, held, here] + current) * scales[step]
-                result[part, 1, step, :, here] = (parts[1, step, held, here] + adjoint) * scales[step]
+                result[side, 0, step, :, here] = (parts[2 * step, held, here] + current) * scales[step]
+                result[side, 1, step, :, here] = (parts[2 * step + 1, held, here] + adjoint) * scales[step]
                 previous = current
 
         each_block(cells, 4 * LANES, one)
-        rows = pl.ds(pl.multiple_of(start if part == 0 else depth - tile - start, 8), tile)
         for field, out in enumerate((state_out, adjoint_out)):
-            copies.append(pltpu.make_async_copy(result.at[part, field], out.at[:, rows, :], sems.at[part, field]))
+            copies.append(pltpu.make_async_copy(result.at[side, field], out.at[:, rows, :], sems.at[side, field]))
             copies[-1].start()
     for copy in copies:
         copy.wait()
-
-
-def either(flag, one, other):
-    return tuple(jnp.where(flag, a, b) for a, b in zip(one, other))
 
 
 def body(state_rhs, adjoint_rhs, diffusivity, velocity):
@@ -571,46 +599,55 @@
     core = this_core()
     f32 = jnp.float32
     anywhere = pl.BlockSpec(memory_space=pl.ANY)
+    vmem = pl.BlockSpec(memory_space=pltpu.VMEM)
 
     def partner(value, mask):
         return lax.ppermute(value, "tm", [(i, i ^ mask) for i in range(ranks)])
 
-    def outward(value, flip):
+    def outward(value):
         pairs = []
         for t in range(ranks):
             for g in range(slabs):
-                down = (t + flip) % 2 == 1
-                to = g - 1 if down else g + 1
+                to = g - 1 if t % 2 == 0 else g + 1
                 if 0 <= to < slabs:
-                    pairs.append((t * slabs + g, (t ^ flip) * slabs + to))
+                    pairs.append((t * slabs + g, (t ^ 1) * slabs + to))
         return lax.ppermute(value, ("tm", "gz"), pairs)
 
-    def call(kernel, name, out_shape, *args, room=32, **kwargs):
+    def call(kernel, name, out_shape, *args, **kwargs):
         shapes = [jax.ShapeDtypeStruct(s, f32) for s in out_shape]
+        micros = next(value for word, value in MICROSECONDS.items() if word in name)
         return pl.pallas_call(
             kernel,
             out_shape=shapes,
-            compiler_params=pltpu.CompilerParams(vmem_limit_bytes=room * 1024 * 1024),
+            compiler_params=pltpu.CompilerParams(vmem_limit_bytes=32 * 1024 * 1024),
+            cost_estimate=pl.CostEstimate(flops=0, transcendentals=0, bytes_accessed=int(micros * 3.7e6)),
             name=name,
             **kwargs,
         )(*args)
 
     layer = (groups, LANES)
-    halves = (2, steps_local, half, cells)
-    keep, send, slab, cross, straight, inner_keep, inner_send, layers = call(
+    halves = (2, steps_local, half, cells + LANES)
+    keep, send, slab, edge, edge_send, layers = call(
         pack_kernel,
         "halves_and_layers",
-        [halves, halves, (depth, cells), (steps + 2,) + layer, (steps,) + layer, (steps,) + layer, (steps,) + layer, (4,) + layer],
-        state_rhs,
-        adjoint_rhs,
-        diffusivity,
-        in_specs=[pl.BlockSpec(memory_space=pltpu.HBM)] * 3,
+        [halves, halves, (depth, cells), (steps + 2,) + layer, (steps,) + layer, (4,) + layer],
+        *[pltpu.with_memory_space_constraint(x, pltpu.HBM) for x in (state_rhs, adjoint_rhs, diffusivity)],
+        in_specs=[anywhere] * 3,
         scratch_shapes=[pltpu.SemaphoreType.DMA((5,))],
     )
+    cut, send = call(
+        join_kernel,
+        "outermost_layer",
+        [(2 * steps + 2,) + layer, halves],
+        edge,
+        partner(edge_send, 1),
+        send,
+        in_specs=[vmem, vmem, anywhere],
+        out_specs=[vmem, anywhere],
+        input_output_aliases={2: 1},
+    )
     other = partner(send, 1)
-    inner_other = partner(inner_send, 1)
-    cross = outward(cross, 1)
-    straight = outward(straight, 0)
+    cut = outward(cut)
 
     def first_ends(side, *args):
         return call(
@@ -620,11 +657,12 @@
             keep,
             other,
             slab,
+            layers,
             *args,
         )
 
-    inner_raw, inner_factors, inner_ends = first_ends(INNER, inner_keep, inner_other, layers)
-    outer_raw, outer_factors, outer_ends = first_ends(OUTER, straight, cross, layers, cross)
+    inner_raw, inner_factors, inner_ends = first_ends(INNER)
+    outer_raw, outer_factors, outer_ends = first_ends(OUTER, cut, inner_ends)
 
     def exchange(side, mine, factors):
         width = mine.shape[2]
@@ -675,8 +713,6 @@
     outer_first, outer_turned, outer_layer = first_sweep(
         OUTER, outer_raw, outer_factors, exchange(OUTER, outer_ends, outer_factors)
     )
-    inner_factors_other = partner(inner_factors, 1)
-    outer_factors_other = partner(outer_factors, 1)
 
     def couplings(side, *args):
         return call(
@@ -690,14 +726,14 @@
         INNER, inner_first, inner_turned, outer_first, inner_layer, slab, velocity, inner_factors
     )
     outer_coupled, outer_ends = couplings(
-        OUTER, outer_first, outer_turned, inner_first, outer_layer, slab, velocity, outer_factors, cross
+        OUTER, outer_first, outer_turned, inner_first, outer_layer, slab, velocity, outer_factors, cut
     )
     inner_entered = exchange(INNER, inner_ends, inner_factors)
     outer_entered = exchange(OUTER, outer_ends, outer_factors)
     keep, send, middle = call(
         functools.partial(parts_kernel, ratio),
         "own_steps",
-        [halves, halves, (2, half, cells)],
+        [(steps, half, cells), (steps + 3, half, cells), (2, half, cells)],
         outer_coupled,
         outer_first,
         outer_factors,
@@ -707,7 +743,7 @@
     )
     other = partner(send, 1)
 
-    def finish(side, entered, factors, factors_other, results):
+    def enter(side, entered, factors):
         keep_in, send_in = call(
             functools.partial(carry_kernel, side, steps_local),
             ("outer", "inner")[side] + "_entering",
@@ -716,28 +752,25 @@
             middle,
             *entered,
         )
-        other_in = partner(send_in, 1)
-        vmem = pl.BlockSpec(memory_space=pltpu.VMEM)
+        return keep_in, partner(send_in, 1)
+
+    def finish(theirs, results, *args):
         return call(
-            functools.partial(finish_kernel, side, ratio, chips),
-            ("outer", "inner")[side] + "_finish",
+            functools.partial(finish_kernel, theirs, ratio, chips),
+            ("finish_own", "finish_other")[theirs],
             [(steps_local, depth, cells)] * 2,
-            keep,
-            other,
-            keep_in,
-            other_in,
-            factors,
-            factors_other,
+            *args,
             *results,
-            in_specs=[vmem] * 6 + [anywhere] * len(results),
+            in_specs=[vmem] * len(args) + [anywhere] * len(results),
             out_specs=[anywhere] * 2,
             scratch_shapes=[pltpu.VMEM((2, 2, steps_local, tile, cells), f32), pltpu.SemaphoreType.DMA((2, 2))],
-            input_output_aliases={6 + i: i for i in range(len(results))},
-            room=40,
+            input_output_aliases={len(args) + i: i for i in range(len(results))},
         )
 
-    results = finish(INNER, inner_entered, inner_factors, inner_factors_other, ())
-    return finish(OUTER, outer_entered, outer_factors, outer_factors_other, results)
+    outer_own, outer_other = enter(OUTER, outer_entered, outer_factors)
+    inner_own, inner_other = enter(INNER, inner_entered, inner_factors)
+    results = finish(False, (), keep, outer_own, inner_own, outer_factors, inner_factors)
+    return finish(True, results, other, outer_other, inner_other)
 
 
 def solution(mesh):

time: 49.5 us -> 44.4 us (0.90)
  starting transfers between devices: 19.4 us -> 14.3 us
  local copies, waits for them, and re-layouts: 3.4 us -> 0.01 us
  waiting for transfers between devices: 14.2 us -> 16.1 us
  Pallas kernels: 11.5 us -> 12.8 us
    ppermute x2 -> x1, starting transfers between devices: 6.41 us -> 0.66 us  [outward(): return lax.ppermute(value, ('tm', 'gz'), pairs)]
    ppermute x15 -> x13, waiting for transfers between devices: 12.4 us -> 16.1 us  [partner(): return lax.ppermute(value, 'tm', [(i, i ^ mask) for i in range(ranks)])]
    unnamed x8 -> x2, local copies, waits for them, and re-layouts: 3.4 us -> 0.01 us
    ppermute x2 -> x1, waiting for transfers between devices: 1.81 us -> 0.01 us  [outward(): return lax.ppermute(value, ('tm', 'gz'), pairs)]
    pallas_call x16 -> x17, Pallas kernels: 11.5 us -> 12.8 us  [call(): pl.pallas_call(kernel, out_shape=shapes, compiler_params=pltpu.CompilerPa...]
    ppermute x15 -> x13, starting transfers between devices: 13 us -> 13.6 us  [partner(): return lax.ppermute(value, 'tm', [(i, i ^ mask) for i in range(ranks)])]
  transfers between devices with their start and end apart: 17 -> 14, of which waited for: 9 -> 11; matrix products, arithmetic and copies ran while one was open for 0% -> 0% of each run, Pallas kernels for 10% -> 11%
where the time goes in v4:
time: 44.4 us; the launch traced here: 44 us
  waiting for transfers between devices  16.1 us (36%)
  starting transfers between devices  14.3 us (32%)
  Pallas kernels  12.8 us (29%)
  between operations  0.79 us (2%)
    ppermute x13, waiting for transfers between devices, partner(): return lax.ppermute(value, 'tm', [(i, i ^ mask) for i in range(ranks)])  16.1 us
    ppermute x13, starting transfers between devices, partner(): return lax.ppermute(value, 'tm', [(i, i ^ mask) for i in range(ranks)])  13.6 us
    pallas_call x17, Pallas kernels, call(): pl.pallas_call(kernel, out_shape=shapes, compiler_params=pltpu.CompilerPa...  12.8 us
  transfers between devices with their start and end apart: 14, of which 11 were waited for; matrix products, arithmetic and copies ran while one was open for 0% of the time, Pallas kernels for 11%

profile of v4, /device:TPU:0, one launch (start us, length us, event | category | flops | bytes accessed | tf_op | source)
XLA Modules:
  0.0 44.0 jit_solution(13923547919617001132)
XLA Ops:
  0.6 1.8 %halves_and_layers.1 = (f32[2,4,16,2176]{3,2,1,0:T(8,128)S(1)}, f32[2,4,16,2176]{3,2,1,0:T(8,128)S(1)}, f32[32,2048]{1,0:T(8,128)S(1)}, f32[10,16,128]{2,1,0:T(8...) custom-call(f32[4,32,2048]{2,1,0:T(8,128)} %state.1, f32[4,32,2048]{2,1,0:T(8,128)} %adjoint.1, ...), custom_call_target="tpu_custom_call" | custom-call | bytes 7400000 | tf_op jit(solution)/shard_map/halves_and_layers/pallas_call | solution.py:619
  2.5 0.5 %collective-permute-start = (f32[8,16,128]{2,1,0:T(8,128)S(1)}, f32[8,16,128]{2,1,0:T(8,128)S(1)}, u32[]{:S(2)}, u32[]{:S(2)}) collective-permute-start(f32[8,16,128]{2,1,0:T(8,128)S(1)} %get-tuple-element.37), channel_id=1, source_target_pairs={{0,4},{4,0},{8,12},{12,8},{16,20},{20,16},{24,28},{28,24},{1,5},{5... | collective-permute-start | bytes 196616 | tf_op jit(solution)/shard_map/ppermute | solution.py:605
  3.0 0.9 %collective-permute-done.edge_other = f32[8,16,128]{2,1,0:T(8,128)S(1)} collective-permute-done((f32[8,16,128]{2,1,0:T(8,128)S(1)}, f32[8,16,128]{2,1,0:T(8,128)S(1)}, u32[]{:S(2)}, u32[]{:S(2)}) %collective-permute-start) | collective-permute-done | bytes 65568 | tf_op jit(solution)/shard_map/ppermute | solution.py:605
  3.9 0.4 collective-permute-start.1
  4.3 0.7 %collective-permute-start.2 = (f32[18,16,128]{2,1,0:T(8,128)S(1)}, f32[18,16,128]{2,1,0:T(8,128)S(1)}, u32[]{:S(2)}, u32[]{:S(2)}) collective-permute-start(f32[18,16,128]{2,1,0:T(8,128)S(1)} %get-tuple-element.42), channel_id=1, source_target_pairs={{1,4},{2,5},{3,6},{4,1},{5,2},{6,3},{9,12},{10,13},{11,14},{12,9},... | collective-permute-start | bytes 442376 | tf_op jit(solution)/shard_map/ppermute | solution.py:614
  5.0 1.7 %collective-permute-done.1.other = f32[2,4,16,2176]{3,2,1,0:T(8,128)S(1)} collective-permute-done((f32[2,4,16,2176]{3,2,1,0:T(8,128)S(1)}, f32[2,4,16,2176]{3,2,1,0:T(8,128)S(1)}, u32[]{:S(2)}, u32[]{:S(2)}) %collective-permute-start.1) | collective-permute-done | bytes 1114144 | tf_op jit(solution)/shard_map/ppermute | solution.py:605
  6.7 0.9 %inner_ends.1 = (f32[16,8,2304]{2,1,0:T(8,128)S(1)}, f32[4,8,2304]{2,1,0:T(8,128)S(1)}, f32[2,8,2304]{2,1,0:T(8,128)S(1)}) custom-call(f32[2,4,16,2176]{3,2,1,0:T(8,128)S(1)} %get-tuple-element.35.keep, f32[2,4,16,2176]{3,2,1,0:T(8,128)S(1)} %collective-permute-done.1.other, f32[32,2048]{1,0:T(8,128)S(1)} %get-tuple-element.40.slab, ...), custom_call_target="tpu_custom_call" | custom-call | bytes 3700000 | tf_op jit(solution)/shard_map/inner_ends/pallas_call | solution.py:619
  7.6 2.9 %collective-permute-start.5 = (f32[2,8,2304]{2,1,0:T(8,128)S(1)}, f32[2,8,2304]{2,1,0:T(8,128)S(1)}, u32[]{:S(2)}, u32[]{:S(2)}) collective-permute-start(f32[2,8,2304]{2,1,0:T(8,128)S(1)} %get-tuple-element.43.rest_1_.mine.rest_0_), channel_id=1, source_target_pairs={{0,16},{4,20},{8,24},{12,28},{16,0},{20,4},{24,8},{28,12},{1,17},{... | collective-permute-start | bytes 442376 | tf_op jit(solution)/shard_map/ppermute | solution.py:605
  10.6 0.9 %outer_ends.1 = (f32[16,8,2304]{2,1,0:T(8,128)S(1)}, f32[4,8,2304]{2,1,0:T(8,128)S(1)}, f32[2,8,2304]{2,1,0:T(8,128)S(1)}) custom-call(f32[2,4,16,2176]{3,2,1,0:T(8,128)S(1)} %get-tuple-element.35.keep, f32[2,4,16,2176]{3,2,1,0:T(8,128)S(1)} %collective-permute-done.1.other, f32[32,2048]{1,0:T(8,128)S(1)} %get-tuple-element.40.slab, ...), custom_call_target="tpu_custom_call" | custom-call | bytes 3700000 | tf_op jit(solution)/shard_map/outer_ends/pallas_call | solution.py:619
  11.4 1.6 %collective-permute-start.3 = (f32[2,8,2304]{2,1,0:T(8,128)S(1)}, f32[2,8,2304]{2,1,0:T(8,128)S(1)}, u32[]{:S(2)}, u32[]{:S(2)}) collective-permute-start(f32[2,8,2304]{2,1,0:T(8,128)S(1)} %get-tuple-element.46.mine.rest_0_), channel_id=1, source_target_pairs={{0,8},{4,12},{8,0},{12,4},{16,24},{20,28},{24,16},{28,20},{1,9},{5... | collective-permute-start | bytes 442376 | tf_op jit(solution)/shard_map/ppermute | solution.py:605
  13.0 1.7 %collective-permute-done.5.theirs.rest_1_ = f32[2,8,2304]{2,1,0:T(8,128)S(1)} collective-permute-done((f32[2,8,2304]{2,1,0:T(8,128)S(1)}, f32[2,8,2304]{2,1,0:T(8,128)S(1)}, u32[]{:S(2)}, u32[]{:S(2)}) %collective-permute-start.5) | collective-permute-done | bytes 147488 | tf_op jit(solution)/shard_map/ppermute | solution.py:605
  14.9 2.5 %collective-permute-start.6 = (f32[2,8,2304]{2,1,0:T(8,128)S(1)}, f32[2,8,2304]{2,1,0:T(8,128)S(1)}, u32[]{:S(2)}, u32[]{:S(2)}) collective-permute-start(f32[2,8,2304]{2,1,0:T(8,128)S(1)} %inner_relay.2), channel_id=1, source_target_pairs={{0,8},{4,12},{8,0},{12,4},{16,24},{20,28},{24,16},{28,20},{1,9},{5... | collective-permute-start | bytes 442376 | tf_op jit(solution)/shard_map/ppermute | solution.py:605
  17.4 0.4 collective-permute-done.3.theirs.rest_1_
  18.0 1.2 %collective-permute-start.4 = (f32[2,8,2304]{2,1,0:T(8,128)S(1)}, f32[2,8,2304]{2,1,0:T(8,128)S(1)}, u32[]{:S(2)}, u32[]{:S(2)}) collective-permute-start(f32[2,8,2304]{2,1,0:T(8,128)S(1)} %outer_relay.2), channel_id=1, source_target_pairs={{0,16},{4,20},{8,24},{12,28},{16,0},{20,4},{24,8},{28,12},{1,17},{... | collective-permute-start | bytes 442376 | tf_op jit(solution)/shard_map/ppermute | solution.py:605
  19.2 2.4 %collective-permute-done.6.rest_2_ = f32[2,8,2304]{2,1,0:T(8,128)S(1)} collective-permute-done((f32[2,8,2304]{2,1,0:T(8,128)S(1)}, f32[2,8,2304]{2,1,0:T(8,128)S(1)}, u32[]{:S(2)}, u32[]{:S(2)}) %collective-permute-start.6) | collective-permute-done | bytes 147488 | tf_op jit(solution)/shard_map/ppermute | solution.py:605
  21.6 1.1 %inner_first_sweep.1 = (f32[16,8,2048]{2,1,0:T(8,128)S(1)}, f32[16,8,2048]{2,1,0:T(8,128)S(1)}, f32[16,16,128]{2,1,0:T(8,128)S(1)}) custom-call(f32[16,8,2304]{2,1,0:T(8,128)S(1)} %get-tuple-element.49.raw_ref, f32[4,8,2304]{2,1,0:T(8,128)S(1)} %get-tuple-element.50.factor_ref.inner_factors.rest_3_, ...), custom_call_target="tpu_custom_call" | custom-call | bytes 4070000 | tf_op jit(solution)/shard_map/inner_first_sweep/pallas_call | solution.py:619
  22.7 1.3 %collective-permute-done.4.rest_2_ = f32[2,8,2304]{2,1,0:T(8,128)S(1)} collective-permute-done((f32[2,8,2304]{2,1,0:T(8,128)S(1)}, f32[2,8,2304]{2,1,0:T(8,128)S(1)}, u32[]{:S(2)}, u32[]{:S(2)}) %collective-permute-start.4) | collective-permute-done | bytes 147488 | tf_op jit(solution)/shard_map/ppermute | solution.py:605
  24.0 1.1 %outer_first_sweep.1 = (f32[16,8,2048]{2,1,0:T(8,128)S(1)}, f32[16,8,2048]{2,1,0:T(8,128)S(1)}, f32[16,16,128]{2,1,0:T(8,128)S(1)}) custom-call(f32[16,8,2304]{2,1,0:T(8,128)S(1)} %get-tuple-element.44.raw_ref, f32[4,8,2304]{2,1,0:T(8,128)S(1)} %get-tuple-element.45.factor_ref.outer_factors.rest_2_, f32[2,8,2304]{2,1,0:T(8,128)S(1)} %get-tuple-element.46.mine.rest_0_, ...), custom_call_target="tpu_custom_call" | custom-call | bytes 4070000 | tf_op jit(solution)/shard_map/outer_first_sweep/pallas_call | solution.py:619
  25.2 1.5 %inner_couplings.1 = (f32[16,8,2048]{2,1,0:T(8,128)S(1)}, f32[2,8,2048]{2,1,0:T(8,128)S(1)}) custom-call(f32[16,8,2048]{2,1,0:T(8,128)S(1)} %get-tuple-element.51.next_ref.first_ref.inner_first, f32[16,8,2048]{2,1,0:T(8,128)S(1)} %get-tuple-element.54.turned_ref, f32[16,8,2048]{2,1,0:T(8,128)S(1)} %get-tuple-element.47.first_ref.next_ref.outer_first, ...), custom_call_target="tpu_custom_call" | custom-call | bytes 5550000 | tf_op jit(solution)/shard_map/inner_couplings/pallas_call | solution.py:619
  26.7 1.5 %outer_couplings.1 = (f32[16,8,2048]{2,1,0:T(8,128)S(1)}, f32[2,8,2048]{2,1,0:T(8,128)S(1)}) custom-call(f32[16,8,2048]{2,1,0:T(8,128)S(1)} %get-tuple-element.47.first_ref.next_ref.outer_first, f32[16,8,2048]{2,1,0:T(8,128)S(1)} %get-tuple-element.48.turned_ref, f32[16,8,2048]{2,1,0:T(8,128)S(1)} %get-tuple-element.51.next_ref.first_ref.inner_first, ...), custom_call_target="tpu_custom_call" | custom-call | bytes 5550000 | tf_op jit(solution)/shard_map/outer_couplings/pallas_call | solution.py:619
  28.3 0.6 %own_steps.1 = (f32[8,16,2048]{2,1,0:T(8,128)S(1)}, f32[11,16,2048]{2,1,0:T(8,128)S(1)}, f32[2,16,2048]{2,1,0:T(8,128)S(1)}) custom-call(f32[16,8,2048]{2,1,0:T(8,128)S(1)} %get-tuple-element.53.outer, f32[16,8,2048]{2,1,0:T(8,128)S(1)} %get-tuple-element.47.first_ref.next_ref.outer_first, ...), custom_call_target="tpu_custom_call" | custom-call | bytes 2590000 | tf_op jit(solution)/shard_map/own_steps/pallas_call | solution.py:619
  29.0 1.6 %collective-permute-start.8 = (f32[2,8,2048]{2,1,0:T(8,128)S(1)}, f32[2,8,2048]{2,1,0:T(8,128)S(1)}, u32[]{:S(2)}, u32[]{:S(2)}) collective-permute-start(f32[2,8,2048]{2,1,0:T(8,128)S(1)} %get-tuple-element.59.mine.rest_0_), channel_id=1, source_target_pairs={{0,8},{4,12},{8,0},{12,4},{16,24},{20,28},{24,16},{28,20},{1,9},{5... | collective-permute-start | bytes 393224 | tf_op jit(solution)/shard_map/ppermute | solution.py:605
  30.5 0.7 %collective-permute-start.11 = (f32[2,8,2048]{2,1,0:T(8,128)S(1)}, f32[2,8,2048]{2,1,0:T(8,128)S(1)}, u32[]{:S(2)}, u32[]{:S(2)}) collective-permute-start(f32[2,8,2048]{2,1,0:T(8,128)S(1)} %get-tuple-element.61.mine.rest_0_), channel_id=1, source_target_pairs={{0,16},{4,20},{8,24},{12,28},{16,0},{20,4},{24,8},{28,12},{1,17},{... | collective-permute-start | bytes 393224 | tf_op jit(solution)/shard_map/ppermute | solution.py:605
  31.2 3.7 %collective-permute-done.8.theirs.rest_1_ = f32[2,8,2048]{2,1,0:T(8,128)S(1)} collective-permute-done((f32[2,8,2048]{2,1,0:T(8,128)S(1)}, f32[2,8,2048]{2,1,0:T(8,128)S(1)}, u32[]{:S(2)}, u32[]{:S(2)}) %collective-permute-start.8) | collective-permute-done | bytes 131104 | tf_op jit(solution)/shard_map/ppermute | solution.py:605
  35.0 0.8 %collective-permute-start.9 = (f32[2,8,2048]{2,1,0:T(8,128)S(1)}, f32[2,8,2048]{2,1,0:T(8,128)S(1)}, u32[]{:S(2)}, u32[]{:S(2)}) collective-permute-start(f32[2,8,2048]{2,1,0:T(8,128)S(1)} %outer_relay.3), channel_id=1, source_target_pairs={{0,16},{4,20},{8,24},{12,28},{16,0},{20,4},{24,8},{28,12},{1,17},{... | collective-permute-start | bytes 393224 | tf_op jit(solution)/shard_map/ppermute | solution.py:605
  35.8 0.3 collective-permute-done.11.theirs.rest_1_
  36.3 1.3 %collective-permute-start.12 = (f32[2,8,2048]{2,1,0:T(8,128)S(1)}, f32[2,8,2048]{2,1,0:T(8,128)S(1)}, u32[]{:S(2)}, u32[]{:S(2)}) collective-permute-start(f32[2,8,2048]{2,1,0:T(8,128)S(1)} %inner_relay.3), channel_id=1, source_target_pairs={{0,8},{4,12},{8,0},{12,4},{16,24},{20,28},{24,16},{28,20},{1,9},{5... | collective-permute-start | bytes 393224 | tf_op jit(solution)/shard_map/ppermute | solution.py:605
  37.5 2.7 %collective-permute-done.9.rest_2_ = f32[2,8,2048]{2,1,0:T(8,128)S(1)} collective-permute-done((f32[2,8,2048]{2,1,0:T(8,128)S(1)}, f32[2,8,2048]{2,1,0:T(8,128)S(1)}, u32[]{:S(2)}, u32[]{:S(2)}) %collective-permute-start.9) | collective-permute-done | bytes 131104 | tf_op jit(solution)/shard_map/ppermute | solution.py:605
  40.2 0.2 outer_entering.1
  40.5 0.8 %collective-permute-done.12.rest_2_ = f32[2,8,2048]{2,1,0:T(8,128)S(1)} collective-permute-done((f32[2,8,2048]{2,1,0:T(8,128)S(1)}, f32[2,8,2048]{2,1,0:T(8,128)S(1)}, u32[]{:S(2)}, u32[]{:S(2)}) %collective-permute-start.12) | collective-permute-done | bytes 131104 | tf_op jit(solution)/shard_map/ppermute | solution.py:605
  41.6 1.1 %finish_own.1 = (f32[4,32,2048]{2,1,0:T(8,128)}, f32[4,32,2048]{2,1,0:T(8,128)}) custom-call(f32[8,16,2048]{2,1,0:T(8,128)S(1)} %get-tuple-element.63.parts, f32[2,8,2048]{2,1,0:T(8,128)S(1)} %get-tuple-element.64.rest_0_, f32[2,8,2048]{2,1,0:T(8,128)S(1)} %get-tuple-element.65.rest_1_, f32[4,8,2304]{2,1,0:T(8,128)S(1)} %get-tuple-element.45.factor_ref.outer_factors.rest_2_, ...), custom_call_target="tpu_custom_call" | custom-call | bytes 4440000 | tf_op jit(solution)/shard_map/finish_own/pallas_call | solution.py:619
  42.9 1.1 %finish_other.1 = (f32[4,32,2048]{2,1,0:T(8,128)}, f32[4,32,2048]{2,1,0:T(8,128)}) custom-call(f32[11,16,2048]{2,1,0:T(8,128)S(1)} %collective-permute-done.7.parts, f32[2,8,2048]{2,1,0:T(8,128)S(1)} %collective-permute-done.10.rest_0_, f32[2,8,2048]{2,1,0:T(8,128)S(1)} %collective-permute-done.13.rest_1_, ...), custom_call_target="tpu_custom_call", output_to_operand_aliasing={{0}: (3, {}), {1}: (4, {})} | custom-call | bytes 4440000 | tf_op jit(solution)/shard_map/finish_other/pallas_call | solution.py:619
  (15 shorter events, 1.2 us)
Async XLA Ops:
  2.5 1.4 %collective-permute-start = (f32[8,16,128]{2,1,0:T(8,128)S(1)}, f32[8,16,128]{2,1,0:T(8,128)S(1)}, u32[]{:S(2)}, u32[]{:S(2)}) collective-permute-start(f32[8,16,128]{2,1,0:T(8,128)S(1)} %get-tuple-element.37), channel_id=1, source_target_pairs={{0,4},{4,0},{8,12},{12,8},{16,20},{20,16},{24,28},{28,24},{1,5},{5... | collective-permute-start | bytes 196616 | tf_op jit(solution)/shard_map/ppermute | solution.py:605
  3.9 2.8 %collective-permute-start.1 = (f32[2,4,16,2176]{3,2,1,0:T(8,128)S(1)}, f32[2,4,16,2176]{3,2,1,0:T(8,128)S(1)}, u32[]{:S(2)}, u32[]{:S(2)}) collective-permute-start(f32[2,4,16,2176]{3,2,1,0:T(8,128)S(1)} %get-tuple-element.39), channel_id=1, source_target_pairs={{0,4},{4,0},{8,12},{12,8},{16,20},{20,16},{24,28},{28,24},{1,5},{5... | collective-permute-start | bytes 3342344 | tf_op jit(solution)/shard_map/ppermute | solution.py:605
  4.3 6.2 %collective-permute-start.2 = (f32[18,16,128]{2,1,0:T(8,128)S(1)}, f32[18,16,128]{2,1,0:T(8,128)S(1)}, u32[]{:S(2)}, u32[]{:S(2)}) collective-permute-start(f32[18,16,128]{2,1,0:T(8,128)S(1)} %get-tuple-element.42), channel_id=1, source_target_pairs={{1,4},{2,5},{3,6},{4,1},{5,2},{6,3},{9,12},{10,13},{11,14},{12,9},... | collective-permute-start | bytes 442376 | tf_op jit(solution)/shard_map/ppermute | solution.py:614
  7.6 7.1 %collective-permute-start.5 = (f32[2,8,2304]{2,1,0:T(8,128)S(1)}, f32[2,8,2304]{2,1,0:T(8,128)S(1)}, u32[]{:S(2)}, u32[]{:S(2)}) collective-permute-start(f32[2,8,2304]{2,1,0:T(8,128)S(1)} %get-tuple-element.43.rest_1_.mine.rest_0_), channel_id=1, source_target_pairs={{0,16},{4,20},{8,24},{12,28},{16,0},{20,4},{24,8},{28,12},{1,17},{... | collective-permute-start | bytes 442376 | tf_op jit(solution)/shard_map/ppermute | solution.py:605
  11.4 6.3 %collective-permute-start.3 = (f32[2,8,2304]{2,1,0:T(8,128)S(1)}, f32[2,8,2304]{2,1,0:T(8,128)S(1)}, u32[]{:S(2)}, u32[]{:S(2)}) collective-permute-start(f32[2,8,2304]{2,1,0:T(8,128)S(1)} %get-tuple-element.46.mine.rest_0_), channel_id=1, source_target_pairs={{0,8},{4,12},{8,0},{12,4},{16,24},{20,28},{24,16},{28,20},{1,9},{5... | collective-permute-start | bytes 442376 | tf_op jit(solution)/shard_map/ppermute | solution.py:605
  14.9 6.7 %collective-permute-start.6 = (f32[2,8,2304]{2,1,0:T(8,128)S(1)}, f32[2,8,2304]{2,1,0:T(8,128)S(1)}, u32[]{:S(2)}, u32[]{:S(2)}) collective-permute-start(f32[2,8,2304]{2,1,0:T(8,128)S(1)} %inner_relay.2), channel_id=1, source_target_pairs={{0,8},{4,12},{8,0},{12,4},{16,24},{20,28},{24,16},{28,20},{1,9},{5... | collective-permute-start | bytes 442376 | tf_op jit(solution)/shard_map/ppermute | solution.py:605
  18.0 6.1 %collective-permute-start.4 = (f32[2,8,2304]{2,1,0:T(8,128)S(1)}, f32[2,8,2304]{2,1,0:T(8,128)S(1)}, u32[]{:S(2)}, u32[]{:S(2)}) collective-permute-start(f32[2,8,2304]{2,1,0:T(8,128)S(1)} %outer_relay.2), channel_id=1, source_target_pairs={{0,16},{4,20},{8,24},{12,28},{16,0},{20,4},{24,8},{28,12},{1,17},{... | collective-permute-start | bytes 442376 | tf_op jit(solution)/shard_map/ppermute | solution.py:605
  22.7 2.5 %copy-start = (f32[3,32,2048]{2,1,0:T(8,128)S(1)}, f32[3,32,2048]{2,1,0:T(8,128)}, u32[]{:S(2)}) copy-start(f32[3,32,2048]{2,1,0:T(8,128)} %velocity_ref.3) | copy-start | bytes 2359300
  28.9 14.0 %collective-permute-start.7 = (f32[11,16,2048]{2,1,0:T(8,128)S(1)}, f32[11,16,2048]{2,1,0:T(8,128)S(1)}, u32[]{:S(2)}, u32[]{:S(2)}) collective-permute-start(f32[11,16,2048]{2,1,0:T(8,128)S(1)} %get-tuple-element.57), channel_id=1, source_target_pairs={{0,4},{4,0},{8,12},{12,8},{16,20},{20,16},{24,28},{28,24},{1,5},{5... | collective-permute-start | bytes 4325384 | tf_op jit(solution)/shard_map/ppermute | solution.py:605
  29.0 5.9 %collective-permute-start.8 = (f32[2,8,2048]{2,1,0:T(8,128)S(1)}, f32[2,8,2048]{2,1,0:T(8,128)S(1)}, u32[]{:S(2)}, u32[]{:S(2)}) collective-permute-start(f32[2,8,2048]{2,1,0:T(8,128)S(1)} %get-tuple-element.59.mine.rest_0_), channel_id=1, source_target_pairs={{0,8},{4,12},{8,0},{12,4},{16,24},{20,28},{24,16},{28,20},{1,9},{5... | collective-permute-start | bytes 393224 | tf_op jit(solution)/shard_map/ppermute | solution.py:605
  30.5 5.6 %collective-permute-start.11 = (f32[2,8,2048]{2,1,0:T(8,128)S(1)}, f32[2,8,2048]{2,1,0:T(8,128)S(1)}, u32[]{:S(2)}, u32[]{:S(2)}) collective-permute-start(f32[2,8,2048]{2,1,0:T(8,128)S(1)} %get-tuple-element.61.mine.rest_0_), channel_id=1, source_target_pairs={{0,16},{4,20},{8,24},{12,28},{16,0},{20,4},{24,8},{28,12},{1,17},{... | collective-permute-start | bytes 393224 | tf_op jit(solution)/shard_map/ppermute | solution.py:605
  35.0 5.1 %collective-permute-start.9 = (f32[2,8,2048]{2,1,0:T(8,128)S(1)}, f32[2,8,2048]{2,1,0:T(8,128)S(1)}, u32[]{:S(2)}, u32[]{:S(2)}) collective-permute-start(f32[2,8,2048]{2,1,0:T(8,128)S(1)} %outer_relay.3), channel_id=1, source_target_pairs={{0,16},{4,20},{8,24},{12,28},{16,0},{20,4},{24,8},{28,12},{1,17},{... | collective-permute-start | bytes 393224 | tf_op jit(solution)/shard_map/ppermute | solution.py:605
  36.3 5.0 %collective-permute-start.12 = (f32[2,8,2048]{2,1,0:T(8,128)S(1)}, f32[2,8,2048]{2,1,0:T(8,128)S(1)}, u32[]{:S(2)}, u32[]{:S(2)}) collective-permute-start(f32[2,8,2048]{2,1,0:T(8,128)S(1)} %inner_relay.3), channel_id=1, source_target_pairs={{0,8},{4,12},{8,0},{12,4},{16,24},{20,28},{24,16},{28,20},{1,9},{5... | collective-permute-start | bytes 393224 | tf_op jit(solution)/shard_map/ppermute | solution.py:605
  40.4 2.3 %collective-permute-start.10 = (f32[2,8,2048]{2,1,0:T(8,128)S(1)}, f32[2,8,2048]{2,1,0:T(8,128)S(1)}, u32[]{:S(2)}, u32[]{:S(2)}) collective-permute-start(f32[2,8,2048]{2,1,0:T(8,128)S(1)} %get-tuple-element.60), channel_id=1, source_target_pairs={{0,4},{4,0},{8,12},{12,8},{16,20},{20,16},{24,28},{28,24},{1,5},{5... | collective-permute-start | bytes 393224 | tf_op jit(solution)/shard_map/ppermute | solution.py:605
  41.5 1.4 %collective-permute-start.13 = (f32[2,8,2048]{2,1,0:T(8,128)S(1)}, f32[2,8,2048]{2,1,0:T(8,128)S(1)}, u32[]{:S(2)}, u32[]{:S(2)}) collective-permute-start(f32[2,8,2048]{2,1,0:T(8,128)S(1)} %get-tuple-element.62), channel_id=1, source_target_pairs={{0,4},{4,0},{8,12},{12,8},{16,20},{20,16},{24,28},{28,24},{1,5},{5... | collective-permute-start | bytes 393224 | tf_op jit(solution)/shard_map/ppermute | solution.py:605

commit v5 on v4

--- a/solution.py
+++ b/solution.py
@@ -67,13 +67,12 @@
     'ends': 1,
     'relay': 0.2,
     'first_sweep': 1.1,
-    'couplings': 1.5,
-    'own_steps': 0.7,
+    'couplings': 3,
     'entering': 0.2,
     'finish_own': 1.2,
     'finish_other': 1.2,
 }
-UNROLL_ENDS = 4
+UNROLL_ENDS = 8
 UNROLL_COUPLINGS = 2
 
 
@@ -328,62 +327,59 @@
     return block, response_of(decay, upright, steps), 1.0 / (1.0 - power(block, chips))
 
 
-def contribution(ends, offset, block, response, closing):
+def choose(flag, one, other):
+    return tuple(jnp.where(flag, a, b) for a, b in zip(one, other))
+
+
+def ring_weights(factors, steps):
+    block, response, closing = ring_factors(factors, steps, 4)
+    square = block * block
+    cross = response * closing * closing
+    near = cross * block * (1.0 + square) * (1.0 + square)
+    once = closing * block
+    twice = closing * square
+    thrice = once * square
+    return (
+        (thrice, thrice, cross * (1.0 + square) * (1.0 + square * square)),
+        (closing, twice, near),
+        (once, once, 2.0 * cross * square * (1.0 + square)),
+        (twice, closing, near),
+    )
+
+
+def weighted(weights, ends):
     back, last = ends
-    square = block * block
-    if offset == 0:
-        up, down, cross = square * block, square * block, 1.0 + square + square * square * (1.0 + square)
-    elif offset == 1:
-        up, down, cross = None, square, block * (1.0 + square) * (1.0 + square)
-    elif offset == 2:
-        up, down, cross = block, block, 2.0 * square * (1.0 + square)
-    else:
-        up, down, cross = square, None, block * (1.0 + square) * (1.0 + square)
-    entering_back = back if up is None else up * back
-    entering_state = last if down is None else down * last
-    entering_state = entering_state + (cross * response * closing) * back
-    return closing * entering_back, closing * entering_state
-
-
-def either(flag, one, other):
-    return tuple(jnp.where(flag, a, b) for a, b in zip(one, other))
-
-
-def relay_kernel(side, steps, factor_ref, mine, theirs, out):
+    return weights[0] * back, weights[1] * last + weights[2] * back
+
+
+def relay_kernel(steps, factor_ref, mine, theirs, passed):
     odd = lax.rem(this_chip(), 2) == 1
+    along_x = this_core() == 0
 
     def one(here):
-        ring = ring_factors([factor_ref[slot, :, here] for slot in range(4)], steps, 4)
-        a = (mine[0, :, here], mine[1, :, here])
-        b = (theirs[0, :, here], theirs[1, :, here])
-        if side == OUTER:
-            one_part = contribution(a, 2, *ring)
-            other_part = either(odd, contribution(b, 1, *ring), contribution(b, 3, *ring))
-        else:
-            one_part = either(odd, contribution(a, 1, *ring), contribution(a, 3, *ring))
-            other_part = either(odd, contribution(b, 3, *ring), contribution(b, 1, *ring))
-        out[0, :, here] = one_part[0] + other_part[0]
-        out[1, :, here] = one_part[1] + other_part[1]
+        _, next_, across, before = ring_weights([factor_ref[slot, :, here] for slot in range(4)], steps)
+        beside = choose(odd, next_, before)
+        a = weighted(choose(along_x, across, beside), (mine[0, :, here], mine[1, :, here]))
+        b = weighted(choose(along_x, beside, choose(odd, before, next_)), (theirs[0, :, here], theirs[1, :, here]))
+        passed[0, :, here] = a[0] + b[0]
+        passed[1, :, here] = a[1] + b[1]
 
     each_block(mine.shape[2], 4 * LANES, one)
 
 
-def entering(side, factors, ends, here, steps):
+def entering(factors, ends, here, steps):
     if len(ends) == 1:
         return ends[0][0, :, here], ends[0][1, :, here]
+    mine, theirs, tail = ends
+    own, next_, across, before = ring_weights(factors, steps)
     odd = lax.rem(this_chip(), 2) == 1
-    mine, theirs, tail = ends
-    ring = ring_factors(factors, steps, 4)
-    own = contribution((mine[0, :, here], mine[1, :, here]), 0, *ring)
-    b = (theirs[0, :, here], theirs[1, :, here])
-    if side == OUTER:
-        near_by = either(odd, contribution(b, 3, *ring), contribution(b, 1, *ring))
-    else:
-        near_by = contribution(b, 2, *ring)
-    return own[0] + near_by[0] + tail[0, :, here], own[1] + near_by[1] + tail[1, :, here]
-
-
-def sweep_kernel(side, ratio, raw_ref, factor_ref, *rest):
+    along_x = this_core() == 0
+    a = weighted(own, (mine[0, :, here], mine[1, :, here]))
+    b = weighted(choose(along_x, choose(odd, before, next_), across), (theirs[0, :, here], theirs[1, :, here]))
+    return a[0] + b[0] + tail[0, :, here], a[1] + b[1] + tail[1, :, here]
+
+
+def sweep_kernel(ratio, raw_ref, factor_ref, *rest):
     *ends, first_ref, turned_ref, layer_ref = rest
     tile = raw_ref.shape[1]
     steps = raw_ref.shape[0] // 2
@@ -392,7 +388,7 @@
     def sweep(put, here):
         factors = [factor_ref[slot, :, here] for slot in range(4)]
         values = lambda step: (raw_ref[2 * step, :, here], raw_ref[2 * step + 1, :, here])
-        solve_steps(values, *factors, ratio, *entering(side, factors, ends, here, steps), steps, put)
+        solve_steps(values, *factors, ratio, *entering(factors, ends, here, steps), steps, put)
 
     def own(here):
         def put(step, state, adjoint):
@@ -418,15 +414,24 @@
     return parts[0] if len(parts) == 1 else jnp.concatenate(parts, axis=1)
 
 
-def couplings_kernel(side, first_ref, turned_ref, next_ref, layer_ref, slab, velocity_ref, factor_ref, *rest):
-    coupled_ref, ends_ref = rest[-2:]
+def couplings_kernel(ratio, slab, velocity_ref, cut_ref, *refs):
+    *results, outer_ends, inner_ends = refs[-5:]
+    outer, inner = refs[:4], refs[4:8]
+    work = functools.partial(couple_tile, ratio, slab, velocity_ref, cut_ref)
+    work(OUTER, *outer, inner[0], *results, outer_ends)
+    work(INNER, *inner, outer[0], *results, inner_ends)
+
+
+def couple_tile(ratio, slab, velocity_ref, cut_ref, side, first_ref, turned_ref, layer_ref, factor_ref, next_ref, keep, send, middle, ends_ref):
     slots, tile, cells = first_ref.shape
     steps = slots // 2
+    steps_local = steps // 2
     depth = slab.shape[0]
     half = 2 * tile
     groups = cells // LANES
     core = this_core()
     own = pl.ds(pl.multiple_of(tile_rows(side, half, depth), 8), tile)
+    held = slice(side * tile, (side + 1) * tile)
     out_shift, in_shift = z_shifts(tile)
 
     def one(group, carry):
@@ -434,7 +439,7 @@
         left = lane_block(jnp.maximum(group - 1, 0) * LANES)
         right = lane_block(jnp.minimum(group + 1, groups - 1) * LANES)
         row = pl.ds(group, 1)
-        beyond = rest[0][steps, row, :] if side == OUTER else None
+        beyond = cut_ref[steps, row, :] if side == OUTER else None
         weights = faces(side, slab, beyond, group, half)
         lane = lax.broadcasted_iota(jnp.int32, (tile, LANES), 1)
         low = lane < NY
@@ -452,30 +457,50 @@
             tables.append((one_way[0], other_way[0], x_same, x_next, one_way[2], other_way[2]))
         factors = [factor_ref[slot, :, here] for slot in range(4)]
 
-        def values(step):
-            results = []
+        def coupled(slot):
+            c_out, c_in, x_same, x_next, c_ahead, c_behind = tables[slot % 2]
+            value = first_ref[slot, :, here]
+            following = next_ref[slot, :, here]
+            cut = layer_ref[slot, row, :]
+            if side == OUTER:
+                outward = jnp.where(first, cut, pltpu.roll(value, out_shift, 0))
+                inward = pltpu.roll(jnp.where(first, following, value), in_shift, 0)
+            else:
+                outward = pltpu.roll(jnp.where(last, following, value), out_shift, 0)
+                inward = jnp.where(last, cut, pltpu.roll(value, in_shift, 0))
+            result = c_out * outward + c_in * inward
+            beside = jnp.where(low, turned_ref[slot, :, left], turned_ref[slot, :, right])
+            result = result + (x_same * turned_ref[slot, :, here] + x_next * beside)
+            return result + (c_ahead * pltpu.roll(value, LANES - 1, 1) + c_behind * pltpu.roll(value, 1, 1))
+
+        results = {}
+        ends = []
+        for sub in range(2):
+            offset = 2 * steps_local * sub
+            drives = [coupled(offset + slot) for slot in range(2 * steps_local)]
+
+            def put(step, state, adjoint):
+                results[sub, step] = (state, adjoint)
+
+            values = lambda step: (drives[2 * step], drives[2 * step + 1])
+            ends.append(solve_steps(values, *factors, ratio, None, None, steps_local, put))
+        for step in range(steps_local):
             for field in range(2):
                 slot = 2 * step + field
-                c_out, c_in, x_same, x_next, c_ahead, c_behind = tables[field]
-                value = first_ref[slot, :, here]
-                following = next_ref[slot, :, here]
-                cut = layer_ref[slot, row, :]
-                if side == OUTER:
-                    outward = jnp.where(first, cut, pltpu.roll(value, out_shift, 0))
-                    inward = pltpu.roll(jnp.where(first, following, value), in_shift, 0)
-                else:
-                    outward = pltpu.roll(jnp.where(last, following, value), out_shift, 0)
-                    inward = jnp.where(last, cut, pltpu.roll(value, in_shift, 0))
-                result = c_out * outward + c_in * inward
-                beside = jnp.where(low, turned_ref[slot, :, left], turned_ref[slot, :, right])
-                result = result + (x_same * turned_ref[slot, :, here] + x_next * beside)
-                result = result + (c_ahead * pltpu.roll(value, LANES - 1, 1) + c_behind * pltpu.roll(value, 1, 1))
-                coupled_ref[slot, :, here] = result
-                results.append(result)
-            return results
-
-        for slot, value in enumerate(local_ends(values, *factors, steps)):
-            ends_ref[slot, :, here] = value
+                early, late = [
+                    first_ref[2 * steps_local * sub + slot, :, here] + results[sub, step][field] for sub in range(2)
+                ]
+                keep[slot, held, here] = jnp.where(core == 0, early, late)
+                send[slot, held, here] = jnp.where(core == 0, late, early)
+        for slot, value in enumerate(finish_factors(ratio, factors)):
+            send[2 * steps_local + slot, held, here] = value
+        (early_back, early_last), (late_back, late_last) = ends
+        decay, _, _, upright = factors
+        block = power(decay, steps_local)
+        middle[0, held, here] = late_back
+        middle[1, held, here] = early_last
+        ends_ref[0, :, here] = early_back + block * late_back
+        ends_ref[1, :, here] = late_last + block * (early_last + response_of(decay, upright, steps_local) * late_back)
         return carry
 
     lax.fori_loop(0, groups, one, 0, unroll=UNROLL_COUPLINGS)
@@ -486,75 +511,38 @@
     return decay, ratio * mixed, 0.5 * upright
 
 
-def parts_kernel(ratio, outer, outer_first, outer_factors, inner, inner_first, inner_factors, *rest):
-    keep, send, middle = rest[-3:]
-    steps_local = keep.shape[0] // 2
-    tile, cells = outer.shape[1:]
-    core = this_core()
-    for side, (coupled_ref, first_ref, factor_ref) in enumerate(
-        ((outer, outer_first, outer_factors), (inner, inner_first, inner_factors))
-    ):
-        rows = slice(side * tile, (side + 1) * tile)
+def carry_kernel(steps_local, middle, outer_factors, inner_factors, *rest):
+    *ends, keep, send = rest
+    half, cells = middle.shape[1:]
+    tile = half // 2
+    core = this_core()
+    for side, factor_ref in enumerate((outer_factors, inner_factors)):
+        held = slice(side * tile, (side + 1) * tile)
 
         def one(here):
             factors = [factor_ref[slot, :, here] for slot in range(4)]
-            for slot, value in enumerate(finish_factors(ratio, factors)):
-                send[2 * steps_local + slot, rows, here] = value
-            results = {}
-            for sub in range(2):
-                offset = 2 * steps_local * sub
-
-                def values(step):
-                    return coupled_ref[offset + 2 * step, :, here], coupled_ref[offset + 2 * step + 1, :, here]
-
-                def put(step, state, adjoint):
-                    results[sub, step] = (state, adjoint)
-
-                back, last = solve_steps(values, *factors, ratio, None, None, steps_local, put)
-                middle[1 - sub, rows, here] = last if sub == 0 else back
-            for step in range(steps_local):
-                for field in range(2):
-                    early, late = [
-                        first_ref[2 * steps_local * sub + 2 * step + field, :, here] + results[sub, step][field]
-                        for sub in range(2)
-                    ]
-                    slot = 2 * step + field
-                    keep[slot, rows, here] = jnp.where(core == 0, early, late)
-                    send[slot, rows, here] = jnp.where(core == 0, late, early)
-
-        each_block(cells, 2 * LANES, one)
-
-
-def carry_kernel(side, steps_local, factor_ref, middle, *rest):
-    *ends, keep, send = rest
-    tile, cells = keep.shape[1:]
-    rows = slice(side * tile, (side + 1) * tile)
-    core = this_core()
-
-    def one(here):
-        factors = [factor_ref[slot, :, here] for slot in range(4)]
-        decay, _, _, upright = factors
-        back, state = entering(side, factors, ends, here, 2 * steps_local)
-        block = power(decay, steps_local)
-        early_back = middle[0, rows, here] + block * back
-        late_state = middle[1, rows, here] + block * state + response_of(decay, upright, steps_local) * early_back
-        for slot, (early, late) in enumerate(((early_back, back), (state, late_state))):
-            keep[slot, :, here] = jnp.where(core == 0, early, late)
-            send[slot, :, here] = jnp.where(core == 0, late, early)
-
-    each_block(cells, 4 * LANES, one)
-
-
-def finish_kernel(theirs, ratio, chips, parts, *rest):
+            decay, _, _, upright = factors
+            back, state = entering(factors, ends[side * len(ends) // 2 : (side + 1) * len(ends) // 2], here, 2 * steps_local)
+            block = power(decay, steps_local)
+            early_back = middle[0, held, here] + block * back
+            late_state = middle[1, held, here] + block * state + response_of(decay, upright, steps_local) * early_back
+            for slot, (early, late) in enumerate(((early_back, back), (state, late_state))):
+                keep[slot, held, here] = jnp.where(core == 0, early, late)
+                send[slot, held, here] = jnp.where(core == 0, late, early)
+
+        each_block(cells, 4 * LANES, one)
+
+
+def finish_kernel(theirs, ratio, chips, *rest):
     state_out, adjoint_out, result, sems = rest[-4:]
-    tile, cells = rest[0].shape[1:]
-    steps_local, depth = state_out.shape[:2]
+    parts, entered = rest[:2]
+    steps_local, depth, cells = state_out.shape
+    tile = depth // 4
     core = this_core()
     whole = step_scale(ratio, 2 * steps_local, chips, -1)
     scales = [jnp.where(core == 0, whole[step], whole[steps_local + step]) for step in range(steps_local)]
     copies = []
     for side in (OUTER, INNER):
-        entered = rest[side]
         held = slice(side * tile, (side + 1) * tile)
         start = tile_rows(side, 2 * tile, depth)
         rows = pl.ds(pl.multiple_of(depth - tile - start if theirs else start, 8), tile)
@@ -564,11 +552,11 @@
                 decay, gain, half_up = [parts[2 * steps_local + slot, held, here] for slot in range(3)]
             else:
                 decay, gain, half_up = finish_factors(ratio, [rest[2 + side][slot, :, here] for slot in range(4)])
-            backs = [entered[0, :, here]]
+            backs = [entered[0, held, here]]
             for _ in range(steps_local):
                 backs.append(decay * backs[-1])
             backs = backs[:0:-1]
-            previous = entered[1, :, here]
+            previous = entered[1, held, here]
             for step in range(steps_local):
                 current = decay * previous + half_up * backs[step]
                 adjoint = backs[step] - gain * previous
@@ -664,42 +652,40 @@
     inner_raw, inner_factors, inner_ends = first_ends(INNER)
     outer_raw, outer_factors, outer_ends = first_ends(OUTER, cut, inner_ends)
 
-    def exchange(side, mine, factors):
+    def beside(value, masks):
+        return lax.ppermute(value, "tm", [(i, i ^ masks[i % 2]) for i in range(ranks)])
+
+    def exchange(mine, factors):
+        if chips != 4:
+            return [gathered(mine, factors)]
+        theirs = beside(mine, (2, 4))
+        (passed,) = call(functools.partial(relay_kernel, steps), "relay", [mine.shape], factors, mine, theirs)
+        return [mine, theirs, beside(passed, (4, 2))]
+
+    def gathered(mine, factors):
         width = mine.shape[2]
-        if chips != 4:
-            gathered = lax.dynamic_index_in_dim(
-                lax.all_gather(mine, "tm").reshape((chips, 2) + mine.shape), core, 1, keepdims=False
-            )
-            block, response, closing = ring_factors([factors[i, :, :width] for i in range(4)], steps, chips)
-            at = lambda array, index: lax.dynamic_index_in_dim(array, lax.rem(index + 2 * chips, chips), 0, keepdims=False)
-            chip = this_chip()
-
-            def entering_back(where):
-                value = jnp.zeros((tile, width), f32)
-                for offset in reversed(range(chips)):
-                    value = block * value + at(gathered[:, 0], where + 1 + offset)
-                return value * closing
-
+        every = lax.dynamic_index_in_dim(
+            lax.all_gather(mine, "tm").reshape((chips, 2) + mine.shape), core, 1, keepdims=False
+        )
+        block, response, closing = ring_factors([factors[i, :, :width] for i in range(4)], steps, chips)
+        at = lambda array, index: lax.dynamic_index_in_dim(array, lax.rem(index + 2 * chips, chips), 0, keepdims=False)
+        chip = this_chip()
+
+        def entering_back(where):
             value = jnp.zeros((tile, width), f32)
             for offset in reversed(range(chips)):
-                source = chip - 1 - offset
-                value = block * value + at(gathered[:, 1], source) + response * entering_back(source)
-            return [jnp.stack([entering_back(chip), value * closing])]
-        masks = (2, 4) if side == OUTER else (4, 2)
-        theirs = partner(mine, masks[0])
-        (passed,) = call(
-            functools.partial(relay_kernel, side, steps),
-            ("outer", "inner")[side] + "_relay",
-            [mine.shape],
-            factors,
-            mine,
-            theirs,
-        )
-        return [mine, theirs, partner(passed, masks[1])]
+                value = block * value + at(every[:, 0], where + 1 + offset)
+            return value * closing
+
+        value = jnp.zeros((tile, width), f32)
+        for offset in reversed(range(chips)):
+            source = chip - 1 - offset
+            value = block * value + at(every[:, 1], source) + response * entering_back(source)
+        return jnp.stack([entering_back(chip), value * closing])
 
     def first_sweep(side, raw, factors, ends):
         return call(
-            functools.partial(sweep_kernel, side, ratio),
+            functools.partial(sweep_kernel, ratio),
             ("outer", "inner")[side] + "_first_sweep",
             [(2 * steps, tile, cells)] * 2 + [(2 * steps,) + layer],
             raw,
@@ -708,51 +694,41 @@
         )
 
     inner_first, inner_turned, inner_layer = first_sweep(
-        INNER, inner_raw, inner_factors, exchange(INNER, inner_ends, inner_factors)
+        INNER, inner_raw, inner_factors, exchange(inner_ends, inner_factors)
     )
     outer_first, outer_turned, outer_layer = first_sweep(
-        OUTER, outer_raw, outer_factors, exchange(OUTER, outer_ends, outer_factors)
-    )
-
-    def couplings(side, *args):
-        return call(
-            functools.partial(couplings_kernel, side),
-            ("outer", "inner")[side] + "_couplings",
-            [(2 * steps, tile, cells), (2, tile, cells)],
-            *args,
-        )
-
-    inner_coupled, inner_ends = couplings(
-        INNER, inner_first, inner_turned, outer_first, inner_layer, slab, velocity, inner_factors
-    )
-    outer_coupled, outer_ends = couplings(
-        OUTER, outer_first, outer_turned, inner_first, outer_layer, slab, velocity, outer_factors, cut
-    )
-    inner_entered = exchange(INNER, inner_ends, inner_factors)
-    outer_entered = exchange(OUTER, outer_ends, outer_factors)
-    keep, send, middle = call(
-        functools.partial(parts_kernel, ratio),
-        "own_steps",
-        [(steps, half, cells), (steps + 3, half, cells), (2, half, cells)],
-        outer_coupled,
+        OUTER, outer_raw, outer_factors, exchange(outer_ends, outer_factors)
+    )
+
+    keep, send, middle, *ends = call(
+        functools.partial(couplings_kernel, ratio),
+        "couplings",
+        [(steps, half, cells), (steps + 3, half, cells), (2, half, cells), (2, tile, cells), (2, tile, cells)],
+        slab,
+        velocity,
+        cut,
         outer_first,
+        outer_turned,
+        outer_layer,
         outer_factors,
-        inner_coupled,
         inner_first,
+        inner_turned,
+        inner_layer,
         inner_factors,
     )
     other = partner(send, 1)
-
-    def enter(side, entered, factors):
-        keep_in, send_in = call(
-            functools.partial(carry_kernel, side, steps_local),
-            ("outer", "inner")[side] + "_entering",
-            [(2, tile, cells)] * 2,
-            factors,
-            middle,
-            *entered,
-        )
-        return keep_in, partner(send_in, 1)
+    entered = [exchange(mine, table) for mine, table in zip(ends, (outer_factors, inner_factors))]
+    own_in, send_in = call(
+        functools.partial(carry_kernel, steps_local),
+        "entering",
+        [(2, half, cells)] * 2,
+        middle,
+        outer_factors,
+        inner_factors,
+        *entered[OUTER],
+        *entered[INNER],
+    )
+    other_in = partner(send_in, 1)
 
     def finish(theirs, results, *args):
         return call(
@@ -767,10 +743,8 @@
             input_output_aliases={len(args) + i: i for i in range(len(results))},
         )
 
-    outer_own, outer_other = enter(OUTER, outer_entered, outer_factors)
-    inner_own, inner_other = enter(INNER, inner_entered, inner_factors)
-    results = finish(False, (), keep, outer_own, inner_own, outer_factors, inner_factors)
-    return finish(True, results, other, outer_other, inner_other)
+    results = finish(False, (), keep, own_in, outer_factors, inner_factors)
+    return finish(True, results, other, other_in)
 
 
 def solution(mesh):

time: 44.4 us -> 43.2 us (0.973)
  the two profiles are of different devices: /device:TPU:0 before, /device:TPU:25 now
where the time goes in v5:
time: 43.2 us; the launch traced here: 43 us
  starting transfers between devices  16.9 us (39%)
  waiting for transfers between devices  13.6 us (31%)
  Pallas kernels  11.8 us (27%)
  between operations  0.75 us (2%)
    pallas_call x14, Pallas kernels, call(): pl.pallas_call(kernel, out_shape=shapes, compiler_params=pltpu.CompilerPa...  11.8 us
    ppermute x8, waiting for transfers between devices, beside(): lax.ppermute(value, 'tm', [(i, i ^ masks[i % 2]) for i in range(ranks)])  10.9 us
    ppermute x8, starting transfers between devices, beside(): lax.ppermute(value, 'tm', [(i, i ^ masks[i % 2]) for i in range(ranks)])  8.13 us
    ppermute x4, starting transfers between devices, partner(): return lax.ppermute(value, 'tm', [(i, i ^ mask) for i in range(ranks)])  8.08 us
    ppermute x4, waiting for transfers between devices, partner(): return lax.ppermute(value, 'tm', [(i, i ^ mask) for i in range(ranks)])  2.69 us
  transfers between devices with their start and end apart: 13, of which 9 were waited for; matrix products, arithmetic and copies ran while one was open for 0% of the time, Pallas kernels for 11%

profile of v5, /device:TPU:25, one launch (start us, length us, event | category | flops | bytes accessed | tf_op | source)
XLA Modules:
  0.0 43.0 jit_solution(2492598989047633439)
XLA Ops:
  0.6 1.8 %halves_and_layers.1 = (f32[2,4,16,2176]{3,2,1,0:T(8,128)S(1)}, f32[2,4,16,2176]{3,2,1,0:T(8,128)S(1)}, f32[32,2048]{1,0:T(8,128)S(1)}, f32[10,16,128]{2,1,0:T(8...) custom-call(f32[4,32,2048]{2,1,0:T(8,128)} %state.1, f32[4,32,2048]{2,1,0:T(8,128)} %adjoint.1, ...), custom_call_target="tpu_custom_call" | custom-call | bytes 7400000 | tf_op jit(solution)/shard_map/halves_and_layers/pallas_call | solution.py:607
  2.5 0.7 %collective-permute-start = (f32[8,16,128]{2,1,0:T(8,128)S(1)}, f32[8,16,128]{2,1,0:T(8,128)S(1)}, u32[]{:S(2)}, u32[]{:S(2)}) collective-permute-start(f32[8,16,128]{2,1,0:T(8,128)S(1)} %get-tuple-element.33), channel_id=1, source_target_pairs={{0,4},{4,0},{8,12},{12,8},{16,20},{20,16},{24,28},{28,24},{1,5},{5... | collective-permute-start | bytes 196616 | tf_op jit(solution)/shard_map/ppermute | solution.py:593
  3.2 0.9 %collective-permute-done.edge_other = f32[8,16,128]{2,1,0:T(8,128)S(1)} collective-permute-done((f32[8,16,128]{2,1,0:T(8,128)S(1)}, f32[8,16,128]{2,1,0:T(8,128)S(1)}, u32[]{:S(2)}, u32[]{:S(2)}) %collective-permute-start) | collective-permute-done | bytes 65568 | tf_op jit(solution)/shard_map/ppermute | solution.py:593
  4.1 0.4 collective-permute-start.2
  4.5 0.7 %collective-permute-start.1 = (f32[18,16,128]{2,1,0:T(8,128)S(1)}, f32[18,16,128]{2,1,0:T(8,128)S(1)}, u32[]{:S(2)}, u32[]{:S(2)}) collective-permute-start(f32[18,16,128]{2,1,0:T(8,128)S(1)} %get-tuple-element.35), channel_id=1, source_target_pairs={{1,4},{2,5},{3,6},{4,1},{5,2},{6,3},{9,12},{10,13},{11,14},{12,9},... | collective-permute-start | bytes 442376 | tf_op jit(solution)/shard_map/ppermute | solution.py:602
  5.2 1.7 %collective-permute-done.2.other = f32[2,4,16,2176]{3,2,1,0:T(8,128)S(1)} collective-permute-done((f32[2,4,16,2176]{3,2,1,0:T(8,128)S(1)}, f32[2,4,16,2176]{3,2,1,0:T(8,128)S(1)}, u32[]{:S(2)}, u32[]{:S(2)}) %collective-permute-start.2) | collective-permute-done | bytes 1114144 | tf_op jit(solution)/shard_map/ppermute | solution.py:593
  6.9 0.7 %inner_ends.1 = (f32[16,8,2304]{2,1,0:T(8,128)S(1)}, f32[4,8,2304]{2,1,0:T(8,128)S(1)}, f32[2,8,2304]{2,1,0:T(8,128)S(1)}) custom-call(f32[2,4,16,2176]{3,2,1,0:T(8,128)S(1)} %get-tuple-element.36.keep, f32[2,4,16,2176]{3,2,1,0:T(8,128)S(1)} %collective-permute-done.2.other, f32[32,2048]{1,0:T(8,128)S(1)} %get-tuple-element.31.slab, ...), custom_call_target="tpu_custom_call" | custom-call | bytes 3700000 | tf_op jit(solution)/shard_map/inner_ends/pallas_call | solution.py:607
  7.6 1.3 %collective-permute-start.5 = (f32[2,8,2304]{2,1,0:T(8,128)S(1)}, f32[2,8,2304]{2,1,0:T(8,128)S(1)}, u32[]{:S(2)}, u32[]{:S(2)}) collective-permute-start(f32[2,8,2304]{2,1,0:T(8,128)S(1)} %get-tuple-element.39.rest_1_.mine.rest_0_), channel_id=1, source_target_pairs={{0,8},{4,20},{8,0},{12,28},{16,24},{20,4},{24,16},{28,12},{1,9},{5... | collective-permute-start | bytes 442376 | tf_op jit(solution)/shard_map/ppermute | solution.py:656
  9.0 0.7 %outer_ends.1 = (f32[16,8,2304]{2,1,0:T(8,128)S(1)}, f32[4,8,2304]{2,1,0:T(8,128)S(1)}, f32[2,8,2304]{2,1,0:T(8,128)S(1)}) custom-call(f32[2,4,16,2176]{3,2,1,0:T(8,128)S(1)} %get-tuple-element.36.keep, f32[2,4,16,2176]{3,2,1,0:T(8,128)S(1)} %collective-permute-done.2.other, f32[32,2048]{1,0:T(8,128)S(1)} %get-tuple-element.31.slab, ...), custom_call_target="tpu_custom_call" | custom-call | bytes 3700000 | tf_op jit(solution)/shard_map/outer_ends/pallas_call | solution.py:607
  9.7 0.3 collective-permute-start.3
  9.9 2.1 %collective-permute-done.5.theirs.rest_1_ = f32[2,8,2304]{2,1,0:T(8,128)S(1)} collective-permute-done((f32[2,8,2304]{2,1,0:T(8,128)S(1)}, f32[2,8,2304]{2,1,0:T(8,128)S(1)}, u32[]{:S(2)}, u32[]{:S(2)}) %collective-permute-start.5) | collective-permute-done | bytes 147488 | tf_op jit(solution)/shard_map/ppermute | solution.py:656
  12.2 1.3 %collective-permute-start.6 = (f32[2,8,2304]{2,1,0:T(8,128)S(1)}, f32[2,8,2304]{2,1,0:T(8,128)S(1)}, u32[]{:S(2)}, u32[]{:S(2)}) collective-permute-start(f32[2,8,2304]{2,1,0:T(8,128)S(1)} %relay.5), channel_id=1, source_target_pairs={{0,16},{4,12},{8,24},{12,4},{16,0},{20,28},{24,8},{28,20},{1,17},{... | collective-permute-start | bytes 442376 | tf_op jit(solution)/shard_map/ppermute | solution.py:656
  13.5 0.3 collective-permute-done.3.theirs.rest_1_
  13.7 0.2 relay.4
  13.9 1.3 %collective-permute-start.4 = (f32[2,8,2304]{2,1,0:T(8,128)S(1)}, f32[2,8,2304]{2,1,0:T(8,128)S(1)}, u32[]{:S(2)}, u32[]{:S(2)}) collective-permute-start(f32[2,8,2304]{2,1,0:T(8,128)S(1)} %relay.4), channel_id=1, source_target_pairs={{0,16},{4,12},{8,24},{12,4},{16,0},{20,28},{24,8},{28,20},{1,17},{... | collective-permute-start | bytes 442376 | tf_op jit(solution)/shard_map/ppermute | solution.py:656
  15.2 2.8 %collective-permute-done.6.rest_2_ = f32[2,8,2304]{2,1,0:T(8,128)S(1)} collective-permute-done((f32[2,8,2304]{2,1,0:T(8,128)S(1)}, f32[2,8,2304]{2,1,0:T(8,128)S(1)}, u32[]{:S(2)}, u32[]{:S(2)}) %collective-permute-start.6) | collective-permute-done | bytes 147488 | tf_op jit(solution)/shard_map/ppermute | solution.py:656
  18.0 1.2 %inner_first_sweep.1 = (f32[16,8,2048]{2,1,0:T(8,128)S(1)}, f32[16,8,2048]{2,1,0:T(8,128)S(1)}, f32[16,16,128]{2,1,0:T(8,128)S(1)}) custom-call(f32[16,8,2304]{2,1,0:T(8,128)S(1)} %get-tuple-element.46.raw_ref, f32[4,8,2304]{2,1,0:T(8,128)S(1)} %get-tuple-element.47.factor_ref.refs_7_.inner_factors.rest_3_, ...), custom_call_target="tpu_custom_call" | custom-call | bytes 4070000 | tf_op jit(solution)/shard_map/inner_first_sweep/pallas_call | solution.py:607
  19.1 0.3 collective-permute-done.4.rest_2_
  19.4 1.2 %outer_first_sweep.1 = (f32[16,8,2048]{2,1,0:T(8,128)S(1)}, f32[16,8,2048]{2,1,0:T(8,128)S(1)}, f32[16,16,128]{2,1,0:T(8,128)S(1)}) custom-call(f32[16,8,2304]{2,1,0:T(8,128)S(1)} %get-tuple-element.40.raw_ref, f32[4,8,2304]{2,1,0:T(8,128)S(1)} %get-tuple-element.41.factor_ref.refs_3_.outer_factors.rest_2_, ...), custom_call_target="tpu_custom_call" | custom-call | bytes 4070000 | tf_op jit(solution)/shard_map/outer_first_sweep/pallas_call | solution.py:607
  20.6 3.0 %couplings.1 = (f32[8,16,2048]{2,1,0:T(8,128)S(1)}, f32[11,16,2048]{2,1,0:T(8,128)S(1)}, f32[2,16,2048]{2,1,0:T(8,128)S(1)}, f32[2,8,2048]{2,1,0:T(8,128)S(1)}, f32[2,8,2048]{2,1,0:T(8,128)S(1)}) custom-call(f32[32,2048]{1,0:T(8,128)S(1)} %get-tuple-element.31.slab, f32[3,32,2048]{2,1,0:T(8,128)S(1)} %copy-done, ...), custom_call_target="tpu_custom_call" | custom-call | bytes 11100000 | tf_op jit(solution)/shard_map/couplings/pallas_call | solution.py:607
  23.6 4.7 %collective-permute-start.7 = (f32[11,16,2048]{2,1,0:T(8,128)S(1)}, f32[11,16,2048]{2,1,0:T(8,128)S(1)}, u32[]{:S(2)}, u32[]{:S(2)}) collective-permute-start(f32[11,16,2048]{2,1,0:T(8,128)S(1)} %get-tuple-element.51), channel_id=1, source_target_pairs={{0,4},{4,0},{8,12},{12,8},{16,20},{20,16},{24,28},{28,24},{1,5},{5... | collective-permute-start | bytes 4325384 | tf_op jit(solution)/shard_map/ppermute | solution.py:593
  28.3 1.2 %collective-permute-start.8 = (f32[2,8,2048]{2,1,0:T(8,128)S(1)}, f32[2,8,2048]{2,1,0:T(8,128)S(1)}, u32[]{:S(2)}, u32[]{:S(2)}) collective-permute-start(f32[2,8,2048]{2,1,0:T(8,128)S(1)} %get-tuple-element.53.mine.rest_0_), channel_id=1, source_target_pairs={{0,8},{4,20},{8,0},{12,28},{16,24},{20,4},{24,16},{28,12},{1,9},{5... | collective-permute-start | bytes 393224 | tf_op jit(solution)/shard_map/ppermute | solution.py:656
  29.5 0.2 collective-permute-start.10
  29.7 2.6 %collective-permute-done.8.theirs.rest_1_ = f32[2,8,2048]{2,1,0:T(8,128)S(1)} collective-permute-done((f32[2,8,2048]{2,1,0:T(8,128)S(1)}, f32[2,8,2048]{2,1,0:T(8,128)S(1)}, u32[]{:S(2)}, u32[]{:S(2)}) %collective-permute-start.8) | collective-permute-done | bytes 131104 | tf_op jit(solution)/shard_map/ppermute | solution.py:656
  32.5 1.3 %collective-permute-start.9 = (f32[2,8,2048]{2,1,0:T(8,128)S(1)}, f32[2,8,2048]{2,1,0:T(8,128)S(1)}, u32[]{:S(2)}, u32[]{:S(2)}) collective-permute-start(f32[2,8,2048]{2,1,0:T(8,128)S(1)} %relay.6), channel_id=1, source_target_pairs={{0,16},{4,12},{8,24},{12,4},{16,0},{20,28},{24,8},{28,20},{1,17},{... | collective-permute-start | bytes 393224 | tf_op jit(solution)/shard_map/ppermute | solution.py:656
  34.0 1.2 %collective-permute-start.11 = (f32[2,8,2048]{2,1,0:T(8,128)S(1)}, f32[2,8,2048]{2,1,0:T(8,128)S(1)}, u32[]{:S(2)}, u32[]{:S(2)}) collective-permute-start(f32[2,8,2048]{2,1,0:T(8,128)S(1)} %relay.7), channel_id=1, source_target_pairs={{0,16},{4,12},{8,24},{12,4},{16,0},{20,28},{24,8},{28,20},{1,17},{... | collective-permute-start | bytes 393224 | tf_op jit(solution)/shard_map/ppermute | solution.py:656
  35.2 1.5 %collective-permute-done.9.rest_2_ = f32[2,8,2048]{2,1,0:T(8,128)S(1)} collective-permute-done((f32[2,8,2048]{2,1,0:T(8,128)S(1)}, f32[2,8,2048]{2,1,0:T(8,128)S(1)}, u32[]{:S(2)}, u32[]{:S(2)}) %collective-permute-start.9) | collective-permute-done | bytes 131104 | tf_op jit(solution)/shard_map/ppermute | solution.py:656
  36.7 1.4 %collective-permute-done.11.rest_5_ = f32[2,8,2048]{2,1,0:T(8,128)S(1)} collective-permute-done((f32[2,8,2048]{2,1,0:T(8,128)S(1)}, f32[2,8,2048]{2,1,0:T(8,128)S(1)}, u32[]{:S(2)}, u32[]{:S(2)}) %collective-permute-start.11) | collective-permute-done | bytes 131104 | tf_op jit(solution)/shard_map/ppermute | solution.py:656
  38.1 0.4 entering.1
  38.5 2.2 %collective-permute-start.12 = (f32[2,16,2048]{2,1,0:T(8,128)S(1)}, f32[2,16,2048]{2,1,0:T(8,128)S(1)}, u32[]{:S(2)}, u32[]{:S(2)}) collective-permute-start(f32[2,16,2048]{2,1,0:T(8,128)S(1)} %get-tuple-element.55), channel_id=1, source_target_pairs={{0,4},{4,0},{8,12},{12,8},{16,20},{20,16},{24,28},{28,24},{1,5},{5... | collective-permute-start | bytes 786440 | tf_op jit(solution)/shard_map/ppermute | solution.py:593
  40.7 1.1 %finish_own.1 = (f32[4,32,2048]{2,1,0:T(8,128)}, f32[4,32,2048]{2,1,0:T(8,128)}) custom-call(f32[8,16,2048]{2,1,0:T(8,128)S(1)} %get-tuple-element.56.rest_0_, f32[2,16,2048]{2,1,0:T(8,128)S(1)} %get-tuple-element.57.rest_1_, f32[4,8,2304]{2,1,0:T(8,128)S(1)} %get-tuple-element.41.factor_ref.refs_3_.outer_factors.rest_2_, ...), custom_call_target="tpu_custom_call" | custom-call | bytes 4440000 | tf_op jit(solution)/shard_map/finish_own/pallas_call | solution.py:607
  41.9 1.1 %finish_other.1 = (f32[4,32,2048]{2,1,0:T(8,128)}, f32[4,32,2048]{2,1,0:T(8,128)}) custom-call(f32[11,16,2048]{2,1,0:T(8,128)S(1)} %collective-permute-done.7.rest_0_, f32[2,16,2048]{2,1,0:T(8,128)S(1)} %collective-permute-done.12.rest_1_, f32[4,32,2048]{2,1,0:T(8,128)} %get-tuple-element.58.rest_2_, ...), custom_call_target="tpu_custom_call", output_to_operand_aliasing={{0}: (2, {}), {1}: (3, {})} | custom-call | bytes 4440000 | tf_op jit(solution)/shard_map/finish_other/pallas_call | solution.py:607
  (10 shorter events, 0.5 us)
Async XLA Ops:
  2.5 1.6 %collective-permute-start = (f32[8,16,128]{2,1,0:T(8,128)S(1)}, f32[8,16,128]{2,1,0:T(8,128)S(1)}, u32[]{:S(2)}, u32[]{:S(2)}) collective-permute-start(f32[8,16,128]{2,1,0:T(8,128)S(1)} %get-tuple-element.33), channel_id=1, source_target_pairs={{0,4},{4,0},{8,12},{12,8},{16,20},{20,16},{24,28},{28,24},{1,5},{5... | collective-permute-start | bytes 196616 | tf_op jit(solution)/shard_map/ppermute | solution.py:593
  4.1 2.8 %collective-permute-start.2 = (f32[2,4,16,2176]{3,2,1,0:T(8,128)S(1)}, f32[2,4,16,2176]{3,2,1,0:T(8,128)S(1)}, u32[]{:S(2)}, u32[]{:S(2)}) collective-permute-start(f32[2,4,16,2176]{3,2,1,0:T(8,128)S(1)} %get-tuple-element.37), channel_id=1, source_target_pairs={{0,4},{4,0},{8,12},{12,8},{16,20},{20,16},{24,28},{28,24},{1,5},{5... | collective-permute-start | bytes 3342344 | tf_op jit(solution)/shard_map/ppermute | solution.py:593
  4.5 4.4 %collective-permute-start.1 = (f32[18,16,128]{2,1,0:T(8,128)S(1)}, f32[18,16,128]{2,1,0:T(8,128)S(1)}, u32[]{:S(2)}, u32[]{:S(2)}) collective-permute-start(f32[18,16,128]{2,1,0:T(8,128)S(1)} %get-tuple-element.35), channel_id=1, source_target_pairs={{1,4},{2,5},{3,6},{4,1},{5,2},{6,3},{9,12},{10,13},{11,14},{12,9},... | collective-permute-start | bytes 442376 | tf_op jit(solution)/shard_map/ppermute | solution.py:602
  7.6 4.4 %collective-permute-start.5 = (f32[2,8,2304]{2,1,0:T(8,128)S(1)}, f32[2,8,2304]{2,1,0:T(8,128)S(1)}, u32[]{:S(2)}, u32[]{:S(2)}) collective-permute-start(f32[2,8,2304]{2,1,0:T(8,128)S(1)} %get-tuple-element.39.rest_1_.mine.rest_0_), channel_id=1, source_target_pairs={{0,8},{4,20},{8,0},{12,28},{16,24},{20,4},{24,16},{28,12},{1,9},{5... | collective-permute-start | bytes 442376 | tf_op jit(solution)/shard_map/ppermute | solution.py:656
  9.7 4.1 %collective-permute-start.3 = (f32[2,8,2304]{2,1,0:T(8,128)S(1)}, f32[2,8,2304]{2,1,0:T(8,128)S(1)}, u32[]{:S(2)}, u32[]{:S(2)}) collective-permute-start(f32[2,8,2304]{2,1,0:T(8,128)S(1)} %get-tuple-element.42.mine.rest_0_), channel_id=1, source_target_pairs={{0,8},{4,20},{8,0},{12,28},{16,24},{20,4},{24,16},{28,12},{1,9},{5... | collective-permute-start | bytes 442376 | tf_op jit(solution)/shard_map/ppermute | solution.py:656
  12.2 5.8 %collective-permute-start.6 = (f32[2,8,2304]{2,1,0:T(8,128)S(1)}, f32[2,8,2304]{2,1,0:T(8,128)S(1)}, u32[]{:S(2)}, u32[]{:S(2)}) collective-permute-start(f32[2,8,2304]{2,1,0:T(8,128)S(1)} %relay.5), channel_id=1, source_target_pairs={{0,16},{4,12},{8,24},{12,4},{16,0},{20,28},{24,8},{28,20},{1,17},{... | collective-permute-start | bytes 442376 | tf_op jit(solution)/shard_map/ppermute | solution.py:656
  13.9 5.5 %collective-permute-start.4 = (f32[2,8,2304]{2,1,0:T(8,128)S(1)}, f32[2,8,2304]{2,1,0:T(8,128)S(1)}, u32[]{:S(2)}, u32[]{:S(2)}) collective-permute-start(f32[2,8,2304]{2,1,0:T(8,128)S(1)} %relay.4), channel_id=1, source_target_pairs={{0,16},{4,12},{8,24},{12,4},{16,0},{20,28},{24,8},{28,20},{1,17},{... | collective-permute-start | bytes 442376 | tf_op jit(solution)/shard_map/ppermute | solution.py:656
  19.1 1.4 %copy-start = (f32[3,32,2048]{2,1,0:T(8,128)S(1)}, f32[3,32,2048]{2,1,0:T(8,128)}, u32[]{:S(2)}) copy-start(f32[3,32,2048]{2,1,0:T(8,128)} %velocity_ref.1) | copy-start | bytes 2359300
  23.6 18.3 %collective-permute-start.7 = (f32[11,16,2048]{2,1,0:T(8,128)S(1)}, f32[11,16,2048]{2,1,0:T(8,128)S(1)}, u32[]{:S(2)}, u32[]{:S(2)}) collective-permute-start(f32[11,16,2048]{2,1,0:T(8,128)S(1)} %get-tuple-element.51), channel_id=1, source_target_pairs={{0,4},{4,0},{8,12},{12,8},{16,20},{20,16},{24,28},{28,24},{1,5},{5... | collective-permute-start | bytes 4325384 | tf_op jit(solution)/shard_map/ppermute | solution.py:593
  28.3 4.1 %collective-permute-start.8 = (f32[2,8,2048]{2,1,0:T(8,128)S(1)}, f32[2,8,2048]{2,1,0:T(8,128)S(1)}, u32[]{:S(2)}, u32[]{:S(2)}) collective-permute-start(f32[2,8,2048]{2,1,0:T(8,128)S(1)} %get-tuple-element.53.mine.rest_0_), channel_id=1, source_target_pairs={{0,8},{4,20},{8,0},{12,28},{16,24},{20,4},{24,16},{28,12},{1,9},{5... | collective-permute-start | bytes 393224 | tf_op jit(solution)/shard_map/ppermute | solution.py:656
  29.5 4.3 %collective-permute-start.10 = (f32[2,8,2048]{2,1,0:T(8,128)S(1)}, f32[2,8,2048]{2,1,0:T(8,128)S(1)}, u32[]{:S(2)}, u32[]{:S(2)}) collective-permute-start(f32[2,8,2048]{2,1,0:T(8,128)S(1)} %get-tuple-element.54.mine.rest_3_), channel_id=1, source_target_pairs={{0,8},{4,20},{8,0},{12,28},{16,24},{20,4},{24,16},{28,12},{1,9},{5... | collective-permute-start | bytes 393224 | tf_op jit(solution)/shard_map/ppermute | solution.py:656
  32.5 4.2 %collective-permute-start.9 = (f32[2,8,2048]{2,1,0:T(8,128)S(1)}, f32[2,8,2048]{2,1,0:T(8,128)S(1)}, u32[]{:S(2)}, u32[]{:S(2)}) collective-permute-start(f32[2,8,2048]{2,1,0:T(8,128)S(1)} %relay.6), channel_id=1, source_target_pairs={{0,16},{4,12},{8,24},{12,4},{16,0},{20,28},{24,8},{28,20},{1,17},{... | collective-permute-start | bytes 393224 | tf_op jit(solution)/shard_map/ppermute | solution.py:656
  34.0 4.1 %collective-permute-start.11 = (f32[2,8,2048]{2,1,0:T(8,128)S(1)}, f32[2,8,2048]{2,1,0:T(8,128)S(1)}, u32[]{:S(2)}, u32[]{:S(2)}) collective-permute-start(f32[2,8,2048]{2,1,0:T(8,128)S(1)} %relay.7), channel_id=1, source_target_pairs={{0,16},{4,12},{8,24},{12,4},{16,0},{20,28},{24,8},{28,20},{1,17},{... | collective-permute-start | bytes 393224 | tf_op jit(solution)/shard_map/ppermute | solution.py:656
  38.5 3.4 %collective-permute-start.12 = (f32[2,16,2048]{2,1,0:T(8,128)S(1)}, f32[2,16,2048]{2,1,0:T(8,128)S(1)}, u32[]{:S(2)}, u32[]{:S(2)}) collective-permute-start(f32[2,16,2048]{2,1,0:T(8,128)S(1)} %get-tuple-element.55), channel_id=1, source_target_pairs={{0,4},{4,0},{8,12},{12,8},{16,20},{20,16},{24,28},{28,24},{1,5},{5... | collective-permute-start | bytes 786440 | tf_op jit(solution)/shard_map/ppermute | solution.py:593

commit v6 on v5

--- a/solution.py
+++ b/solution.py
@@ -66,14 +66,13 @@
     'outermost': 0.3,
     'ends': 1,
     'relay': 0.2,
-    'first_sweep': 1.1,
+    'first_sweep': 1,
     'couplings': 3,
     'entering': 0.2,
-    'finish_own': 1.2,
-    'finish_other': 1.2,
+    'finish': 1,
 }
 UNROLL_ENDS = 8
-UNROLL_COUPLINGS = 2
+UNROLL_COUPLINGS = 4
 
 
 def tile_rows(side, half, depth):
@@ -114,6 +113,11 @@
     return [[(jnp.where(ok, 0.5 * (kappa + value), kappa), ok) for value, ok in pair] for pair in pairs]
 
 
+def cut_inside():
+    slab = lax.axis_index("gz")
+    return jnp.where(this_core() == 0, slab > 0, slab < lax.axis_size("gz") - 1)
+
+
 def edge_rows(shape):
     core = this_core()
     row = lax.broadcasted_iota(jnp.int32, shape, 0)
@@ -281,7 +285,7 @@
 
     def one(group, carry):
         here = lane_block(group * LANES)
-        beyond = cut[steps, pl.ds(group, 1), :] if side == OUTER else None
+        beyond = jnp.where(cut_inside(), cut[steps, pl.ds(group, 1), :], 0.0) if side == OUTER else None
         diagonal = total_weight(faces(side, slab, beyond, group, half))
 
         def stores(ref, slot, value):
@@ -399,7 +403,7 @@
 
         sweep(put, here)
 
-    each_block(cells, 2 * LANES, own)
+    each_block(cells, 4 * LANES, own)
 
     def put_layer(step, state, adjoint):
         for field, value in enumerate((state, adjoint)):
@@ -439,7 +443,7 @@
         left = lane_block(jnp.maximum(group - 1, 0) * LANES)
         right = lane_block(jnp.minimum(group + 1, groups - 1) * LANES)
         row = pl.ds(group, 1)
-        beyond = cut_ref[steps, row, :] if side == OUTER else None
+        beyond = jnp.where(cut_inside(), cut_ref[steps, row, :], 0.0) if side == OUTER else None
         weights = faces(side, slab, beyond, group, half)
         lane = lax.broadcasted_iota(jnp.int32, (tile, LANES), 1)
         low = lane < NY
@@ -511,38 +515,36 @@
     return decay, ratio * mixed, 0.5 * upright
 
 
-def carry_kernel(steps_local, middle, outer_factors, inner_factors, *rest):
+def carry_kernel(side, steps_local, middle, factor_ref, *rest):
     *ends, keep, send = rest
-    half, cells = middle.shape[1:]
-    tile = half // 2
-    core = this_core()
-    for side, factor_ref in enumerate((outer_factors, inner_factors)):
-        held = slice(side * tile, (side + 1) * tile)
-
-        def one(here):
-            factors = [factor_ref[slot, :, here] for slot in range(4)]
-            decay, _, _, upright = factors
-            back, state = entering(factors, ends[side * len(ends) // 2 : (side + 1) * len(ends) // 2], here, 2 * steps_local)
-            block = power(decay, steps_local)
-            early_back = middle[0, held, here] + block * back
-            late_state = middle[1, held, here] + block * state + response_of(decay, upright, steps_local) * early_back
-            for slot, (early, late) in enumerate(((early_back, back), (state, late_state))):
-                keep[slot, held, here] = jnp.where(core == 0, early, late)
-                send[slot, held, here] = jnp.where(core == 0, late, early)
-
-        each_block(cells, 4 * LANES, one)
-
-
-def finish_kernel(theirs, ratio, chips, *rest):
-    state_out, adjoint_out, result, sems = rest[-4:]
-    parts, entered = rest[:2]
+    tile, cells = keep.shape[1:]
+    held = slice(side * tile, (side + 1) * tile)
+    core = this_core()
+
+    def one(here):
+        factors = [factor_ref[slot, :, here] for slot in range(4)]
+        decay, _, _, upright = factors
+        back, state = entering(factors, ends, here, 2 * steps_local)
+        block = power(decay, steps_local)
+        early_back = middle[0, held, here] + block * back
+        late_state = middle[1, held, here] + block * state + response_of(decay, upright, steps_local) * early_back
+        for slot, (early, late) in enumerate(((early_back, back), (state, late_state))):
+            keep[slot, :, here] = jnp.where(core == 0, early, late)
+            send[slot, :, here] = jnp.where(core == 0, late, early)
+
+    each_block(cells, 4 * LANES, one)
+
+
+def finish_kernel(jobs, ratio, chips, *refs):
+    state_out, adjoint_out, result, sems = refs[-4:]
     steps_local, depth, cells = state_out.shape
     tile = depth // 4
     core = this_core()
     whole = step_scale(ratio, 2 * steps_local, chips, -1)
     scales = [jnp.where(core == 0, whole[step], whole[steps_local + step]) for step in range(steps_local)]
     copies = []
-    for side in (OUTER, INNER):
+    for job, (theirs, side) in enumerate(jobs):
+        parts, entered, factor_ref = refs[3 * job : 3 * job + 3]
         held = slice(side * tile, (side + 1) * tile)
         start = tile_rows(side, 2 * tile, depth)
         rows = pl.ds(pl.multiple_of(depth - tile - start if theirs else start, 8), tile)
@@ -551,22 +553,22 @@
             if theirs:
                 decay, gain, half_up = [parts[2 * steps_local + slot, held, here] for slot in range(3)]
             else:
-                decay, gain, half_up = finish_factors(ratio, [rest[2 + side][slot, :, here] for slot in range(4)])
-            backs = [entered[0, held, here]]
+                decay, gain, half_up = finish_factors(ratio, [factor_ref[slot, :, here] for slot in range(4)])
+            backs = [entered[0, :, here]]
             for _ in range(steps_local):
                 backs.append(decay * backs[-1])
             backs = backs[:0:-1]
-            previous = entered[1, held, here]
+            previous = entered[1, :, here]
             for step in range(steps_local):
                 current = decay * previous + half_up * backs[step]
                 adjoint = backs[step] - gain * previous
-                result[side, 0, step, :, here] = (parts[2 * step, held, here] + current) * scales[step]
-                result[side, 1, step, :, here] = (parts[2 * step + 1, held, here] + adjoint) * scales[step]
+                result[job, 0, step, :, here] = (parts[2 * step, held, here] + current) * scales[step]
+                result[job, 1, step, :, here] = (parts[2 * step + 1, held, here] + adjoint) * scales[step]
                 previous = current
 
         each_block(cells, 4 * LANES, one)
         for field, out in enumerate((state_out, adjoint_out)):
-            copies.append(pltpu.make_async_copy(result.at[side, field], out.at[:, rows, :], sems.at[side, field]))
+            copies.append(pltpu.make_async_copy(result.at[job, field], out.at[:, rows, :], sems.at[job, field]))
             copies[-1].start()
     for copy in copies:
         copy.wait()
@@ -594,11 +596,12 @@
 
     def outward(value):
         pairs = []
+        spare = (4, 2) if ranks % 8 == 0 else (0, 0)
         for t in range(ranks):
             for g in range(slabs):
                 to = g - 1 if t % 2 == 0 else g + 1
-                if 0 <= to < slabs:
-                    pairs.append((t * slabs + g, (t ^ 1) * slabs + to))
+                other = (t ^ 1) * slabs + to if 0 <= to < slabs else (t ^ spare[t % 2]) * slabs + g
+                pairs.append((t * slabs + g, other))
         return lax.ppermute(value, ("tm", "gz"), pairs)
 
     def call(kernel, name, out_shape, *args, **kwargs):
@@ -718,33 +721,42 @@
     )
     other = partner(send, 1)
     entered = [exchange(mine, table) for mine, table in zip(ends, (outer_factors, inner_factors))]
-    own_in, send_in = call(
-        functools.partial(carry_kernel, steps_local),
-        "entering",
-        [(2, half, cells)] * 2,
-        middle,
-        outer_factors,
-        inner_factors,
-        *entered[OUTER],
-        *entered[INNER],
-    )
-    other_in = partner(send_in, 1)
-
-    def finish(theirs, results, *args):
+    factors = (outer_factors, inner_factors)
+
+    def enter(side):
+        own_in, send_in = call(
+            functools.partial(carry_kernel, side, steps_local),
+            ("outer", "inner")[side] + "_entering",
+            [(2, tile, cells)] * 2,
+            middle,
+            factors[side],
+            *entered[side],
+        )
+        return own_in, partner(send_in, 1)
+
+    own_in, other_in = zip(enter(OUTER), enter(INNER))
+
+    def finish(results, *jobs):
+        args = []
+        for theirs, side in jobs:
+            args += [other if theirs else keep, (other_in if theirs else own_in)[side], factors[side]]
         return call(
-            functools.partial(finish_kernel, theirs, ratio, chips),
-            ("finish_own", "finish_other")[theirs],
+            functools.partial(finish_kernel, jobs, ratio, chips),
+            "finish",
             [(steps_local, depth, cells)] * 2,
             *args,
             *results,
             in_specs=[vmem] * len(args) + [anywhere] * len(results),
             out_specs=[anywhere] * 2,
-            scratch_shapes=[pltpu.VMEM((2, 2, steps_local, tile, cells), f32), pltpu.SemaphoreType.DMA((2, 2))],
+            scratch_shapes=[
+                pltpu.VMEM((len(jobs), 2, steps_local, tile, cells), f32),
+                pltpu.SemaphoreType.DMA((len(jobs), 2)),
+            ],
             input_output_aliases={len(args) + i: i for i in range(len(results))},
         )
 
-    results = finish(False, (), keep, own_in, outer_factors, inner_factors)
-    return finish(True, results, other, other_in)
+    results = finish((), (False, OUTER), (False, INNER), (True, OUTER))
+    return finish(results, (True, INNER))
 
 
 def solution(mesh):

time: 43.2 us -> 40.9 us (0.947)
  the two profiles are of different devices: /device:TPU:25 before, /device:TPU:0 now
where the time goes in v6:
time: 40.9 us; the launch traced here: 40.8 us
  starting transfers between devices  17.7 us (43%)
  Pallas kernels  11.2 us (27%)
  waiting for transfers between devices  11.1 us (27%)
  between operations  0.79 us (2%)
    ppermute x8, starting transfers between devices, beside(): lax.ppermute(value, 'tm', [(i, i ^ masks[i % 2]) for i in range(ranks)])  13.9 us
    pallas_call x15, Pallas kernels, call(): pl.pallas_call(kernel, out_shape=shapes, compiler_params=pltpu.CompilerPa...  11.2 us
    ppermute x8, waiting for transfers between devices, beside(): lax.ppermute(value, 'tm', [(i, i ^ masks[i % 2]) for i in range(ranks)])  10.2 us
    ppermute x1, starting transfers between devices, outward(): return lax.ppermute(value, ('tm', 'gz'), pairs)  2.67 us
    ppermute x5, starting transfers between devices, partner(): return lax.ppermute(value, 'tm', [(i, i ^ mask) for i in range(ranks)])  1.15 us
    ppermute x5, waiting for transfers between devices, partner(): return lax.ppermute(value, 'tm', [(i, i ^ mask) for i in range(ranks)])  0.91 us
  transfers between devices with their start and end apart: 14, of which 8 were waited for; matrix products, arithmetic and copies ran while one was open for 0% of the time, Pallas kernels for 12%

profile of v6, /device:TPU:0, one launch (start us, length us, event | category | flops | bytes accessed | tf_op | source)
XLA Modules:
  0.0 40.8 jit_solution(14884642312501167607)
XLA Ops:
  0.6 1.8 %halves_and_layers.1 = (f32[2,4,16,2176]{3,2,1,0:T(8,128)S(1)}, f32[2,4,16,2176]{3,2,1,0:T(8,128)S(1)}, f32[32,2048]{1,0:T(8,128)S(1)}, f32[10,16,128]{2,1,0:T(8...) custom-call(f32[4,32,2048]{2,1,0:T(8,128)} %state.1, f32[4,32,2048]{2,1,0:T(8,128)} %adjoint.1, ...), custom_call_target="tpu_custom_call" | custom-call | bytes 7400000 | tf_op jit(solution)/shard_map/halves_and_layers/pallas_call | solution.py:610
  2.5 0.5 %collective-permute-start = (f32[8,16,128]{2,1,0:T(8,128)S(1)}, f32[8,16,128]{2,1,0:T(8,128)S(1)}, u32[]{:S(2)}, u32[]{:S(2)}) collective-permute-start(f32[8,16,128]{2,1,0:T(8,128)S(1)} %get-tuple-element.35), channel_id=1, source_target_pairs={{0,4},{4,0},{8,12},{12,8},{16,20},{20,16},{24,28},{28,24},{1,5},{5... | collective-permute-start | bytes 196616 | tf_op jit(solution)/shard_map/ppermute | solution.py:595
  3.0 0.9 %collective-permute-done.edge_other = f32[8,16,128]{2,1,0:T(8,128)S(1)} collective-permute-done((f32[8,16,128]{2,1,0:T(8,128)S(1)}, f32[8,16,128]{2,1,0:T(8,128)S(1)}, u32[]{:S(2)}, u32[]{:S(2)}) %collective-permute-start) | collective-permute-done | bytes 65568 | tf_op jit(solution)/shard_map/ppermute | solution.py:595
  3.9 0.4 %collective-permute-start.2 = (f32[2,4,16,2176]{3,2,1,0:T(8,128)S(1)}, f32[2,4,16,2176]{3,2,1,0:T(8,128)S(1)}, u32[]{:S(2)}, u32[]{:S(2)}) collective-permute-start(f32[2,4,16,2176]{3,2,1,0:T(8,128)S(1)} %get-tuple-element.39), channel_id=1, source_target_pairs={{0,4},{4,0},{8,12},{12,8},{16,20},{20,16},{24,28},{28,24},{1,5},{5... | collective-permute-start | bytes 3342344 | tf_op jit(solution)/shard_map/ppermute | solution.py:595
  4.3 2.7 %collective-permute-start.1 = (f32[18,16,128]{2,1,0:T(8,128)S(1)}, f32[18,16,128]{2,1,0:T(8,128)S(1)}, u32[]{:S(2)}, u32[]{:S(2)}) collective-permute-start(f32[18,16,128]{2,1,0:T(8,128)S(1)} %get-tuple-element.37), channel_id=1, source_target_pairs={{0,16},{1,4},{2,5},{3,6},{4,1},{5,2},{6,3},{7,15},{8,24},{9,12},{1... | collective-permute-start | bytes 442376 | tf_op jit(solution)/shard_map/ppermute | solution.py:605
  7.0 0.7 %inner_ends.1 = (f32[16,8,2304]{2,1,0:T(8,128)S(1)}, f32[4,8,2304]{2,1,0:T(8,128)S(1)}, f32[2,8,2304]{2,1,0:T(8,128)S(1)}) custom-call(f32[2,4,16,2176]{3,2,1,0:T(8,128)S(1)} %get-tuple-element.38.keep, f32[2,4,16,2176]{3,2,1,0:T(8,128)S(1)} %collective-permute-done.2.other, f32[32,2048]{1,0:T(8,128)S(1)} %get-tuple-element.33.slab, ...), custom_call_target="tpu_custom_call" | custom-call | bytes 3700000 | tf_op jit(solution)/shard_map/inner_ends/pallas_call | solution.py:610
  7.7 2.6 %collective-permute-start.5 = (f32[2,8,2304]{2,1,0:T(8,128)S(1)}, f32[2,8,2304]{2,1,0:T(8,128)S(1)}, u32[]{:S(2)}, u32[]{:S(2)}) collective-permute-start(f32[2,8,2304]{2,1,0:T(8,128)S(1)} %get-tuple-element.41.rest_1_.mine.rest_0_), channel_id=1, source_target_pairs={{0,8},{4,20},{8,0},{12,28},{16,24},{20,4},{24,16},{28,12},{1,9},{5... | collective-permute-start | bytes 442376 | tf_op jit(solution)/shard_map/ppermute | solution.py:659
  10.3 0.7 %outer_ends.1 = (f32[16,8,2304]{2,1,0:T(8,128)S(1)}, f32[4,8,2304]{2,1,0:T(8,128)S(1)}, f32[2,8,2304]{2,1,0:T(8,128)S(1)}) custom-call(f32[2,4,16,2176]{3,2,1,0:T(8,128)S(1)} %get-tuple-element.38.keep, f32[2,4,16,2176]{3,2,1,0:T(8,128)S(1)} %collective-permute-done.2.other, f32[32,2048]{1,0:T(8,128)S(1)} %get-tuple-element.33.slab, ...), custom_call_target="tpu_custom_call" | custom-call | bytes 3700000 | tf_op jit(solution)/shard_map/outer_ends/pallas_call | solution.py:610
  11.1 1.8 %collective-permute-start.3 = (f32[2,8,2304]{2,1,0:T(8,128)S(1)}, f32[2,8,2304]{2,1,0:T(8,128)S(1)}, u32[]{:S(2)}, u32[]{:S(2)}) collective-permute-start(f32[2,8,2304]{2,1,0:T(8,128)S(1)} %get-tuple-element.44.mine.rest_0_), channel_id=1, source_target_pairs={{0,8},{4,20},{8,0},{12,28},{16,24},{20,4},{24,16},{28,12},{1,9},{5... | collective-permute-start | bytes 442376 | tf_op jit(solution)/shard_map/ppermute | solution.py:659
  12.9 0.5 %collective-permute-done.5.theirs.rest_1_ = f32[2,8,2304]{2,1,0:T(8,128)S(1)} collective-permute-done((f32[2,8,2304]{2,1,0:T(8,128)S(1)}, f32[2,8,2304]{2,1,0:T(8,128)S(1)}, u32[]{:S(2)}, u32[]{:S(2)}) %collective-permute-start.5) | collective-permute-done | bytes 147488 | tf_op jit(solution)/shard_map/ppermute | solution.py:659
  13.5 0.2 relay.5
  13.6 2.1 %collective-permute-start.6 = (f32[2,8,2304]{2,1,0:T(8,128)S(1)}, f32[2,8,2304]{2,1,0:T(8,128)S(1)}, u32[]{:S(2)}, u32[]{:S(2)}) collective-permute-start(f32[2,8,2304]{2,1,0:T(8,128)S(1)} %relay.5), channel_id=1, source_target_pairs={{0,16},{4,12},{8,24},{12,4},{16,0},{20,28},{24,8},{28,20},{1,17},{... | collective-permute-start | bytes 442376 | tf_op jit(solution)/shard_map/ppermute | solution.py:659
  15.7 0.9 %collective-permute-done.3.theirs.rest_1_ = f32[2,8,2304]{2,1,0:T(8,128)S(1)} collective-permute-done((f32[2,8,2304]{2,1,0:T(8,128)S(1)}, f32[2,8,2304]{2,1,0:T(8,128)S(1)}, u32[]{:S(2)}, u32[]{:S(2)}) %collective-permute-start.3) | collective-permute-done | bytes 147488 | tf_op jit(solution)/shard_map/ppermute | solution.py:659
  16.7 0.2 relay.4
  16.8 1.9 %collective-permute-start.4 = (f32[2,8,2304]{2,1,0:T(8,128)S(1)}, f32[2,8,2304]{2,1,0:T(8,128)S(1)}, u32[]{:S(2)}, u32[]{:S(2)}) collective-permute-start(f32[2,8,2304]{2,1,0:T(8,128)S(1)} %relay.4), channel_id=1, source_target_pairs={{0,16},{4,12},{8,24},{12,4},{16,0},{20,28},{24,8},{28,20},{1,17},{... | collective-permute-start | bytes 442376 | tf_op jit(solution)/shard_map/ppermute | solution.py:659
  18.9 0.9 %inner_first_sweep.1 = (f32[16,8,2048]{2,1,0:T(8,128)S(1)}, f32[16,8,2048]{2,1,0:T(8,128)S(1)}, f32[16,16,128]{2,1,0:T(8,128)S(1)}) custom-call(f32[16,8,2304]{2,1,0:T(8,128)S(1)} %get-tuple-element.48.raw_ref, f32[4,8,2304]{2,1,0:T(8,128)S(1)} %get-tuple-element.49.factor_ref.refs_7_.refs_5_.refs_2_, ...), custom_call_target="tpu_custom_call" | custom-call | bytes 3700000 | tf_op jit(solution)/shard_map/inner_first_sweep/pallas_call | solution.py:610
  19.8 2.3 %collective-permute-done.4.rest_2_ = f32[2,8,2304]{2,1,0:T(8,128)S(1)} collective-permute-done((f32[2,8,2304]{2,1,0:T(8,128)S(1)}, f32[2,8,2304]{2,1,0:T(8,128)S(1)}, u32[]{:S(2)}, u32[]{:S(2)}) %collective-permute-start.4) | collective-permute-done | bytes 147488 | tf_op jit(solution)/shard_map/ppermute | solution.py:659
  22.0 0.9 %outer_first_sweep.1 = (f32[16,8,2048]{2,1,0:T(8,128)S(1)}, f32[16,8,2048]{2,1,0:T(8,128)S(1)}, f32[16,16,128]{2,1,0:T(8,128)S(1)}) custom-call(f32[16,8,2304]{2,1,0:T(8,128)S(1)} %get-tuple-element.42.raw_ref, f32[4,8,2304]{2,1,0:T(8,128)S(1)} %get-tuple-element.43.factor_ref.refs_3_.refs_2_.refs_8_, f32[2,8,2304]{2,1,0:T(8,128)S(1)} %get-tuple-element.44.mine.rest_0_, ...), custom_call_target="tpu_custom_call" | custom-call | bytes 3700000 | tf_op jit(solution)/shard_map/outer_first_sweep/pallas_call | solution.py:610
  23.0 2.8 %couplings.1 = (f32[8,16,2048]{2,1,0:T(8,128)S(1)}, f32[11,16,2048]{2,1,0:T(8,128)S(1)}, f32[2,16,2048]{2,1,0:T(8,128)S(1)}, f32[2,8,2048]{2,1,0:T(8,128)S(1)}, f32[2,8,2048]{2,1,0:T(8,128)S(1)}) custom-call(f32[32,2048]{1,0:T(8,128)S(1)} %get-tuple-element.33.slab, f32[3,32,2048]{2,1,0:T(8,128)S(1)} %copy-done, ...), custom_call_target="tpu_custom_call" | custom-call | bytes 11100000 | tf_op jit(solution)/shard_map/couplings/pallas_call | solution.py:610
  25.8 1.9 %collective-permute-start.11 = (f32[2,8,2048]{2,1,0:T(8,128)S(1)}, f32[2,8,2048]{2,1,0:T(8,128)S(1)}, u32[]{:S(2)}, u32[]{:S(2)}) collective-permute-start(f32[2,8,2048]{2,1,0:T(8,128)S(1)} %get-tuple-element.58.mine.rest_0_), channel_id=1, source_target_pairs={{0,8},{4,20},{8,0},{12,28},{16,24},{20,4},{24,16},{28,12},{1,9},{5... | collective-permute-start | bytes 393224 | tf_op jit(solution)/shard_map/ppermute | solution.py:659
  27.7 0.2 collective-permute-start.8
  27.9 2.9 %collective-permute-done.11.theirs.rest_1_ = f32[2,8,2048]{2,1,0:T(8,128)S(1)} collective-permute-done((f32[2,8,2048]{2,1,0:T(8,128)S(1)}, f32[2,8,2048]{2,1,0:T(8,128)S(1)}, u32[]{:S(2)}, u32[]{:S(2)}) %collective-permute-start.11) | collective-permute-done | bytes 131104 | tf_op jit(solution)/shard_map/ppermute | solution.py:659
  30.9 0.2 relay.7
  31.0 1.9 %collective-permute-start.12 = (f32[2,8,2048]{2,1,0:T(8,128)S(1)}, f32[2,8,2048]{2,1,0:T(8,128)S(1)}, u32[]{:S(2)}, u32[]{:S(2)}) collective-permute-start(f32[2,8,2048]{2,1,0:T(8,128)S(1)} %relay.7), channel_id=1, source_target_pairs={{0,16},{4,12},{8,24},{12,4},{16,0},{20,28},{24,8},{28,20},{1,17},{... | collective-permute-start | bytes 393224 | tf_op jit(solution)/shard_map/ppermute | solution.py:659
  33.0 0.2 relay.6
  33.1 1.3 %collective-permute-start.9 = (f32[2,8,2048]{2,1,0:T(8,128)S(1)}, f32[2,8,2048]{2,1,0:T(8,128)S(1)}, u32[]{:S(2)}, u32[]{:S(2)}) collective-permute-start(f32[2,8,2048]{2,1,0:T(8,128)S(1)} %relay.6), channel_id=1, source_target_pairs={{0,16},{4,12},{8,24},{12,4},{16,0},{20,28},{24,8},{28,20},{1,17},{... | collective-permute-start | bytes 393224 | tf_op jit(solution)/shard_map/ppermute | solution.py:659
  34.5 1.6 %collective-permute-done.12.rest_2_ = f32[2,8,2048]{2,1,0:T(8,128)S(1)} collective-permute-done((f32[2,8,2048]{2,1,0:T(8,128)S(1)}, f32[2,8,2048]{2,1,0:T(8,128)S(1)}, u32[]{:S(2)}, u32[]{:S(2)}) %collective-permute-start.12) | collective-permute-done | bytes 131104 | tf_op jit(solution)/shard_map/ppermute | solution.py:659
  36.1 0.2 outer_entering.1
  36.3 1.8 %collective-permute-done.9.rest_2_ = f32[2,8,2048]{2,1,0:T(8,128)S(1)} collective-permute-done((f32[2,8,2048]{2,1,0:T(8,128)S(1)}, f32[2,8,2048]{2,1,0:T(8,128)S(1)}, u32[]{:S(2)}, u32[]{:S(2)}) %collective-permute-start.9) | collective-permute-done | bytes 131104 | tf_op jit(solution)/shard_map/ppermute | solution.py:659
  38.2 0.2 inner_entering.1
  38.5 1.3 %finish.2 = (f32[4,32,2048]{2,1,0:T(8,128)}, f32[4,32,2048]{2,1,0:T(8,128)}) custom-call(f32[8,16,2048]{2,1,0:T(8,128)S(1)} %get-tuple-element.57.refs_0_.refs_3_, f32[2,8,2048]{2,1,0:T(8,128)S(1)} %get-tuple-element.59.refs_1_, f32[4,8,2304]{2,1,0:T(8,128)S(1)} %get-tuple-element.43.factor_ref.refs_3_.refs_2_.refs_8_, ...), custom_call_target="tpu_custom_call" | custom-call | bytes 3700000 | tf_op jit(solution)/shard_map/finish/pallas_call | solution.py:610
  39.8 0.9 %finish.3 = (f32[4,32,2048]{2,1,0:T(8,128)}, f32[4,32,2048]{2,1,0:T(8,128)}) custom-call(f32[11,16,2048]{2,1,0:T(8,128)S(1)} %collective-permute-done.7.refs_6_.refs_0_, f32[2,8,2048]{2,1,0:T(8,128)S(1)} %collective-permute-done.10.refs_1_, ...), custom_call_target="tpu_custom_call", output_to_operand_aliasing={{0}: (3, {}), {1}: (4, {})} | custom-call | bytes 3700000 | tf_op jit(solution)/shard_map/finish/pallas_call | solution.py:610
  (13 shorter events, 0.3 us)
Async XLA Ops:
  2.5 1.4 %collective-permute-start = (f32[8,16,128]{2,1,0:T(8,128)S(1)}, f32[8,16,128]{2,1,0:T(8,128)S(1)}, u32[]{:S(2)}, u32[]{:S(2)}) collective-permute-start(f32[8,16,128]{2,1,0:T(8,128)S(1)} %get-tuple-element.35), channel_id=1, source_target_pairs={{0,4},{4,0},{8,12},{12,8},{16,20},{20,16},{24,28},{28,24},{1,5},{5... | collective-permute-start | bytes 196616 | tf_op jit(solution)/shard_map/ppermute | solution.py:595
  3.9 3.1 %collective-permute-start.2 = (f32[2,4,16,2176]{3,2,1,0:T(8,128)S(1)}, f32[2,4,16,2176]{3,2,1,0:T(8,128)S(1)}, u32[]{:S(2)}, u32[]{:S(2)}) collective-permute-start(f32[2,4,16,2176]{3,2,1,0:T(8,128)S(1)} %get-tuple-element.39), channel_id=1, source_target_pairs={{0,4},{4,0},{8,12},{12,8},{16,20},{20,16},{24,28},{28,24},{1,5},{5... | collective-permute-start | bytes 3342344 | tf_op jit(solution)/shard_map/ppermute | solution.py:595
  4.3 6.0 %collective-permute-start.1 = (f32[18,16,128]{2,1,0:T(8,128)S(1)}, f32[18,16,128]{2,1,0:T(8,128)S(1)}, u32[]{:S(2)}, u32[]{:S(2)}) collective-permute-start(f32[18,16,128]{2,1,0:T(8,128)S(1)} %get-tuple-element.37), channel_id=1, source_target_pairs={{0,16},{1,4},{2,5},{3,6},{4,1},{5,2},{6,3},{7,15},{8,24},{9,12},{1... | collective-permute-start | bytes 442376 | tf_op jit(solution)/shard_map/ppermute | solution.py:605
  7.7 5.8 %collective-permute-start.5 = (f32[2,8,2304]{2,1,0:T(8,128)S(1)}, f32[2,8,2304]{2,1,0:T(8,128)S(1)}, u32[]{:S(2)}, u32[]{:S(2)}) collective-permute-start(f32[2,8,2304]{2,1,0:T(8,128)S(1)} %get-tuple-element.41.rest_1_.mine.rest_0_), channel_id=1, source_target_pairs={{0,8},{4,20},{8,0},{12,28},{16,24},{20,4},{24,16},{28,12},{1,9},{5... | collective-permute-start | bytes 442376 | tf_op jit(solution)/shard_map/ppermute | solution.py:659
  11.1 5.6 %collective-permute-start.3 = (f32[2,8,2304]{2,1,0:T(8,128)S(1)}, f32[2,8,2304]{2,1,0:T(8,128)S(1)}, u32[]{:S(2)}, u32[]{:S(2)}) collective-permute-start(f32[2,8,2304]{2,1,0:T(8,128)S(1)} %get-tuple-element.44.mine.rest_0_), channel_id=1, source_target_pairs={{0,8},{4,20},{8,0},{12,28},{16,24},{20,4},{24,16},{28,12},{1,9},{5... | collective-permute-start | bytes 442376 | tf_op jit(solution)/shard_map/ppermute | solution.py:659
  13.6 5.2 %collective-permute-start.6 = (f32[2,8,2304]{2,1,0:T(8,128)S(1)}, f32[2,8,2304]{2,1,0:T(8,128)S(1)}, u32[]{:S(2)}, u32[]{:S(2)}) collective-permute-start(f32[2,8,2304]{2,1,0:T(8,128)S(1)} %relay.5), channel_id=1, source_target_pairs={{0,16},{4,12},{8,24},{12,4},{16,0},{20,28},{24,8},{28,20},{1,17},{... | collective-permute-start | bytes 442376 | tf_op jit(solution)/shard_map/ppermute | solution.py:659
  16.8 5.2 %collective-permute-start.4 = (f32[2,8,2304]{2,1,0:T(8,128)S(1)}, f32[2,8,2304]{2,1,0:T(8,128)S(1)}, u32[]{:S(2)}, u32[]{:S(2)}) collective-permute-start(f32[2,8,2304]{2,1,0:T(8,128)S(1)} %relay.4), channel_id=1, source_target_pairs={{0,16},{4,12},{8,24},{12,4},{16,0},{20,28},{24,8},{28,20},{1,17},{... | collective-permute-start | bytes 442376 | tf_op jit(solution)/shard_map/ppermute | solution.py:659
  19.8 3.2 %copy-start = (f32[3,32,2048]{2,1,0:T(8,128)S(1)}, f32[3,32,2048]{2,1,0:T(8,128)}, u32[]{:S(2)}) copy-start(f32[3,32,2048]{2,1,0:T(8,128)} %velocity_ref.1) | copy-start | bytes 2359300
  25.8 12.7 %collective-permute-start.7 = (f32[11,16,2048]{2,1,0:T(8,128)S(1)}, f32[11,16,2048]{2,1,0:T(8,128)S(1)}, u32[]{:S(2)}, u32[]{:S(2)}) collective-permute-start(f32[11,16,2048]{2,1,0:T(8,128)S(1)} %get-tuple-element.53), channel_id=1, source_target_pairs={{0,4},{4,0},{8,12},{12,8},{16,20},{20,16},{24,28},{28,24},{1,5},{5... | collective-permute-start | bytes 4325384 | tf_op jit(solution)/shard_map/ppermute | solution.py:595
  25.8 5.0 %collective-permute-start.11 = (f32[2,8,2048]{2,1,0:T(8,128)S(1)}, f32[2,8,2048]{2,1,0:T(8,128)S(1)}, u32[]{:S(2)}, u32[]{:S(2)}) collective-permute-start(f32[2,8,2048]{2,1,0:T(8,128)S(1)} %get-tuple-element.58.mine.rest_0_), channel_id=1, source_target_pairs={{0,8},{4,20},{8,0},{12,28},{16,24},{20,4},{24,16},{28,12},{1,9},{5... | collective-permute-start | bytes 393224 | tf_op jit(solution)/shard_map/ppermute | solution.py:659
  27.7 5.2 %collective-permute-start.8 = (f32[2,8,2048]{2,1,0:T(8,128)S(1)}, f32[2,8,2048]{2,1,0:T(8,128)S(1)}, u32[]{:S(2)}, u32[]{:S(2)}) collective-permute-start(f32[2,8,2048]{2,1,0:T(8,128)S(1)} %get-tuple-element.55.mine.rest_0_), channel_id=1, source_target_pairs={{0,8},{4,20},{8,0},{12,28},{16,24},{20,4},{24,16},{28,12},{1,9},{5... | collective-permute-start | bytes 393224 | tf_op jit(solution)/shard_map/ppermute | solution.py:659
  31.0 5.0 %collective-permute-start.12 = (f32[2,8,2048]{2,1,0:T(8,128)S(1)}, f32[2,8,2048]{2,1,0:T(8,128)S(1)}, u32[]{:S(2)}, u32[]{:S(2)}) collective-permute-start(f32[2,8,2048]{2,1,0:T(8,128)S(1)} %relay.7), channel_id=1, source_target_pairs={{0,16},{4,12},{8,24},{12,4},{16,0},{20,28},{24,8},{28,20},{1,17},{... | collective-permute-start | bytes 393224 | tf_op jit(solution)/shard_map/ppermute | solution.py:659
  33.1 5.0 %collective-permute-start.9 = (f32[2,8,2048]{2,1,0:T(8,128)S(1)}, f32[2,8,2048]{2,1,0:T(8,128)S(1)}, u32[]{:S(2)}, u32[]{:S(2)}) collective-permute-start(f32[2,8,2048]{2,1,0:T(8,128)S(1)} %relay.6), channel_id=1, source_target_pairs={{0,16},{4,12},{8,24},{12,4},{16,0},{20,28},{24,8},{28,20},{1,17},{... | collective-permute-start | bytes 393224 | tf_op jit(solution)/shard_map/ppermute | solution.py:659
  36.3 2.2 %collective-permute-start.13 = (f32[2,8,2048]{2,1,0:T(8,128)S(1)}, f32[2,8,2048]{2,1,0:T(8,128)S(1)}, u32[]{:S(2)}, u32[]{:S(2)}) collective-permute-start(f32[2,8,2048]{2,1,0:T(8,128)S(1)} %get-tuple-element.61), channel_id=1, source_target_pairs={{0,4},{4,0},{8,12},{12,8},{16,20},{20,16},{24,28},{28,24},{1,5},{5... | collective-permute-start | bytes 393224 | tf_op jit(solution)/shard_map/ppermute | solution.py:595
  38.4 1.4 %collective-permute-start.10 = (f32[2,8,2048]{2,1,0:T(8,128)S(1)}, f32[2,8,2048]{2,1,0:T(8,128)S(1)}, u32[]{:S(2)}, u32[]{:S(2)}) collective-permute-start(f32[2,8,2048]{2,1,0:T(8,128)S(1)} %get-tuple-element.56), channel_id=1, source_target_pairs={{0,4},{4,0},{8,12},{12,8},{16,20},{20,16},{24,28},{28,24},{1,5},{5... | collective-permute-start | bytes 393224 | tf_op jit(solution)/shard_map/ppermute | solution.py:595

commit v7 on v6

--- a/solution.py
+++ b/solution.py
@@ -63,7 +63,6 @@
 OUTER, INNER = 0, 1
 MICROSECONDS = {
     'halves': 2,
-    'outermost': 0.3,
     'ends': 1,
     'relay': 0.2,
     'first_sweep': 1,
@@ -226,18 +225,19 @@
             one, other = [source[row : row + 1, lanes] for row in rows]
             target[group : group + 1, :] = jnp.where(core == 0, one, other)
 
-    copies[0].wait()
+    slab_copy, *tile_copies = copies
+    slab_copy.wait()
     last = depth - 1
     lay(slab, (0, last), edge.at[2 * steps_local])
     lay(slab, (1, last - 1), edge.at[2 * steps_local + 1])
     for slot, row in enumerate((0, half - 1, half, half + 1)):
         lay(slab, (row, last - row), layers.at[slot])
-    for copy in copies[1:]:
-        copy.wait()
     near, far = (0, half - 1), (half - 1, 0)
     beyond = pl.ds(cells, LANES)
-    for index in range(steps_local):
-        for field in range(2):
+    for field in range(2):
+        for copy in tile_copies[2 * field : 2 * field + 2]:
+            copy.wait()
+        for index in range(steps_local):
             slot = 2 * index + field
             lay(keep.at[field, index], near, edge.at[slot])
             lay(send.at[field, index], far, edge_send.at[slot])
@@ -245,14 +245,8 @@
             lay(keep.at[field, index], far, send.at[field, index, :, beyond])
 
 
-def join_kernel(edge, edge_other, swap, both, swap_out):
-    count = edge.shape[0]
-    both[:count] = edge[...]
-    both[count:] = edge_other[...]
-
-
 def ends_kernel(side, ratio, chips, keep, other, slab, layers, *rest):
-    cut = rest[0] if side == OUTER else None
+    cut, cut_straight = rest[:2] if side == OUTER else (None, None)
     raw_ref, factor_ref, ends_ref = rest[-3:]
     steps_local, half, cells = keep.shape[1:]
     cells = cells - LANES
@@ -304,8 +298,7 @@
 
     if side == OUTER:
         diagonal = layer_diagonal(cut[steps], layers[0], cut[steps + 1])
-        starts = (steps + 2, 0)
-        loads = lambda position, index, field: cut[starts[position] + 2 * index + field]
+        loads = lambda position, index, field: (cut_straight, cut)[position][2 * index + field]
     else:
         diagonal = layer_diagonal(layers[2], layers[1], layers[3])
         loads = lambda position, index, field: (keep, other)[position][field, index, :, cells:]
@@ -595,12 +588,21 @@
         return lax.ppermute(value, "tm", [(i, i ^ mask) for i in range(ranks)])
 
     def outward(value):
+        spare = (4, 2) if ranks % 8 == 0 else (0, 0)
         pairs = []
-        spare = (4, 2) if ranks % 8 == 0 else (0, 0)
         for t in range(ranks):
             for g in range(slabs):
                 to = g - 1 if t % 2 == 0 else g + 1
                 other = (t ^ 1) * slabs + to if 0 <= to < slabs else (t ^ spare[t % 2]) * slabs + g
+                pairs.append((t * slabs + g, other))
+        return lax.ppermute(value, ("tm", "gz"), pairs)
+
+    def onward(value):
+        pairs = []
+        for t in range(ranks):
+            for g in range(slabs):
+                to = g + 1 if t % 2 == 0 else g - 1
+                other = t * slabs + to if 0 <= to < slabs else (t ^ 1) * slabs + g
                 pairs.append((t * slabs + g, other))
         return lax.ppermute(value, ("tm", "gz"), pairs)
 
@@ -626,19 +628,9 @@
         in_specs=[anywhere] * 3,
         scratch_shapes=[pltpu.SemaphoreType.DMA((5,))],
     )
-    cut, send = call(
-        join_kernel,
-        "outermost_layer",
-        [(2 * steps + 2,) + layer, halves],
-        edge,
-        partner(edge_send, 1),
-        send,
-        in_specs=[vmem, vmem, anywhere],
-        out_specs=[vmem, anywhere],
-        input_output_aliases={2: 1},
-    )
     other = partner(send, 1)
-    cut = outward(cut)
+    cut = outward(edge)
+    cut_straight = onward(edge_send)
 
     def first_ends(side, *args):
         return call(
@@ -653,7 +645,7 @@
         )
 
     inner_raw, inner_factors, inner_ends = first_ends(INNER)
-    outer_raw, outer_factors, outer_ends = first_ends(OUTER, cut, inner_ends)
+    outer_raw, outer_factors, outer_ends = first_ends(OUTER, cut, cut_straight, inner_ends)
 
     def beside(value, masks):
         return lax.ppermute(value, "tm", [(i, i ^ masks[i % 2]) for i in range(ranks)])

time: 40.9 us -> 38.9 us (0.951)
  starting transfers between devices: 17.7 us -> 15.2 us
  waiting for transfers between devices: 11.1 us -> 11.7 us
    ppermute x8, starting transfers between devices: 13.9 us -> 11.8 us  [beside(): lax.ppermute(value, 'tm', [(i, i ^ masks[i % 2]) for i in range(ranks)])]
    ppermute x8, waiting for transfers between devices: 10.2 us -> 11.7 us  [beside(): lax.ppermute(value, 'tm', [(i, i ^ masks[i % 2]) for i in range(ranks)])]
    ppermute x5 -> x4, waiting for transfers between devices: 0.91 us -> 0.01 us  [partner(): return lax.ppermute(value, 'tm', [(i, i ^ mask) for i in range(ranks)])]
    ppermute x5 -> x4, starting transfers between devices: 1.15 us -> 0.73 us  [partner(): return lax.ppermute(value, 'tm', [(i, i ^ mask) for i in range(ranks)])]
    pallas_call x15 -> x14, Pallas kernels: 11.2 us -> 11.1 us  [call(): pl.pallas_call(kernel, out_shape=shapes, compiler_params=pltpu.CompilerPa...]
  transfers between devices with their start and end apart: 14 -> 14, of which waited for: 8 -> 7; matrix products, arithmetic and copies ran while one was open for 0% -> 0% of each run, Pallas kernels for 12% -> 12%
where the time goes in v7:
time: 38.9 us; the launch traced here: 38.8 us
  starting transfers between devices  15.2 us (39%)
  waiting for transfers between devices  11.7 us (30%)
  Pallas kernels  11.1 us (29%)
  between operations  0.79 us (2%)
    ppermute x8, starting transfers between devices, beside(): lax.ppermute(value, 'tm', [(i, i ^ masks[i % 2]) for i in range(ranks)])  11.8 us
    ppermute x8, waiting for transfers between devices, beside(): lax.ppermute(value, 'tm', [(i, i ^ masks[i % 2]) for i in range(ranks)])  11.7 us
    pallas_call x14, Pallas kernels, call(): pl.pallas_call(kernel, out_shape=shapes, compiler_params=pltpu.CompilerPa...  11.1 us
    ppermute x1, starting transfers between devices, outward(): return lax.ppermute(value, ('tm', 'gz'), pairs)  2.59 us
  transfers between devices with their start and end apart: 14, of which 7 were waited for; matrix products, arithmetic and copies ran while one was open for 0% of the time, Pallas kernels for 12%

profile of v7, /device:TPU:0, one launch (start us, length us, event | category | flops | bytes accessed | tf_op | source)
XLA Modules:
  0.0 38.8 jit_solution(10309654072051433387)
XLA Ops:
  0.6 1.7 %halves_and_layers.1 = (f32[2,4,16,2176]{3,2,1,0:T(8,128)S(1)}, f32[2,4,16,2176]{3,2,1,0:T(8,128)S(1)}, f32[32,2048]{1,0:T(8,128)S(1)}, f32[10,16,128]{2,1,0:T(8...) custom-call(f32[4,32,2048]{2,1,0:T(8,128)} %state.1, f32[4,32,2048]{2,1,0:T(8,128)} %adjoint.1, ...), custom_call_target="tpu_custom_call" | custom-call | bytes 7400000 | tf_op jit(solution)/shard_map/halves_and_layers/pallas_call | solution.py:612
  2.4 0.5 %collective-permute-start.1 = (f32[2,4,16,2176]{3,2,1,0:T(8,128)S(1)}, f32[2,4,16,2176]{3,2,1,0:T(8,128)S(1)}, u32[]{:S(2)}, u32[]{:S(2)}) collective-permute-start(f32[2,4,16,2176]{3,2,1,0:T(8,128)S(1)} %get-tuple-element.34), channel_id=1, source_target_pairs={{0,4},{4,0},{8,12},{12,8},{16,20},{20,16},{24,28},{28,24},{1,5},{5... | collective-permute-start | bytes 3342344 | tf_op jit(solution)/shard_map/ppermute | solution.py:588
  2.9 2.6 %collective-permute-start = (f32[10,16,128]{2,1,0:T(8,128)S(1)}, f32[10,16,128]{2,1,0:T(8,128)S(1)}, u32[]{:S(2)}, u32[]{:S(2)}) collective-permute-start(f32[10,16,128]{2,1,0:T(8,128)S(1)} %get-tuple-element.32), channel_id=1, source_target_pairs={{0,16},{1,4},{2,5},{3,6},{4,1},{5,2},{6,3},{7,15},{8,24},{9,12},{1... | collective-permute-start | bytes 245768 | tf_op jit(solution)/shard_map/ppermute | solution.py:598
  5.5 0.1 collective-permute-start.2
  5.6 0.7 %inner_ends.1 = (f32[16,8,2304]{2,1,0:T(8,128)S(1)}, f32[4,8,2304]{2,1,0:T(8,128)S(1)}, f32[2,8,2304]{2,1,0:T(8,128)S(1)}) custom-call(f32[2,4,16,2176]{3,2,1,0:T(8,128)S(1)} %get-tuple-element.33.keep, f32[2,4,16,2176]{3,2,1,0:T(8,128)S(1)} %collective-permute-done.1.other, f32[32,2048]{1,0:T(8,128)S(1)} %get-tuple-element.31.slab, ...), custom_call_target="tpu_custom_call" | custom-call | bytes 3700000 | tf_op jit(solution)/shard_map/inner_ends/pallas_call | solution.py:612
  6.3 2.6 %collective-permute-start.5 = (f32[2,8,2304]{2,1,0:T(8,128)S(1)}, f32[2,8,2304]{2,1,0:T(8,128)S(1)}, u32[]{:S(2)}, u32[]{:S(2)}) collective-permute-start(f32[2,8,2304]{2,1,0:T(8,128)S(1)} %get-tuple-element.37.rest_2_.mine.rest_0_), channel_id=1, source_target_pairs={{0,8},{4,20},{8,0},{12,28},{16,24},{20,4},{24,16},{28,12},{1,9},{5... | collective-permute-start | bytes 442376 | tf_op jit(solution)/shard_map/ppermute | solution.py:651
  8.9 0.7 %outer_ends.1 = (f32[16,8,2304]{2,1,0:T(8,128)S(1)}, f32[4,8,2304]{2,1,0:T(8,128)S(1)}, f32[2,8,2304]{2,1,0:T(8,128)S(1)}) custom-call(f32[2,4,16,2176]{3,2,1,0:T(8,128)S(1)} %get-tuple-element.33.keep, f32[2,4,16,2176]{3,2,1,0:T(8,128)S(1)} %collective-permute-done.1.other, f32[32,2048]{1,0:T(8,128)S(1)} %get-tuple-element.31.slab, ...), custom_call_target="tpu_custom_call" | custom-call | bytes 3700000 | tf_op jit(solution)/shard_map/outer_ends/pallas_call | solution.py:612
  9.7 1.1 %collective-permute-start.3 = (f32[2,8,2304]{2,1,0:T(8,128)S(1)}, f32[2,8,2304]{2,1,0:T(8,128)S(1)}, u32[]{:S(2)}, u32[]{:S(2)}) collective-permute-start(f32[2,8,2304]{2,1,0:T(8,128)S(1)} %get-tuple-element.40.mine.rest_0_), channel_id=1, source_target_pairs={{0,8},{4,20},{8,0},{12,28},{16,24},{20,4},{24,16},{28,12},{1,9},{5... | collective-permute-start | bytes 442376 | tf_op jit(solution)/shard_map/ppermute | solution.py:651
  10.7 1.3 %collective-permute-done.5.theirs.rest_1_ = f32[2,8,2304]{2,1,0:T(8,128)S(1)} collective-permute-done((f32[2,8,2304]{2,1,0:T(8,128)S(1)}, f32[2,8,2304]{2,1,0:T(8,128)S(1)}, u32[]{:S(2)}, u32[]{:S(2)}) %collective-permute-start.5) | collective-permute-done | bytes 147488 | tf_op jit(solution)/shard_map/ppermute | solution.py:651
  12.0 0.2 relay.5
  12.2 2.1 %collective-permute-start.6 = (f32[2,8,2304]{2,1,0:T(8,128)S(1)}, f32[2,8,2304]{2,1,0:T(8,128)S(1)}, u32[]{:S(2)}, u32[]{:S(2)}) collective-permute-start(f32[2,8,2304]{2,1,0:T(8,128)S(1)} %relay.5), channel_id=1, source_target_pairs={{0,16},{4,12},{8,24},{12,4},{16,0},{20,28},{24,8},{28,20},{1,17},{... | collective-permute-start | bytes 442376 | tf_op jit(solution)/shard_map/ppermute | solution.py:651
  14.3 0.9 %collective-permute-done.3.theirs.rest_1_ = f32[2,8,2304]{2,1,0:T(8,128)S(1)} collective-permute-done((f32[2,8,2304]{2,1,0:T(8,128)S(1)}, f32[2,8,2304]{2,1,0:T(8,128)S(1)}, u32[]{:S(2)}, u32[]{:S(2)}) %collective-permute-start.3) | collective-permute-done | bytes 147488 | tf_op jit(solution)/shard_map/ppermute | solution.py:651
  15.3 0.2 relay.4
  15.4 1.3 %collective-permute-start.4 = (f32[2,8,2304]{2,1,0:T(8,128)S(1)}, f32[2,8,2304]{2,1,0:T(8,128)S(1)}, u32[]{:S(2)}, u32[]{:S(2)}) collective-permute-start(f32[2,8,2304]{2,1,0:T(8,128)S(1)} %relay.4), channel_id=1, source_target_pairs={{0,16},{4,12},{8,24},{12,4},{16,0},{20,28},{24,8},{28,20},{1,17},{... | collective-permute-start | bytes 442376 | tf_op jit(solution)/shard_map/ppermute | solution.py:651
  16.8 0.7 %collective-permute-done.6.rest_2_ = f32[2,8,2304]{2,1,0:T(8,128)S(1)} collective-permute-done((f32[2,8,2304]{2,1,0:T(8,128)S(1)}, f32[2,8,2304]{2,1,0:T(8,128)S(1)}, u32[]{:S(2)}, u32[]{:S(2)}) %collective-permute-start.6) | collective-permute-done | bytes 147488 | tf_op jit(solution)/shard_map/ppermute | solution.py:651
  17.4 0.9 %inner_first_sweep.1 = (f32[16,8,2048]{2,1,0:T(8,128)S(1)}, f32[16,8,2048]{2,1,0:T(8,128)S(1)}, f32[16,16,128]{2,1,0:T(8,128)S(1)}) custom-call(f32[16,8,2304]{2,1,0:T(8,128)S(1)} %get-tuple-element.44.raw_ref, f32[4,8,2304]{2,1,0:T(8,128)S(1)} %get-tuple-element.45.factor_ref.refs_7_.refs_5_.refs_2_, ...), custom_call_target="tpu_custom_call" | custom-call | bytes 3700000 | tf_op jit(solution)/shard_map/inner_first_sweep/pallas_call | solution.py:612
  18.4 2.3 %collective-permute-done.4.rest_2_ = f32[2,8,2304]{2,1,0:T(8,128)S(1)} collective-permute-done((f32[2,8,2304]{2,1,0:T(8,128)S(1)}, f32[2,8,2304]{2,1,0:T(8,128)S(1)}, u32[]{:S(2)}, u32[]{:S(2)}) %collective-permute-start.4) | collective-permute-done | bytes 147488 | tf_op jit(solution)/shard_map/ppermute | solution.py:651
  20.7 0.9 %outer_first_sweep.1 = (f32[16,8,2048]{2,1,0:T(8,128)S(1)}, f32[16,8,2048]{2,1,0:T(8,128)S(1)}, f32[16,16,128]{2,1,0:T(8,128)S(1)}) custom-call(f32[16,8,2304]{2,1,0:T(8,128)S(1)} %get-tuple-element.38.raw_ref, f32[4,8,2304]{2,1,0:T(8,128)S(1)} %get-tuple-element.39.factor_ref.refs_3_.refs_2_.refs_8_, f32[2,8,2304]{2,1,0:T(8,128)S(1)} %get-tuple-element.40.mine.rest_0_, ...), custom_call_target="tpu_custom_call" | custom-call | bytes 3700000 | tf_op jit(solution)/shard_map/outer_first_sweep/pallas_call | solution.py:612
  21.6 2.8 %couplings.1 = (f32[8,16,2048]{2,1,0:T(8,128)S(1)}, f32[11,16,2048]{2,1,0:T(8,128)S(1)}, f32[2,16,2048]{2,1,0:T(8,128)S(1)}, f32[2,8,2048]{2,1,0:T(8,128)S(1)}, f32[2,8,2048]{2,1,0:T(8,128)S(1)}) custom-call(f32[32,2048]{1,0:T(8,128)S(1)} %get-tuple-element.31.slab, f32[3,32,2048]{2,1,0:T(8,128)S(1)} %copy-done, ...), custom_call_target="tpu_custom_call" | custom-call | bytes 11100000 | tf_op jit(solution)/shard_map/couplings/pallas_call | solution.py:612
  24.4 0.7 %collective-permute-start.11 = (f32[2,8,2048]{2,1,0:T(8,128)S(1)}, f32[2,8,2048]{2,1,0:T(8,128)S(1)}, u32[]{:S(2)}, u32[]{:S(2)}) collective-permute-start(f32[2,8,2048]{2,1,0:T(8,128)S(1)} %get-tuple-element.54.mine.rest_0_), channel_id=1, source_target_pairs={{0,8},{4,20},{8,0},{12,28},{16,24},{20,4},{24,16},{28,12},{1,9},{5... | collective-permute-start | bytes 393224 | tf_op jit(solution)/shard_map/ppermute | solution.py:651
  25.1 1.4 %collective-permute-start.8 = (f32[2,8,2048]{2,1,0:T(8,128)S(1)}, f32[2,8,2048]{2,1,0:T(8,128)S(1)}, u32[]{:S(2)}, u32[]{:S(2)}) collective-permute-start(f32[2,8,2048]{2,1,0:T(8,128)S(1)} %get-tuple-element.51.mine.rest_0_), channel_id=1, source_target_pairs={{0,8},{4,20},{8,0},{12,28},{16,24},{20,4},{24,16},{28,12},{1,9},{5... | collective-permute-start | bytes 393224 | tf_op jit(solution)/shard_map/ppermute | solution.py:651
  26.5 2.9 %collective-permute-done.11.theirs.rest_1_ = f32[2,8,2048]{2,1,0:T(8,128)S(1)} collective-permute-done((f32[2,8,2048]{2,1,0:T(8,128)S(1)}, f32[2,8,2048]{2,1,0:T(8,128)S(1)}, u32[]{:S(2)}, u32[]{:S(2)}) %collective-permute-start.11) | collective-permute-done | bytes 131104 | tf_op jit(solution)/shard_map/ppermute | solution.py:651
  29.5 0.2 relay.7
  29.6 1.3 %collective-permute-start.12 = (f32[2,8,2048]{2,1,0:T(8,128)S(1)}, f32[2,8,2048]{2,1,0:T(8,128)S(1)}, u32[]{:S(2)}, u32[]{:S(2)}) collective-permute-start(f32[2,8,2048]{2,1,0:T(8,128)S(1)} %relay.7), channel_id=1, source_target_pairs={{0,16},{4,12},{8,24},{12,4},{16,0},{20,28},{24,8},{28,20},{1,17},{... | collective-permute-start | bytes 393224 | tf_op jit(solution)/shard_map/ppermute | solution.py:651
  31.0 0.2 relay.6
  31.1 1.2 %collective-permute-start.9 = (f32[2,8,2048]{2,1,0:T(8,128)S(1)}, f32[2,8,2048]{2,1,0:T(8,128)S(1)}, u32[]{:S(2)}, u32[]{:S(2)}) collective-permute-start(f32[2,8,2048]{2,1,0:T(8,128)S(1)} %relay.6), channel_id=1, source_target_pairs={{0,16},{4,12},{8,24},{12,4},{16,0},{20,28},{24,8},{28,20},{1,17},{... | collective-permute-start | bytes 393224 | tf_op jit(solution)/shard_map/ppermute | solution.py:651
  32.4 2.3 %collective-permute-done.12.rest_2_ = f32[2,8,2048]{2,1,0:T(8,128)S(1)} collective-permute-done((f32[2,8,2048]{2,1,0:T(8,128)S(1)}, f32[2,8,2048]{2,1,0:T(8,128)S(1)}, u32[]{:S(2)}, u32[]{:S(2)}) %collective-permute-start.12) | collective-permute-done | bytes 131104 | tf_op jit(solution)/shard_map/ppermute | solution.py:651
  34.7 0.2 outer_entering.1
  34.9 1.2 %collective-permute-done.9.rest_2_ = f32[2,8,2048]{2,1,0:T(8,128)S(1)} collective-permute-done((f32[2,8,2048]{2,1,0:T(8,128)S(1)}, f32[2,8,2048]{2,1,0:T(8,128)S(1)}, u32[]{:S(2)}, u32[]{:S(2)}) %collective-permute-start.9) | collective-permute-done | bytes 131104 | tf_op jit(solution)/shard_map/ppermute | solution.py:651
  36.2 0.2 inner_entering.1
  36.5 1.3 %finish.2 = (f32[4,32,2048]{2,1,0:T(8,128)}, f32[4,32,2048]{2,1,0:T(8,128)}) custom-call(f32[8,16,2048]{2,1,0:T(8,128)S(1)} %get-tuple-element.53.refs_0_.refs_3_, f32[2,8,2048]{2,1,0:T(8,128)S(1)} %get-tuple-element.55.refs_1_, f32[4,8,2304]{2,1,0:T(8,128)S(1)} %get-tuple-element.39.factor_ref.refs_3_.refs_2_.refs_8_, ...), custom_call_target="tpu_custom_call" | custom-call | bytes 3700000 | tf_op jit(solution)/shard_map/finish/pallas_call | solution.py:612
  37.8 0.9 %finish.3 = (f32[4,32,2048]{2,1,0:T(8,128)}, f32[4,32,2048]{2,1,0:T(8,128)}) custom-call(f32[11,16,2048]{2,1,0:T(8,128)S(1)} %collective-permute-done.7.refs_6_.refs_0_, f32[2,8,2048]{2,1,0:T(8,128)S(1)} %collective-permute-done.10.refs_1_, ...), custom_call_target="tpu_custom_call", output_to_operand_aliasing={{0}: (3, {}), {1}: (4, {})} | custom-call | bytes 3700000 | tf_op jit(solution)/shard_map/finish/pallas_call | solution.py:612
  (12 shorter events, 0.2 us)
Async XLA Ops:
  2.4 3.2 %collective-permute-start.1 = (f32[2,4,16,2176]{3,2,1,0:T(8,128)S(1)}, f32[2,4,16,2176]{3,2,1,0:T(8,128)S(1)}, u32[]{:S(2)}, u32[]{:S(2)}) collective-permute-start(f32[2,4,16,2176]{3,2,1,0:T(8,128)S(1)} %get-tuple-element.34), channel_id=1, source_target_pairs={{0,4},{4,0},{8,12},{12,8},{16,20},{20,16},{24,28},{28,24},{1,5},{5... | collective-permute-start | bytes 3342344 | tf_op jit(solution)/shard_map/ppermute | solution.py:588
  2.9 6.0 %collective-permute-start = (f32[10,16,128]{2,1,0:T(8,128)S(1)}, f32[10,16,128]{2,1,0:T(8,128)S(1)}, u32[]{:S(2)}, u32[]{:S(2)}) collective-permute-start(f32[10,16,128]{2,1,0:T(8,128)S(1)} %get-tuple-element.32), channel_id=1, source_target_pairs={{0,16},{1,4},{2,5},{3,6},{4,1},{5,2},{6,3},{7,15},{8,24},{9,12},{1... | collective-permute-start | bytes 245768 | tf_op jit(solution)/shard_map/ppermute | solution.py:598
  5.5 3.4 %collective-permute-start.2 = (f32[8,16,128]{2,1,0:T(8,128)S(1)}, f32[8,16,128]{2,1,0:T(8,128)S(1)}, u32[]{:S(2)}, u32[]{:S(2)}) collective-permute-start(f32[8,16,128]{2,1,0:T(8,128)S(1)} %get-tuple-element.36), channel_id=1, source_target_pairs={{0,1},{1,2},{2,3},{3,7},{4,0},{5,4},{6,5},{7,6},{8,9},{9,10},{10,1... | collective-permute-start | bytes 196616 | tf_op jit(solution)/shard_map/ppermute | solution.py:607
  6.3 5.7 %collective-permute-start.5 = (f32[2,8,2304]{2,1,0:T(8,128)S(1)}, f32[2,8,2304]{2,1,0:T(8,128)S(1)}, u32[]{:S(2)}, u32[]{:S(2)}) collective-permute-start(f32[2,8,2304]{2,1,0:T(8,128)S(1)} %get-tuple-element.37.rest_2_.mine.rest_0_), channel_id=1, source_target_pairs={{0,8},{4,20},{8,0},{12,28},{16,24},{20,4},{24,16},{28,12},{1,9},{5... | collective-permute-start | bytes 442376 | tf_op jit(solution)/shard_map/ppermute | solution.py:651
  9.7 5.6 %collective-permute-start.3 = (f32[2,8,2304]{2,1,0:T(8,128)S(1)}, f32[2,8,2304]{2,1,0:T(8,128)S(1)}, u32[]{:S(2)}, u32[]{:S(2)}) collective-permute-start(f32[2,8,2304]{2,1,0:T(8,128)S(1)} %get-tuple-element.40.mine.rest_0_), channel_id=1, source_target_pairs={{0,8},{4,20},{8,0},{12,28},{16,24},{20,4},{24,16},{28,12},{1,9},{5... | collective-permute-start | bytes 442376 | tf_op jit(solution)/shard_map/ppermute | solution.py:651
  12.2 5.2 %collective-permute-start.6 = (f32[2,8,2304]{2,1,0:T(8,128)S(1)}, f32[2,8,2304]{2,1,0:T(8,128)S(1)}, u32[]{:S(2)}, u32[]{:S(2)}) collective-permute-start(f32[2,8,2304]{2,1,0:T(8,128)S(1)} %relay.5), channel_id=1, source_target_pairs={{0,16},{4,12},{8,24},{12,4},{16,0},{20,28},{24,8},{28,20},{1,17},{... | collective-permute-start | bytes 442376 | tf_op jit(solution)/shard_map/ppermute | solution.py:651
  15.4 5.2 %collective-permute-start.4 = (f32[2,8,2304]{2,1,0:T(8,128)S(1)}, f32[2,8,2304]{2,1,0:T(8,128)S(1)}, u32[]{:S(2)}, u32[]{:S(2)}) collective-permute-start(f32[2,8,2304]{2,1,0:T(8,128)S(1)} %relay.4), channel_id=1, source_target_pairs={{0,16},{4,12},{8,24},{12,4},{16,0},{20,28},{24,8},{28,20},{1,17},{... | collective-permute-start | bytes 442376 | tf_op jit(solution)/shard_map/ppermute | solution.py:651
  18.4 3.2 %copy-start = (f32[3,32,2048]{2,1,0:T(8,128)S(1)}, f32[3,32,2048]{2,1,0:T(8,128)}, u32[]{:S(2)}) copy-start(f32[3,32,2048]{2,1,0:T(8,128)} %velocity_ref.1) | copy-start | bytes 2359300
  24.4 12.1 %collective-permute-start.7 = (f32[11,16,2048]{2,1,0:T(8,128)S(1)}, f32[11,16,2048]{2,1,0:T(8,128)S(1)}, u32[]{:S(2)}, u32[]{:S(2)}) collective-permute-start(f32[11,16,2048]{2,1,0:T(8,128)S(1)} %get-tuple-element.49), channel_id=1, source_target_pairs={{0,4},{4,0},{8,12},{12,8},{16,20},{20,16},{24,28},{28,24},{1,5},{5... | collective-permute-start | bytes 4325384 | tf_op jit(solution)/shard_map/ppermute | solution.py:588
  24.4 5.0 %collective-permute-start.11 = (f32[2,8,2048]{2,1,0:T(8,128)S(1)}, f32[2,8,2048]{2,1,0:T(8,128)S(1)}, u32[]{:S(2)}, u32[]{:S(2)}) collective-permute-start(f32[2,8,2048]{2,1,0:T(8,128)S(1)} %get-tuple-element.54.mine.rest_0_), channel_id=1, source_target_pairs={{0,8},{4,20},{8,0},{12,28},{16,24},{20,4},{24,16},{28,12},{1,9},{5... | collective-permute-start | bytes 393224 | tf_op jit(solution)/shard_map/ppermute | solution.py:651
  25.1 5.9 %collective-permute-start.8 = (f32[2,8,2048]{2,1,0:T(8,128)S(1)}, f32[2,8,2048]{2,1,0:T(8,128)S(1)}, u32[]{:S(2)}, u32[]{:S(2)}) collective-permute-start(f32[2,8,2048]{2,1,0:T(8,128)S(1)} %get-tuple-element.51.mine.rest_0_), channel_id=1, source_target_pairs={{0,8},{4,20},{8,0},{12,28},{16,24},{20,4},{24,16},{28,12},{1,9},{5... | collective-permute-start | bytes 393224 | tf_op jit(solution)/shard_map/ppermute | solution.py:651
  29.6 5.0 %collective-permute-start.12 = (f32[2,8,2048]{2,1,0:T(8,128)S(1)}, f32[2,8,2048]{2,1,0:T(8,128)S(1)}, u32[]{:S(2)}, u32[]{:S(2)}) collective-permute-start(f32[2,8,2048]{2,1,0:T(8,128)S(1)} %relay.7), channel_id=1, source_target_pairs={{0,16},{4,12},{8,24},{12,4},{16,0},{20,28},{24,8},{28,20},{1,17},{... | collective-permute-start | bytes 393224 | tf_op jit(solution)/shard_map/ppermute | solution.py:651
  31.1 5.0 %collective-permute-start.9 = (f32[2,8,2048]{2,1,0:T(8,128)S(1)}, f32[2,8,2048]{2,1,0:T(8,128)S(1)}, u32[]{:S(2)}, u32[]{:S(2)}) collective-permute-start(f32[2,8,2048]{2,1,0:T(8,128)S(1)} %relay.6), channel_id=1, source_target_pairs={{0,16},{4,12},{8,24},{12,4},{16,0},{20,28},{24,8},{28,20},{1,17},{... | collective-permute-start | bytes 393224 | tf_op jit(solution)/shard_map/ppermute | solution.py:651
  34.9 1.6 %collective-permute-start.13 = (f32[2,8,2048]{2,1,0:T(8,128)S(1)}, f32[2,8,2048]{2,1,0:T(8,128)S(1)}, u32[]{:S(2)}, u32[]{:S(2)}) collective-permute-start(f32[2,8,2048]{2,1,0:T(8,128)S(1)} %get-tuple-element.57), channel_id=1, source_target_pairs={{0,4},{4,0},{8,12},{12,8},{16,20},{20,16},{24,28},{28,24},{1,5},{5... | collective-permute-start | bytes 393224 | tf_op jit(solution)/shard_map/ppermute | solution.py:588
  36.4 1.4 %collective-permute-start.10 = (f32[2,8,2048]{2,1,0:T(8,128)S(1)}, f32[2,8,2048]{2,1,0:T(8,128)S(1)}, u32[]{:S(2)}, u32[]{:S(2)}) collective-permute-start(f32[2,8,2048]{2,1,0:T(8,128)S(1)} %get-tuple-element.52), channel_id=1, source_target_pairs={{0,4},{4,0},{8,12},{12,8},{16,20},{20,16},{24,28},{28,24},{1,5},{5... | collective-permute-start | bytes 393224 | tf_op jit(solution)/shard_map/ppermute | solution.py:588

commit v8 on v7

--- a/solution.py
+++ b/solution.py
@@ -28,14 +28,9 @@
     return pl.ds(pl.multiple_of(start, LANES), width)
 
 
-def each_block(cells, width, work):
-    def one(index, carry):
-        work(lane_block(index * width, width))
-        return carry
-
-    lax.fori_loop(0, cells // width, one, 0)
-    if cells % width:
-        work(slice(cells - cells % width, cells))
+def each_block(cells, width, work, first=0):
+    for start in range(0, cells, width):
+        work(slice(first + start, first + min(start + width, cells)))
 
 
 def power(value, count):
@@ -61,6 +56,7 @@
 
 
 OUTER, INNER = 0, 1
+PIECES = 2
 MICROSECONDS = {
     'halves': 2,
     'ends': 1,
@@ -70,8 +66,8 @@
     'entering': 0.2,
     'finish': 1,
 }
-UNROLL_ENDS = 8
-UNROLL_COUPLINGS = 4
+UNROLL_ENDS = 16
+UNROLL_COUPLINGS = 16
 
 
 def tile_rows(side, half, depth):
@@ -361,7 +357,7 @@
         passed[0, :, here] = a[0] + b[0]
         passed[1, :, here] = a[1] + b[1]
 
-    each_block(mine.shape[2], 4 * LANES, one)
+    each_block(mine.shape[2], 3 * LANES, one)
 
 
 def entering(factors, ends, here, steps):
@@ -559,10 +555,17 @@
                 result[job, 1, step, :, here] = (parts[2 * step + 1, held, here] + adjoint) * scales[step]
                 previous = current
 
-        each_block(cells, 4 * LANES, one)
-        for field, out in enumerate((state_out, adjoint_out)):
-            copies.append(pltpu.make_async_copy(result.at[job, field], out.at[:, rows, :], sems.at[job, field]))
-            copies[-1].start()
+        for piece in range(PIECES):
+            first = piece * (cells // PIECES)
+            each_block(cells // PIECES, 4 * LANES, one, first)
+            lanes = pl.ds(first, cells // PIECES)
+            for field, out in enumerate((state_out, adjoint_out)):
+                copies.append(
+                    pltpu.make_async_copy(
+                        result.at[job, field, :, :, lanes], out.at[:, rows, lanes], sems.at[job, field, piece]
+                    )
+                )
+                copies[-1].start()
     for copy in copies:
         copy.wait()
 
@@ -742,7 +745,7 @@
             out_specs=[anywhere] * 2,
             scratch_shapes=[
                 pltpu.VMEM((len(jobs), 2, steps_local, tile, cells), f32),
-                pltpu.SemaphoreType.DMA((len(jobs), 2)),
+                pltpu.SemaphoreType.DMA((len(jobs), 2, PIECES)),
             ],
             input_output_aliases={len(args) + i: i for i in range(len(results))},
         )

time: 38.9 us -> 37.1 us (0.954)
  Pallas kernels: 11.1 us -> 8.89 us
    pallas_call x14, Pallas kernels: 11.1 us -> 8.89 us  [call(): pl.pallas_call(kernel, out_shape=shapes, compiler_params=pltpu.CompilerPa...]
  transfers between devices with their start and end apart: 14 -> 14, of which waited for: 7 -> 7; matrix products, arithmetic and copies ran while one was open for 0% -> 0% of each run, Pallas kernels for 12% -> 10%
where the time goes in v8:
time: 37.1 us; the launch traced here: 36.9 us
  starting transfers between devices  15.5 us (42%)
  waiting for transfers between devices  11.7 us (32%)
  Pallas kernels  8.89 us (24%)
  between operations  0.74 us (2%)
    ppermute x8, starting transfers between devices, beside(): lax.ppermute(value, 'tm', [(i, i ^ masks[i % 2]) for i in range(ranks)])  12.1 us
    ppermute x8, waiting for transfers between devices, beside(): lax.ppermute(value, 'tm', [(i, i ^ masks[i % 2]) for i in range(ranks)])  11.7 us
    pallas_call x14, Pallas kernels, call(): pl.pallas_call(kernel, out_shape=shapes, compiler_params=pltpu.CompilerPa...  8.89 us
    ppermute x1, starting transfers between devices, outward(): return lax.ppermute(value, ('tm', 'gz'), pairs)  2.59 us
  transfers between devices with their start and end apart: 14, of which 7 were waited for; matrix products, arithmetic and copies ran while one was open for 0% of the time, Pallas kernels for 10%

profile of v8, /device:TPU:0, one launch (start us, length us, event | category | flops | bytes accessed | tf_op | source)
XLA Modules:
  0.0 36.9 jit_solution(4268131329326230235)
XLA Ops:
  0.6 1.7 %halves_and_layers.1 = (f32[2,4,16,2176]{3,2,1,0:T(8,128)S(1)}, f32[2,4,16,2176]{3,2,1,0:T(8,128)S(1)}, f32[32,2048]{1,0:T(8,128)S(1)}, f32[10,16,128]{2,1,0:T(8...) custom-call(f32[4,32,2048]{2,1,0:T(8,128)} %state.1, f32[4,32,2048]{2,1,0:T(8,128)} %adjoint.1, ...), custom_call_target="tpu_custom_call" | custom-call | bytes 7400000 | tf_op jit(solution)/shard_map/halves_and_layers/pallas_call | solution.py:615
  2.4 0.5 %collective-permute-start.1 = (f32[2,4,16,2176]{3,2,1,0:T(8,128)S(1)}, f32[2,4,16,2176]{3,2,1,0:T(8,128)S(1)}, u32[]{:S(2)}, u32[]{:S(2)}) collective-permute-start(f32[2,4,16,2176]{3,2,1,0:T(8,128)S(1)} %get-tuple-element.34), channel_id=1, source_target_pairs={{0,4},{4,0},{8,12},{12,8},{16,20},{20,16},{24,28},{28,24},{1,5},{5... | collective-permute-start | bytes 3342344 | tf_op jit(solution)/shard_map/ppermute | solution.py:591
  2.9 2.6 %collective-permute-start = (f32[10,16,128]{2,1,0:T(8,128)S(1)}, f32[10,16,128]{2,1,0:T(8,128)S(1)}, u32[]{:S(2)}, u32[]{:S(2)}) collective-permute-start(f32[10,16,128]{2,1,0:T(8,128)S(1)} %get-tuple-element.32), channel_id=1, source_target_pairs={{0,16},{1,4},{2,5},{3,6},{4,1},{5,2},{6,3},{7,15},{8,24},{9,12},{1... | collective-permute-start | bytes 245768 | tf_op jit(solution)/shard_map/ppermute | solution.py:601
  5.5 0.1 collective-permute-start.2
  5.6 0.5 %inner_ends.1 = (f32[16,8,2304]{2,1,0:T(8,128)S(1)}, f32[4,8,2304]{2,1,0:T(8,128)S(1)}, f32[2,8,2304]{2,1,0:T(8,128)S(1)}) custom-call(f32[2,4,16,2176]{3,2,1,0:T(8,128)S(1)} %get-tuple-element.33.keep, f32[2,4,16,2176]{3,2,1,0:T(8,128)S(1)} %collective-permute-done.1.other, f32[32,2048]{1,0:T(8,128)S(1)} %get-tuple-element.31.slab, ...), custom_call_target="tpu_custom_call" | custom-call | bytes 3700000 | tf_op jit(solution)/shard_map/inner_ends/pallas_call | solution.py:615
  6.1 2.6 %collective-permute-start.5 = (f32[2,8,2304]{2,1,0:T(8,128)S(1)}, f32[2,8,2304]{2,1,0:T(8,128)S(1)}, u32[]{:S(2)}, u32[]{:S(2)}) collective-permute-start(f32[2,8,2304]{2,1,0:T(8,128)S(1)} %get-tuple-element.37.rest_2_.mine.rest_0_), channel_id=1, source_target_pairs={{0,8},{4,20},{8,0},{12,28},{16,24},{20,4},{24,16},{28,12},{1,9},{5... | collective-permute-start | bytes 442376 | tf_op jit(solution)/shard_map/ppermute | solution.py:654
  8.7 0.5 %outer_ends.1 = (f32[16,8,2304]{2,1,0:T(8,128)S(1)}, f32[4,8,2304]{2,1,0:T(8,128)S(1)}, f32[2,8,2304]{2,1,0:T(8,128)S(1)}) custom-call(f32[2,4,16,2176]{3,2,1,0:T(8,128)S(1)} %get-tuple-element.33.keep, f32[2,4,16,2176]{3,2,1,0:T(8,128)S(1)} %collective-permute-done.1.other, f32[32,2048]{1,0:T(8,128)S(1)} %get-tuple-element.31.slab, ...), custom_call_target="tpu_custom_call" | custom-call | bytes 3700000 | tf_op jit(solution)/shard_map/outer_ends/pallas_call | solution.py:615
  9.3 1.2 %collective-permute-start.3 = (f32[2,8,2304]{2,1,0:T(8,128)S(1)}, f32[2,8,2304]{2,1,0:T(8,128)S(1)}, u32[]{:S(2)}, u32[]{:S(2)}) collective-permute-start(f32[2,8,2304]{2,1,0:T(8,128)S(1)} %get-tuple-element.40.mine.rest_0_), channel_id=1, source_target_pairs={{0,8},{4,20},{8,0},{12,28},{16,24},{20,4},{24,16},{28,12},{1,9},{5... | collective-permute-start | bytes 442376 | tf_op jit(solution)/shard_map/ppermute | solution.py:654
  10.5 1.4 %collective-permute-done.5.theirs.rest_1_ = f32[2,8,2304]{2,1,0:T(8,128)S(1)} collective-permute-done((f32[2,8,2304]{2,1,0:T(8,128)S(1)}, f32[2,8,2304]{2,1,0:T(8,128)S(1)}, u32[]{:S(2)}, u32[]{:S(2)}) %collective-permute-start.5) | collective-permute-done | bytes 147488 | tf_op jit(solution)/shard_map/ppermute | solution.py:654
  11.9 0.1 relay.5
  12.0 2.1 %collective-permute-start.6 = (f32[2,8,2304]{2,1,0:T(8,128)S(1)}, f32[2,8,2304]{2,1,0:T(8,128)S(1)}, u32[]{:S(2)}, u32[]{:S(2)}) collective-permute-start(f32[2,8,2304]{2,1,0:T(8,128)S(1)} %relay.5), channel_id=1, source_target_pairs={{0,16},{4,12},{8,24},{12,4},{16,0},{20,28},{24,8},{28,20},{1,17},{... | collective-permute-start | bytes 442376 | tf_op jit(solution)/shard_map/ppermute | solution.py:654
  14.1 0.6 %collective-permute-done.3.theirs.rest_1_ = f32[2,8,2304]{2,1,0:T(8,128)S(1)} collective-permute-done((f32[2,8,2304]{2,1,0:T(8,128)S(1)}, f32[2,8,2304]{2,1,0:T(8,128)S(1)}, u32[]{:S(2)}, u32[]{:S(2)}) %collective-permute-start.3) | collective-permute-done | bytes 147488 | tf_op jit(solution)/shard_map/ppermute | solution.py:654
  14.7 0.1 relay.4
  14.8 1.4 %collective-permute-start.4 = (f32[2,8,2304]{2,1,0:T(8,128)S(1)}, f32[2,8,2304]{2,1,0:T(8,128)S(1)}, u32[]{:S(2)}, u32[]{:S(2)}) collective-permute-start(f32[2,8,2304]{2,1,0:T(8,128)S(1)} %relay.4), channel_id=1, source_target_pairs={{0,16},{4,12},{8,24},{12,4},{16,0},{20,28},{24,8},{28,20},{1,17},{... | collective-permute-start | bytes 442376 | tf_op jit(solution)/shard_map/ppermute | solution.py:654
  16.2 1.0 %collective-permute-done.6.rest_2_ = f32[2,8,2304]{2,1,0:T(8,128)S(1)} collective-permute-done((f32[2,8,2304]{2,1,0:T(8,128)S(1)}, f32[2,8,2304]{2,1,0:T(8,128)S(1)}, u32[]{:S(2)}, u32[]{:S(2)}) %collective-permute-start.6) | collective-permute-done | bytes 147488 | tf_op jit(solution)/shard_map/ppermute | solution.py:654
  17.2 0.5 %inner_first_sweep.1 = (f32[16,8,2048]{2,1,0:T(8,128)S(1)}, f32[16,8,2048]{2,1,0:T(8,128)S(1)}, f32[16,16,128]{2,1,0:T(8,128)S(1)}) custom-call(f32[16,8,2304]{2,1,0:T(8,128)S(1)} %get-tuple-element.44.raw_ref, f32[4,8,2304]{2,1,0:T(8,128)S(1)} %get-tuple-element.45.factor_ref.refs_7_.refs_5_.refs_2_, ...), custom_call_target="tpu_custom_call" | custom-call | bytes 3700000 | tf_op jit(solution)/shard_map/inner_first_sweep/pallas_call | solution.py:615
  17.7 2.3 %collective-permute-done.4.rest_2_ = f32[2,8,2304]{2,1,0:T(8,128)S(1)} collective-permute-done((f32[2,8,2304]{2,1,0:T(8,128)S(1)}, f32[2,8,2304]{2,1,0:T(8,128)S(1)}, u32[]{:S(2)}, u32[]{:S(2)}) %collective-permute-start.4) | collective-permute-done | bytes 147488 | tf_op jit(solution)/shard_map/ppermute | solution.py:654
  20.0 0.5 %outer_first_sweep.1 = (f32[16,8,2048]{2,1,0:T(8,128)S(1)}, f32[16,8,2048]{2,1,0:T(8,128)S(1)}, f32[16,16,128]{2,1,0:T(8,128)S(1)}) custom-call(f32[16,8,2304]{2,1,0:T(8,128)S(1)} %get-tuple-element.38.raw_ref, f32[4,8,2304]{2,1,0:T(8,128)S(1)} %get-tuple-element.39.factor_ref.refs_3_.refs_2_.refs_8_, f32[2,8,2304]{2,1,0:T(8,128)S(1)} %get-tuple-element.40.mine.rest_0_, ...), custom_call_target="tpu_custom_call" | custom-call | bytes 3700000 | tf_op jit(solution)/shard_map/outer_first_sweep/pallas_call | solution.py:615
  20.5 2.1 %couplings.1 = (f32[8,16,2048]{2,1,0:T(8,128)S(1)}, f32[11,16,2048]{2,1,0:T(8,128)S(1)}, f32[2,16,2048]{2,1,0:T(8,128)S(1)}, f32[2,8,2048]{2,1,0:T(8,128)S(1)}, f32[2,8,2048]{2,1,0:T(8,128)S(1)}) custom-call(f32[32,2048]{1,0:T(8,128)S(1)} %get-tuple-element.31.slab, f32[3,32,2048]{2,1,0:T(8,128)S(1)} %copy-done, ...), custom_call_target="tpu_custom_call" | custom-call | bytes 11100000 | tf_op jit(solution)/shard_map/couplings/pallas_call | solution.py:615
  22.7 1.0 %collective-permute-start.11 = (f32[2,8,2048]{2,1,0:T(8,128)S(1)}, f32[2,8,2048]{2,1,0:T(8,128)S(1)}, u32[]{:S(2)}, u32[]{:S(2)}) collective-permute-start(f32[2,8,2048]{2,1,0:T(8,128)S(1)} %get-tuple-element.54.mine.rest_0_), channel_id=1, source_target_pairs={{0,8},{4,20},{8,0},{12,28},{16,24},{20,4},{24,16},{28,12},{1,9},{5... | collective-permute-start | bytes 393224 | tf_op jit(solution)/shard_map/ppermute | solution.py:654
  23.8 1.1 %collective-permute-start.8 = (f32[2,8,2048]{2,1,0:T(8,128)S(1)}, f32[2,8,2048]{2,1,0:T(8,128)S(1)}, u32[]{:S(2)}, u32[]{:S(2)}) collective-permute-start(f32[2,8,2048]{2,1,0:T(8,128)S(1)} %get-tuple-element.51.mine.rest_0_), channel_id=1, source_target_pairs={{0,8},{4,20},{8,0},{12,28},{16,24},{20,4},{24,16},{28,12},{1,9},{5... | collective-permute-start | bytes 393224 | tf_op jit(solution)/shard_map/ppermute | solution.py:654
  24.8 2.9 %collective-permute-done.11.theirs.rest_1_ = f32[2,8,2048]{2,1,0:T(8,128)S(1)} collective-permute-done((f32[2,8,2048]{2,1,0:T(8,128)S(1)}, f32[2,8,2048]{2,1,0:T(8,128)S(1)}, u32[]{:S(2)}, u32[]{:S(2)}) %collective-permute-start.11) | collective-permute-done | bytes 131104 | tf_op jit(solution)/shard_map/ppermute | solution.py:654
  27.8 0.1 relay.7
  27.9 1.4 %collective-permute-start.12 = (f32[2,8,2048]{2,1,0:T(8,128)S(1)}, f32[2,8,2048]{2,1,0:T(8,128)S(1)}, u32[]{:S(2)}, u32[]{:S(2)}) collective-permute-start(f32[2,8,2048]{2,1,0:T(8,128)S(1)} %relay.7), channel_id=1, source_target_pairs={{0,16},{4,12},{8,24},{12,4},{16,0},{20,28},{24,8},{28,20},{1,17},{... | collective-permute-start | bytes 393224 | tf_op jit(solution)/shard_map/ppermute | solution.py:654
  29.3 0.1 relay.6
  29.4 1.3 %collective-permute-start.9 = (f32[2,8,2048]{2,1,0:T(8,128)S(1)}, f32[2,8,2048]{2,1,0:T(8,128)S(1)}, u32[]{:S(2)}, u32[]{:S(2)}) collective-permute-start(f32[2,8,2048]{2,1,0:T(8,128)S(1)} %relay.6), channel_id=1, source_target_pairs={{0,16},{4,12},{8,24},{12,4},{16,0},{20,28},{24,8},{28,20},{1,17},{... | collective-permute-start | bytes 393224 | tf_op jit(solution)/shard_map/ppermute | solution.py:654
  30.7 2.2 %collective-permute-done.12.rest_2_ = f32[2,8,2048]{2,1,0:T(8,128)S(1)} collective-permute-done((f32[2,8,2048]{2,1,0:T(8,128)S(1)}, f32[2,8,2048]{2,1,0:T(8,128)S(1)}, u32[]{:S(2)}, u32[]{:S(2)}) %collective-permute-start.12) | collective-permute-done | bytes 131104 | tf_op jit(solution)/shard_map/ppermute | solution.py:654
  32.9 0.2 outer_entering.1
  33.2 1.3 %collective-permute-done.9.rest_2_ = f32[2,8,2048]{2,1,0:T(8,128)S(1)} collective-permute-done((f32[2,8,2048]{2,1,0:T(8,128)S(1)}, f32[2,8,2048]{2,1,0:T(8,128)S(1)}, u32[]{:S(2)}, u32[]{:S(2)}) %collective-permute-start.9) | collective-permute-done | bytes 131104 | tf_op jit(solution)/shard_map/ppermute | solution.py:654
  34.4 0.2 inner_entering.1
  34.7 1.3 %finish.2 = (f32[4,32,2048]{2,1,0:T(8,128)}, f32[4,32,2048]{2,1,0:T(8,128)}) custom-call(f32[8,16,2048]{2,1,0:T(8,128)S(1)} %get-tuple-element.53.refs_0_.refs_3_, f32[2,8,2048]{2,1,0:T(8,128)S(1)} %get-tuple-element.55.refs_1_, f32[4,8,2304]{2,1,0:T(8,128)S(1)} %get-tuple-element.39.factor_ref.refs_3_.refs_2_.refs_8_, ...), custom_call_target="tpu_custom_call" | custom-call | bytes 3700000 | tf_op jit(solution)/shard_map/finish/pallas_call | solution.py:615
  36.0 0.9 %finish.3 = (f32[4,32,2048]{2,1,0:T(8,128)}, f32[4,32,2048]{2,1,0:T(8,128)}) custom-call(f32[11,16,2048]{2,1,0:T(8,128)S(1)} %collective-permute-done.7.refs_6_.refs_0_, f32[2,8,2048]{2,1,0:T(8,128)S(1)} %collective-permute-done.10.refs_1_, ...), custom_call_target="tpu_custom_call", output_to_operand_aliasing={{0}: (3, {}), {1}: (4, {})} | custom-call | bytes 3700000 | tf_op jit(solution)/shard_map/finish/pallas_call | solution.py:615
  (12 shorter events, 0.3 us)
Async XLA Ops:
  2.4 3.2 %collective-permute-start.1 = (f32[2,4,16,2176]{3,2,1,0:T(8,128)S(1)}, f32[2,4,16,2176]{3,2,1,0:T(8,128)S(1)}, u32[]{:S(2)}, u32[]{:S(2)}) collective-permute-start(f32[2,4,16,2176]{3,2,1,0:T(8,128)S(1)} %get-tuple-element.34), channel_id=1, source_target_pairs={{0,4},{4,0},{8,12},{12,8},{16,20},{20,16},{24,28},{28,24},{1,5},{5... | collective-permute-start | bytes 3342344 | tf_op jit(solution)/shard_map/ppermute | solution.py:591
  2.9 5.8 %collective-permute-start = (f32[10,16,128]{2,1,0:T(8,128)S(1)}, f32[10,16,128]{2,1,0:T(8,128)S(1)}, u32[]{:S(2)}, u32[]{:S(2)}) collective-permute-start(f32[10,16,128]{2,1,0:T(8,128)S(1)} %get-tuple-element.32), channel_id=1, source_target_pairs={{0,16},{1,4},{2,5},{3,6},{4,1},{5,2},{6,3},{7,15},{8,24},{9,12},{1... | collective-permute-start | bytes 245768 | tf_op jit(solution)/shard_map/ppermute | solution.py:601
  5.5 3.2 %collective-permute-start.2 = (f32[8,16,128]{2,1,0:T(8,128)S(1)}, f32[8,16,128]{2,1,0:T(8,128)S(1)}, u32[]{:S(2)}, u32[]{:S(2)}) collective-permute-start(f32[8,16,128]{2,1,0:T(8,128)S(1)} %get-tuple-element.36), channel_id=1, source_target_pairs={{0,1},{1,2},{2,3},{3,7},{4,0},{5,4},{6,5},{7,6},{8,9},{9,10},{10,1... | collective-permute-start | bytes 196616 | tf_op jit(solution)/shard_map/ppermute | solution.py:610
  6.1 5.7 %collective-permute-start.5 = (f32[2,8,2304]{2,1,0:T(8,128)S(1)}, f32[2,8,2304]{2,1,0:T(8,128)S(1)}, u32[]{:S(2)}, u32[]{:S(2)}) collective-permute-start(f32[2,8,2304]{2,1,0:T(8,128)S(1)} %get-tuple-element.37.rest_2_.mine.rest_0_), channel_id=1, source_target_pairs={{0,8},{4,20},{8,0},{12,28},{16,24},{20,4},{24,16},{28,12},{1,9},{5... | collective-permute-start | bytes 442376 | tf_op jit(solution)/shard_map/ppermute | solution.py:654
  9.3 5.4 %collective-permute-start.3 = (f32[2,8,2304]{2,1,0:T(8,128)S(1)}, f32[2,8,2304]{2,1,0:T(8,128)S(1)}, u32[]{:S(2)}, u32[]{:S(2)}) collective-permute-start(f32[2,8,2304]{2,1,0:T(8,128)S(1)} %get-tuple-element.40.mine.rest_0_), channel_id=1, source_target_pairs={{0,8},{4,20},{8,0},{12,28},{16,24},{20,4},{24,16},{28,12},{1,9},{5... | collective-permute-start | bytes 442376 | tf_op jit(solution)/shard_map/ppermute | solution.py:654
  12.0 5.2 %collective-permute-start.6 = (f32[2,8,2304]{2,1,0:T(8,128)S(1)}, f32[2,8,2304]{2,1,0:T(8,128)S(1)}, u32[]{:S(2)}, u32[]{:S(2)}) collective-permute-start(f32[2,8,2304]{2,1,0:T(8,128)S(1)} %relay.5), channel_id=1, source_target_pairs={{0,16},{4,12},{8,24},{12,4},{16,0},{20,28},{24,8},{28,20},{1,17},{... | collective-permute-start | bytes 442376 | tf_op jit(solution)/shard_map/ppermute | solution.py:654
  14.8 5.2 %collective-permute-start.4 = (f32[2,8,2304]{2,1,0:T(8,128)S(1)}, f32[2,8,2304]{2,1,0:T(8,128)S(1)}, u32[]{:S(2)}, u32[]{:S(2)}) collective-permute-start(f32[2,8,2304]{2,1,0:T(8,128)S(1)} %relay.4), channel_id=1, source_target_pairs={{0,16},{4,12},{8,24},{12,4},{16,0},{20,28},{24,8},{28,20},{1,17},{... | collective-permute-start | bytes 442376 | tf_op jit(solution)/shard_map/ppermute | solution.py:654
  17.7 2.8 %copy-start = (f32[3,32,2048]{2,1,0:T(8,128)S(1)}, f32[3,32,2048]{2,1,0:T(8,128)}, u32[]{:S(2)}) copy-start(f32[3,32,2048]{2,1,0:T(8,128)} %velocity_ref.1) | copy-start | bytes 2359300
  22.6 12.0 %collective-permute-start.7 = (f32[11,16,2048]{2,1,0:T(8,128)S(1)}, f32[11,16,2048]{2,1,0:T(8,128)S(1)}, u32[]{:S(2)}, u32[]{:S(2)}) collective-permute-start(f32[11,16,2048]{2,1,0:T(8,128)S(1)} %get-tuple-element.49), channel_id=1, source_target_pairs={{0,4},{4,0},{8,12},{12,8},{16,20},{20,16},{24,28},{28,24},{1,5},{5... | collective-permute-start | bytes 4325384 | tf_op jit(solution)/shard_map/ppermute | solution.py:591
  22.7 5.0 %collective-permute-start.11 = (f32[2,8,2048]{2,1,0:T(8,128)S(1)}, f32[2,8,2048]{2,1,0:T(8,128)S(1)}, u32[]{:S(2)}, u32[]{:S(2)}) collective-permute-start(f32[2,8,2048]{2,1,0:T(8,128)S(1)} %get-tuple-element.54.mine.rest_0_), channel_id=1, source_target_pairs={{0,8},{4,20},{8,0},{12,28},{16,24},{20,4},{24,16},{28,12},{1,9},{5... | collective-permute-start | bytes 393224 | tf_op jit(solution)/shard_map/ppermute | solution.py:654
  23.8 5.5 %collective-permute-start.8 = (f32[2,8,2048]{2,1,0:T(8,128)S(1)}, f32[2,8,2048]{2,1,0:T(8,128)S(1)}, u32[]{:S(2)}, u32[]{:S(2)}) collective-permute-start(f32[2,8,2048]{2,1,0:T(8,128)S(1)} %get-tuple-element.51.mine.rest_0_), channel_id=1, source_target_pairs={{0,8},{4,20},{8,0},{12,28},{16,24},{20,4},{24,16},{28,12},{1,9},{5... | collective-permute-start | bytes 393224 | tf_op jit(solution)/shard_map/ppermute | solution.py:654
  27.9 5.0 %collective-permute-start.12 = (f32[2,8,2048]{2,1,0:T(8,128)S(1)}, f32[2,8,2048]{2,1,0:T(8,128)S(1)}, u32[]{:S(2)}, u32[]{:S(2)}) collective-permute-start(f32[2,8,2048]{2,1,0:T(8,128)S(1)} %relay.7), channel_id=1, source_target_pairs={{0,16},{4,12},{8,24},{12,4},{16,0},{20,28},{24,8},{28,20},{1,17},{... | collective-permute-start | bytes 393224 | tf_op jit(solution)/shard_map/ppermute | solution.py:654
  29.4 5.0 %collective-permute-start.9 = (f32[2,8,2048]{2,1,0:T(8,128)S(1)}, f32[2,8,2048]{2,1,0:T(8,128)S(1)}, u32[]{:S(2)}, u32[]{:S(2)}) collective-permute-start(f32[2,8,2048]{2,1,0:T(8,128)S(1)} %relay.6), channel_id=1, source_target_pairs={{0,16},{4,12},{8,24},{12,4},{16,0},{20,28},{24,8},{28,20},{1,17},{... | collective-permute-start | bytes 393224 | tf_op jit(solution)/shard_map/ppermute | solution.py:654
  33.1 1.6 %collective-permute-start.13 = (f32[2,8,2048]{2,1,0:T(8,128)S(1)}, f32[2,8,2048]{2,1,0:T(8,128)S(1)}, u32[]{:S(2)}, u32[]{:S(2)}) collective-permute-start(f32[2,8,2048]{2,1,0:T(8,128)S(1)} %get-tuple-element.57), channel_id=1, source_target_pairs={{0,4},{4,0},{8,12},{12,8},{16,20},{20,16},{24,28},{28,24},{1,5},{5... | collective-permute-start | bytes 393224 | tf_op jit(solution)/shard_map/ppermute | solution.py:591
  34.6 1.4 %collective-permute-start.10 = (f32[2,8,2048]{2,1,0:T(8,128)S(1)}, f32[2,8,2048]{2,1,0:T(8,128)S(1)}, u32[]{:S(2)}, u32[]{:S(2)}) collective-permute-start(f32[2,8,2048]{2,1,0:T(8,128)S(1)} %get-tuple-element.52), channel_id=1, source_target_pairs={{0,4},{4,0},{8,12},{12,8},{16,20},{20,16},{24,28},{28,24},{1,5},{5... | collective-permute-start | bytes 393224 | tf_op jit(solution)/shard_map/ppermute | solution.py:591

commit v9 on v8

--- a/solution.py
+++ b/solution.py
@@ -16,8 +16,21 @@
 gamma_couple = 0.5
 
 
+FIXED = []
+
+
 def this_core():
-    return lax.rem(lax.axis_index("tm"), 2)
+    return FIXED[-1] if FIXED else lax.rem(lax.axis_index("tm"), 2)
+
+
+def pick(flag, one, other):
+    if isinstance(flag, bool):
+        return one if flag else other
+    return jnp.where(flag, one, other)
+
+
+def aligned(start, size):
+    return slice(start, start + size) if isinstance(start, int) else pl.ds(pl.multiple_of(start, 8), size)
 
 
 def this_chip():
@@ -81,12 +94,12 @@
     depth, cells = slab.shape
     tile = half // 2
     groups = cells // LANES
-    own = pl.ds(pl.multiple_of(tile_rows(side, half, depth), 8), tile)
+    own = aligned(tile_rows(side, half, depth), tile)
     here = lane_block(group * LANES)
     kappa = slab[own, here]
     left = slab[own, lane_block(jnp.maximum(group - 1, 0) * LANES)]
     right = slab[own, lane_block(jnp.minimum(group + 1, groups - 1) * LANES)]
-    mirrored = lambda row: jnp.where(core == 0, slab[row : row + 1, here], slab[depth - 1 - row : depth - row, here])
+    mirrored = lambda row: pick(core == 0, slab[row : row + 1, here], slab[depth - 1 - row : depth - row, here])
     outward = outer if side == OUTER else mirrored(tile - 1)
     inward = mirrored(tile if side == OUTER else half)
     first, last = edge_rows(kappa.shape)
@@ -110,7 +123,7 @@
 
 def cut_inside():
     slab = lax.axis_index("gz")
-    return jnp.where(this_core() == 0, slab > 0, slab < lax.axis_size("gz") - 1)
+    return pick(this_core() == 0, slab > 0, slab < lax.axis_size("gz") - 1)
 
 
 def edge_rows(shape):
@@ -219,7 +232,7 @@
         for group in range(cells // LANES):
             lanes = slice(group * LANES, (group + 1) * LANES)
             one, other = [source[row : row + 1, lanes] for row in rows]
-            target[group : group + 1, :] = jnp.where(core == 0, one, other)
+            target[group : group + 1, :] = pick(core == 0, one, other)
 
     slab_copy, *tile_copies = copies
     slab_copy.wait()
@@ -407,7 +420,19 @@
     return parts[0] if len(parts) == 1 else jnp.concatenate(parts, axis=1)
 
 
-def couplings_kernel(ratio, slab, velocity_ref, cut_ref, *refs):
+def couplings_kernel(ratio, *refs):
+    core = this_core()
+
+    def work(which):
+        FIXED.append(which)
+        couple_tiles(ratio, *refs)
+        FIXED.pop()
+
+    for which in range(2):
+        pl.when(core == which)(functools.partial(work, which))
+
+
+def couple_tiles(ratio, slab, velocity_ref, cut_ref, *refs):
     *results, outer_ends, inner_ends = refs[-5:]
     outer, inner = refs[:4], refs[4:8]
     work = functools.partial(couple_tile, ratio, slab, velocity_ref, cut_ref)
@@ -423,7 +448,7 @@
     half = 2 * tile
     groups = cells // LANES
     core = this_core()
-    own = pl.ds(pl.multiple_of(tile_rows(side, half, depth), 8), tile)
+    own = aligned(tile_rows(side, half, depth), tile)
     held = slice(side * tile, (side + 1) * tile)
     out_shift, in_shift = z_shifts(tile)
 
@@ -438,7 +463,7 @@
         low = lane < NY
         first, last = edge_rows((tile, LANES))
         drifts = [0.5 * velocity_ref[component, own, here] for component in (2, 0, 1)]
-        drifts[0] = jnp.where(core == 0, -drifts[0], drifts[0])
+        drifts[0] = pick(core == 0, -drifts[0], drifts[0])
         tables = []
         for sign in (1.0, -1.0):
             one_way, other_way = [], []
@@ -483,8 +508,8 @@
                 early, late = [
                     first_ref[2 * steps_local * sub + slot, :, here] + results[sub, step][field] for sub in range(2)
                 ]
-                keep[slot, held, here] = jnp.where(core == 0, early, late)
-                send[slot, held, here] = jnp.where(core == 0, late, early)
+                keep[slot, held, here] = pick(core == 0, early, late)
+                send[slot, held, here] = pick(core == 0, late, early)
         for slot, value in enumerate(finish_factors(ratio, factors)):
             send[2 * steps_local + slot, held, here] = value
         (early_back, early_last), (late_back, late_last) = ends
@@ -518,8 +543,8 @@
         early_back = middle[0, held, here] + block * back
         late_state = middle[1, held, here] + block * state + response_of(decay, upright, steps_local) * early_back
         for slot, (early, late) in enumerate(((early_back, back), (state, late_state))):
-            keep[slot, :, here] = jnp.where(core == 0, early, late)
-            send[slot, :, here] = jnp.where(core == 0, late, early)
+            keep[slot, :, here] = pick(core == 0, early, late)
+            send[slot, :, here] = pick(core == 0, late, early)
 
     each_block(cells, 4 * LANES, one)
 
@@ -530,7 +555,7 @@
     tile = depth // 4
     core = this_core()
     whole = step_scale(ratio, 2 * steps_local, chips, -1)
-    scales = [jnp.where(core == 0, whole[step], whole[steps_local + step]) for step in range(steps_local)]
+    scales = [pick(core == 0, whole[step], whole[steps_local + step]) for step in range(steps_local)]
     copies = []
     for job, (theirs, side) in enumerate(jobs):
         parts, entered, factor_ref = refs[3 * job : 3 * job + 3]

time: 37.1 us -> 36.9 us (level)
  no operation moved by 1% of the time
where the time goes in v9:
time: 36.9 us; the launch traced here: 36.7 us
  starting transfers between devices  15.5 us (42%)
  waiting for transfers between devices  11.7 us (32%)
  Pallas kernels  8.74 us (24%)
  between operations  0.74 us (2%)
    ppermute x8, starting transfers between devices, beside(): lax.ppermute(value, 'tm', [(i, i ^ masks[i % 2]) for i in range(ranks)])  12.1 us
    ppermute x8, waiting for transfers between devices, beside(): lax.ppermute(value, 'tm', [(i, i ^ masks[i % 2]) for i in range(ranks)])  11.7 us
    pallas_call x14, Pallas kernels, call(): pl.pallas_call(kernel, out_shape=shapes, compiler_params=pltpu.CompilerPa...  8.74 us
    ppermute x1, starting transfers between devices, outward(): return lax.ppermute(value, ('tm', 'gz'), pairs)  2.59 us
  transfers between devices with their start and end apart: 14, of which 7 were waited for; matrix products, arithmetic and copies ran while one was open for 0% of the time, Pallas kernels for 10%

profile of v9, /device:TPU:0, one launch (start us, length us, event | category | flops | bytes accessed | tf_op | source)
XLA Modules:
  0.0 36.7 jit_solution(4061090433113444753)
XLA Ops:
  0.6 1.7 %halves_and_layers.1 = (f32[2,4,16,2176]{3,2,1,0:T(8,128)S(1)}, f32[2,4,16,2176]{3,2,1,0:T(8,128)S(1)}, f32[32,2048]{1,0:T(8,128)S(1)}, f32[10,16,128]{2,1,0:T(8...) custom-call(f32[4,32,2048]{2,1,0:T(8,128)} %state.1, f32[4,32,2048]{2,1,0:T(8,128)} %adjoint.1, ...), custom_call_target="tpu_custom_call" | custom-call | bytes 7400000 | tf_op jit(solution)/shard_map/halves_and_layers/pallas_call | solution.py:640
  2.4 0.5 %collective-permute-start.1 = (f32[2,4,16,2176]{3,2,1,0:T(8,128)S(1)}, f32[2,4,16,2176]{3,2,1,0:T(8,128)S(1)}, u32[]{:S(2)}, u32[]{:S(2)}) collective-permute-start(f32[2,4,16,2176]{3,2,1,0:T(8,128)S(1)} %get-tuple-element.34), channel_id=1, source_target_pairs={{0,4},{4,0},{8,12},{12,8},{16,20},{20,16},{24,28},{28,24},{1,5},{5... | collective-permute-start | bytes 3342344 | tf_op jit(solution)/shard_map/ppermute | solution.py:616
  2.9 2.6 %collective-permute-start = (f32[10,16,128]{2,1,0:T(8,128)S(1)}, f32[10,16,128]{2,1,0:T(8,128)S(1)}, u32[]{:S(2)}, u32[]{:S(2)}) collective-permute-start(f32[10,16,128]{2,1,0:T(8,128)S(1)} %get-tuple-element.32), channel_id=1, source_target_pairs={{0,16},{1,4},{2,5},{3,6},{4,1},{5,2},{6,3},{7,15},{8,24},{9,12},{1... | collective-permute-start | bytes 245768 | tf_op jit(solution)/shard_map/ppermute | solution.py:626
  5.5 0.1 collective-permute-start.2
  5.6 0.5 %inner_ends.1 = (f32[16,8,2304]{2,1,0:T(8,128)S(1)}, f32[4,8,2304]{2,1,0:T(8,128)S(1)}, f32[2,8,2304]{2,1,0:T(8,128)S(1)}) custom-call(f32[2,4,16,2176]{3,2,1,0:T(8,128)S(1)} %get-tuple-element.33.keep, f32[2,4,16,2176]{3,2,1,0:T(8,128)S(1)} %collective-permute-done.1.other, f32[32,2048]{1,0:T(8,128)S(1)} %get-tuple-element.31.slab.refs_0_, ...), custom_call_target="tpu_custom_call" | custom-call | bytes 3700000 | tf_op jit(solution)/shard_map/inner_ends/pallas_call | solution.py:640
  6.1 2.6 %collective-permute-start.5 = (f32[2,8,2304]{2,1,0:T(8,128)S(1)}, f32[2,8,2304]{2,1,0:T(8,128)S(1)}, u32[]{:S(2)}, u32[]{:S(2)}) collective-permute-start(f32[2,8,2304]{2,1,0:T(8,128)S(1)} %get-tuple-element.37.rest_2_.mine.rest_0_), channel_id=1, source_target_pairs={{0,8},{4,20},{8,0},{12,28},{16,24},{20,4},{24,16},{28,12},{1,9},{5... | collective-permute-start | bytes 442376 | tf_op jit(solution)/shard_map/ppermute | solution.py:679
  8.7 0.5 %outer_ends.1 = (f32[16,8,2304]{2,1,0:T(8,128)S(1)}, f32[4,8,2304]{2,1,0:T(8,128)S(1)}, f32[2,8,2304]{2,1,0:T(8,128)S(1)}) custom-call(f32[2,4,16,2176]{3,2,1,0:T(8,128)S(1)} %get-tuple-element.33.keep, f32[2,4,16,2176]{3,2,1,0:T(8,128)S(1)} %collective-permute-done.1.other, f32[32,2048]{1,0:T(8,128)S(1)} %get-tuple-element.31.slab.refs_0_, ...), custom_call_target="tpu_custom_call" | custom-call | bytes 3700000 | tf_op jit(solution)/shard_map/outer_ends/pallas_call | solution.py:640
  9.3 1.2 %collective-permute-start.3 = (f32[2,8,2304]{2,1,0:T(8,128)S(1)}, f32[2,8,2304]{2,1,0:T(8,128)S(1)}, u32[]{:S(2)}, u32[]{:S(2)}) collective-permute-start(f32[2,8,2304]{2,1,0:T(8,128)S(1)} %get-tuple-element.40.mine.rest_0_), channel_id=1, source_target_pairs={{0,8},{4,20},{8,0},{12,28},{16,24},{20,4},{24,16},{28,12},{1,9},{5... | collective-permute-start | bytes 442376 | tf_op jit(solution)/shard_map/ppermute | solution.py:679
  10.5 1.4 %collective-permute-done.5.theirs.rest_1_ = f32[2,8,2304]{2,1,0:T(8,128)S(1)} collective-permute-done((f32[2,8,2304]{2,1,0:T(8,128)S(1)}, f32[2,8,2304]{2,1,0:T(8,128)S(1)}, u32[]{:S(2)}, u32[]{:S(2)}) %collective-permute-start.5) | collective-permute-done | bytes 147488 | tf_op jit(solution)/shard_map/ppermute | solution.py:679
  11.9 0.1 relay.5
  12.0 2.1 %collective-permute-start.6 = (f32[2,8,2304]{2,1,0:T(8,128)S(1)}, f32[2,8,2304]{2,1,0:T(8,128)S(1)}, u32[]{:S(2)}, u32[]{:S(2)}) collective-permute-start(f32[2,8,2304]{2,1,0:T(8,128)S(1)} %relay.5), channel_id=1, source_target_pairs={{0,16},{4,12},{8,24},{12,4},{16,0},{20,28},{24,8},{28,20},{1,17},{... | collective-permute-start | bytes 442376 | tf_op jit(solution)/shard_map/ppermute | solution.py:679
  14.1 0.6 %collective-permute-done.3.theirs.rest_1_ = f32[2,8,2304]{2,1,0:T(8,128)S(1)} collective-permute-done((f32[2,8,2304]{2,1,0:T(8,128)S(1)}, f32[2,8,2304]{2,1,0:T(8,128)S(1)}, u32[]{:S(2)}, u32[]{:S(2)}) %collective-permute-start.3) | collective-permute-done | bytes 147488 | tf_op jit(solution)/shard_map/ppermute | solution.py:679
  14.7 0.1 relay.4
  14.8 1.4 %collective-permute-start.4 = (f32[2,8,2304]{2,1,0:T(8,128)S(1)}, f32[2,8,2304]{2,1,0:T(8,128)S(1)}, u32[]{:S(2)}, u32[]{:S(2)}) collective-permute-start(f32[2,8,2304]{2,1,0:T(8,128)S(1)} %relay.4), channel_id=1, source_target_pairs={{0,16},{4,12},{8,24},{12,4},{16,0},{20,28},{24,8},{28,20},{1,17},{... | collective-permute-start | bytes 442376 | tf_op jit(solution)/shard_map/ppermute | solution.py:679
  16.2 1.0 %collective-permute-done.6.rest_2_ = f32[2,8,2304]{2,1,0:T(8,128)S(1)} collective-permute-done((f32[2,8,2304]{2,1,0:T(8,128)S(1)}, f32[2,8,2304]{2,1,0:T(8,128)S(1)}, u32[]{:S(2)}, u32[]{:S(2)}) %collective-permute-start.6) | collective-permute-done | bytes 147488 | tf_op jit(solution)/shard_map/ppermute | solution.py:679
  17.2 0.5 %inner_first_sweep.1 = (f32[16,8,2048]{2,1,0:T(8,128)S(1)}, f32[16,8,2048]{2,1,0:T(8,128)S(1)}, f32[16,16,128]{2,1,0:T(8,128)S(1)}) custom-call(f32[16,8,2304]{2,1,0:T(8,128)S(1)} %get-tuple-element.44.raw_ref, f32[4,8,2304]{2,1,0:T(8,128)S(1)} %get-tuple-element.45.factor_ref.refs_10_.refs_5_.refs_2_, ...), custom_call_target="tpu_custom_call" | custom-call | bytes 3700000 | tf_op jit(solution)/shard_map/inner_first_sweep/pallas_call | solution.py:640
  17.7 2.3 %collective-permute-done.4.rest_2_ = f32[2,8,2304]{2,1,0:T(8,128)S(1)} collective-permute-done((f32[2,8,2304]{2,1,0:T(8,128)S(1)}, f32[2,8,2304]{2,1,0:T(8,128)S(1)}, u32[]{:S(2)}, u32[]{:S(2)}) %collective-permute-start.4) | collective-permute-done | bytes 147488 | tf_op jit(solution)/shard_map/ppermute | solution.py:679
  20.0 0.5 %outer_first_sweep.1 = (f32[16,8,2048]{2,1,0:T(8,128)S(1)}, f32[16,8,2048]{2,1,0:T(8,128)S(1)}, f32[16,16,128]{2,1,0:T(8,128)S(1)}) custom-call(f32[16,8,2304]{2,1,0:T(8,128)S(1)} %get-tuple-element.38.raw_ref, f32[4,8,2304]{2,1,0:T(8,128)S(1)} %get-tuple-element.39.factor_ref.refs_6_.refs_2_.refs_8_, f32[2,8,2304]{2,1,0:T(8,128)S(1)} %get-tuple-element.40.mine.rest_0_, ...), custom_call_target="tpu_custom_call" | custom-call | bytes 3700000 | tf_op jit(solution)/shard_map/outer_first_sweep/pallas_call | solution.py:640
  20.5 2.0 %couplings.1 = (f32[8,16,2048]{2,1,0:T(8,128)S(1)}, f32[11,16,2048]{2,1,0:T(8,128)S(1)}, f32[2,16,2048]{2,1,0:T(8,128)S(1)}, f32[2,8,2048]{2,1,0:T(8,128)S(1)}, f32[2,8,2048]{2,1,0:T(8,128)S(1)}) custom-call(f32[32,2048]{1,0:T(8,128)S(1)} %get-tuple-element.31.slab.refs_0_, f32[3,32,2048]{2,1,0:T(8,128)S(1)} %copy-done, ...), custom_call_target="tpu_custom_call" | custom-call | bytes 11100000 | tf_op jit(solution)/shard_map/couplings/pallas_call | solution.py:640
  22.6 1.0 %collective-permute-start.11 = (f32[2,8,2048]{2,1,0:T(8,128)S(1)}, f32[2,8,2048]{2,1,0:T(8,128)S(1)}, u32[]{:S(2)}, u32[]{:S(2)}) collective-permute-start(f32[2,8,2048]{2,1,0:T(8,128)S(1)} %get-tuple-element.54.mine.rest_0_), channel_id=1, source_target_pairs={{0,8},{4,20},{8,0},{12,28},{16,24},{20,4},{24,16},{28,12},{1,9},{5... | collective-permute-start | bytes 393224 | tf_op jit(solution)/shard_map/ppermute | solution.py:679
  23.6 1.1 %collective-permute-start.8 = (f32[2,8,2048]{2,1,0:T(8,128)S(1)}, f32[2,8,2048]{2,1,0:T(8,128)S(1)}, u32[]{:S(2)}, u32[]{:S(2)}) collective-permute-start(f32[2,8,2048]{2,1,0:T(8,128)S(1)} %get-tuple-element.51.mine.rest_0_), channel_id=1, source_target_pairs={{0,8},{4,20},{8,0},{12,28},{16,24},{20,4},{24,16},{28,12},{1,9},{5... | collective-permute-start | bytes 393224 | tf_op jit(solution)/shard_map/ppermute | solution.py:679
  24.7 2.9 %collective-permute-done.11.theirs.rest_1_ = f32[2,8,2048]{2,1,0:T(8,128)S(1)} collective-permute-done((f32[2,8,2048]{2,1,0:T(8,128)S(1)}, f32[2,8,2048]{2,1,0:T(8,128)S(1)}, u32[]{:S(2)}, u32[]{:S(2)}) %collective-permute-start.11) | collective-permute-done | bytes 131104 | tf_op jit(solution)/shard_map/ppermute | solution.py:679
  27.6 0.1 relay.7
  27.7 1.4 %collective-permute-start.12 = (f32[2,8,2048]{2,1,0:T(8,128)S(1)}, f32[2,8,2048]{2,1,0:T(8,128)S(1)}, u32[]{:S(2)}, u32[]{:S(2)}) collective-permute-start(f32[2,8,2048]{2,1,0:T(8,128)S(1)} %relay.7), channel_id=1, source_target_pairs={{0,16},{4,12},{8,24},{12,4},{16,0},{20,28},{24,8},{28,20},{1,17},{... | collective-permute-start | bytes 393224 | tf_op jit(solution)/shard_map/ppermute | solution.py:679
  29.1 0.1 relay.6
  29.2 1.3 %collective-permute-start.9 = (f32[2,8,2048]{2,1,0:T(8,128)S(1)}, f32[2,8,2048]{2,1,0:T(8,128)S(1)}, u32[]{:S(2)}, u32[]{:S(2)}) collective-permute-start(f32[2,8,2048]{2,1,0:T(8,128)S(1)} %relay.6), channel_id=1, source_target_pairs={{0,16},{4,12},{8,24},{12,4},{16,0},{20,28},{24,8},{28,20},{1,17},{... | collective-permute-start | bytes 393224 | tf_op jit(solution)/shard_map/ppermute | solution.py:679
  30.5 2.2 %collective-permute-done.12.rest_2_ = f32[2,8,2048]{2,1,0:T(8,128)S(1)} collective-permute-done((f32[2,8,2048]{2,1,0:T(8,128)S(1)}, f32[2,8,2048]{2,1,0:T(8,128)S(1)}, u32[]{:S(2)}, u32[]{:S(2)}) %collective-permute-start.12) | collective-permute-done | bytes 131104 | tf_op jit(solution)/shard_map/ppermute | solution.py:679
  32.8 0.2 outer_entering.1
  33.0 1.3 %collective-permute-done.9.rest_2_ = f32[2,8,2048]{2,1,0:T(8,128)S(1)} collective-permute-done((f32[2,8,2048]{2,1,0:T(8,128)S(1)}, f32[2,8,2048]{2,1,0:T(8,128)S(1)}, u32[]{:S(2)}, u32[]{:S(2)}) %collective-permute-start.9) | collective-permute-done | bytes 131104 | tf_op jit(solution)/shard_map/ppermute | solution.py:679
  34.3 0.2 inner_entering.1
  34.5 1.3 %finish.2 = (f32[4,32,2048]{2,1,0:T(8,128)}, f32[4,32,2048]{2,1,0:T(8,128)}) custom-call(f32[8,16,2048]{2,1,0:T(8,128)S(1)} %get-tuple-element.53.refs_0_.refs_3_, f32[2,8,2048]{2,1,0:T(8,128)S(1)} %get-tuple-element.55.refs_1_, f32[4,8,2304]{2,1,0:T(8,128)S(1)} %get-tuple-element.39.factor_ref.refs_6_.refs_2_.refs_8_, ...), custom_call_target="tpu_custom_call" | custom-call | bytes 3700000 | tf_op jit(solution)/shard_map/finish/pallas_call | solution.py:640
  35.9 0.9 %finish.3 = (f32[4,32,2048]{2,1,0:T(8,128)}, f32[4,32,2048]{2,1,0:T(8,128)}) custom-call(f32[11,16,2048]{2,1,0:T(8,128)S(1)} %collective-permute-done.7.refs_6_.refs_0_, f32[2,8,2048]{2,1,0:T(8,128)S(1)} %collective-permute-done.10.refs_1_, ...), custom_call_target="tpu_custom_call", output_to_operand_aliasing={{0}: (3, {}), {1}: (4, {})} | custom-call | bytes 3700000 | tf_op jit(solution)/shard_map/finish/pallas_call | solution.py:640
  (12 shorter events, 0.3 us)
Async XLA Ops:
  2.4 3.2 %collective-permute-start.1 = (f32[2,4,16,2176]{3,2,1,0:T(8,128)S(1)}, f32[2,4,16,2176]{3,2,1,0:T(8,128)S(1)}, u32[]{:S(2)}, u32[]{:S(2)}) collective-permute-start(f32[2,4,16,2176]{3,2,1,0:T(8,128)S(1)} %get-tuple-element.34), channel_id=1, source_target_pairs={{0,4},{4,0},{8,12},{12,8},{16,20},{20,16},{24,28},{28,24},{1,5},{5... | collective-permute-start | bytes 3342344 | tf_op jit(solution)/shard_map/ppermute | solution.py:616
  2.9 5.8 %collective-permute-start = (f32[10,16,128]{2,1,0:T(8,128)S(1)}, f32[10,16,128]{2,1,0:T(8,128)S(1)}, u32[]{:S(2)}, u32[]{:S(2)}) collective-permute-start(f32[10,16,128]{2,1,0:T(8,128)S(1)} %get-tuple-element.32), channel_id=1, source_target_pairs={{0,16},{1,4},{2,5},{3,6},{4,1},{5,2},{6,3},{7,15},{8,24},{9,12},{1... | collective-permute-start | bytes 245768 | tf_op jit(solution)/shard_map/ppermute | solution.py:626
  5.5 3.2 %collective-permute-start.2 = (f32[8,16,128]{2,1,0:T(8,128)S(1)}, f32[8,16,128]{2,1,0:T(8,128)S(1)}, u32[]{:S(2)}, u32[]{:S(2)}) collective-permute-start(f32[8,16,128]{2,1,0:T(8,128)S(1)} %get-tuple-element.36), channel_id=1, source_target_pairs={{0,1},{1,2},{2,3},{3,7},{4,0},{5,4},{6,5},{7,6},{8,9},{9,10},{10,1... | collective-permute-start | bytes 196616 | tf_op jit(solution)/shard_map/ppermute | solution.py:635
  6.1 5.7 %collective-permute-start.5 = (f32[2,8,2304]{2,1,0:T(8,128)S(1)}, f32[2,8,2304]{2,1,0:T(8,128)S(1)}, u32[]{:S(2)}, u32[]{:S(2)}) collective-permute-start(f32[2,8,2304]{2,1,0:T(8,128)S(1)} %get-tuple-element.37.rest_2_.mine.rest_0_), channel_id=1, source_target_pairs={{0,8},{4,20},{8,0},{12,28},{16,24},{20,4},{24,16},{28,12},{1,9},{5... | collective-permute-start | bytes 442376 | tf_op jit(solution)/shard_map/ppermute | solution.py:679
  9.3 5.4 %collective-permute-start.3 = (f32[2,8,2304]{2,1,0:T(8,128)S(1)}, f32[2,8,2304]{2,1,0:T(8,128)S(1)}, u32[]{:S(2)}, u32[]{:S(2)}) collective-permute-start(f32[2,8,2304]{2,1,0:T(8,128)S(1)} %get-tuple-element.40.mine.rest_0_), channel_id=1, source_target_pairs={{0,8},{4,20},{8,0},{12,28},{16,24},{20,4},{24,16},{28,12},{1,9},{5... | collective-permute-start | bytes 442376 | tf_op jit(solution)/shard_map/ppermute | solution.py:679
  12.0 5.2 %collective-permute-start.6 = (f32[2,8,2304]{2,1,0:T(8,128)S(1)}, f32[2,8,2304]{2,1,0:T(8,128)S(1)}, u32[]{:S(2)}, u32[]{:S(2)}) collective-permute-start(f32[2,8,2304]{2,1,0:T(8,128)S(1)} %relay.5), channel_id=1, source_target_pairs={{0,16},{4,12},{8,24},{12,4},{16,0},{20,28},{24,8},{28,20},{1,17},{... | collective-permute-start | bytes 442376 | tf_op jit(solution)/shard_map/ppermute | solution.py:679
  14.8 5.2 %collective-permute-start.4 = (f32[2,8,2304]{2,1,0:T(8,128)S(1)}, f32[2,8,2304]{2,1,0:T(8,128)S(1)}, u32[]{:S(2)}, u32[]{:S(2)}) collective-permute-start(f32[2,8,2304]{2,1,0:T(8,128)S(1)} %relay.4), channel_id=1, source_target_pairs={{0,16},{4,12},{8,24},{12,4},{16,0},{20,28},{24,8},{28,20},{1,17},{... | collective-permute-start | bytes 442376 | tf_op jit(solution)/shard_map/ppermute | solution.py:679
  17.7 2.8 %copy-start = (f32[3,32,2048]{2,1,0:T(8,128)S(1)}, f32[3,32,2048]{2,1,0:T(8,128)}, u32[]{:S(2)}) copy-start(f32[3,32,2048]{2,1,0:T(8,128)} %refs_1_.1) | copy-start | bytes 2359300
  22.5 12.0 %collective-permute-start.7 = (f32[11,16,2048]{2,1,0:T(8,128)S(1)}, f32[11,16,2048]{2,1,0:T(8,128)S(1)}, u32[]{:S(2)}, u32[]{:S(2)}) collective-permute-start(f32[11,16,2048]{2,1,0:T(8,128)S(1)} %get-tuple-element.49), channel_id=1, source_target_pairs={{0,4},{4,0},{8,12},{12,8},{16,20},{20,16},{24,28},{28,24},{1,5},{5... | collective-permute-start | bytes 4325384 | tf_op jit(solution)/shard_map/ppermute | solution.py:616
  22.6 5.0 %collective-permute-start.11 = (f32[2,8,2048]{2,1,0:T(8,128)S(1)}, f32[2,8,2048]{2,1,0:T(8,128)S(1)}, u32[]{:S(2)}, u32[]{:S(2)}) collective-permute-start(f32[2,8,2048]{2,1,0:T(8,128)S(1)} %get-tuple-element.54.mine.rest_0_), channel_id=1, source_target_pairs={{0,8},{4,20},{8,0},{12,28},{16,24},{20,4},{24,16},{28,12},{1,9},{5... | collective-permute-start | bytes 393224 | tf_op jit(solution)/shard_map/ppermute | solution.py:679
  23.6 5.5 %collective-permute-start.8 = (f32[2,8,2048]{2,1,0:T(8,128)S(1)}, f32[2,8,2048]{2,1,0:T(8,128)S(1)}, u32[]{:S(2)}, u32[]{:S(2)}) collective-permute-start(f32[2,8,2048]{2,1,0:T(8,128)S(1)} %get-tuple-element.51.mine.rest_0_), channel_id=1, source_target_pairs={{0,8},{4,20},{8,0},{12,28},{16,24},{20,4},{24,16},{28,12},{1,9},{5... | collective-permute-start | bytes 393224 | tf_op jit(solution)/shard_map/ppermute | solution.py:679
  27.7 5.0 %collective-permute-start.12 = (f32[2,8,2048]{2,1,0:T(8,128)S(1)}, f32[2,8,2048]{2,1,0:T(8,128)S(1)}, u32[]{:S(2)}, u32[]{:S(2)}) collective-permute-start(f32[2,8,2048]{2,1,0:T(8,128)S(1)} %relay.7), channel_id=1, source_target_pairs={{0,16},{4,12},{8,24},{12,4},{16,0},{20,28},{24,8},{28,20},{1,17},{... | collective-permute-start | bytes 393224 | tf_op jit(solution)/shard_map/ppermute | solution.py:679
  29.2 5.0 %collective-permute-start.9 = (f32[2,8,2048]{2,1,0:T(8,128)S(1)}, f32[2,8,2048]{2,1,0:T(8,128)S(1)}, u32[]{:S(2)}, u32[]{:S(2)}) collective-permute-start(f32[2,8,2048]{2,1,0:T(8,128)S(1)} %relay.6), channel_id=1, source_target_pairs={{0,16},{4,12},{8,24},{12,4},{16,0},{20,28},{24,8},{28,20},{1,17},{... | collective-permute-start | bytes 393224 | tf_op jit(solution)/shard_map/ppermute | solution.py:679
  32.9 1.6 %collective-permute-start.13 = (f32[2,8,2048]{2,1,0:T(8,128)S(1)}, f32[2,8,2048]{2,1,0:T(8,128)S(1)}, u32[]{:S(2)}, u32[]{:S(2)}) collective-permute-start(f32[2,8,2048]{2,1,0:T(8,128)S(1)} %get-tuple-element.57), channel_id=1, source_target_pairs={{0,4},{4,0},{8,12},{12,8},{16,20},{20,16},{24,28},{28,24},{1,5},{5... | collective-permute-start | bytes 393224 | tf_op jit(solution)/shard_map/ppermute | solution.py:616
  34.4 1.4 %collective-permute-start.10 = (f32[2,8,2048]{2,1,0:T(8,128)S(1)}, f32[2,8,2048]{2,1,0:T(8,128)S(1)}, u32[]{:S(2)}, u32[]{:S(2)}) collective-permute-start(f32[2,8,2048]{2,1,0:T(8,128)S(1)} %get-tuple-element.52), channel_id=1, source_target_pairs={{0,4},{4,0},{8,12},{12,8},{16,20},{20,16},{24,28},{28,24},{1,5},{5... | collective-permute-start | bytes 393224 | tf_op jit(solution)/shard_map/ppermute | solution.py:616
